TPU v7x, 256 devices: a whole 4x4x8 slice. The times are simulated.
256 devices in a mesh: gx: 8 (over z), gy: 32 (over y, x, core).
Axes of the slice: x: 4, y: 4, z: 8, core: 2. Of those that a mesh axis runs over, the one named last changes fastest.
Arguments:
- source: float32 [2, 256, 1024, 256], P(None, 'gx', 'gy'), may hold values from -4 to 4
- wavenumber_sq: float32 [256, 1024, 256], P('gx', 'gy'), may hold values from 0.1 to 0.8
Outputs:
- fine_iterate: float32 [2, 256, 1024, 256], P(None, 'gx', 'gy')
- second_iterate: float32 [2, 128, 512, 128], P(None, 'gx', 'gy')
- third_iterate: float32 [2, 64, 256, 64], P(None, 'gx', 'gy')
- coarse_iterate: float32 [2, 32, 128, 32], P(None, 'gx', 'gy')
All inputs are finite; a program needn't handle non-finite values.
Results may differ from a plain program's by a relative error of at most 0.0001.
Values sent between devices are 32-bit elements; how exact they have to be, the bound alone decides.
No kernel may reach another device: no remote copies, remote signals or barrier semaphores. Data moves between devices by JAX's collectives and lax.ppermute only.
A program may use at most 192 MiB of HBM per device.

v0:
```python
import jax
import jax.numpy as jnp
from jax import lax
from jax.sharding import PartitionSpec as P

LEVELS = 3
COARSE_SWEEPS = 4


DAMPING = 0.8
SHIFT_IMAG = 0.5


def padded_2(array, sides, width):
    for axis, dim in sides:
        devices, length = (lax.axis_size(axis), array.shape[dim])
        up = [(i, (i + 1) % devices) for i in range(devices - 1)]
        down = [(j, i) for i, j in up]
        last = lax.slice_in_dim(array, length - width, length, axis=dim)
        initial = lax.slice_in_dim(array, 0, width, axis=dim)
        before = lax.ppermute(last, axis, up)
        after = lax.ppermute(initial, axis, down)
        array = jnp.concatenate([before, array, after], axis=dim)
    return array


def beside_all(padded):
    zpadded = jnp.pad(padded, ((0, 0), (0, 0), (0, 0), (1, 1)))
    middle = zpadded[:, 1:-1, 1:-1, :]
    sides = (
        padded[:, 2:, 1:-1, :]
        + padded[:, :-2, 1:-1, :]
        + padded[:, 1:-1, 2:, :]
        + padded[:, 1:-1, :-2, :]
    )
    return sides + middle[..., 2:] + middle[..., :-2]


def combine(field, neighbours, wavenum, spacing):
    real_part = (6.0 * field[0] - neighbours[0]) / spacing - wavenum * (
        field[0] + SHIFT_IMAG * field[1]
    )
    imag_part = (6.0 * field[1] - neighbours[1]) / spacing - wavenum * (
        field[1] - SHIFT_IMAG * field[0]
    )
    return jnp.stack([real_part, imag_part])


def divide(resid, wavenum, spacing):
    diag_real = 6.0 / spacing - wavenum
    diag_imag = SHIFT_IMAG * wavenum
    modulus = diag_real * diag_real + diag_imag * diag_imag
    return jnp.stack(
        [
            (resid[0] * diag_real + resid[1] * diag_imag) / modulus,
            (resid[1] * diag_real - resid[0] * diag_imag) / modulus,
        ]
    )


def halves(padded, axis):
    length = padded.shape[axis] - 2
    parts = [lax.slice_in_dim(padded, start, start + length - 1, 2, axis) for start in range(4)]
    return (parts[0] + 3.0 * parts[1] + 3.0 * parts[2] + parts[3]) / 8.0


def restrict_padded(padded):
    padded = jnp.pad(padded, ((0, 0), (0, 0), (0, 0), (1, 1)))
    return halves(halves(halves(padded, 1), 2), 3)


def coarsen(wavenum):
    xsize, ysize, zsize = wavenum.shape
    return wavenum.reshape(xsize // 2, 2, ysize // 2, 2, zsize // 2, 2).mean(axis=(1, 3, 5))


def body(source, wavenumber_sq):
    rhs_level = source
    wavenum = wavenumber_sq
    results = []
    for level_index in range(LEVELS):
        spacing = 4.0**level_index
        field = DAMPING * divide(rhs_level, wavenum, spacing)
        padded = padded_2(field, (("gx", 1), ("gy", 2)), 1)
        field = field + DAMPING * divide(
            rhs_level - combine(field, beside_all(padded), wavenum, spacing), wavenum, spacing
        )
        padded = padded_2(field, (("gx", 1), ("gy", 2)), 1)
        residual = rhs_level - combine(field, beside_all(padded), wavenum, spacing)
        results.append(field)
        rimmed = padded_2(residual, (("gx", 1), ("gy", 2)), 1)
        rhs_level = restrict_padded(rimmed)
        wavenum = coarsen(wavenum)
    spacing = 4.0**LEVELS
    field = DAMPING * divide(rhs_level, wavenum, spacing)
    for sweep_index in range(COARSE_SWEEPS - 1):
        padded = padded_2(field, (("gx", 1), ("gy", 2)), 1)
        field = field + DAMPING * divide(
            rhs_level - combine(field, beside_all(padded), wavenum, spacing), wavenum, spacing
        )
    return (results[0], results[1], results[2], field)


def solution(mesh):
    placed = (P(None, "gx", "gy", None), P("gx", "gy", None))
    return jax.shard_map(
        body,
        mesh=mesh,
        in_specs=placed,
        out_specs=(
            P(None, "gx", "gy", None),
            P(None, "gx", "gy", None),
            P(None, "gx", "gy", None),
            P(None, "gx", "gy", None),
        ),
        check_vma=False,
    )
```

profile of v0, /device:TPU:120, one launch (start us, length us, event | category | flops | bytes accessed | tf_op | source)
XLA Modules:
  0.0 403.0 jit_solution(1678375969638629022)
XLA Ops:
  3.5 5.0 %collective-permute-start.1 = (f32[2,1,32,256]{3,2,1,0:T(8,128)S(1)}, f32[2,1,32,256]{3,2,1,0:T(8,128)S(1)}, u32[]{:S(2)}, u32[]{:S(2)}) collective-permute-start(f32[2,1,32,256]{3,2,1,0:T(8,128)S(1)} %get-tuple-element.26), channel_id=1, source_target_pairs={{0,32},{32,64},{64,96},{96,128},{128,160},{160,192},{192,224},{1,3... | collective-permute-start | bytes 196616 | tf_op jit(solution)/shard_map/ppermute | solution.py:21
  10.5 5.4 %collective-permute-done = f32[2,1,32,256]{3,2,1,0:T(8,128)S(1)} collective-permute-done((f32[2,1,32,256]{3,2,1,0:T(8,128)S(1)}, f32[2,1,32,256]{3,2,1,0:T(8,128)S(1)}, u32[]{:S(2)}, u32[]{:S(2)}) %collective-permute-start) | collective-permute-done | bytes 65568 | tf_op jit(solution)/shard_map/ppermute | solution.py:22
  17.9 5.8 %collective-permute-start.2 = (f32[2,34,1,256]{3,2,1,0:T(1,128)S(1)}, f32[2,34,1,256]{3,2,1,0:T(1,128)S(1)}, u32[]{:S(2)}, u32[]{:S(2)}) collective-permute-start(f32[2,34,1,256]{3,2,1,0:T(1,128)S(1)} %get-tuple-element.21), channel_id=1, source_target_pairs={{1,0},{2,1},{3,2},{4,3},{5,4},{6,5},{7,6},{8,7},{9,8},{10,9},{11,1... | collective-permute-start | bytes 208904 | tf_op jit(solution)/shard_map/ppermute | solution.py:22
  42.8 4.7 %collective-permute-start.6 = (f32[2,34,1,256]{3,1,2,0:T(8,128)S(1)}, f32[2,34,1,256]{3,1,2,0:T(8,128)S(1)}, u32[]{:S(2)}, u32[]{:S(2)}) collective-permute-start(f32[2,34,1,256]{3,1,2,0:T(8,128)S(1)} %copy.22), channel_id=1, source_target_pairs={{1,0},{2,1},{3,2},{4,3},{5,4},{6,5},{7,6},{8,7},{9,8},{10,9},{11,1... | collective-permute-start | bytes 208904 | tf_op jit(solution)/shard_map/ppermute | solution.py:22
  49.6 5.8 %collective-permute-done.7 = f32[2,34,1,256]{3,1,2,0:T(8,128)S(1)} collective-permute-done((f32[2,34,1,256]{3,1,2,0:T(8,128)S(1)}, f32[2,34,1,256]{3,1,2,0:T(8,128)S(1)}, u32[]{:S(2)}, u32[]{:S(2)}) %collective-permute-start.7) | collective-permute-done | bytes 69664 | tf_op jit(solution)/shard_map/ppermute | solution.py:21
  63.2 3.9 collective-permute-start.9
  72.6 5.9 %collective-permute-start.11 = (f32[2,34,1,256]{3,2,1,0:T(1,128)S(1)}, f32[2,34,1,256]{3,2,1,0:T(1,128)S(1)}, u32[]{:S(2)}, u32[]{:S(2)}) collective-permute-start(f32[2,34,1,256]{3,2,1,0:T(1,128)S(1)} %get-tuple-element.17), channel_id=1, source_target_pairs={{1,0},{2,1},{3,2},{4,3},{5,4},{6,5},{7,6},{8,7},{9,8},{10,9},{11,1... | collective-permute-start | bytes 208904 | tf_op jit(solution)/shard_map/ppermute | solution.py:22
  78.5 68.4 %reshape.151 = f32[16,2,16,2,128,2]{5,4,3,2,1,0:T(8,128)} reshape(f32[32,32,256]{2,1,0:T(8,128)S(1)} %copy-done.1) | data formatting | bytes 2097152 | tf_op jit(solution)/shard_map/reshape | solution.py:74
  146.9 20.8 %reduce_sum.27 = f32[16,16,128]{2,1,0:T(8,128)S(1)} reduce(f32[16,2,16,2,128,2]{5,4,3,2,1,0:T(8,128)} %reshape.151, f32[]{:T(128)} %constant.33.clone.1), dimensions={1,3,5}, to_apply=%region_0.1 | reduce | flops 229376 | bytes 1179652 | tf_op jit(solution)/shard_map/reduce_sum | solution.py:74
  182.2 9.0 %slice.748 = f32[2,16,16,128]{3,2,1,0:T(8,128)S(1)} slice(f32[2,16,16,258]{3,2,1,0:T(8,128)S(1)} %add_multiply_fusion.1), slice={[0:2:1], [0:16:1], [0:16:1], [3:258:2]} | slice | bytes 524288 | tf_op jit(solution)/shard_map/slice | solution.py:63
  191.1 9.0 %slice.747 = f32[2,16,16,128]{3,2,1,0:T(8,128)S(1)} slice(f32[2,16,16,258]{3,2,1,0:T(8,128)S(1)} %add_multiply_fusion.1), slice={[0:2:1], [0:16:1], [0:16:1], [2:257:2]} | slice | bytes 524288 | tf_op jit(solution)/shard_map/slice | solution.py:63
  200.1 9.0 %slice.746 = f32[2,16,16,128]{3,2,1,0:T(8,128)S(1)} slice(f32[2,16,16,258]{3,2,1,0:T(8,128)S(1)} %add_multiply_fusion.1), slice={[0:2:1], [0:16:1], [0:16:1], [1:256:2]} | slice | bytes 524288 | tf_op jit(solution)/shard_map/slice | solution.py:63
  209.1 9.0 %slice.745 = f32[2,16,16,128]{3,2,1,0:T(8,128)S(1)} slice(f32[2,16,16,258]{3,2,1,0:T(8,128)S(1)} %add_multiply_fusion.1), slice={[0:2:1], [0:16:1], [0:16:1], [0:255:2]} | slice | bytes 524288 | tf_op jit(solution)/shard_map/slice | solution.py:63
  229.0 6.0 %collective-permute-start.14 = (f32[2,18,1,128]{3,2,1,0:T(1,128)S(1)}, f32[2,18,1,128]{3,2,1,0:T(1,128)S(1)}, u32[]{:S(2)}, u32[]{:S(2)}) collective-permute-start(f32[2,18,1,128]{3,2,1,0:T(1,128)S(1)} %get-tuple-element.41), channel_id=1, source_target_pairs={{1,0},{2,1},{3,2},{4,3},{5,4},{6,5},{7,6},{8,7},{9,8},{10,9},{11,1... | collective-permute-start | bytes 55304 | tf_op jit(solution)/shard_map/ppermute | solution.py:22
  247.8 5.8 %collective-permute-start.18 = (f32[2,18,1,128]{3,2,1,0:T(1,128)S(1)}, f32[2,18,1,128]{3,2,1,0:T(1,128)S(1)}, u32[]{:S(2)}, u32[]{:S(2)}) collective-permute-start(f32[2,18,1,128]{3,2,1,0:T(1,128)S(1)} %get-tuple-element.39), channel_id=1, source_target_pairs={{1,0},{2,1},{3,2},{4,3},{5,4},{6,5},{7,6},{8,7},{9,8},{10,9},{11,1... | collective-permute-start | bytes 55304 | tf_op jit(solution)/shard_map/ppermute | solution.py:22
  266.5 5.8 %collective-permute-start.23 = (f32[2,18,1,128]{3,2,1,0:T(1,128)S(1)}, f32[2,18,1,128]{3,2,1,0:T(1,128)S(1)}, u32[]{:S(2)}, u32[]{:S(2)}) collective-permute-start(f32[2,18,1,128]{3,2,1,0:T(1,128)S(1)} %get-tuple-element.37), channel_id=1, source_target_pairs={{1,0},{2,1},{3,2},{4,3},{5,4},{6,5},{7,6},{8,7},{9,8},{10,9},{11,1... | collective-permute-start | bytes 55304 | tf_op jit(solution)/shard_map/ppermute | solution.py:22
  272.3 9.8 %div.231 = f32[8,2,8,2,64,2]{5,4,3,2,1,0:T(8,128)} reshape(f32[16,16,128]{2,1,0:T(8,128)S(1)} %broadcast_multiply_fusion) | data formatting | bytes 262144 | tf_op jit(solution)/shard_map/div | solution.py:74
  282.1 4.0 reduce_sum.28
  303.1 5.8 %collective-permute-start.26 = (f32[2,10,1,64]{3,2,1,0:T(1,128)S(1)}, f32[2,10,1,64]{3,2,1,0:T(1,128)S(1)}, u32[]{:S(2)}, u32[]{:S(2)}) collective-permute-start(f32[2,10,1,64]{3,2,1,0:T(1,128)S(1)} %get-tuple-element.61), channel_id=1, source_target_pairs={{1,0},{2,1},{3,2},{4,3},{5,4},{6,5},{7,6},{8,7},{9,8},{10,9},{11,1... | collective-permute-start | bytes 15368 | tf_op jit(solution)/shard_map/ppermute | solution.py:22
  321.3 5.8 %collective-permute-start.30 = (f32[2,10,1,64]{3,2,1,0:T(1,128)S(1)}, f32[2,10,1,64]{3,2,1,0:T(1,128)S(1)}, u32[]{:S(2)}, u32[]{:S(2)}) collective-permute-start(f32[2,10,1,64]{3,2,1,0:T(1,128)S(1)} %get-tuple-element.59), channel_id=1, source_target_pairs={{1,0},{2,1},{3,2},{4,3},{5,4},{6,5},{7,6},{8,7},{9,8},{10,9},{11,1... | collective-permute-start | bytes 15368 | tf_op jit(solution)/shard_map/ppermute | solution.py:22
  339.3 5.8 %collective-permute-start.35 = (f32[2,10,1,64]{3,2,1,0:T(1,128)S(1)}, f32[2,10,1,64]{3,2,1,0:T(1,128)S(1)}, u32[]{:S(2)}, u32[]{:S(2)}) collective-permute-start(f32[2,10,1,64]{3,2,1,0:T(1,128)S(1)} %get-tuple-element.57), channel_id=1, source_target_pairs={{1,0},{2,1},{3,2},{4,3},{5,4},{6,5},{7,6},{8,7},{9,8},{10,9},{11,1... | collective-permute-start | bytes 15368 | tf_op jit(solution)/shard_map/ppermute | solution.py:22
  359.1 5.8 %collective-permute-start.38 = (f32[2,6,1,32]{3,2,1,0:T(1,128)S(1)}, f32[2,6,1,32]{3,2,1,0:T(1,128)S(1)}, u32[]{:S(2)}, u32[]{:S(2)}) collective-permute-start(f32[2,6,1,32]{3,2,1,0:T(1,128)S(1)} %get-tuple-element.85), channel_id=1, source_target_pairs={{1,0},{2,1},{3,2},{4,3},{5,4},{6,5},{7,6},{8,7},{9,8},{10,9},{11,1... | collective-permute-start | bytes 4616 | tf_op jit(solution)/shard_map/ppermute | solution.py:22
  377.0 5.8 %collective-permute-start.42 = (f32[2,6,1,32]{3,2,1,0:T(1,128)S(1)}, f32[2,6,1,32]{3,2,1,0:T(1,128)S(1)}, u32[]{:S(2)}, u32[]{:S(2)}) collective-permute-start(f32[2,6,1,32]{3,2,1,0:T(1,128)S(1)} %get-tuple-element.81), channel_id=1, source_target_pairs={{1,0},{2,1},{3,2},{4,3},{5,4},{6,5},{7,6},{8,7},{9,8},{10,9},{11,1... | collective-permute-start | bytes 4616 | tf_op jit(solution)/shard_map/ppermute | solution.py:22
  395.0 5.8 %collective-permute-start.46 = (f32[2,6,1,32]{3,2,1,0:T(1,128)S(1)}, f32[2,6,1,32]{3,2,1,0:T(1,128)S(1)}, u32[]{:S(2)}, u32[]{:S(2)}) collective-permute-start(f32[2,6,1,32]{3,2,1,0:T(1,128)S(1)} %get-tuple-element.77), channel_id=1, source_target_pairs={{1,0},{2,1},{3,2},{4,3},{5,4},{6,5},{7,6},{8,7},{9,8},{10,9},{11,1... | collective-permute-start | bytes 4616 | tf_op jit(solution)/shard_map/ppermute | solution.py:22
  (210 shorter events, 173.6 us)
Async XLA Ops:
  8.5 7.4 %collective-permute-start = (f32[2,1,32,256]{3,2,1,0:T(8,128)S(1)}, f32[2,1,32,256]{3,2,1,0:T(8,128)S(1)}, u32[]{:S(2)}, u32[]{:S(2)}) collective-permute-start(f32[2,1,32,256]{3,2,1,0:T(8,128)S(1)} %get-tuple-element.27), channel_id=1, source_target_pairs={{32,0},{64,32},{96,64},{128,96},{160,128},{192,160},{224,192},{33,... | collective-permute-start | bytes 196616 | tf_op jit(solution)/shard_map/ppermute | solution.py:22
  16.0 7.7 %collective-permute-start.3 = (f32[2,34,1,256]{3,2,1,0:T(1,128)S(1)}, f32[2,34,1,256]{3,2,1,0:T(1,128)S(1)}, u32[]{:S(2)}, u32[]{:S(2)}) collective-permute-start(f32[2,34,1,256]{3,2,1,0:T(1,128)S(1)} %get-tuple-element.20), channel_id=1, source_target_pairs={{0,1},{1,2},{2,3},{3,4},{4,5},{5,6},{6,7},{7,8},{8,9},{9,10},{10,1... | collective-permute-start | bytes 208904 | tf_op jit(solution)/shard_map/ppermute | solution.py:21
  17.9 7.7 %collective-permute-start.2 = (f32[2,34,1,256]{3,2,1,0:T(1,128)S(1)}, f32[2,34,1,256]{3,2,1,0:T(1,128)S(1)}, u32[]{:S(2)}, u32[]{:S(2)}) collective-permute-start(f32[2,34,1,256]{3,2,1,0:T(1,128)S(1)} %get-tuple-element.21), channel_id=1, source_target_pairs={{1,0},{2,1},{3,2},{4,3},{5,4},{6,5},{7,6},{8,7},{9,8},{10,9},{11,1... | collective-permute-start | bytes 208904 | tf_op jit(solution)/shard_map/ppermute | solution.py:22
  35.3 7.4 %collective-permute-start.4 = (f32[2,1,32,256]{3,2,1,0:T(8,128)S(1)}, f32[2,1,32,256]{3,2,1,0:T(8,128)S(1)}, u32[]{:S(2)}, u32[]{:S(2)}) collective-permute-start(f32[2,1,32,256]{3,2,1,0:T(8,128)S(1)} %get-tuple-element.25), channel_id=1, source_target_pairs={{32,0},{64,32},{96,64},{128,96},{160,128},{192,160},{224,192},{33,... | collective-permute-start | bytes 196616 | tf_op jit(solution)/shard_map/ppermute | solution.py:22
  47.5 7.9 %collective-permute-start.7 = (f32[2,34,1,256]{3,1,2,0:T(8,128)S(1)}, f32[2,34,1,256]{3,1,2,0:T(8,128)S(1)}, u32[]{:S(2)}, u32[]{:S(2)}) collective-permute-start(f32[2,34,1,256]{3,1,2,0:T(8,128)S(1)} %copy.24), channel_id=1, source_target_pairs={{0,1},{1,2},{2,3},{3,4},{4,5},{5,6},{6,7},{7,8},{8,9},{9,10},{10,1... | collective-permute-start | bytes 208904 | tf_op jit(solution)/shard_map/ppermute | solution.py:21
  63.2 7.4 %collective-permute-start.9 = (f32[2,1,32,256]{3,2,1,0:T(8,128)S(1)}, f32[2,1,32,256]{3,2,1,0:T(8,128)S(1)}, u32[]{:S(2)}, u32[]{:S(2)}) collective-permute-start(f32[2,1,32,256]{3,2,1,0:T(8,128)S(1)} %get-tuple-element.23), channel_id=1, source_target_pairs={{32,0},{64,32},{96,64},{128,96},{160,128},{192,160},{224,192},{33,... | collective-permute-start | bytes 196616 | tf_op jit(solution)/shard_map/ppermute | solution.py:22
  70.6 97.0 %collective-permute-start.10 = (f32[2,34,1,256]{3,2,1,0:T(1,128)S(1)}, f32[2,34,1,256]{3,2,1,0:T(1,128)S(1)}, u32[]{:S(2)}, u32[]{:S(2)}) collective-permute-start(f32[2,34,1,256]{3,2,1,0:T(1,128)S(1)} %get-tuple-element.16), channel_id=1, source_target_pairs={{0,1},{1,2},{2,3},{3,4},{4,5},{5,6},{6,7},{7,8},{8,9},{9,10},{10,1... | collective-permute-start | bytes 208904 | tf_op jit(solution)/shard_map/ppermute | solution.py:21
  72.6 95.1 %collective-permute-start.11 = (f32[2,34,1,256]{3,2,1,0:T(1,128)S(1)}, f32[2,34,1,256]{3,2,1,0:T(1,128)S(1)}, u32[]{:S(2)}, u32[]{:S(2)}) collective-permute-start(f32[2,34,1,256]{3,2,1,0:T(1,128)S(1)} %get-tuple-element.17), channel_id=1, source_target_pairs={{1,0},{2,1},{3,2},{4,3},{5,4},{6,5},{7,6},{8,7},{9,8},{10,9},{11,1... | collective-permute-start | bytes 208904 | tf_op jit(solution)/shard_map/ppermute | solution.py:22
  227.1 7.9 %collective-permute-start.15 = (f32[2,18,1,128]{3,2,1,0:T(1,128)S(1)}, f32[2,18,1,128]{3,2,1,0:T(1,128)S(1)}, u32[]{:S(2)}, u32[]{:S(2)}) collective-permute-start(f32[2,18,1,128]{3,2,1,0:T(1,128)S(1)} %get-tuple-element.40), channel_id=1, source_target_pairs={{0,1},{1,2},{2,3},{3,4},{4,5},{5,6},{6,7},{7,8},{8,9},{9,10},{10,1... | collective-permute-start | bytes 55304 | tf_op jit(solution)/shard_map/ppermute | solution.py:21
  229.0 7.2 %collective-permute-start.14 = (f32[2,18,1,128]{3,2,1,0:T(1,128)S(1)}, f32[2,18,1,128]{3,2,1,0:T(1,128)S(1)}, u32[]{:S(2)}, u32[]{:S(2)}) collective-permute-start(f32[2,18,1,128]{3,2,1,0:T(1,128)S(1)} %get-tuple-element.41), channel_id=1, source_target_pairs={{1,0},{2,1},{3,2},{4,3},{5,4},{6,5},{7,6},{8,7},{9,8},{10,9},{11,1... | collective-permute-start | bytes 55304 | tf_op jit(solution)/shard_map/ppermute | solution.py:22
  245.9 7.7 %collective-permute-start.19 = (f32[2,18,1,128]{3,2,1,0:T(1,128)S(1)}, f32[2,18,1,128]{3,2,1,0:T(1,128)S(1)}, u32[]{:S(2)}, u32[]{:S(2)}) collective-permute-start(f32[2,18,1,128]{3,2,1,0:T(1,128)S(1)} %get-tuple-element.38), channel_id=1, source_target_pairs={{0,1},{1,2},{2,3},{3,4},{4,5},{5,6},{6,7},{7,8},{8,9},{9,10},{10,1... | collective-permute-start | bytes 55304 | tf_op jit(solution)/shard_map/ppermute | solution.py:21
  247.8 7.2 %collective-permute-start.18 = (f32[2,18,1,128]{3,2,1,0:T(1,128)S(1)}, f32[2,18,1,128]{3,2,1,0:T(1,128)S(1)}, u32[]{:S(2)}, u32[]{:S(2)}) collective-permute-start(f32[2,18,1,128]{3,2,1,0:T(1,128)S(1)} %get-tuple-element.39), channel_id=1, source_target_pairs={{1,0},{2,1},{3,2},{4,3},{5,4},{6,5},{7,6},{8,7},{9,8},{10,9},{11,1... | collective-permute-start | bytes 55304 | tf_op jit(solution)/shard_map/ppermute | solution.py:22
  264.6 21.5 %collective-permute-start.22 = (f32[2,18,1,128]{3,2,1,0:T(1,128)S(1)}, f32[2,18,1,128]{3,2,1,0:T(1,128)S(1)}, u32[]{:S(2)}, u32[]{:S(2)}) collective-permute-start(f32[2,18,1,128]{3,2,1,0:T(1,128)S(1)} %get-tuple-element.36), channel_id=1, source_target_pairs={{0,1},{1,2},{2,3},{3,4},{4,5},{5,6},{6,7},{7,8},{8,9},{9,10},{10,1... | collective-permute-start | bytes 55304 | tf_op jit(solution)/shard_map/ppermute | solution.py:21
  266.5 19.6 %collective-permute-start.23 = (f32[2,18,1,128]{3,2,1,0:T(1,128)S(1)}, f32[2,18,1,128]{3,2,1,0:T(1,128)S(1)}, u32[]{:S(2)}, u32[]{:S(2)}) collective-permute-start(f32[2,18,1,128]{3,2,1,0:T(1,128)S(1)} %get-tuple-element.37), channel_id=1, source_target_pairs={{1,0},{2,1},{3,2},{4,3},{5,4},{6,5},{7,6},{8,7},{9,8},{10,9},{11,1... | collective-permute-start | bytes 55304 | tf_op jit(solution)/shard_map/ppermute | solution.py:22
  301.2 7.7 %collective-permute-start.27 = (f32[2,10,1,64]{3,2,1,0:T(1,128)S(1)}, f32[2,10,1,64]{3,2,1,0:T(1,128)S(1)}, u32[]{:S(2)}, u32[]{:S(2)}) collective-permute-start(f32[2,10,1,64]{3,2,1,0:T(1,128)S(1)} %get-tuple-element.60), channel_id=1, source_target_pairs={{0,1},{1,2},{2,3},{3,4},{4,5},{5,6},{6,7},{7,8},{8,9},{9,10},{10,1... | collective-permute-start | bytes 15368 | tf_op jit(solution)/shard_map/ppermute | solution.py:21
  303.1 7.1 %collective-permute-start.26 = (f32[2,10,1,64]{3,2,1,0:T(1,128)S(1)}, f32[2,10,1,64]{3,2,1,0:T(1,128)S(1)}, u32[]{:S(2)}, u32[]{:S(2)}) collective-permute-start(f32[2,10,1,64]{3,2,1,0:T(1,128)S(1)} %get-tuple-element.61), channel_id=1, source_target_pairs={{1,0},{2,1},{3,2},{4,3},{5,4},{6,5},{7,6},{8,7},{9,8},{10,9},{11,1... | collective-permute-start | bytes 15368 | tf_op jit(solution)/shard_map/ppermute | solution.py:22
  319.3 7.7 %collective-permute-start.31 = (f32[2,10,1,64]{3,2,1,0:T(1,128)S(1)}, f32[2,10,1,64]{3,2,1,0:T(1,128)S(1)}, u32[]{:S(2)}, u32[]{:S(2)}) collective-permute-start(f32[2,10,1,64]{3,2,1,0:T(1,128)S(1)} %get-tuple-element.58), channel_id=1, source_target_pairs={{0,1},{1,2},{2,3},{3,4},{4,5},{5,6},{6,7},{7,8},{8,9},{9,10},{10,1... | collective-permute-start | bytes 15368 | tf_op jit(solution)/shard_map/ppermute | solution.py:21
  321.3 7.1 %collective-permute-start.30 = (f32[2,10,1,64]{3,2,1,0:T(1,128)S(1)}, f32[2,10,1,64]{3,2,1,0:T(1,128)S(1)}, u32[]{:S(2)}, u32[]{:S(2)}) collective-permute-start(f32[2,10,1,64]{3,2,1,0:T(1,128)S(1)} %get-tuple-element.59), channel_id=1, source_target_pairs={{1,0},{2,1},{3,2},{4,3},{5,4},{6,5},{7,6},{8,7},{9,8},{10,9},{11,1... | collective-permute-start | bytes 15368 | tf_op jit(solution)/shard_map/ppermute | solution.py:22
  337.4 8.9 %collective-permute-start.34 = (f32[2,10,1,64]{3,2,1,0:T(1,128)S(1)}, f32[2,10,1,64]{3,2,1,0:T(1,128)S(1)}, u32[]{:S(2)}, u32[]{:S(2)}) collective-permute-start(f32[2,10,1,64]{3,2,1,0:T(1,128)S(1)} %get-tuple-element.56), channel_id=1, source_target_pairs={{0,1},{1,2},{2,3},{3,4},{4,5},{5,6},{6,7},{7,8},{8,9},{9,10},{10,1... | collective-permute-start | bytes 15368 | tf_op jit(solution)/shard_map/ppermute | solution.py:21
  339.3 7.1 %collective-permute-start.35 = (f32[2,10,1,64]{3,2,1,0:T(1,128)S(1)}, f32[2,10,1,64]{3,2,1,0:T(1,128)S(1)}, u32[]{:S(2)}, u32[]{:S(2)}) collective-permute-start(f32[2,10,1,64]{3,2,1,0:T(1,128)S(1)} %get-tuple-element.57), channel_id=1, source_target_pairs={{1,0},{2,1},{3,2},{4,3},{5,4},{6,5},{7,6},{8,7},{9,8},{10,9},{11,1... | collective-permute-start | bytes 15368 | tf_op jit(solution)/shard_map/ppermute | solution.py:22
  357.1 7.7 %collective-permute-start.39 = (f32[2,6,1,32]{3,2,1,0:T(1,128)S(1)}, f32[2,6,1,32]{3,2,1,0:T(1,128)S(1)}, u32[]{:S(2)}, u32[]{:S(2)}) collective-permute-start(f32[2,6,1,32]{3,2,1,0:T(1,128)S(1)} %get-tuple-element.84), channel_id=1, source_target_pairs={{0,1},{1,2},{2,3},{3,4},{4,5},{5,6},{6,7},{7,8},{8,9},{9,10},{10,1... | collective-permute-start | bytes 4616 | tf_op jit(solution)/shard_map/ppermute | solution.py:21
  359.1 7.1 %collective-permute-start.38 = (f32[2,6,1,32]{3,2,1,0:T(1,128)S(1)}, f32[2,6,1,32]{3,2,1,0:T(1,128)S(1)}, u32[]{:S(2)}, u32[]{:S(2)}) collective-permute-start(f32[2,6,1,32]{3,2,1,0:T(1,128)S(1)} %get-tuple-element.85), channel_id=1, source_target_pairs={{1,0},{2,1},{3,2},{4,3},{5,4},{6,5},{7,6},{8,7},{9,8},{10,9},{11,1... | collective-permute-start | bytes 4616 | tf_op jit(solution)/shard_map/ppermute | solution.py:22
  375.1 7.7 %collective-permute-start.43 = (f32[2,6,1,32]{3,2,1,0:T(1,128)S(1)}, f32[2,6,1,32]{3,2,1,0:T(1,128)S(1)}, u32[]{:S(2)}, u32[]{:S(2)}) collective-permute-start(f32[2,6,1,32]{3,2,1,0:T(1,128)S(1)} %get-tuple-element.80), channel_id=1, source_target_pairs={{0,1},{1,2},{2,3},{3,4},{4,5},{5,6},{6,7},{7,8},{8,9},{9,10},{10,1... | collective-permute-start | bytes 4616 | tf_op jit(solution)/shard_map/ppermute | solution.py:21
  393.1 7.7 %collective-permute-start.47 = (f32[2,6,1,32]{3,2,1,0:T(1,128)S(1)}, f32[2,6,1,32]{3,2,1,0:T(1,128)S(1)}, u32[]{:S(2)}, u32[]{:S(2)}) collective-permute-start(f32[2,6,1,32]{3,2,1,0:T(1,128)S(1)} %get-tuple-element.76), channel_id=1, source_target_pairs={{0,1},{1,2},{2,3},{3,4},{4,5},{5,6},{6,7},{7,8},{8,9},{9,10},{10,1... | collective-permute-start | bytes 4616 | tf_op jit(solution)/shard_map/ppermute | solution.py:21
  (29 other events, 239.4 us)
where the time goes:
time: 408 us; the launch traced here: 403 us
  starting transfers between devices  163 us (40%)
  local copies, waits for them, and re-layouts  133 us (33%)
  waiting for transfers between devices  55 us (13%)
  other arithmetic  50.1 us (12%)
    ppermute x24, starting transfers between devices, padded_2(): after = lax.ppermute(initial, axis, down)  113 us
    reshape x1, local copies, waits for them, and re-layouts, coarsen(): wavenum.reshape(xsize // 2, 2, ysize // 2, 2, zsize // 2, 2)  68.4 us
    slice x24, local copies, waits for them, and re-layouts, halves(): lax.slice_in_dim(padded, start, start + length - 1, 2, axis)  52.7 us
    ppermute x24, starting transfers between devices, padded_2(): before = lax.ppermute(last, axis, up)  49.2 us
    ppermute x24, waiting for transfers between devices, padded_2(): after = lax.ppermute(initial, axis, down)  48.5 us
    reduce_sum x3, other arithmetic, coarsen(): wavenum.reshape(xsize // 2, 2, ysize // 2, 2, zsize // 2, 2)  24.9 us
    div x2, local copies, waits for them, and re-layouts, coarsen(): wavenum.reshape(xsize // 2, 2, ysize // 2, 2, zsize // 2, 2)  10.9 us
    concatenate x21, other arithmetic, padded_2(): array = jnp.concatenate([before, array, after], axis=dim)  10.5 us
  transfers between devices with their start and end apart: 48, of which 25 were waited for; matrix products, arithmetic and copies ran while one was open for 26% of the time, Pallas kernels for 0%

commit v1 on v0

v1 whole, which is shorter than its diff:
```python
import functools
import jax
import jax.numpy as jnp
import numpy as np
from jax import lax
from jax.experimental import pallas as pl
from jax.experimental.pallas import tpu as pltpu
from jax.sharding import PartitionSpec as P

DAMPING = 0.8
SHIFT_IMAG = 0.5
VMEM = pl.BlockSpec(memory_space=pltpu.VMEM)
SMEM = pl.BlockSpec(memory_space=pltpu.SMEM)


def params():
    return pltpu.CompilerParams(vmem_limit_bytes=40 * 1024 * 1024)


def around(ref, k, x, full_lanes):
    mid = ref[k, x]
    rows, lanes = mid.shape
    up = pltpu.roll(mid, 1, 1)
    down = pltpu.roll(mid, lanes - 1, 1)
    if full_lanes:
        lane = lax.broadcasted_iota(jnp.int32, mid.shape, 1)
        up = jnp.where(lane == 0, 0.0, up)
        down = jnp.where(lane == lanes - 1, 0.0, down)
    sides = pltpu.roll(mid, 1, 0) + pltpu.roll(mid, rows - 1, 0)
    return (ref[k, x - 1] + ref[k, x + 1]) + sides + (up + down)


def inside(shape, x, x0, xsize, y0, ysize, zsize):
    row = lax.broadcasted_iota(jnp.int32, shape, 0) + y0
    ok = (row >= 0) & (row < ysize)
    if zsize < shape[1]:
        ok = ok & (lax.broadcasted_iota(jnp.int32, shape, 1) < zsize)
    gx = x + x0
    return ok & ((gx >= 0) & (gx < xsize))


def first_pass(f, c, ga, gb, u, scale, count, where):
    def step(x, carry):
        cc = c(x)
        a = 6.0 / scale - cc
        b = SHIFT_IMAG * cc
        g = jnp.where(where(x, cc.shape), DAMPING / (a * a + b * b), 0.0)
        a = g * a
        b = g * b
        re, im = f(0, x), f(1, x)
        ga[x] = a
        gb[x] = b
        u[0, x] = re * a + im * b
        u[1, x] = im * a - re * b
        return carry

    lax.fori_loop(0, count, step, 0)


def turned(ga, gb, x, s_re, s_im, scale):
    a, b = ga[x], gb[x]
    if scale != 1.0:
        a, b = a * (1.0 / scale), b * (1.0 / scale)
    return s_re * a + s_im * b, s_im * a - s_re * b


def smooth(f, ga, gb, u, e, r, scale, count, full_lanes, where, put):
    def second(x, carry):
        d_re, d_im = turned(ga, gb, x, around(u, 0, x, full_lanes), around(u, 1, x, full_lanes), scale)
        for k, d in ((0, d_re), (1, d_im)):
            first = u[k, x]
            e[k, x] = 0.4 * first + d
            put(k, x, 1.2 * first + d)
        return carry

    lax.fori_loop(1, count - 1, second, 0)

    def third(x, carry):
        for k in (0, 1):
            s = around(e, k, x, full_lanes)
            val = 0.04 * f(k, x) + (s if scale == 1.0 else s * (1.0 / scale))
            r[k, x] = jnp.where(where(x, val.shape), val, 0.0)
        return carry

    lax.fori_loop(2, count - 2, third, 0)


def restrict_xy(r, c, t, out, planes, rows, plane0, row0):
    halves = t.shape[1]

    def step(i, carry):
        p = plane0 + 2 * i
        for k in range(3):
            if k < 2:
                val = (r[k, p] + r[k, p + 3]) + 3.0 * (r[k, p + 1] + r[k, p + 2])
            else:
                val = c(p + 1) + c(p + 2)
            for half in range(halves):
                lanes = slice(128 * half, 128 * half + 128)
                t[k, half] = val[:, lanes]
                part = [t[k, half, pl.ds(row0 + j, rows, 2), :] for j in range(4)]
                inner = part[1] + part[2]
                out[k, i, pl.ds(0, rows), lanes] = inner if k == 2 else (part[0] + part[3]) + 3.0 * inner
        return carry

    lax.fori_loop(0, planes, step, 0)


def weights(zsize, lanes_in, lanes_out):
    full = np.zeros((lanes_in, lanes_out), np.float32)
    mean = np.zeros((lanes_in, lanes_out), np.float32)
    for i in range(zsize // 2):
        for j, w in enumerate((1.0, 3.0, 3.0, 1.0)):
            z = 2 * i - 1 + j
            if 0 <= z < zsize:
                full[z, i] = w / 512.0
        mean[2 * i, i] = mean[2 * i + 1, i] = 0.125
    return jnp.asarray(full, jnp.bfloat16), jnp.asarray(mean, jnp.bfloat16)


def exact_dot(x, w):
    hi = x.astype(jnp.bfloat16)
    rest = x - hi.astype(jnp.float32)
    mid = rest.astype(jnp.bfloat16)
    low = (rest - mid.astype(jnp.float32)).astype(jnp.bfloat16)
    dot = functools.partial(jnp.dot, preferred_element_type=jnp.float32)
    return dot(hi, w) + (dot(mid, w) + dot(low, w))


def restrict_z(t, w_full, w_mean, k):
    planes, rows, lanes = t.shape[1:]
    flat = t[k].reshape(planes * rows, lanes)
    w = w_mean[...] if k == 2 else w_full[...]
    return exact_dot(flat, w).reshape(planes, rows, w.shape[1])


def pack_kernel(h, f_lo, f_hi, c_lo, c_hi, lo, hi):
    for k in range(3):
        for j in range(h):
            lo[k, j] = f_lo[k, :, j, :] if k < 2 else c_lo[:, j, :]
            hi[k, j] = f_hi[k, :, 8 - h + j, :] if k < 2 else c_hi[:, 8 - h + j, :]


def fine_kernel(h, xsize, ysize, place, f_own, c_own, xlo, xhi, ylo, yhi, w_full, w_mean, u_out, fc_out, fc, ga, gb, u, e, t, part):
    n, rows, lanes = c_own.shape
    count = n + 2 * h
    for k in range(3):
        fc[k, pl.ds(h, n), pl.ds(8, rows), :] = f_own[k] if k < 2 else c_own[...]
        for base, side in ((0, xlo), (n + h, xhi)):
            fc[k, pl.ds(base, h), pl.ds(8, rows), :] = side[k, :, pl.ds(0, rows), :]
            fc[k, pl.ds(base, h), pl.ds(8 - h, h), :] = side[k, :, pl.ds(rows, h), :]
            fc[k, pl.ds(base, h), pl.ds(8 + rows, h), :] = side[k, :, pl.ds(rows + h, h), :]
        for j in range(h):
            fc[k, pl.ds(h, n), 8 - h + j, :] = ylo[k, j]
            fc[k, pl.ds(h, n), 8 + rows + j, :] = yhi[k, j]
    x0, y0 = place[0] * n - h, place[1] * rows - 8

    def where(x, shape):
        return inside(shape, x, x0, xsize, y0, ysize, lanes)

    def put(k, x, val):
        @pl.when((x >= h) & (x < n + h))
        def _():
            u_out[k, x - h] = val[8 : 8 + rows]

    f = lambda k, x: fc[k, x]
    c = lambda x: fc[2, x]
    first_pass(f, c, ga, gb, u, 1.0, count, where)
    smooth(f, ga, gb, u, e, u, 1.0, count, True, where, put)
    restrict_xy(u, c, t, part, n // 2, rows // 2, h - 1, 7)
    for k in range(3):
        fc_out[k] = restrict_z(part, w_full, w_mean, k)


def middle_kernel(h, over, xsize, ysize, place, fc_own, xlo, xhi, ylo, yhi, w_full, w_mean, u_out, fc_out, fc, ga, gb, u, e, t, part):
    n, rows, lanes = fc_own.shape[1:]
    count = n + 2 * h
    for k in range(3):
        fc[k, pl.ds(h, n), pl.ds(8, rows), :] = fc_own[k]
        fc[k, pl.ds(0, h), pl.ds(8, rows), :] = xlo[k]
        fc[k, pl.ds(n + h, h), pl.ds(8, rows), :] = xhi[k]
        fc[k, :, pl.ds(0, 8), :] = ylo[k]
        fc[k, :, pl.ds(8 + rows, 8), :] = yhi[k]
    x0, y0 = place[0] * n - h, place[1] * rows - 8

    def where(x, shape):
        return inside(shape, x, x0, xsize, y0, ysize, lanes)

    def put(k, x, val):
        @pl.when((x >= h) & (x < n + h))
        def _():
            u_out[k, x - h] = val[8 : 8 + rows]

    f = lambda k, x: fc[k, x]
    c = lambda x: fc[2, x]
    first_pass(f, c, ga, gb, u, 4.0, count, where)
    smooth(f, ga, gb, u, e, u, 4.0, count, True, where, put)
    planes, width = n // 2 + 2 * over, rows // 2 + 2 * over
    restrict_xy(u, c, t, part, planes, width, h - 1 - 2 * over, 7 - 2 * over)
    for k in range(3):
        fc_out[k] = restrict_z(part, w_full, w_mean, k)[:, :width]


def coarse_kernel(n, sweeps, xsize, ysize, zsize, place, fc_own, xlo, xhi, ylo, yhi, w_full, w_mean, u_out, v_out, fc, ga, gb, u, e, t, part, fd, gc, gd, v, w):
    lanes = fc_own.shape[3]
    count = n + 18
    for k in range(3):
        fc[k, pl.ds(8, n + 2), pl.ds(8, n + 2), :] = fc_own[k]
        fc[k, pl.ds(0, 8), pl.ds(8, n + 2), :] = xlo[k]
        fc[k, pl.ds(n + 10, 8), pl.ds(8, n + 2), :] = xhi[k]
        fc[k, :, pl.ds(0, 8), :] = ylo[k]
        fc[k, :, pl.ds(n + 10, 8), :] = yhi[k]
    x0, y0 = place[0] * n - 9, place[1] * n - 9

    def where(x, shape):
        return inside(shape, x, x0, xsize, y0, ysize, zsize)

    def put(k, x, val):
        @pl.when((x >= 9) & (x < n + 9))
        def _():
            u_out[k, x - 9] = val[9 : 9 + n, :zsize]

    f = lambda k, x: fc[k, x]
    c = lambda x: fc[2, x]
    first_pass(f, c, ga, gb, u, 16.0, count, where)
    smooth(f, ga, gb, u, e, u, 16.0, count, False, where, put)
    m = n // 2
    width = m + 6
    restrict_xy(u, c, t, part, width, width, 2, 2)
    for k in range(3):
        fd[k] = restrict_z(part, w_full, w_mean, k)
    x1, y1 = place[0] * m - 3, place[1] * m - 3

    def where_c(x, shape):
        return inside(shape, x, x1, xsize // 2, y1, ysize // 2, zsize // 2)

    first_pass(lambda k, x: fd[k, x], lambda x: fd[2, x], gc, gd, v, 64.0, width, where_c)
    old, new = v, w
    for sweep in range(sweeps - 1):
        for x in range(1 + sweep, width - 1 - sweep):
            d = turned(gc, gd, x, around(old, 0, x, False), around(old, 1, x, False), 64.0)
            for k in (0, 1):
                val = (v[k, x] if sweep == 0 else 0.2 * old[k, x] + v[k, x]) + d[k]
                if sweep == 0:
                    val = 0.2 * v[k, x] + val
                if sweep == sweeps - 2:
                    v_out[k, x - 3] = val[3 : 3 + m, : zsize // 2]
                else:
                    new[sweep % 2, k, x] = val
        old = _Half(w, sweep % 2)


class _Half:
    def __init__(self, ref, half):
        self.ref, self.half = ref, half

    def __getitem__(self, index):
        return self.ref[(self.half,) + tuple(index)]


def body(source, wavenumber_sq):
    f32 = jnp.float32
    xdev, ydev = lax.axis_size("gx"), lax.axis_size("gy")
    place = jnp.stack([lax.axis_index("gx"), lax.axis_index("gy")]).astype(jnp.int32)

    def swap(axis, devices, first, last):
        before = lax.ppermute(last, axis, [(i, (i + 1) % devices) for i in range(devices)])
        after = lax.ppermute(first, axis, [((i + 1) % devices, i) for i in range(devices)])
        return before, after

    _, n, rows, lanes = source.shape
    xsize, ysize = n * xdev, rows * ydev
    S = lambda *shape: jax.ShapeDtypeStruct(shape, f32)
    V = lambda *shape: pltpu.VMEM(shape, f32)

    h = 3
    fblock = lambda j: pl.BlockSpec((2, n, 8, lanes), lambda i, j=j: (0, 0, j, 0))
    cblock = lambda j: pl.BlockSpec((n, 8, lanes), lambda i, j=j: (0, j, 0))
    last = rows // 8 - 1
    side = pl.BlockSpec((3, h, n, lanes), lambda i: (0, 0, 0, 0))
    first_rows, last_rows = pl.pallas_call(
        functools.partial(pack_kernel, h),
        grid=(1,),
        in_specs=[fblock(0), fblock(last), cblock(0), cblock(last)],
        out_specs=[side, side],
        out_shape=[S(3, h, n, lanes)] * 2,
        compiler_params=params(),
        name="pack_rows",
    )(source, source, wavenumber_sq, wavenumber_sq)
    ylo, yhi = swap("gy", ydev, first_rows, last_rows)

    def planes(start):
        own = jnp.concatenate([source[:, start : start + h], wavenumber_sq[None, start : start + h]], 0)
        lo = ylo[:, :, start : start + h].transpose(0, 2, 1, 3)
        hi = yhi[:, :, start : start + h].transpose(0, 2, 1, 3)
        return jnp.concatenate([own, lo, hi, jnp.zeros((3, h, 8 - 2 * h, lanes), f32)], 2)

    xlo, xhi = swap("gx", xdev, planes(0), planes(n - h))
    zsize = lanes
    w_full, w_mean = weights(zsize, lanes, lanes // 2)
    full = (n + 2 * h, rows + 16, lanes)
    fine, fc = pl.pallas_call(
        functools.partial(fine_kernel, h, xsize, ysize),
        in_specs=[SMEM] + [VMEM] * 8,
        out_specs=[VMEM] * 2,
        out_shape=[S(2, n, rows, lanes), S(3, n // 2, rows // 2, lanes // 2)],
        scratch_shapes=[V(3, *full), V(*full), V(*full), V(2, *full), V(2, *full), V(3, lanes // 128, full[1], 128), V(3, n // 2, rows // 2, lanes)],
        compiler_params=params(),
        name="fine_level",
    )(place, source, wavenumber_sq, xlo, xhi, ylo, yhi, w_full, w_mean)

    n, rows, lanes, xsize, ysize, zsize = n // 2, rows // 2, lanes // 2, xsize // 2, ysize // 2, zsize // 2
    h, over = 5, 1
    xlo, xhi = swap("gx", xdev, fc[:, :h], fc[:, n - h :])
    first_rows, last_rows = [jnp.concatenate([a[:, :, s : s + 8] for a in (xlo, fc, xhi)], 1) for s in (0, rows - 8)]
    ylo, yhi = swap("gy", ydev, first_rows, last_rows)
    w_full, w_mean = weights(zsize, lanes, lanes)
    full = (n + 2 * h, rows + 16, lanes)
    width = n // 2 + 2 * over
    second, fc = pl.pallas_call(
        functools.partial(middle_kernel, h, over, xsize, ysize),
        in_specs=[SMEM] + [VMEM] * 7,
        out_specs=[VMEM] * 2,
        out_shape=[S(2, n, rows, lanes), S(3, width, width, lanes)],
        scratch_shapes=[V(3, *full), V(*full), V(*full), V(2, *full), V(2, *full), V(3, lanes // 128, full[1], 128), V(3, width, 16, lanes)],
        compiler_params=params(),
        name="second_level",
    )(place, fc, xlo, xhi, ylo, yhi, w_full, w_mean)

    n, xsize, ysize, zsize = n // 2, xsize // 2, ysize // 2, zsize // 2
    xlo, xhi = swap("gx", xdev, fc[:, 2:], fc[:, :n])
    first_rows, last_rows = [jnp.concatenate([a[:, :, s : s + 8] for a in (xlo, fc, xhi)], 1) for s in (2, 0)]
    ylo, yhi = swap("gy", ydev, first_rows, last_rows)
    w_full, w_mean = weights(zsize, lanes, lanes)
    full = (n + 18, 32, lanes)
    m = n // 2
    small = (m + 6, 16, lanes)
    third, coarse = pl.pallas_call(
        functools.partial(coarse_kernel, n, 4, xsize, ysize, zsize),
        in_specs=[SMEM] + [VMEM] * 7,
        out_specs=[VMEM] * 2,
        out_shape=[S(2, n, n, zsize), S(2, m, m, zsize // 2)],
        scratch_shapes=[V(3, *full), V(*full), V(*full), V(2, *full), V(2, *full), V(3, lanes // 128, full[1], 128), V(3, *small)]
        + [V(3, *small), V(*small), V(*small), V(2, *small), V(2, 2, *small)],
        compiler_params=params(),
        name="coarse_levels",
    )(place, fc, xlo, xhi, ylo, yhi, w_full, w_mean)
    return fine, second, third, coarse


def solution(mesh):
    placed = (P(None, "gx", "gy", None), P("gx", "gy", None))
    return jax.shard_map(body, mesh=mesh, in_specs=placed, out_specs=(P(None, "gx", "gy", None),) * 4, check_vma=False)
```

time: 408 us -> 95.1 us (0.23)
  the two profiles are of different devices: /device:TPU:120 before, /device:TPU:31 now
where the time goes in v1:
time: 95.1 us; the launch traced here: 94.8 us
  waiting for transfers between devices  46.2 us (49%)
  Pallas kernels  28.2 us (30%)
  starting transfers between devices  12.7 us (13%)
  local copies, waits for them, and re-layouts  5.67 us (6%)
  other arithmetic  1.17 us (1%)
    ppermute x6, waiting for transfers between devices, swap(): lax.ppermute(first, axis, [((i + 1) % devices, i) for i in range(devices)])  29.7 us
    ppermute x6, waiting for transfers between devices, swap(): lax.ppermute(last, axis, [(i, (i + 1) % devices) for i in range(devices)])  16.5 us
    pallas_call x1, Pallas kernels, body(): pl.pallas_call(functools.partial(fine_kernel, h, xsize, ysize), in_specs=...  14.4 us
    ppermute x6, starting transfers between devices, swap(): lax.ppermute(last, axis, [(i, (i + 1) % devices) for i in range(devices)])  8.54 us
    pallas_call x1, Pallas kernels, body(): pl.pallas_call(functools.partial(coarse_kernel, n, 4, xsize, ysize, zsize...  7.08 us
    pallas_call x1, Pallas kernels, body(): pl.pallas_call(functools.partial(middle_kernel, h, over, xsize, ysize), i...  6.48 us
    unnamed x24, local copies, waits for them, and re-layouts  5.35 us
    ppermute x6, starting transfers between devices, swap(): lax.ppermute(first, axis, [((i + 1) % devices, i) for i in range(devices)])  4.18 us
  transfers between devices with their start and end apart: 12, of which 12 were waited for; matrix products, arithmetic and copies ran while one was open for 0% of the time, Pallas kernels for 0%

profile of v1, /device:TPU:31, one launch (start us, length us, event | category | flops | bytes accessed | tf_op | source)
XLA Modules:
  0.0 94.8 jit_solution(5375431130549025311)
XLA Ops:
  0.6 1.6 %copy-done = f32[2,32,32,256]{3,2,1,0:T(8,128)S(1)} copy-done((f32[2,32,32,256]{3,2,1,0:T(8,128)S(1)}, f32[2,32,32,256]{3,2,1,0:T(8,128)}, u32[]{:S(2)}) %copy-start) | copy-done | bytes 2097176
  2.2 1.2 %copy-done.2 = f32[32,32,256]{2,1,0:T(8,128)S(1)} copy-done((f32[32,32,256]{2,1,0:T(8,128)S(1)}, f32[32,32,256]{2,1,0:T(8,128)}, u32[]{:S(2)}) %copy-start.2) | copy-done | bytes 1048600
  3.8 2.2 %collective-permute-start = (f32[3,3,32,256]{3,2,1,0:T(8,128)S(1)}, f32[3,3,32,256]{3,2,1,0:T(8,128)S(1)}, u32[]{:S(2)}, u32[]{:S(2)}) collective-permute-start(f32[3,3,32,256]{3,2,1,0:T(8,128)S(1)} %get-tuple-element.12), channel_id=1, source_target_pairs={{0,1},{1,2},{2,3},{3,4},{4,5},{5,6},{6,7},{7,8},{8,9},{9,10},{10,1... | collective-permute-start | bytes 884744 | tf_op jit(solution)/shard_map/ppermute | solution.py:267
  6.2 3.5 %collective-permute-done.ylo = f32[3,3,32,256]{3,2,1,0:T(8,128)S(1)} collective-permute-done((f32[3,3,32,256]{3,2,1,0:T(8,128)S(1)}, f32[3,3,32,256]{3,2,1,0:T(8,128)S(1)}, u32[]{:S(2)}, u32[]{:S(2)}) %collective-permute-start) | collective-permute-done | bytes 294944 | tf_op jit(solution)/shard_map/ppermute | solution.py:267
  9.7 5.7 %collective-permute-done.1.yhi = f32[3,3,32,256]{3,2,1,0:T(8,128)S(1)} collective-permute-done((f32[3,3,32,256]{3,2,1,0:T(8,128)S(1)}, f32[3,3,32,256]{3,2,1,0:T(8,128)S(1)}, u32[]{:S(2)}, u32[]{:S(2)}) %collective-permute-start.1) | collective-permute-done | bytes 294944 | tf_op jit(solution)/shard_map/ppermute | solution.py:268
  16.2 1.0 %maximum_maximum_fusion.1 = (f32[3,3,40,256]{3,2,1,0:T(8,128)}, f32[3,3,40,256]{3,2,1,0:T(8,128)}) fusion(f32[3,3,3,256]{3,2,1,0:T(4,128)S(1)} %copy.15, f32[3,3,3,256]{3,2,1,0:T(4,128)S(1)} %copy.14, f32[1,3,32,256]{3,2,1,0:T(8,128)S(1)} %get-tuple-element.22, f32[2,3,32,256]{3,2,1,0:T(8,128)S(1)} %get-tuple-element.20, f32[40]{0:T(128)S(1)} %pad.21.clone, ...), kind=kLoop, calls=%fused_computation.1 | loop fusion | flops 737280 | bytes 1437856 | tf_op jit(solution)/shard_map/concatenate | solution.py:296
  17.3 3.8 %collective-permute-start.3 = (f32[3,3,40,256]{3,2,1,0:T(8,128)}, f32[3,3,40,256]{3,2,1,0:T(8,128)}, u32[]{:S(2)}, u32[]{:S(2)}) collective-permute-start(f32[3,3,40,256]{3,2,1,0:T(8,128)} %get-tuple-element.44), channel_id=1, source_target_pairs={{32,0},{64,32},{96,64},{128,96},{160,128},{192,160},{224,192},{0,2... | collective-permute-start | bytes 1105928 | tf_op jit(solution)/shard_map/ppermute | solution.py:268
  21.2 6.1 %collective-permute-done.3.xhi = f32[3,3,40,256]{3,2,1,0:T(8,128)} collective-permute-done((f32[3,3,40,256]{3,2,1,0:T(8,128)}, f32[3,3,40,256]{3,2,1,0:T(8,128)}, u32[]{:S(2)}, u32[]{:S(2)}) %collective-permute-start.3) | collective-permute-done | bytes 368672 | tf_op jit(solution)/shard_map/ppermute | solution.py:268
  27.3 3.4 %collective-permute-done.2.xlo = f32[3,3,40,256]{3,2,1,0:T(8,128)} collective-permute-done((f32[3,3,40,256]{3,2,1,0:T(8,128)}, f32[3,3,40,256]{3,2,1,0:T(8,128)}, u32[]{:S(2)}, u32[]{:S(2)}) %collective-permute-start.2) | collective-permute-done | bytes 368672 | tf_op jit(solution)/shard_map/ppermute | solution.py:267
  32.5 14.4 %fine_level.1 = (f32[2,32,32,256]{3,2,1,0:T(8,128)}, f32[3,16,16,128]{3,2,1,0:T(8,128)S(1)}) custom-call(s32[2]{0:T(128)S(1)} %pad_add_fusion.place, f32[2,32,32,256]{3,2,1,0:T(8,128)S(1)} %copy-done.1, f32[32,32,256]{2,1,0:T(8,128)S(1)} %copy-done.3, f32[3,3,40,256]{3,2,1,0:T(8,128)} %collective-permute-done.2.xlo, ...), custom_call_target="tpu_custom_call" | custom-call | tf_op jit(solution)/shard_map/fine_level/pallas_call | solution.py:302
  47.0 1.5 %collective-permute-start.4 = (f32[3,5,16,128]{3,2,1,0:T(8,128)S(1)}, f32[3,5,16,128]{3,2,1,0:T(8,128)S(1)}, u32[]{:S(2)}, u32[]{:S(2)}) collective-permute-start(f32[3,5,16,128]{3,2,1,0:T(8,128)S(1)} %get-tuple-element.27), channel_id=1, source_target_pairs={{0,32},{32,64},{64,96},{96,128},{128,160},{160,192},{192,224},{224... | collective-permute-start | bytes 368648 | tf_op jit(solution)/shard_map/ppermute | solution.py:267
  48.5 2.7 %collective-permute-done.5.xhi = f32[3,5,16,128]{3,2,1,0:T(8,128)S(1)} collective-permute-done((f32[3,5,16,128]{3,2,1,0:T(8,128)S(1)}, f32[3,5,16,128]{3,2,1,0:T(8,128)S(1)}, u32[]{:S(2)}, u32[]{:S(2)}) %collective-permute-start.5) | collective-permute-done | bytes 122912 | tf_op jit(solution)/shard_map/ppermute | solution.py:268
  51.1 1.0 %collective-permute-done.4.xlo = f32[3,5,16,128]{3,2,1,0:T(8,128)S(1)} collective-permute-done((f32[3,5,16,128]{3,2,1,0:T(8,128)S(1)}, f32[3,5,16,128]{3,2,1,0:T(8,128)S(1)}, u32[]{:S(2)}, u32[]{:S(2)}) %collective-permute-start.4) | collective-permute-done | bytes 122912 | tf_op jit(solution)/shard_map/ppermute | solution.py:267
  52.2 2.3 %collective-permute-start.6 = (f32[3,26,8,128]{3,2,1,0:T(8,128)S(1)}, f32[3,26,8,128]{3,2,1,0:T(8,128)S(1)}, u32[]{:S(2)}, u32[]{:S(2)}) collective-permute-start(f32[3,26,8,128]{3,2,1,0:T(8,128)S(1)} %pad_maximum_fusion), channel_id=1, source_target_pairs={{0,1},{1,2},{2,3},{3,4},{4,5},{5,6},{6,7},{7,8},{8,9},{9,10},{10,1... | collective-permute-start | bytes 958472 | tf_op jit(solution)/shard_map/ppermute | solution.py:267
  54.6 3.8 %collective-permute-done.6.ylo = f32[3,26,8,128]{3,2,1,0:T(8,128)S(1)} collective-permute-done((f32[3,26,8,128]{3,2,1,0:T(8,128)S(1)}, f32[3,26,8,128]{3,2,1,0:T(8,128)S(1)}, u32[]{:S(2)}, u32[]{:S(2)}) %collective-permute-start.6) | collective-permute-done | bytes 319520 | tf_op jit(solution)/shard_map/ppermute | solution.py:267
  58.4 5.9 %collective-permute-done.7.yhi = f32[3,26,8,128]{3,2,1,0:T(8,128)S(1)} collective-permute-done((f32[3,26,8,128]{3,2,1,0:T(8,128)S(1)}, f32[3,26,8,128]{3,2,1,0:T(8,128)S(1)}, u32[]{:S(2)}, u32[]{:S(2)}) %collective-permute-start.7) | collective-permute-done | bytes 319520 | tf_op jit(solution)/shard_map/ppermute | solution.py:268
  64.3 6.5 %second_level.1 = (f32[2,16,16,128]{3,2,1,0:T(8,128)}, f32[3,10,10,128]{3,2,1,0:T(8,128)S(1)}) custom-call(s32[2]{0:T(128)S(1)} %pad_add_fusion.place, f32[3,16,16,128]{3,2,1,0:T(8,128)S(1)} %get-tuple-element.15.fc_own, f32[3,5,16,128]{3,2,1,0:T(8,128)S(1)} %collective-permute-done.4.xlo, f32[3,5,16,128]{3,2,1,0:T(8,128)S(1)} %collective-permute-done.5.xhi, ...), custom_call_target="tpu_custom_call" | custom-call | tf_op jit(solution)/shard_map/second_level/pallas_call | solution.py:320
  70.9 1.5 %collective-permute-start.8 = (f32[3,8,10,128]{3,2,1,0:T(8,128)S(1)}, f32[3,8,10,128]{3,2,1,0:T(8,128)S(1)}, u32[]{:S(2)}, u32[]{:S(2)}) collective-permute-start(f32[3,8,10,128]{3,2,1,0:T(8,128)S(1)} %get-tuple-element.35), channel_id=1, source_target_pairs={{0,32},{32,64},{64,96},{96,128},{128,160},{160,192},{192,224},{224... | collective-permute-start | bytes 368648 | tf_op jit(solution)/shard_map/ppermute | solution.py:267
  72.4 3.3 %collective-permute-done.9.xhi = f32[3,8,10,128]{3,2,1,0:T(8,128)S(1)} collective-permute-done((f32[3,8,10,128]{3,2,1,0:T(8,128)S(1)}, f32[3,8,10,128]{3,2,1,0:T(8,128)S(1)}, u32[]{:S(2)}, u32[]{:S(2)}) %collective-permute-start.9) | collective-permute-done | bytes 122912 | tf_op jit(solution)/shard_map/ppermute | solution.py:268
  75.8 1.0 %collective-permute-done.8.xlo = f32[3,8,10,128]{3,2,1,0:T(8,128)S(1)} collective-permute-done((f32[3,8,10,128]{3,2,1,0:T(8,128)S(1)}, f32[3,8,10,128]{3,2,1,0:T(8,128)S(1)}, u32[]{:S(2)}, u32[]{:S(2)}) %collective-permute-start.8) | collective-permute-done | bytes 122912 | tf_op jit(solution)/shard_map/ppermute | solution.py:267
  76.8 1.1 %collective-permute-start.10 = (f32[3,26,8,128]{3,2,1,0:T(8,128)S(1)}, f32[3,26,8,128]{3,2,1,0:T(8,128)S(1)}, u32[]{:S(2)}, u32[]{:S(2)}) collective-permute-start(f32[3,26,8,128]{3,2,1,0:T(8,128)S(1)} %pad_maximum_fusion.2), channel_id=1, source_target_pairs={{0,1},{1,2},{2,3},{3,4},{4,5},{5,6},{6,7},{7,8},{8,9},{9,10},{10,1... | collective-permute-start | bytes 958472 | tf_op jit(solution)/shard_map/ppermute | solution.py:267
  78.0 3.8 %collective-permute-done.10.ylo = f32[3,26,8,128]{3,2,1,0:T(8,128)S(1)} collective-permute-done((f32[3,26,8,128]{3,2,1,0:T(8,128)S(1)}, f32[3,26,8,128]{3,2,1,0:T(8,128)S(1)}, u32[]{:S(2)}, u32[]{:S(2)}) %collective-permute-start.10) | collective-permute-done | bytes 319520 | tf_op jit(solution)/shard_map/ppermute | solution.py:267
  81.8 5.9 %collective-permute-done.11.yhi = f32[3,26,8,128]{3,2,1,0:T(8,128)S(1)} collective-permute-done((f32[3,26,8,128]{3,2,1,0:T(8,128)S(1)}, f32[3,26,8,128]{3,2,1,0:T(8,128)S(1)}, u32[]{:S(2)}, u32[]{:S(2)}) %collective-permute-start.11) | collective-permute-done | bytes 319520 | tf_op jit(solution)/shard_map/ppermute | solution.py:268
  87.7 7.1 %coarse_levels.1 = (f32[2,8,8,64]{3,2,1,0:T(8,128)}, f32[2,4,4,32]{3,2,1,0:T(4,128)}) custom-call(s32[2]{0:T(128)S(1)} %pad_add_fusion.place, f32[3,10,10,128]{3,2,1,0:T(8,128)S(1)} %get-tuple-element.17.fc_own, f32[3,8,10,128]{3,2,1,0:T(8,128)S(1)} %collective-permute-done.8.xlo, f32[3,8,10,128]{3,2,1,0:T(8,128)S(1)} %collective-permute-done.9.xhi, ...), custom_call_target="tpu_custom_call" | custom-call | tf_op jit(solution)/shard_map/coarse_levels/pallas_call | solution.py:338
  (52 shorter events, 3.7 us)
Async XLA Ops:
  0.6 1.6 %copy-start = (f32[2,32,32,256]{3,2,1,0:T(8,128)S(1)}, f32[2,32,32,256]{3,2,1,0:T(8,128)}, u32[]{:S(2)}) copy-start(f32[2,32,32,256]{3,2,1,0:T(8,128)} %f_own.1) | copy-start | bytes 6291460
  2.2 1.2 %copy-start.2 = (f32[32,32,256]{2,1,0:T(8,128)S(1)}, f32[32,32,256]{2,1,0:T(8,128)}, u32[]{:S(2)}) copy-start(f32[32,32,256]{2,1,0:T(8,128)} %c_own.1) | copy-start | bytes 3145732
  3.8 26.9 %copy-start.1 = (f32[2,32,32,256]{3,2,1,0:T(8,128)S(1)}, f32[2,32,32,256]{3,2,1,0:T(8,128)}, u32[]{:S(2)}) copy-start(f32[2,32,32,256]{3,2,1,0:T(8,128)} %f_own.1) | copy-start | bytes 6291460
  3.8 26.9 %copy-start.3 = (f32[32,32,256]{2,1,0:T(8,128)S(1)}, f32[32,32,256]{2,1,0:T(8,128)}, u32[]{:S(2)}) copy-start(f32[32,32,256]{2,1,0:T(8,128)} %c_own.1) | copy-start | bytes 3145732
  3.8 26.9 %copy-start.6 = (bf16[256,128]{1,0:T(8,128)(2,1)S(1)}, bf16[256,128]{1,0:T(8,128)(2,1)}, u32[]{:S(2)}) copy-start(bf16[256,128]{1,0:T(8,128)(2,1)} %constant.24.clone.w_mean) | copy-start | bytes 196612
  3.8 5.9 %collective-permute-start = (f32[3,3,32,256]{3,2,1,0:T(8,128)S(1)}, f32[3,3,32,256]{3,2,1,0:T(8,128)S(1)}, u32[]{:S(2)}, u32[]{:S(2)}) collective-permute-start(f32[3,3,32,256]{3,2,1,0:T(8,128)S(1)} %get-tuple-element.12), channel_id=1, source_target_pairs={{0,1},{1,2},{2,3},{3,4},{4,5},{5,6},{6,7},{7,8},{8,9},{9,10},{10,1... | collective-permute-start | bytes 884744 | tf_op jit(solution)/shard_map/ppermute | solution.py:267
  6.0 9.5 %collective-permute-start.1 = (f32[3,3,32,256]{3,2,1,0:T(8,128)S(1)}, f32[3,3,32,256]{3,2,1,0:T(8,128)S(1)}, u32[]{:S(2)}, u32[]{:S(2)}) collective-permute-start(f32[3,3,32,256]{3,2,1,0:T(8,128)S(1)} %get-tuple-element.13), channel_id=1, source_target_pairs={{1,0},{2,1},{3,2},{4,3},{5,4},{6,5},{7,6},{8,7},{9,8},{10,9},{11,1... | collective-permute-start | bytes 884744 | tf_op jit(solution)/shard_map/ppermute | solution.py:268
  15.5 0.7 copy-start.4
  17.3 10.0 %collective-permute-start.3 = (f32[3,3,40,256]{3,2,1,0:T(8,128)}, f32[3,3,40,256]{3,2,1,0:T(8,128)}, u32[]{:S(2)}, u32[]{:S(2)}) collective-permute-start(f32[3,3,40,256]{3,2,1,0:T(8,128)} %get-tuple-element.44), channel_id=1, source_target_pairs={{32,0},{64,32},{96,64},{128,96},{160,128},{192,160},{224,192},{0,2... | collective-permute-start | bytes 1105928 | tf_op jit(solution)/shard_map/ppermute | solution.py:268
  21.1 9.6 %collective-permute-start.2 = (f32[3,3,40,256]{3,2,1,0:T(8,128)}, f32[3,3,40,256]{3,2,1,0:T(8,128)}, u32[]{:S(2)}, u32[]{:S(2)}) collective-permute-start(f32[3,3,40,256]{3,2,1,0:T(8,128)} %get-tuple-element.45), channel_id=1, source_target_pairs={{0,32},{32,64},{64,96},{96,128},{128,160},{160,192},{192,224},{224... | collective-permute-start | bytes 1105928 | tf_op jit(solution)/shard_map/ppermute | solution.py:267
  30.7 1.0 %copy-start.5 = (f32[3,3,32,256]{3,2,1,0:T(8,128)S(1)}, f32[3,3,32,256]{3,2,1,0:T(8,128)}, u32[]{:S(2)}) copy-start(f32[3,3,32,256]{3,2,1,0:T(8,128)} %copy-done.4) | copy-start | bytes 884740
  31.7 0.8 copy-start.7
  46.9 17.5 %copy-start.10 = (bf16[128,128]{1,0:T(8,128)(2,1)S(1)}, bf16[128,128]{1,0:T(8,128)(2,1)}, u32[]{:S(2)}) copy-start(bf16[128,128]{1,0:T(8,128)(2,1)} %constant.26.clone.w_mean) | copy-start | bytes 98308
  46.9 17.5 %copy-start.11 = (bf16[128,128]{1,0:T(8,128)(2,1)S(1)}, bf16[128,128]{1,0:T(8,128)(2,1)}, u32[]{:S(2)}) copy-start(bf16[128,128]{1,0:T(8,128)(2,1)} %constant.25.clone.w_full) | copy-start | bytes 98308
  46.9 4.2 %collective-permute-start.5 = (f32[3,5,16,128]{3,2,1,0:T(8,128)S(1)}, f32[3,5,16,128]{3,2,1,0:T(8,128)S(1)}, u32[]{:S(2)}, u32[]{:S(2)}) collective-permute-start(f32[3,5,16,128]{3,2,1,0:T(8,128)S(1)} %get-tuple-element.26), channel_id=1, source_target_pairs={{32,0},{64,32},{96,64},{128,96},{160,128},{192,160},{224,192},{0,2... | collective-permute-start | bytes 368648 | tf_op jit(solution)/shard_map/ppermute | solution.py:268
  47.0 5.2 %collective-permute-start.4 = (f32[3,5,16,128]{3,2,1,0:T(8,128)S(1)}, f32[3,5,16,128]{3,2,1,0:T(8,128)S(1)}, u32[]{:S(2)}, u32[]{:S(2)}) collective-permute-start(f32[3,5,16,128]{3,2,1,0:T(8,128)S(1)} %get-tuple-element.27), channel_id=1, source_target_pairs={{0,32},{32,64},{64,96},{96,128},{128,160},{160,192},{192,224},{224... | collective-permute-start | bytes 368648 | tf_op jit(solution)/shard_map/ppermute | solution.py:267
  52.2 6.2 %collective-permute-start.6 = (f32[3,26,8,128]{3,2,1,0:T(8,128)S(1)}, f32[3,26,8,128]{3,2,1,0:T(8,128)S(1)}, u32[]{:S(2)}, u32[]{:S(2)}) collective-permute-start(f32[3,26,8,128]{3,2,1,0:T(8,128)S(1)} %pad_maximum_fusion), channel_id=1, source_target_pairs={{0,1},{1,2},{2,3},{3,4},{4,5},{5,6},{6,7},{7,8},{8,9},{9,10},{10,1... | collective-permute-start | bytes 958472 | tf_op jit(solution)/shard_map/ppermute | solution.py:267
  54.5 33.2 %copy-start.8 = (bf16[128,128]{1,0:T(8,128)(2,1)S(1)}, bf16[128,128]{1,0:T(8,128)(2,1)}, u32[]{:S(2)}) copy-start(bf16[128,128]{1,0:T(8,128)(2,1)} %constant.28.clone.w_mean) | copy-start | bytes 98308
  54.5 33.2 %copy-start.9 = (bf16[128,128]{1,0:T(8,128)(2,1)S(1)}, bf16[128,128]{1,0:T(8,128)(2,1)}, u32[]{:S(2)}) copy-start(bf16[128,128]{1,0:T(8,128)(2,1)} %constant.27.clone.w_full) | copy-start | bytes 98308
  54.5 9.8 %collective-permute-start.7 = (f32[3,26,8,128]{3,2,1,0:T(8,128)S(1)}, f32[3,26,8,128]{3,2,1,0:T(8,128)S(1)}, u32[]{:S(2)}, u32[]{:S(2)}) collective-permute-start(f32[3,26,8,128]{3,2,1,0:T(8,128)S(1)} %pad_maximum_fusion.1), channel_id=1, source_target_pairs={{1,0},{2,1},{3,2},{4,3},{5,4},{6,5},{7,6},{8,7},{9,8},{10,9},{11,1... | collective-permute-start | bytes 958472 | tf_op jit(solution)/shard_map/ppermute | solution.py:268
  70.8 4.9 %collective-permute-start.9 = (f32[3,8,10,128]{3,2,1,0:T(8,128)S(1)}, f32[3,8,10,128]{3,2,1,0:T(8,128)S(1)}, u32[]{:S(2)}, u32[]{:S(2)}) collective-permute-start(f32[3,8,10,128]{3,2,1,0:T(8,128)S(1)} %get-tuple-element.34), channel_id=1, source_target_pairs={{32,0},{64,32},{96,64},{128,96},{160,128},{192,160},{224,192},{0,2... | collective-permute-start | bytes 368648 | tf_op jit(solution)/shard_map/ppermute | solution.py:268
  70.9 5.8 %collective-permute-start.8 = (f32[3,8,10,128]{3,2,1,0:T(8,128)S(1)}, f32[3,8,10,128]{3,2,1,0:T(8,128)S(1)}, u32[]{:S(2)}, u32[]{:S(2)}) collective-permute-start(f32[3,8,10,128]{3,2,1,0:T(8,128)S(1)} %get-tuple-element.35), channel_id=1, source_target_pairs={{0,32},{32,64},{64,96},{96,128},{128,160},{160,192},{192,224},{224... | collective-permute-start | bytes 368648 | tf_op jit(solution)/shard_map/ppermute | solution.py:267
  76.8 5.0 %collective-permute-start.10 = (f32[3,26,8,128]{3,2,1,0:T(8,128)S(1)}, f32[3,26,8,128]{3,2,1,0:T(8,128)S(1)}, u32[]{:S(2)}, u32[]{:S(2)}) collective-permute-start(f32[3,26,8,128]{3,2,1,0:T(8,128)S(1)} %pad_maximum_fusion.2), channel_id=1, source_target_pairs={{0,1},{1,2},{2,3},{3,4},{4,5},{5,6},{6,7},{7,8},{8,9},{9,10},{10,1... | collective-permute-start | bytes 958472 | tf_op jit(solution)/shard_map/ppermute | solution.py:267
  77.9 9.8 %collective-permute-start.11 = (f32[3,26,8,128]{3,2,1,0:T(8,128)S(1)}, f32[3,26,8,128]{3,2,1,0:T(8,128)S(1)}, u32[]{:S(2)}, u32[]{:S(2)}) collective-permute-start(f32[3,26,8,128]{3,2,1,0:T(8,128)S(1)} %pad_maximum_fusion.3), channel_id=1, source_target_pairs={{1,0},{2,1},{3,2},{4,3},{5,4},{6,5},{7,6},{8,7},{9,8},{10,9},{11,1... | collective-permute-start | bytes 958472 | tf_op jit(solution)/shard_map/ppermute | solution.py:268

commit v2 on v0

v2 whole, which is shorter than its diff:
```python
import functools
import jax
import jax.numpy as jnp
import numpy as np
from jax import lax
from jax.experimental import pallas as pl
from jax.experimental.pallas import tpu as pltpu
from jax.sharding import PartitionSpec as P

DAMPING = 0.8
SHIFT_IMAG = 0.5
LANES = 128
VMEM = pl.BlockSpec(memory_space=pltpu.VMEM)
SMEM = pl.BlockSpec(memory_space=pltpu.SMEM)


def params(mib):
    return pltpu.CompilerParams(vmem_limit_bytes=mib * 1024 * 1024)


def around(ref, k, x, row, rows, full):
    halves = ref.shape[2]
    mid = [ref[k, x, h, pl.ds(row, rows), :] for h in range(halves)]
    up = [pltpu.roll(m, 1, 1) for m in mid]
    down = [pltpu.roll(m, LANES - 1, 1) for m in mid]
    if full:
        lane = lax.broadcasted_iota(jnp.int32, mid[0].shape, 1)
        first, last = lane == 0, lane == LANES - 1
        up = [jnp.where(first, up[h - 1] if h else 0.0, up[h]) for h in range(halves)]
        down = [jnp.where(last, down[h + 1] if h < halves - 1 else 0.0, down[h]) for h in range(halves)]
    sums = []
    for h in range(halves):
        planes = ref[k, x - 1, h, pl.ds(row, rows), :] + ref[k, x + 1, h, pl.ds(row, rows), :]
        sides = ref[k, x, h, pl.ds(row - 1, rows), :] + ref[k, x, h, pl.ds(row + 1, rows), :]
        sums.append((planes + sides) + (up[h] + down[h]))
    return sums


def inverse(c, scale, ok):
    a = 6.0 / scale - c
    b = SHIFT_IMAG * c
    g = DAMPING / (a * a + b * b)
    if ok is not None:
        g = jnp.where(ok, g, 0.0)
    return g * a, g * b


def divided(re, im, a, b):
    return re * a + im * b, im * a - re * b


def point(re, im, c, scale, ok, u, ga, gb, x, h, row):
    a, b = inverse(c, scale, ok)
    at = pl.ds(row, c.shape[0])
    ga[x, h, at, :], gb[x, h, at, :] = a, b
    u[0, x, h, at, :], u[1, x, h, at, :] = divided(re, im, a, b)


def second(u, ga, gb, e, x, row, rows, scale, full):
    s_re, s_im = around(u, 0, x, row, rows, full), around(u, 1, x, row, rows, full)
    at = pl.ds(row, rows)
    for h in range(u.shape[2]):
        a, b = ga[x, h, at, :], gb[x, h, at, :]
        if scale != 1.0:
            a, b = a * (1.0 / scale), b * (1.0 / scale)
        d = divided(s_re[h], s_im[h], a, b)
        for k in (0, 1):
            e[k, x, h, at, :] = 0.4 * u[k, x, h, at, :] + d[k]


def rows_inside(shape, y0, ysize):
    row = lax.broadcasted_iota(jnp.int32, shape, 0) + y0
    return (row >= 0) & (row < ysize)


def restrict_xy(r, t, out, i, plane, row, rows, k):
    for h in range(r.shape[2]):
        val = (r[k, plane, h] + r[k, plane + 3, h]) + 3.0 * (r[k, plane + 1, h] + r[k, plane + 2, h])
        t[k, h] = val
        part = [t[k, h, pl.ds(row + j, rows, 2), :] for j in range(4)]
        out[k, i, pl.ds(0, rows), pl.ds(LANES * h, LANES)] = (part[0] + part[3]) + 3.0 * (part[1] + part[2])


def add_pairs(c0, c1, t, h, out, i, row, rows):
    t[0, h, pl.ds(0, c0.shape[0]), :] = c0 + c1
    val = t[0, h, pl.ds(row, rows, 2), :] + t[0, h, pl.ds(row + 1, rows, 2), :]
    out[i, pl.ds(0, rows), pl.ds(LANES * h, LANES)] = val


def weights(zsize, lanes_in, lanes_out):
    full = np.zeros((lanes_in, lanes_out), np.float32)
    mean = np.zeros((lanes_in, lanes_out), np.float32)
    for i in range(zsize // 2):
        for j, w in enumerate((1.0, 3.0, 3.0, 1.0)):
            z = 2 * i - 1 + j
            if 0 <= z < zsize:
                full[z, i] = w / 512.0
        mean[2 * i, i] = mean[2 * i + 1, i] = 0.125
    return jnp.asarray(full, jnp.bfloat16), jnp.asarray(mean, jnp.bfloat16)


def exact_dot(part, w):
    planes, rows, lanes = part.shape
    x = part.reshape(planes * rows, lanes)
    hi = x.astype(jnp.bfloat16)
    rest = x - hi.astype(jnp.float32)
    mid = rest.astype(jnp.bfloat16)
    low = (rest - mid.astype(jnp.float32)).astype(jnp.bfloat16)
    dot = functools.partial(jnp.dot, preferred_element_type=jnp.float32)
    return (dot(hi, w) + (dot(mid, w) + dot(low, w))).reshape(planes, rows, w.shape[1])


PX, PY = 3, 8


def inner_kernel(f, c, w_mean, u, e, r, ga, gb, c_out, t, part):
    n, rows, lanes = c.shape
    halves = lanes // LANES
    at = pl.ds(PY, rows)
    cut = [pl.ds(LANES * h, LANES) for h in range(halves)]

    def first(x, carry):
        for h in range(halves):
            point(f[0, x, :, cut[h]], f[1, x, :, cut[h]], c[x, :, cut[h]], 1.0, None, u, ga, gb, x + PX, h, PY)
        return carry

    lax.fori_loop(0, n, first, 0, unroll=2)

    def middle(x, carry):
        second(u, ga, gb, e, x + PX, PY, rows, 1.0, True)
        return carry

    lax.fori_loop(1, n - 1, middle, 0, unroll=2)
    row = lax.broadcasted_iota(jnp.int32, (rows, LANES), 0)
    full = (row >= 2) & (row < rows - 2)

    def last(x, carry):
        for k in (0, 1):
            s = around(e, k, x + PX, PY, rows, True)
            for h in range(halves):
                r[k, x + PX, h, at, :] = 0.04 * f[k, x, :, cut[h]] + jnp.where(full, s[h], 0.0)
        return carry

    lax.fori_loop(2, n - 2, last, 0, unroll=2)
    for x in (0, 1, n - 2, n - 1):
        for k in (0, 1):
            for h in range(halves):
                r[k, x + PX, h, at, :] = 0.04 * f[k, x, :, cut[h]]

    def pairs(i, carry):
        for h in range(halves):
            add_pairs(c[2 * i, :, cut[h]], c[2 * i + 1, :, cut[h]], t, h, part, i, 0, rows // 2)
        return carry

    lax.fori_loop(0, n // 2, pairs, 0, unroll=2)
    c_out[...] = exact_dot(part[...], w_mean[...])


def outer_kernel(xsize, ysize, place, u_in, e_in, r_in, ga_in, gb_in, xlo, xhi, ylo, yhi, clo, chi, c_own, w_full, u, e, r, ga, gb, fc_out, t, part):
    n, rows, lanes = ylo.shape[1], xlo.shape[2], xlo.shape[3]
    halves = lanes // LANES
    cut = [pl.ds(LANES * h, LANES) for h in range(halves)]
    x0, y0 = place[0] * n - PX, place[1] * rows - PY
    del u_in, e_in, r_in, ga_in, gb_in

    def ok(x, row, count):
        gx = x + x0
        return rows_inside((count, LANES), y0 + row, ysize) & ((gx >= 0) & (gx < xsize))

    def halo(src, i, x, row):
        for h in range(halves):
            re, im, c = [src[k, i, :, cut[h]] for k in range(3)]
            good = ok(x, row, c.shape[0])
            point(re, im, c, 1.0, good, u, ga, gb, x, h, row)
            at = pl.ds(row, c.shape[0])
            for k, val in ((0, re), (1, im)):
                r[k, x, h, at, :] = jnp.where(good, 0.04 * val, 0.0)

    for i in range(PX):
        for side, x in ((xlo, i), (xhi, n + PX + i)):
            halo(side, i, x, PY)
            j = i if side is xlo else PX + i
            halo(clo, j, x, PY - 4)
            halo(chi, j, x, PY + rows)

    def strips(x, carry):
        halo(ylo, x, x + PX, PY - 4)
        halo(yhi, x, x + PX, PY + rows)
        return carry

    lax.fori_loop(0, n, strips, 0, unroll=2)
    low, high = PY - 4, PY + rows - 4

    for x in (PX - 2, PX - 1, PX, n + PX - 1, n + PX, n + PX + 1):
        second(u, ga, gb, e, x, low, rows + 8, 1.0, True)

    def middle(x, carry):
        for row in (low, high):
            second(u, ga, gb, e, x, row, 8, 1.0, True)
        return carry

    lax.fori_loop(PX + 1, n + PX - 1, middle, 0, unroll=2)

    def finish(x, row, count, good):
        for k in (0, 1):
            s = around(e, k, x, row, count, True)
            for h in range(halves):
                at = pl.ds(row, count)
                r[k, x, h, at, :] = r[k, x, h, at, :] + jnp.where(good, s[h], 0.0)

    for x in (PX - 1, PX, PX + 1, n + PX - 2, n + PX - 1, n + PX):
        finish(x, low, rows + 8, ok(x, low, rows + 8))
    row = lax.broadcasted_iota(jnp.int32, (8, LANES), 0)
    good_low = rows_inside((8, LANES), y0 + low, ysize) & (row < 6)
    good_high = rows_inside((8, LANES), y0 + high, ysize) & (row >= 2)

    def last(x, carry):
        finish(x, low, 8, good_low)
        finish(x, high, 8, good_high)
        return carry

    lax.fori_loop(PX + 2, n + PX - 2, last, 0, unroll=2)

    def coarse(i, carry):
        for k in (0, 1):
            restrict_xy(r, t, part, i, 2 * i + PX - 1, PY - 1, rows // 2, k)
        return carry

    lax.fori_loop(0, n // 2, coarse, 0, unroll=2)
    for k in (0, 1):
        fc_out[k] = exact_dot(part[k], w_full[...])
    fc_out[2] = c_own[...]


def iterate_kernel(u, e, out):
    n, rows = out.shape[1:3]
    at = pl.ds(PY, rows)

    def step(x, carry):
        for k in (0, 1):
            for h in range(u.shape[2]):
                out[k, x, :, pl.ds(LANES * h, LANES)] = e[k, x + PX, h, at, :] + 0.8 * u[k, x + PX, h, at, :]
        return carry

    lax.fori_loop(0, n, step, 0, unroll=2)


def whole_level(fc, u, e, r, ga, gb, planes, used, row, rows, scale, full, ok, u_put):
    first, count = used
    for x in range(planes):
        cells = [fc[k, x, 0, pl.ds(first, count), :] for k in range(3)]
        point(*cells, scale, ok(x, first, count), u, ga, gb, x, 0, first)
    at = pl.ds(row, rows)
    for x in range(1, planes - 1):
        second(u, ga, gb, e, x, row, rows, scale, full)
        u_put(x)
    for x in range(2, planes - 2):
        good = ok(x, row, rows)
        for k in (0, 1):
            s = around(e, k, x, row, rows, full)[0] * (1.0 / scale)
            r[k, x, 0, at, :] = jnp.where(good, 0.04 * fc[k, x, 0, at, :] + s, 0.0)


def middle_kernel(halo, over, xsize, ysize, place, fc_own, xlo, xhi, ylo, yhi, w_full, w_mean, u_out, fc_out, fc, ga, gb, u, e, r, t, part, part_c):
    n, rows = fc_own.shape[1:3]
    planes = n + 2 * halo
    for k in range(3):
        for src, x, count in ((xlo, 0, halo), (fc_own, halo, n), (xhi, n + halo, halo)):
            fc[k, pl.ds(x, count), 0, pl.ds(8, rows), :] = src[k]
        fc[k, :, 0, pl.ds(0, 8), :] = ylo[k]
        fc[k, :, 0, pl.ds(8 + rows, 8), :] = yhi[k]
    x0, y0 = place[0] * n - halo, place[1] * rows - 8

    def ok(x, row, count):
        gx = x + x0
        return rows_inside((count, LANES), y0 + row, ysize) & ((gx >= 0) & (gx < xsize))

    def u_put(x):
        if halo <= x < n + halo:
            at = pl.ds(8, rows)
            for k in (0, 1):
                u_out[k, x - halo] = e[k, x, 0, at, :] + 0.8 * u[k, x, 0, at, :]

    whole_level(fc, u, e, r, ga, gb, planes, (0, rows + 16), 4, rows + 8, 4.0, True, ok, u_put)
    width = n // 2 + 2 * over
    for i in range(width):
        x, row = 2 * i + halo - 1 - 2 * over, 7 - 2 * over
        for k in (0, 1):
            restrict_xy(r, t, part, i, x, row, width, k)
        add_pairs(fc[2, x + 1, 0], fc[2, x + 2, 0], t, 0, part_c, i, row + 1, width)
    for k in (0, 1):
        fc_out[k] = exact_dot(part[k], w_full[...])[:, :width]
    fc_out[2] = exact_dot(part_c[...], w_mean[...])[:, :width]


def coarse_kernel(n, sweeps, xsize, ysize, zsize, place, fc_own, xlo, xhi, ylo, yhi, w_full, w_mean, u_out, v_out, fc, ga, gb, u, e, r, t, part, part_c, gc, gd, v, w):
    m = n // 2
    for k in range(3):
        for src, x, count in ((xlo, 0, 8), (fc_own, 8, n + 2), (xhi, n + 10, 8)):
            fc[k, pl.ds(x, count), 0, pl.ds(15, n + 2), :] = src[k]
        fc[k, :, 0, pl.ds(7, 8), :] = ylo[k]
        fc[k, :, 0, pl.ds(n + 17, 8), :] = yhi[k]
    lane = lax.broadcasted_iota(jnp.int32, (1, LANES), 1)

    def inside(x0, y0, xs, ys, zs):
        def ok(x, row, count):
            gx = x + x0
            here = rows_inside((count, LANES), y0 + row, ys) & (lane < zs)
            return here & ((gx >= 0) & (gx < xs))

        return ok

    def u_put(x):
        if 9 <= x < n + 9:
            at = pl.ds(16, n)
            for k in (0, 1):
                u_out[k, x - 9] = (e[k, x, 0, at, :] + 0.8 * u[k, x, 0, at, :])[:, :zsize]

    ok = inside(place[0] * n - 9, place[1] * n - 16, xsize, ysize, zsize)
    whole_level(fc, u, e, r, ga, gb, n + 18, (7, n + 18), 8, n + 16, 16.0, False, ok, u_put)
    width = m + 6
    for i in range(width):
        for k in (0, 1):
            restrict_xy(r, t, part, i, 2 * i + 2, 9, width, k)
        add_pairs(fc[2, 2 * i + 3, 0], fc[2, 2 * i + 4, 0], t, 0, part_c, i, 10, width)
    f = [exact_dot(part[k], w_full[...]) for k in (0, 1)] + [exact_dot(part_c[...], w_mean[...])]
    ok = inside(place[0] * m - 3, place[1] * m - 3, xsize // 2, ysize // 2, zsize // 2)
    for x in range(width):
        point(f[0][x], f[1][x], f[2][x], 64.0, ok(x, 0, 16), v, gc, gd, x, 0, 0)
    old = v
    for sweep in range(1, sweeps):
        new = w.at[sweep % 2]
        for x in range(sweep, width - sweep):
            at = pl.ds(1, m + 4)
            s = [around(old, k, x, 1, m + 4, False)[0] for k in (0, 1)]
            d = divided(*s, gc[x, 0, at, :] * (1.0 / 64.0), gd[x, 0, at, :] * (1.0 / 64.0))
            for k in (0, 1):
                val = 0.2 * old[k, x, 0, at, :] + v[k, x, 0, at, :] + d[k]
                if sweep < sweeps - 1:
                    new[k, x, 0, at, :] = val
                else:
                    v_out[k, x - 3] = val[2 : 2 + m, : zsize // 2]
        old = new


def body(source, wavenumber_sq):
    f32 = jnp.float32
    xdev, ydev = lax.axis_size("gx"), lax.axis_size("gy")
    place = jnp.stack([lax.axis_index("gx"), lax.axis_index("gy")]).astype(jnp.int32)

    def swap(axis, devices, first, last):
        before = lax.ppermute(last, axis, [(i, (i + 1) % devices) for i in range(devices)])
        after = lax.ppermute(first, axis, [((i + 1) % devices, i) for i in range(devices)])
        return before, after

    _, n, rows, lanes = source.shape
    xsize, ysize = n * xdev, rows * ydev
    S = lambda *shape: jax.ShapeDtypeStruct(shape, f32)
    V = lambda *shape: pltpu.VMEM(shape, f32)

    def both(*cut):
        return jnp.concatenate([source[(slice(None),) + cut], wavenumber_sq[cut][None]], 0)

    whole = slice(None)
    xlo, xhi = swap("gx", xdev, both(slice(0, PX)), both(slice(n - PX, n)))
    ylo, yhi = swap("gy", ydev, both(whole, slice(0, 4)), both(whole, slice(rows - 4, rows)))
    corners = jnp.concatenate([xlo, xhi], 1)
    clo, chi = swap("gy", ydev, corners[:, :, :4], corners[:, :, rows - 4 :])
    halves = lanes // LANES
    w_full, w_mean = weights(lanes, lanes, lanes // 2)
    state = (n + 2 * PX, halves, rows + 2 * PY, LANES)
    part = (n // 2, rows // 2, lanes)
    u, e, r, ga, gb, c_next = pl.pallas_call(
        inner_kernel,
        in_specs=[VMEM] * 3,
        out_specs=[VMEM] * 6,
        out_shape=[S(2, *state)] * 3 + [S(*state)] * 2 + [S(n // 2, rows // 2, lanes // 2)],
        scratch_shapes=[V(1, halves, rows, LANES), V(*part)],
        compiler_params=params(24),
        cost_estimate=pl.CostEstimate(flops=100_000_000, bytes_accessed=16_000_000, transcendentals=0),
        name="inner_cells",
    )(source, wavenumber_sq, w_mean)
    u, e, _, _, _, fc = pl.pallas_call(
        functools.partial(outer_kernel, xsize, ysize),
        in_specs=[SMEM] + [VMEM] * 13,
        out_specs=[VMEM] * 6,
        out_shape=[S(2, *state)] * 3 + [S(*state)] * 2 + [S(3, n // 2, rows // 2, lanes // 2)],
        input_output_aliases={1: 0, 2: 1, 3: 2, 4: 3, 5: 4},
        scratch_shapes=[V(2, halves, rows + 2 * PY, LANES), V(2, *part)],
        compiler_params=params(24),
        name="outer_cells",
    )(place, u, e, r, ga, gb, xlo, xhi, ylo, yhi, clo, chi, c_next, w_full)
    fine = pl.pallas_call(
        iterate_kernel,
        in_specs=[VMEM] * 2,
        out_specs=VMEM,
        out_shape=S(2, n, rows, lanes),
        compiler_params=params(24),
        cost_estimate=pl.CostEstimate(flops=1_000_000, bytes_accessed=8_000_000, transcendentals=0),
        name="fine_iterate",
    )(u, e)

    n, rows, lanes, xsize, ysize, zsize = n // 2, rows // 2, lanes // 2, xsize // 2, ysize // 2, lanes // 2
    h, over = 5, 1
    xlo, xhi = swap("gx", xdev, fc[:, :h], fc[:, n - h :])
    first_rows, last_rows = [jnp.concatenate([a[:, :, s : s + 8] for a in (xlo, fc, xhi)], 1) for s in (0, rows - 8)]
    ylo, yhi = swap("gy", ydev, first_rows, last_rows)
    w_full, w_mean = weights(zsize, lanes, lanes)
    state = (n + 2 * h, 1, rows + 16, LANES)
    scratch = lambda s, width: [V(3, *s), V(*s), V(*s), V(2, *s), V(2, *s), V(2, *s), V(2, 1, *s[2:]), V(2, width, 16, LANES), V(width, 16, LANES)]
    width = n // 2 + 2 * over
    second_u, fc = pl.pallas_call(
        functools.partial(middle_kernel, h, over, xsize, ysize),
        in_specs=[SMEM] + [VMEM] * 7,
        out_specs=[VMEM] * 2,
        out_shape=[S(2, n, rows, lanes), S(3, width, width, lanes)],
        scratch_shapes=scratch(state, width),
        compiler_params=params(24),
        name="second_level",
    )(place, fc, xlo, xhi, ylo, yhi, w_full, w_mean)

    n, xsize, ysize, zsize = n // 2, xsize // 2, ysize // 2, zsize // 2
    xlo, xhi = swap("gx", xdev, fc[:, 2:], fc[:, :n])
    first_rows, last_rows = [jnp.concatenate([a[:, :, s : s + 8] for a in (xlo, fc, xhi)], 1) for s in (2, 0)]
    ylo, yhi = swap("gy", ydev, first_rows, last_rows)
    w_full, w_mean = weights(zsize, lanes, lanes)
    state = (n + 18, 1, 40, LANES)
    m = n // 2
    small = (m + 6, 1, 16, LANES)
    third, coarse = pl.pallas_call(
        functools.partial(coarse_kernel, n, 4, xsize, ysize, zsize),
        in_specs=[SMEM] + [VMEM] * 7,
        out_specs=[VMEM] * 2,
        out_shape=[S(2, n, n, zsize), S(2, m, m, zsize // 2)],
        scratch_shapes=scratch(state, m + 6) + [V(*small), V(*small), V(2, *small), V(2, 2, *small)],
        compiler_params=params(24),
        name="coarse_levels",
    )(place, fc, xlo, xhi, ylo, yhi, w_full, w_mean)
    return fine, second_u, third, coarse


def solution(mesh):
    placed = (P(None, "gx", "gy", None), P("gx", "gy", None))
    return jax.shard_map(body, mesh=mesh, in_specs=placed, out_specs=(P(None, "gx", "gy", None),) * 4, check_vma=False)
```

time: 408 us -> 77.8 us (0.19)
  the two profiles are of different devices: /device:TPU:120 before, /device:TPU:31 now
where the time goes in v2:
time: 77.8 us; the launch traced here: 77.7 us
  waiting for transfers between devices  29.5 us (38%)
  starting transfers between devices  22.5 us (29%)
  Pallas kernels  17.9 us (23%)
  local copies, waits for them, and re-layouts  3.52 us (5%)
  other arithmetic  3.36 us (4%)
  between operations  0.88 us (1%)
    ppermute x7, waiting for transfers between devices, swap(): lax.ppermute(first, axis, [((i + 1) % devices, i) for i in range(devices)])  19.3 us
    ppermute x7, starting transfers between devices, swap(): lax.ppermute(last, axis, [(i, (i + 1) % devices) for i in range(devices)])  14.2 us
    ppermute x7, waiting for transfers between devices, swap(): lax.ppermute(last, axis, [(i, (i + 1) % devices) for i in range(devices)])  10.2 us
    ppermute x7, starting transfers between devices, swap(): lax.ppermute(first, axis, [((i + 1) % devices, i) for i in range(devices)])  8.27 us
    pallas_call x1, Pallas kernels, body(): pl.pallas_call(functools.partial(outer_kernel, xsize, ysize), in_specs=[S...  6.58 us
    pallas_call x1, Pallas kernels, body(): pl.pallas_call(inner_kernel, in_specs=[VMEM] * 3, out_specs=[VMEM] * 6, o...  5.24 us
    concatenate x4, other arithmetic, both(): jnp.concatenate([source[(slice(None),) + cut], wavenumber_sq[cut][None]], 0)  3.2 us
    pallas_call x1, Pallas kernels, body(): pl.pallas_call(functools.partial(coarse_kernel, n, 4, xsize, ysize, zsize...  2.54 us
  transfers between devices with their start and end apart: 14, of which 9 were waited for; matrix products, arithmetic and copies ran while one was open for 5% of the time, Pallas kernels for 9%

profile of v2, /device:TPU:31, one launch (start us, length us, event | category | flops | bytes accessed | tf_op | source)
XLA Modules:
  0.0 77.7 jit_solution(15090664737139775760)
XLA Ops:
  0.7 1.1 %slice_bitcast_fusion.2 = (f32[1,3,32,256]{3,2,1,0:T(8,128)S(1)}, f32[1,3,32,256]{3,2,1,0:T(8,128)S(1)}) fusion(f32[32,32,256]{2,1,0:T(8,128)} %c.1), kind=kLoop, calls=%fused_computation.10 | loop fusion | bytes 393216 | tf_op jit(solution)/shard_map/broadcast_in_dim | solution.py:362
  1.8 1.1 %fusion.1 = (f32[2,3,32,256]{3,2,1,0:T(8,128)S(1)}, f32[2,3,32,256]{3,2,1,0:T(8,128)S(1)}) fusion(f32[2,32,32,256]{3,2,1,0:T(8,128)} %f.1), kind=kLoop, calls=%fused_computation.16 | loop fusion | bytes 786432 | tf_op jit(solution)/shard_map/slice | solution.py:362
  3.6 1.6 %collective-permute-start = (f32[3,3,32,256]{3,2,1,0:T(8,128)}, f32[3,3,32,256]{3,2,1,0:T(8,128)S(1)}, u32[]{:S(2)}, u32[]{:S(2)}) collective-permute-start(f32[3,3,32,256]{3,2,1,0:T(8,128)} %pad_maximum_fusion.6), channel_id=1, source_target_pairs={{0,32},{32,64},{64,96},{96,128},{128,160},{160,192},{192,224},{224... | collective-permute-start | bytes 884744 | tf_op jit(solution)/shard_map/ppermute | solution.py:352
  6.0 3.9 %collective-permute-start.1 = (f32[3,3,32,256]{3,2,1,0:T(8,128)}, f32[3,3,32,256]{3,2,1,0:T(8,128)}, u32[]{:S(2)}, u32[]{:S(2)}) collective-permute-start(f32[3,3,32,256]{3,2,1,0:T(8,128)} %pad_maximum_fusion.7), channel_id=1, source_target_pairs={{32,0},{64,32},{96,64},{128,96},{160,128},{192,160},{224,192},{0,2... | collective-permute-start | bytes 884744 | tf_op jit(solution)/shard_map/ppermute | solution.py:353
  12.7 5.2 %inner_cells.1 = (f32[2,38,2,48,128]{4,3,2,1,0:T(8,128)S(1)}, f32[2,38,2,48,128]{4,3,2,1,0:T(8,128)S(1)}, f32[2,38,2,48,128]{4,3,2,1,0:T(8,128)S(1)}, f32[38,2,4...) custom-call(f32[2,32,32,256]{3,2,1,0:T(8,128)S(1)} %copy-done, ...), custom_call_target="tpu_custom_call" | custom-call | flops 100000000 | bytes 16000000 | tf_op jit(solution)/shard_map/inner_cells/pallas_call | solution.py:373
  19.1 1.8 %collective-permute-start.5 = (f32[3,6,4,256]{3,2,1,0:T(4,128)S(1)}, f32[3,6,4,256]{3,2,1,0:T(4,128)S(1)}, u32[]{:S(2)}, u32[]{:S(2)}) collective-permute-start(f32[3,6,4,256]{3,2,1,0:T(4,128)S(1)} %get-tuple-element.38), channel_id=1, source_target_pairs={{1,0},{2,1},{3,2},{4,3},{5,4},{6,5},{7,6},{8,7},{9,8},{10,9},{11,1... | collective-permute-start | bytes 221192 | tf_op jit(solution)/shard_map/ppermute | solution.py:353
  20.9 3.3 %collective-permute-start.4 = (f32[3,6,4,256]{3,2,1,0:T(4,128)S(1)}, f32[3,6,4,256]{3,2,1,0:T(4,128)S(1)}, u32[]{:S(2)}, u32[]{:S(2)}) collective-permute-start(f32[3,6,4,256]{3,2,1,0:T(4,128)S(1)} %get-tuple-element.39), channel_id=1, source_target_pairs={{0,1},{1,2},{2,3},{3,4},{4,5},{5,6},{6,7},{7,8},{8,9},{9,10},{10,1... | collective-permute-start | bytes 221192 | tf_op jit(solution)/shard_map/ppermute | solution.py:352
  24.3 2.0 %collective-permute-done.5.chi = f32[3,6,4,256]{3,2,1,0:T(4,128)S(1)} collective-permute-done((f32[3,6,4,256]{3,2,1,0:T(4,128)S(1)}, f32[3,6,4,256]{3,2,1,0:T(4,128)S(1)}, u32[]{:S(2)}, u32[]{:S(2)}) %collective-permute-start.5) | collective-permute-done | bytes 73760 | tf_op jit(solution)/shard_map/ppermute | solution.py:353
  26.3 6.6 %outer_cells.1 = (f32[2,38,2,48,128]{4,3,2,1,0:T(8,128)S(1)}, f32[2,38,2,48,128]{4,3,2,1,0:T(8,128)S(1)}, f32[2,38,2,48,128]{4,3,2,1,0:T(8,128)S(1)}, f32[38,2,4...) custom-call(s32[2]{0:T(128)S(1)} %pad_add_fusion.place, ...), custom_call_target="tpu_custom_call", output_to_operand_aliasing={{0}: (1, {}), {1}: (2, {}), {2}: (3, {}), {3}: (4, {}), {4}... | custom-call | tf_op jit(solution)/shard_map/outer_cells/pallas_call | solution.py:383
  32.9 1.8 %collective-permute-start.7 = (f32[3,5,16,128]{3,2,1,0:T(8,128)S(1)}, f32[3,5,16,128]{3,2,1,0:T(8,128)S(1)}, u32[]{:S(2)}, u32[]{:S(2)}) collective-permute-start(f32[3,5,16,128]{3,2,1,0:T(8,128)S(1)} %get-tuple-element.42), channel_id=1, source_target_pairs={{32,0},{64,32},{96,64},{128,96},{160,128},{192,160},{224,192},{0,2... | collective-permute-start | bytes 368648 | tf_op jit(solution)/shard_map/ppermute | solution.py:353
  34.7 2.2 %collective-permute-done.7.xhi = f32[3,5,16,128]{3,2,1,0:T(8,128)S(1)} collective-permute-done((f32[3,5,16,128]{3,2,1,0:T(8,128)S(1)}, f32[3,5,16,128]{3,2,1,0:T(8,128)S(1)}, u32[]{:S(2)}, u32[]{:S(2)}) %collective-permute-start.7) | collective-permute-done | bytes 122912 | tf_op jit(solution)/shard_map/ppermute | solution.py:353
  37.0 3.2 %collective-permute-done.6.xlo = f32[3,5,16,128]{3,2,1,0:T(8,128)S(1)} collective-permute-done((f32[3,5,16,128]{3,2,1,0:T(8,128)S(1)}, f32[3,5,16,128]{3,2,1,0:T(8,128)S(1)}, u32[]{:S(2)}, u32[]{:S(2)}) %collective-permute-start.6) | collective-permute-done | bytes 122912 | tf_op jit(solution)/shard_map/ppermute | solution.py:352
  40.3 6.0 %collective-permute-start.8 = (f32[3,26,8,128]{3,2,1,0:T(8,128)S(1)}, f32[3,26,8,128]{3,2,1,0:T(8,128)S(1)}, u32[]{:S(2)}, u32[]{:S(2)}) collective-permute-start(f32[3,26,8,128]{3,2,1,0:T(8,128)S(1)} %pad_maximum_fusion.2), channel_id=1, source_target_pairs={{0,1},{1,2},{2,3},{3,4},{4,5},{5,6},{6,7},{7,8},{8,9},{9,10},{10,1... | collective-permute-start | bytes 958472 | tf_op jit(solution)/shard_map/ppermute | solution.py:352
  46.4 3.8 %collective-permute-done.8.ylo = f32[3,26,8,128]{3,2,1,0:T(8,128)S(1)} collective-permute-done((f32[3,26,8,128]{3,2,1,0:T(8,128)S(1)}, f32[3,26,8,128]{3,2,1,0:T(8,128)S(1)}, u32[]{:S(2)}, u32[]{:S(2)}) %collective-permute-start.8) | collective-permute-done | bytes 319520 | tf_op jit(solution)/shard_map/ppermute | solution.py:352
  50.2 5.9 %collective-permute-done.9.yhi = f32[3,26,8,128]{3,2,1,0:T(8,128)S(1)} collective-permute-done((f32[3,26,8,128]{3,2,1,0:T(8,128)S(1)}, f32[3,26,8,128]{3,2,1,0:T(8,128)S(1)}, u32[]{:S(2)}, u32[]{:S(2)}) %collective-permute-start.9) | collective-permute-done | bytes 319520 | tf_op jit(solution)/shard_map/ppermute | solution.py:353
  56.1 1.9 %second_level.1 = (f32[2,16,16,128]{3,2,1,0:T(8,128)}, f32[3,10,10,128]{3,2,1,0:T(8,128)S(1)}) custom-call(s32[2]{0:T(128)S(1)} %pad_add_fusion.place, f32[3,16,16,128]{3,2,1,0:T(8,128)S(1)} %get-tuple-element.25.fc_own, f32[3,5,16,128]{3,2,1,0:T(8,128)S(1)} %collective-permute-done.6.xlo, f32[3,5,16,128]{3,2,1,0:T(8,128)S(1)} %collective-permute-done.7.xhi, ...), custom_call_target="tpu_custom_call" | custom-call | tf_op jit(solution)/shard_map/second_level/pallas_call | solution.py:412
  58.3 1.5 %collective-permute-start.10 = (f32[3,8,10,128]{3,2,1,0:T(8,128)S(1)}, f32[3,8,10,128]{3,2,1,0:T(8,128)S(1)}, u32[]{:S(2)}, u32[]{:S(2)}) collective-permute-start(f32[3,8,10,128]{3,2,1,0:T(8,128)S(1)} %get-tuple-element.47), channel_id=1, source_target_pairs={{0,32},{32,64},{64,96},{96,128},{128,160},{160,192},{192,224},{224... | collective-permute-start | bytes 368648 | tf_op jit(solution)/shard_map/ppermute | solution.py:352
  59.8 3.3 %collective-permute-done.11.xhi = f32[3,8,10,128]{3,2,1,0:T(8,128)S(1)} collective-permute-done((f32[3,8,10,128]{3,2,1,0:T(8,128)S(1)}, f32[3,8,10,128]{3,2,1,0:T(8,128)S(1)}, u32[]{:S(2)}, u32[]{:S(2)}) %collective-permute-start.11) | collective-permute-done | bytes 122912 | tf_op jit(solution)/shard_map/ppermute | solution.py:353
  63.1 1.0 %collective-permute-done.10.xlo = f32[3,8,10,128]{3,2,1,0:T(8,128)S(1)} collective-permute-done((f32[3,8,10,128]{3,2,1,0:T(8,128)S(1)}, f32[3,8,10,128]{3,2,1,0:T(8,128)S(1)}, u32[]{:S(2)}, u32[]{:S(2)}) %collective-permute-start.10) | collective-permute-done | bytes 122912 | tf_op jit(solution)/shard_map/ppermute | solution.py:352
  64.2 1.1 %collective-permute-start.12 = (f32[3,26,8,128]{3,2,1,0:T(8,128)S(1)}, f32[3,26,8,128]{3,2,1,0:T(8,128)S(1)}, u32[]{:S(2)}, u32[]{:S(2)}) collective-permute-start(f32[3,26,8,128]{3,2,1,0:T(8,128)S(1)} %pad_maximum_fusion.4), channel_id=1, source_target_pairs={{0,1},{1,2},{2,3},{3,4},{4,5},{5,6},{6,7},{7,8},{8,9},{9,10},{10,1... | collective-permute-start | bytes 958472 | tf_op jit(solution)/shard_map/ppermute | solution.py:352
  65.4 1.7 %fine_iterate.1 = f32[2,32,32,256]{3,2,1,0:T(8,128)} custom-call(f32[2,38,2,48,128]{4,3,2,1,0:T(8,128)S(1)} %get-tuple-element.23.u, f32[2,38,2,48,128]{4,3,2,1,0:T(8,128)S(1)} %get-tuple-element.24.e), custom_call_target="tpu_custom_call" | custom-call | flops 1000000 | bytes 8000000 | tf_op jit(solution)/shard_map/fine_iterate/pallas_call | solution.py:393
  67.1 2.1 %collective-permute-done.12.ylo = f32[3,26,8,128]{3,2,1,0:T(8,128)S(1)} collective-permute-done((f32[3,26,8,128]{3,2,1,0:T(8,128)S(1)}, f32[3,26,8,128]{3,2,1,0:T(8,128)S(1)}, u32[]{:S(2)}, u32[]{:S(2)}) %collective-permute-start.12) | collective-permute-done | bytes 319520 | tf_op jit(solution)/shard_map/ppermute | solution.py:352
  69.2 5.9 %collective-permute-done.13.yhi = f32[3,26,8,128]{3,2,1,0:T(8,128)S(1)} collective-permute-done((f32[3,26,8,128]{3,2,1,0:T(8,128)S(1)}, f32[3,26,8,128]{3,2,1,0:T(8,128)S(1)}, u32[]{:S(2)}, u32[]{:S(2)}) %collective-permute-start.13) | collective-permute-done | bytes 319520 | tf_op jit(solution)/shard_map/ppermute | solution.py:353
  75.1 2.5 %coarse_levels.1 = (f32[2,8,8,64]{3,2,1,0:T(8,128)}, f32[2,4,4,32]{3,2,1,0:T(4,128)}) custom-call(s32[2]{0:T(128)S(1)} %pad_add_fusion.place, f32[3,10,10,128]{3,2,1,0:T(8,128)S(1)} %get-tuple-element.27.fc_own, f32[3,8,10,128]{3,2,1,0:T(8,128)S(1)} %collective-permute-done.10.xlo, f32[3,8,10,128]{3,2,1,0:T(8,128)S(1)} %collective-permute-done.11.xhi, ...), custom_call_target="tpu_custom_call" | custom-call | tf_op jit(solution)/shard_map/coarse_levels/pallas_call | solution.py:430
  (49 shorter events, 6.1 us)
Async XLA Ops:
  0.6 9.3 %copy-start = (f32[2,32,32,256]{3,2,1,0:T(8,128)S(1)}, f32[2,32,32,256]{3,2,1,0:T(8,128)}, u32[]{:S(2)}) copy-start(f32[2,32,32,256]{3,2,1,0:T(8,128)} %f.1) | copy-start | bytes 6291460
  0.6 9.4 %copy-start.1 = (f32[32,32,256]{2,1,0:T(8,128)S(1)}, f32[32,32,256]{2,1,0:T(8,128)}, u32[]{:S(2)}) copy-start(f32[32,32,256]{2,1,0:T(8,128)} %c.1) | copy-start | bytes 3145732
  2.8 9.9 %copy-start.3 = (bf16[256,128]{1,0:T(8,128)(2,1)S(1)}, bf16[256,128]{1,0:T(8,128)(2,1)}, u32[]{:S(2)}) copy-start(bf16[256,128]{1,0:T(8,128)(2,1)} %constant.22.clone.w_mean) | copy-start | bytes 196612
  3.6 14.4 %collective-permute-start = (f32[3,3,32,256]{3,2,1,0:T(8,128)}, f32[3,3,32,256]{3,2,1,0:T(8,128)S(1)}, u32[]{:S(2)}, u32[]{:S(2)}) collective-permute-start(f32[3,3,32,256]{3,2,1,0:T(8,128)} %pad_maximum_fusion.6), channel_id=1, source_target_pairs={{0,32},{32,64},{64,96},{96,128},{128,160},{160,192},{192,224},{224... | collective-permute-start | bytes 884744 | tf_op jit(solution)/shard_map/ppermute | solution.py:352
  6.0 12.1 %collective-permute-start.1 = (f32[3,3,32,256]{3,2,1,0:T(8,128)}, f32[3,3,32,256]{3,2,1,0:T(8,128)}, u32[]{:S(2)}, u32[]{:S(2)}) collective-permute-start(f32[3,3,32,256]{3,2,1,0:T(8,128)} %pad_maximum_fusion.7), channel_id=1, source_target_pairs={{32,0},{64,32},{96,64},{128,96},{160,128},{192,160},{224,192},{0,2... | collective-permute-start | bytes 884744 | tf_op jit(solution)/shard_map/ppermute | solution.py:353
  10.9 15.3 %collective-permute-start.2 = (f32[3,32,4,256]{3,2,1,0:T(4,128)}, f32[3,32,4,256]{3,2,1,0:T(4,128)}, u32[]{:S(2)}, u32[]{:S(2)}) collective-permute-start(f32[3,32,4,256]{3,2,1,0:T(4,128)} %pad_maximum_fusion), channel_id=1, source_target_pairs={{0,1},{1,2},{2,3},{3,4},{4,5},{5,6},{6,7},{7,8},{8,9},{9,10},{10,1... | collective-permute-start | bytes 1179656 | tf_op jit(solution)/shard_map/ppermute | solution.py:352
  12.5 13.8 %collective-permute-start.3 = (f32[3,32,4,256]{3,2,1,0:T(4,128)}, f32[3,32,4,256]{3,2,1,0:T(4,128)}, u32[]{:S(2)}, u32[]{:S(2)}) collective-permute-start(f32[3,32,4,256]{3,2,1,0:T(4,128)} %pad_maximum_fusion.1), channel_id=1, source_target_pairs={{1,0},{2,1},{3,2},{4,3},{5,4},{6,5},{7,6},{8,7},{9,8},{10,9},{11,1... | collective-permute-start | bytes 1179656 | tf_op jit(solution)/shard_map/ppermute | solution.py:353
  12.7 13.5 %copy-start.2 = (bf16[256,128]{1,0:T(8,128)(2,1)S(1)}, bf16[256,128]{1,0:T(8,128)(2,1)}, u32[]{:S(2)}) copy-start(bf16[256,128]{1,0:T(8,128)(2,1)} %constant.21.clone.w_full) | copy-start | bytes 196612
  19.1 7.2 %collective-permute-start.5 = (f32[3,6,4,256]{3,2,1,0:T(4,128)S(1)}, f32[3,6,4,256]{3,2,1,0:T(4,128)S(1)}, u32[]{:S(2)}, u32[]{:S(2)}) collective-permute-start(f32[3,6,4,256]{3,2,1,0:T(4,128)S(1)} %get-tuple-element.38), channel_id=1, source_target_pairs={{1,0},{2,1},{3,2},{4,3},{5,4},{6,5},{7,6},{8,7},{9,8},{10,9},{11,1... | collective-permute-start | bytes 221192 | tf_op jit(solution)/shard_map/ppermute | solution.py:353
  20.9 5.4 %collective-permute-start.4 = (f32[3,6,4,256]{3,2,1,0:T(4,128)S(1)}, f32[3,6,4,256]{3,2,1,0:T(4,128)S(1)}, u32[]{:S(2)}, u32[]{:S(2)}) collective-permute-start(f32[3,6,4,256]{3,2,1,0:T(4,128)S(1)} %get-tuple-element.39), channel_id=1, source_target_pairs={{0,1},{1,2},{2,3},{3,4},{4,5},{5,6},{6,7},{7,8},{8,9},{9,10},{10,1... | collective-permute-start | bytes 221192 | tf_op jit(solution)/shard_map/ppermute | solution.py:352
  32.8 23.2 %copy-start.6 = (bf16[128,128]{1,0:T(8,128)(2,1)S(1)}, bf16[128,128]{1,0:T(8,128)(2,1)}, u32[]{:S(2)}) copy-start(bf16[128,128]{1,0:T(8,128)(2,1)} %constant.24.clone.w_mean) | copy-start | bytes 98308
  32.9 23.2 %copy-start.7 = (bf16[128,128]{1,0:T(8,128)(2,1)S(1)}, bf16[128,128]{1,0:T(8,128)(2,1)}, u32[]{:S(2)}) copy-start(bf16[128,128]{1,0:T(8,128)(2,1)} %constant.23.clone.w_full) | copy-start | bytes 98308
  32.9 4.1 %collective-permute-start.7 = (f32[3,5,16,128]{3,2,1,0:T(8,128)S(1)}, f32[3,5,16,128]{3,2,1,0:T(8,128)S(1)}, u32[]{:S(2)}, u32[]{:S(2)}) collective-permute-start(f32[3,5,16,128]{3,2,1,0:T(8,128)S(1)} %get-tuple-element.42), channel_id=1, source_target_pairs={{32,0},{64,32},{96,64},{128,96},{160,128},{192,160},{224,192},{0,2... | collective-permute-start | bytes 368648 | tf_op jit(solution)/shard_map/ppermute | solution.py:353
  34.7 5.5 %collective-permute-start.6 = (f32[3,5,16,128]{3,2,1,0:T(8,128)S(1)}, f32[3,5,16,128]{3,2,1,0:T(8,128)S(1)}, u32[]{:S(2)}, u32[]{:S(2)}) collective-permute-start(f32[3,5,16,128]{3,2,1,0:T(8,128)S(1)} %get-tuple-element.43), channel_id=1, source_target_pairs={{0,32},{32,64},{64,96},{96,128},{128,160},{160,192},{192,224},{224... | collective-permute-start | bytes 368648 | tf_op jit(solution)/shard_map/ppermute | solution.py:352
  40.3 9.9 %collective-permute-start.8 = (f32[3,26,8,128]{3,2,1,0:T(8,128)S(1)}, f32[3,26,8,128]{3,2,1,0:T(8,128)S(1)}, u32[]{:S(2)}, u32[]{:S(2)}) collective-permute-start(f32[3,26,8,128]{3,2,1,0:T(8,128)S(1)} %pad_maximum_fusion.2), channel_id=1, source_target_pairs={{0,1},{1,2},{2,3},{3,4},{4,5},{5,6},{6,7},{7,8},{8,9},{9,10},{10,1... | collective-permute-start | bytes 958472 | tf_op jit(solution)/shard_map/ppermute | solution.py:352
  46.3 9.8 %collective-permute-start.9 = (f32[3,26,8,128]{3,2,1,0:T(8,128)S(1)}, f32[3,26,8,128]{3,2,1,0:T(8,128)S(1)}, u32[]{:S(2)}, u32[]{:S(2)}) collective-permute-start(f32[3,26,8,128]{3,2,1,0:T(8,128)S(1)} %pad_maximum_fusion.3), channel_id=1, source_target_pairs={{1,0},{2,1},{3,2},{4,3},{5,4},{6,5},{7,6},{8,7},{9,8},{10,9},{11,1... | collective-permute-start | bytes 958472 | tf_op jit(solution)/shard_map/ppermute | solution.py:353
  58.0 5.1 %collective-permute-start.11 = (f32[3,8,10,128]{3,2,1,0:T(8,128)S(1)}, f32[3,8,10,128]{3,2,1,0:T(8,128)S(1)}, u32[]{:S(2)}, u32[]{:S(2)}) collective-permute-start(f32[3,8,10,128]{3,2,1,0:T(8,128)S(1)} %get-tuple-element.46), channel_id=1, source_target_pairs={{32,0},{64,32},{96,64},{128,96},{160,128},{192,160},{224,192},{0,2... | collective-permute-start | bytes 368648 | tf_op jit(solution)/shard_map/ppermute | solution.py:353
  58.3 5.8 %collective-permute-start.10 = (f32[3,8,10,128]{3,2,1,0:T(8,128)S(1)}, f32[3,8,10,128]{3,2,1,0:T(8,128)S(1)}, u32[]{:S(2)}, u32[]{:S(2)}) collective-permute-start(f32[3,8,10,128]{3,2,1,0:T(8,128)S(1)} %get-tuple-element.47), channel_id=1, source_target_pairs={{0,32},{32,64},{64,96},{96,128},{128,160},{160,192},{192,224},{224... | collective-permute-start | bytes 368648 | tf_op jit(solution)/shard_map/ppermute | solution.py:352
  64.2 5.1 %collective-permute-start.12 = (f32[3,26,8,128]{3,2,1,0:T(8,128)S(1)}, f32[3,26,8,128]{3,2,1,0:T(8,128)S(1)}, u32[]{:S(2)}, u32[]{:S(2)}) collective-permute-start(f32[3,26,8,128]{3,2,1,0:T(8,128)S(1)} %pad_maximum_fusion.4), channel_id=1, source_target_pairs={{0,1},{1,2},{2,3},{3,4},{4,5},{5,6},{6,7},{7,8},{8,9},{9,10},{10,1... | collective-permute-start | bytes 958472 | tf_op jit(solution)/shard_map/ppermute | solution.py:352
  65.3 9.8 %collective-permute-start.13 = (f32[3,26,8,128]{3,2,1,0:T(8,128)S(1)}, f32[3,26,8,128]{3,2,1,0:T(8,128)S(1)}, u32[]{:S(2)}, u32[]{:S(2)}) collective-permute-start(f32[3,26,8,128]{3,2,1,0:T(8,128)S(1)} %pad_maximum_fusion.5), channel_id=1, source_target_pairs={{1,0},{2,1},{3,2},{4,3},{5,4},{6,5},{7,6},{8,7},{9,8},{10,9},{11,1... | collective-permute-start | bytes 958472 | tf_op jit(solution)/shard_map/ppermute | solution.py:353
  65.4 9.7 %copy-start.4 = (bf16[128,128]{1,0:T(8,128)(2,1)S(1)}, bf16[128,128]{1,0:T(8,128)(2,1)}, u32[]{:S(2)}) copy-start(bf16[128,128]{1,0:T(8,128)(2,1)} %constant.26.clone.w_mean) | copy-start | bytes 98308
  65.4 9.7 %copy-start.5 = (bf16[128,128]{1,0:T(8,128)(2,1)S(1)}, bf16[128,128]{1,0:T(8,128)(2,1)}, u32[]{:S(2)}) copy-start(bf16[128,128]{1,0:T(8,128)(2,1)} %constant.25.clone.w_full) | copy-start | bytes 98308

commit v3 on v2

--- a/solution.py
+++ b/solution.py
@@ -73,12 +73,13 @@
     return (row >= 0) & (row < ysize)
 
 
-def restrict_xy(r, t, out, i, plane, row, rows, k):
+def restrict_xy(r, t, out, to, plane, row, rows, k, window):
+    at = pl.ds(*window)
     for h in range(r.shape[2]):
-        val = (r[k, plane, h] + r[k, plane + 3, h]) + 3.0 * (r[k, plane + 1, h] + r[k, plane + 2, h])
-        t[k, h] = val
+        val = (r[k, plane, h, at, :] + r[k, plane + 3, h, at, :]) + 3.0 * (r[k, plane + 1, h, at, :] + r[k, plane + 2, h, at, :])
+        t[k, h, at, :] = val
         part = [t[k, h, pl.ds(row + j, rows, 2), :] for j in range(4)]
-        out[k, i, pl.ds(0, rows), pl.ds(LANES * h, LANES)] = (part[0] + part[3]) + 3.0 * (part[1] + part[2])
+        out[k, to, pl.ds(0, rows), pl.ds(LANES * h, LANES)] = (part[0] + part[3]) + 3.0 * (part[1] + part[2])
 
 
 def add_pairs(c0, c1, t, h, out, i, row, rows):
@@ -113,7 +114,45 @@
 PX, PY = 3, 8
 
 
-def inner_kernel(f, c, w_mean, u, e, r, ga, gb, c_out, t, part):
+def pack_kernel(f, c, f_out, c_out, x_first, x_last, y_first, y_last, sems):
+    n, rows, lanes = c_out.shape
+    cuts = [(0, PX), (n - PX, PX)]
+    step = (n - 2 * PX + 3) // 4
+    inner = [(x, min(step, n - PX - x)) for x in range(PX, n - PX, step)]
+    copies = []
+    for x, count in cuts + inner:
+        at = pl.ds(x, count)
+        copies += [(f.at[0, at], f_out.at[0, at]), (f.at[1, at], f_out.at[1, at]), (c.at[at], c_out.at[at])]
+    copies = [pltpu.make_async_copy(src, dst, sems.at[i]) for i, (src, dst) in enumerate(copies)]
+    for copy in copies:
+        copy.start()
+    for copy in copies[:6]:
+        copy.wait()
+    for out, first, c_first in ((x_first, 0, 0), (x_last, n - PX, n - 2)):
+        for j in range(PX):
+            x = first + j
+            a, b = inverse(c_out[x], 1.0, None)
+            out[j], out[PX + j] = divided(f_out[0, x], f_out[1, x], a, b)
+        for j in range(2):
+            out[2 * PX + j] = c_out[c_first + j]
+    for copy in copies[6:]:
+        copy.wait()
+    row = lax.broadcasted_iota(jnp.int32, (8, lanes), 0)
+
+    def strip(x, carry):
+        for out, start, shifts in ((y_first, 0, (0, 3, 6)), (y_last, rows - 8, (3, 6, 0))):
+            at = pl.ds(start, 8)
+            cc = c_out[x, at, :]
+            a, b = inverse(cc, 1.0, None)
+            re, im = divided(f_out[0, x, at, :], f_out[1, x, at, :], a, b)
+            re, im, cc = [pltpu.roll(v, shift, 0) if shift else v for v, shift in zip((re, im, cc), shifts)]
+            out[x] = jnp.where(row < 3, re, jnp.where(row < 6, im, cc))
+        return carry
+
+    lax.fori_loop(0, n, strip, 0, unroll=4)
+
+
+def inner_kernel(f, c, w_full, w_mean, u, e, r, ga, gb, fc_out, t, part):
     n, rows, lanes = c.shape
     halves = lanes // LANES
     at = pl.ds(PY, rows)
@@ -149,87 +188,150 @@
 
     def pairs(i, carry):
         for h in range(halves):
-            add_pairs(c[2 * i, :, cut[h]], c[2 * i + 1, :, cut[h]], t, h, part, i, 0, rows // 2)
+            add_pairs(c[2 * i, :, cut[h]], c[2 * i + 1, :, cut[h]], t, h, part.at[2], i, 0, rows // 2)
         return carry
 
     lax.fori_loop(0, n // 2, pairs, 0, unroll=2)
-    c_out[...] = exact_dot(part[...], w_mean[...])
-
-
-def outer_kernel(xsize, ysize, place, u_in, e_in, r_in, ga_in, gb_in, xlo, xhi, ylo, yhi, clo, chi, c_own, w_full, u, e, r, ga, gb, fc_out, t, part):
-    n, rows, lanes = ylo.shape[1], xlo.shape[2], xlo.shape[3]
-    halves = lanes // LANES
-    cut = [pl.ds(LANES * h, LANES) for h in range(halves)]
+
+    def coarse(i, carry):
+        for k in (0, 1):
+            restrict_xy(r, t, part, i, 2 * i + PX - 1, PY - 1, rows // 2, k, (PY, rows))
+        return carry
+
+    lax.fori_loop(2, n // 2 - 2, coarse, 0, unroll=2)
+    for k in (0, 1):
+        fc_out[k, 2 : n // 2 - 2] = exact_dot(part[k, 2 : n // 2 - 2], w_full[...])
+    fc_out[2] = exact_dot(part[2], w_mean[...])
+
+
+def inside(place, n, rows, xsize, ysize):
     x0, y0 = place[0] * n - PX, place[1] * rows - PY
-    del u_in, e_in, r_in, ga_in, gb_in
 
     def ok(x, row, count):
         gx = x + x0
         return rows_inside((count, LANES), y0 + row, ysize) & ((gx >= 0) & (gx < xsize))
 
-    def halo(src, i, x, row):
-        for h in range(halves):
-            re, im, c = [src[k, i, :, cut[h]] for k in range(3)]
-            good = ok(x, row, c.shape[0])
-            point(re, im, c, 1.0, good, u, ga, gb, x, h, row)
-            at = pl.ds(row, c.shape[0])
-            for k, val in ((0, re), (1, im)):
-                r[k, x, h, at, :] = jnp.where(good, 0.04 * val, 0.0)
-
-    for i in range(PX):
-        for side, x in ((xlo, i), (xhi, n + PX + i)):
-            halo(side, i, x, PY)
-            j = i if side is xlo else PX + i
-            halo(clo, j, x, PY - 4)
-            halo(chi, j, x, PY + rows)
+    return ok
+
+
+def halo(re, im, cc, good, u, ga, gb, r, x, h, row, c_here, r_here):
+    at = pl.ds(row, re.shape[0])
+    re, im = jnp.where(good, re, 0.0), jnp.where(good, im, 0.0)
+    u[0, x, h, at, :], u[1, x, h, at, :] = re, im
+    if c_here:
+        a, b = inverse(cc, 1.0, good)
+        ga[x, h, at, :], gb[x, h, at, :] = a, b
+    if r_here:
+        a, b = 0.05 * (6.0 - cc), (0.05 * SHIFT_IMAG) * cc
+        r[0, x, h, at, :], r[1, x, h, at, :] = re * a - im * b, im * a + re * b
+
+
+def finish(e, r, x, row, count, good):
+    for k in (0, 1):
+        s = around(e, k, x, row, count, True)
+        for h in range(e.shape[2]):
+            at = pl.ds(row, count)
+            r[k, x, h, at, :] = r[k, x, h, at, :] + jnp.where(good, s[h], 0.0)
+
+
+def plane_cells(side, low, i, h):
+    cut = pl.ds(LANES * h, LANES)
+    j = i - 1 if low else i
+    c_here = 0 <= j < 2
+    cc = side[2 * PX + j, :, cut] if c_here else None
+    return side[i, :, cut], side[PX + i, :, cut], cc, c_here, i == (PX - 1 if low else 0)
+
+
+def faces_kernel(xsize, ysize, place, u_in, e_in, r_in, ga_in, gb_in, fc_in, xlo, xhi, ylo, yhi, w_full, u, e, r, ga, gb, fc_out, part, q):
+    n, (rows, lanes) = ylo.shape[0], xlo.shape[1:]
+    halves = lanes // LANES
+    cut = [pl.ds(LANES * h, LANES) for h in range(halves)]
+    ok = inside(place, n, rows, xsize, ysize)
+    del u_in, e_in, r_in, ga_in, gb_in, fc_in
+    for side, low, base in ((xlo, True, 0), (xhi, False, n + PX)):
+        for i in range(PX):
+            good = ok(base + i, PY, rows)
+            for h in range(halves):
+                re, im, cc, c_here, r_here = plane_cells(side, low, i, h)
+                halo(re, im, cc, good, u, ga, gb, r, base + i, h, PY, c_here, r_here)
+    low, high = PY - 4, PY + rows - 4
+    good_lo, good_hi = ok(PX, 0, 8), ok(PX, PY + rows, 8)
 
     def strips(x, carry):
-        halo(ylo, x, x + PX, PY - 4)
-        halo(yhi, x, x + PX, PY + rows)
-        return carry
-
-    lax.fori_loop(0, n, strips, 0, unroll=2)
-    low, high = PY - 4, PY + rows - 4
-
+        for side, good, row, shifts in ((ylo, good_lo, 0, (5, 2, 0)), (yhi, good_hi, PY + rows, (0, 5, 2))):
+            for h in range(halves):
+                tile = side[x, :, cut[h]]
+                re, im, cc = [pltpu.roll(tile, shift, 0) if shift else tile for shift in shifts]
+                halo(re, im, cc, good, u, ga, gb, r, x + PX, h, row, True, True)
+        return carry
+
+    lax.fori_loop(0, n, strips, 0, unroll=4)
     for x in (PX - 2, PX - 1, PX, n + PX - 1, n + PX, n + PX + 1):
-        second(u, ga, gb, e, x, low, rows + 8, 1.0, True)
+        second(u, ga, gb, e, x, PY, rows, 1.0, True)
 
     def middle(x, carry):
         for row in (low, high):
             second(u, ga, gb, e, x, row, 8, 1.0, True)
         return carry
 
-    lax.fori_loop(PX + 1, n + PX - 1, middle, 0, unroll=2)
-
-    def finish(x, row, count, good):
-        for k in (0, 1):
-            s = around(e, k, x, row, count, True)
+    lax.fori_loop(PX + 1, n + PX - 1, middle, 0, unroll=3)
+    for x in (PX - 1, PX, PX + 1, n + PX - 2, n + PX - 1, n + PX):
+        finish(e, r, x, PY + 4, rows - 8, ok(x, PY + 4, rows - 8))
+    row = lax.broadcasted_iota(jnp.int32, (8, LANES), 0)
+    good_low, good_high = ok(PX, low, 8) & (row < 6), ok(PX, high, 8) & (row >= 2)
+
+    def last(x, carry):
+        finish(e, r, x, low, 8, good_low)
+        finish(e, r, x, high, 8, good_high)
+        return carry
+
+    lax.fori_loop(PX + 2, n + PX - 2, last, 0, unroll=4)
+    m = n // 2 - 4
+
+    def coarse(i, carry):
+        x = 2 * i + PX + 3
+        for k in (0, 1):
             for h in range(halves):
-                at = pl.ds(row, count)
-                r[k, x, h, at, :] = r[k, x, h, at, :] + jnp.where(good, s[h], 0.0)
-
+                for j, row in ((0, PY - 1), (8, PY + rows - 7)):
+                    at = pl.ds(row, 8)
+                    part[k, i, pl.ds(j, 8), cut[h]] = (r[k, x, h, at, :] + r[k, x + 3, h, at, :]) + 3.0 * (
+                        r[k, x + 1, h, at, :] + r[k, x + 2, h, at, :]
+                    )
+        return carry
+
+    lax.fori_loop(0, m, coarse, 0, unroll=4)
+    for k in (0, 1):
+        q[k] = exact_dot(part[k], w_full[...])
+        for row, start in ((0, 0), (rows // 2 - 2, 10)):
+            four = [q[k, :, pl.ds(start + j, 2, 2), :] for j in range(4)]
+            fc_out[k, pl.ds(2, m), pl.ds(row, 2), :] = (four[0] + four[3]) + 3.0 * (four[1] + four[2])
+
+
+def corners_kernel(xsize, ysize, n, rows, place, u_in, e_in, r_in, ga_in, gb_in, fc_in, clo, chi, w_full, u, e, r, ga, gb, fc_out, t, part):
+    halves = clo.shape[2] // LANES
+    ok = inside(place, n, rows, xsize, ysize)
+    del u_in, e_in, r_in, ga_in, gb_in, fc_in
+    low, high = PY - 4, PY + rows - 4
+    for side, row in ((clo, PY - 4), (chi, PY + rows)):
+        for planes, is_low, base in ((side.at[pl.ds(0, 8)], True, 0), (side.at[pl.ds(8, 8)], False, n + PX)):
+            for i in range(PX):
+                good = ok(base + i, row, 4)
+                for h in range(halves):
+                    re, im, cc, c_here, r_here = plane_cells(planes, is_low, i, h)
+                    halo(re, im, cc, good, u, ga, gb, r, base + i, h, row, c_here, r_here)
+    for x in (PX - 2, PX - 1, PX, n + PX - 1, n + PX, n + PX + 1):
+        for row in (low, high):
+            second(u, ga, gb, e, x, row, 8, 1.0, True)
     for x in (PX - 1, PX, PX + 1, n + PX - 2, n + PX - 1, n + PX):
-        finish(x, low, rows + 8, ok(x, low, rows + 8))
-    row = lax.broadcasted_iota(jnp.int32, (8, LANES), 0)
-    good_low = rows_inside((8, LANES), y0 + low, ysize) & (row < 6)
-    good_high = rows_inside((8, LANES), y0 + high, ysize) & (row >= 2)
-
-    def last(x, carry):
-        finish(x, low, 8, good_low)
-        finish(x, high, 8, good_high)
-        return carry
-
-    lax.fori_loop(PX + 2, n + PX - 2, last, 0, unroll=2)
-
-    def coarse(i, carry):
-        for k in (0, 1):
-            restrict_xy(r, t, part, i, 2 * i + PX - 1, PY - 1, rows // 2, k)
-        return carry
-
-    lax.fori_loop(0, n // 2, coarse, 0, unroll=2)
+        for row in (low, high):
+            finish(e, r, x, row, 8, ok(x, row, 8))
+    planes = (0, 1, n // 2 - 2, n // 2 - 1)
     for k in (0, 1):
-        fc_out[k] = exact_dot(part[k], w_full[...])
-    fc_out[2] = c_own[...]
+        for j, i in enumerate(planes):
+            restrict_xy(r, t, part, j, 2 * i + PX - 1, PY - 1, rows // 2, k, (low, rows + 8))
+        val = exact_dot(part[k], w_full[...])
+        for j, i in enumerate(planes):
+            fc_out[k, i] = val[j]
 
 
 def iterate_kernel(u, e, out):
@@ -245,11 +347,11 @@
     lax.fori_loop(0, n, step, 0, unroll=2)
 
 
-def whole_level(fc, u, e, r, ga, gb, planes, used, row, rows, scale, full, ok, u_put):
+def whole_level(cells, u, e, r, ga, gb, planes, used, row, rows, scale, full, ok, u_put):
     first, count = used
     for x in range(planes):
-        cells = [fc[k, x, 0, pl.ds(first, count), :] for k in range(3)]
-        point(*cells, scale, ok(x, first, count), u, ga, gb, x, 0, first)
+        at = pl.ds(first, count)
+        point(cells(0, x, at), cells(1, x, at), cells(2, x, at), scale, ok(x, first, count), u, ga, gb, x, 0, first)
     at = pl.ds(row, rows)
     for x in range(1, planes - 1):
         second(u, ga, gb, e, x, row, rows, scale, full)
@@ -258,7 +360,18 @@
         good = ok(x, row, rows)
         for k in (0, 1):
             s = around(e, k, x, row, rows, full)[0] * (1.0 / scale)
-            r[k, x, 0, at, :] = jnp.where(good, 0.04 * fc[k, x, 0, at, :] + s, 0.0)
+            r[k, x, 0, at, :] = jnp.where(good, 0.04 * cells(k, x, at) + s, 0.0)
+
+
+def rows_kernel(xlo, fc, xhi, first, last):
+    halo, n, rows = xlo.shape[1], fc.shape[1], fc.shape[2]
+    row = lax.broadcasted_iota(jnp.int32, (8, LANES), 0)
+    for src, base, count in ((xlo, 0, halo), (fc, halo, n), (xhi, n + halo, halo)):
+        for i in range(count):
+            for out, start, own in ((first, 0, row < 5), (last, rows - 8, row >= 3)):
+                re, im, cc = [src[k, i, pl.ds(start, 8), :] for k in range(3)]
+                out[0, base + i] = jnp.where(own, re, pltpu.roll(cc, 5, 0))
+                out[1, base + i] = jnp.where(own, im, pltpu.roll(cc, 2, 0))
 
 
 def middle_kernel(halo, over, xsize, ysize, place, fc_own, xlo, xhi, ylo, yhi, w_full, w_mean, u_out, fc_out, fc, ga, gb, u, e, r, t, part, part_c):
@@ -267,8 +380,13 @@
     for k in range(3):
         for src, x, count in ((xlo, 0, halo), (fc_own, halo, n), (xhi, n + halo, halo)):
             fc[k, pl.ds(x, count), 0, pl.ds(8, rows), :] = src[k]
-        fc[k, :, 0, pl.ds(0, 8), :] = ylo[k]
-        fc[k, :, 0, pl.ds(8 + rows, 8), :] = yhi[k]
+    row = lax.broadcasted_iota(jnp.int32, (8, LANES), 0)
+    for side, start, split in ((ylo, 0, 6), (yhi, 8 + rows, 3)):
+        at = pl.ds(start, 8)
+        for x in range(planes):
+            one, two = side[0, x], side[1, x]
+            fc[0, x, 0, at, :], fc[1, x, 0, at, :] = one, two
+            fc[2, x, 0, at, :] = jnp.where(row < split, pltpu.roll(one, 3, 0), pltpu.roll(two, 6, 0))
     x0, y0 = place[0] * n - halo, place[1] * rows - 8
 
     def ok(x, row, count):
@@ -281,26 +399,33 @@
             for k in (0, 1):
                 u_out[k, x - halo] = e[k, x, 0, at, :] + 0.8 * u[k, x, 0, at, :]
 
-    whole_level(fc, u, e, r, ga, gb, planes, (0, rows + 16), 4, rows + 8, 4.0, True, ok, u_put)
+    def cells(k, x, at):
+        return fc[k, x, 0, at, :]
+
+    whole_level(cells, u, e, r, ga, gb, planes, (0, rows + 16), 4, rows + 8, 4.0, True, ok, u_put)
     width = n // 2 + 2 * over
+    pairs = width // 2
     for i in range(width):
         x, row = 2 * i + halo - 1 - 2 * over, 7 - 2 * over
         for k in (0, 1):
-            restrict_xy(r, t, part, i, x, row, width, k)
-        add_pairs(fc[2, x + 1, 0], fc[2, x + 2, 0], t, 0, part_c, i, row + 1, width)
-    for k in (0, 1):
-        fc_out[k] = exact_dot(part[k], w_full[...])[:, :width]
-    fc_out[2] = exact_dot(part_c[...], w_mean[...])[:, :width]
+            restrict_xy(r, t, part, i, x, row, width, k, (4, rows + 8))
+        add_pairs(fc[2, x + 1, 0], fc[2, x + 2, 0], t, 0, part_c.at[i % 2], i // 2, row + 1, width)
+    fc_out[pl.ds(0, width)] = (exact_dot(part[0], w_full[0]) + exact_dot(part[1], w_full[1]))[:, :width]
+    fc_out[pl.ds(width, pairs)] = (exact_dot(part_c[0], w_mean[0]) + exact_dot(part_c[1], w_mean[1]))[:, :width]
 
 
 def coarse_kernel(n, sweeps, xsize, ysize, zsize, place, fc_own, xlo, xhi, ylo, yhi, w_full, w_mean, u_out, v_out, fc, ga, gb, u, e, r, t, part, part_c, gc, gd, v, w):
     m = n // 2
-    for k in range(3):
-        for src, x, count in ((xlo, 0, 8), (fc_own, 8, n + 2), (xhi, n + 10, 8)):
-            fc[k, pl.ds(x, count), 0, pl.ds(15, n + 2), :] = src[k]
-        fc[k, :, 0, pl.ds(7, 8), :] = ylo[k]
-        fc[k, :, 0, pl.ds(n + 17, 8), :] = yhi[k]
+    planes = n + 18
+    for src, x, first, count in ((xlo, 0, 0, 8), (fc_own, 8, 0, n + 2), (xhi, n + 10, 0, 8), (xlo, planes, 8, 4), (fc_own, planes + 4, n + 2, m + 1), (xhi, planes + m + 5, 8, 4)):
+        fc[pl.ds(x, count), 0, pl.ds(15, n + 2), :] = src[pl.ds(first, count)]
+    fc[:, 0, pl.ds(7, 8), :] = ylo[...]
+    fc[:, 0, pl.ds(n + 17, 8), :] = yhi[...]
     lane = lax.broadcasted_iota(jnp.int32, (1, LANES), 1)
+
+    def cells(k, x, at):
+        val = fc[planes + x // 2 if k == 2 else x, 0, at, :]
+        return pltpu.roll(val, LANES - zsize, 1) if k == 1 or (k == 2 and x % 2) else val
 
     def inside(x0, y0, xs, ys, zs):
         def ok(x, row, count):
@@ -317,12 +442,14 @@
                 u_out[k, x - 9] = (e[k, x, 0, at, :] + 0.8 * u[k, x, 0, at, :])[:, :zsize]
 
     ok = inside(place[0] * n - 9, place[1] * n - 16, xsize, ysize, zsize)
-    whole_level(fc, u, e, r, ga, gb, n + 18, (7, n + 18), 8, n + 16, 16.0, False, ok, u_put)
+    whole_level(cells, u, e, r, ga, gb, planes, (7, n + 18), 8, n + 16, 16.0, False, ok, u_put)
     width = m + 6
+    every = pl.ds(8, n + 16)
     for i in range(width):
         for k in (0, 1):
-            restrict_xy(r, t, part, i, 2 * i + 2, 9, width, k)
-        add_pairs(fc[2, 2 * i + 3, 0], fc[2, 2 * i + 4, 0], t, 0, part_c, i, 10, width)
+            restrict_xy(r, t, part, i, 2 * i + 2, 9, width, k, (8, n + 16))
+        t[0, 0, every, :] = cells(2, 2 * i + 3, every) + cells(2, 2 * i + 4, every)
+        part_c[i, pl.ds(0, width), :] = t[0, 0, pl.ds(10, width, 2), :] + t[0, 0, pl.ds(11, width, 2), :]
     f = [exact_dot(part[k], w_full[...]) for k in (0, 1)] + [exact_dot(part_c[...], w_mean[...])]
     ok = inside(place[0] * m - 3, place[1] * m - 3, xsize // 2, ysize // 2, zsize // 2)
     for x in range(width):
@@ -358,38 +485,57 @@
     S = lambda *shape: jax.ShapeDtypeStruct(shape, f32)
     V = lambda *shape: pltpu.VMEM(shape, f32)
 
-    def both(*cut):
-        return jnp.concatenate([source[(slice(None),) + cut], wavenumber_sq[cut][None]], 0)
-
-    whole = slice(None)
-    xlo, xhi = swap("gx", xdev, both(slice(0, PX)), both(slice(n - PX, n)))
-    ylo, yhi = swap("gy", ydev, both(whole, slice(0, 4)), both(whole, slice(rows - 4, rows)))
-    corners = jnp.concatenate([xlo, xhi], 1)
-    clo, chi = swap("gy", ydev, corners[:, :, :4], corners[:, :, rows - 4 :])
+    f, c, x_first, x_last, y_first, y_last = pl.pallas_call(
+        pack_kernel,
+        in_specs=[pl.BlockSpec(memory_space=pl.ANY)] * 2,
+        out_specs=[VMEM] * 6,
+        out_shape=[S(2, n, rows, lanes), S(n, rows, lanes)] + [S(8, rows, lanes)] * 2 + [S(n, 8, lanes)] * 2,
+        scratch_shapes=[pltpu.SemaphoreType.DMA((18,))],
+        compiler_params=params(48),
+        name="pack_faces",
+    )(source, wavenumber_sq)
+    xlo, xhi = swap("gx", xdev, x_first, x_last)
+    ylo, yhi = swap("gy", ydev, y_first, y_last)
+    planes = jnp.concatenate([xlo, xhi], 0)
+    clo, chi = swap("gy", ydev, planes[:, :4], planes[:, rows - 4 :])
     halves = lanes // LANES
     w_full, w_mean = weights(lanes, lanes, lanes // 2)
     state = (n + 2 * PX, halves, rows + 2 * PY, LANES)
     part = (n // 2, rows // 2, lanes)
-    u, e, r, ga, gb, c_next = pl.pallas_call(
+    shapes = [S(2, *state)] * 3 + [S(*state)] * 2 + [S(3, n // 2, rows // 2, lanes // 2)]
+    column = V(2, halves, rows + 2 * PY, LANES)
+    held = pl.pallas_call(
         inner_kernel,
-        in_specs=[VMEM] * 3,
+        in_specs=[VMEM] * 4,
         out_specs=[VMEM] * 6,
-        out_shape=[S(2, *state)] * 3 + [S(*state)] * 2 + [S(n // 2, rows // 2, lanes // 2)],
-        scratch_shapes=[V(1, halves, rows, LANES), V(*part)],
+        out_shape=shapes,
+        scratch_shapes=[column, V(3, *part)],
         compiler_params=params(24),
         cost_estimate=pl.CostEstimate(flops=100_000_000, bytes_accessed=16_000_000, transcendentals=0),
         name="inner_cells",
-    )(source, wavenumber_sq, w_mean)
+    )(f, c, w_full, w_mean)
+    in_place = {i + 1: i for i in range(6)}
+    held = pl.pallas_call(
+        functools.partial(faces_kernel, xsize, ysize),
+        in_specs=[SMEM] + [VMEM] * 11,
+        out_specs=[VMEM] * 6,
+        out_shape=shapes,
+        input_output_aliases=in_place,
+        scratch_shapes=[V(2, n // 2 - 4, 16, lanes), V(2, n // 2 - 4, 16, lanes // 2)],
+        compiler_params=params(24),
+        cost_estimate=pl.CostEstimate(flops=50_000_000, bytes_accessed=8_000_000, transcendentals=0),
+        name="face_cells",
+    )(place, *held, xlo, xhi, ylo, yhi, w_full)
     u, e, _, _, _, fc = pl.pallas_call(
-        functools.partial(outer_kernel, xsize, ysize),
-        in_specs=[SMEM] + [VMEM] * 13,
+        functools.partial(corners_kernel, xsize, ysize, n, rows),
+        in_specs=[SMEM] + [VMEM] * 9,
         out_specs=[VMEM] * 6,
-        out_shape=[S(2, *state)] * 3 + [S(*state)] * 2 + [S(3, n // 2, rows // 2, lanes // 2)],
-        input_output_aliases={1: 0, 2: 1, 3: 2, 4: 3, 5: 4},
-        scratch_shapes=[V(2, halves, rows + 2 * PY, LANES), V(2, *part)],
+        out_shape=shapes,
+        input_output_aliases=in_place,
+        scratch_shapes=[column, V(2, 4, rows // 2, lanes)],
         compiler_params=params(24),
-        name="outer_cells",
-    )(place, u, e, r, ga, gb, xlo, xhi, ylo, yhi, clo, chi, c_next, w_full)
+        name="corner_cells",
+    )(place, *held, clo, chi, w_full)
     fine = pl.pallas_call(
         iterate_kernel,
         in_specs=[VMEM] * 2,
@@ -403,39 +549,52 @@
     n, rows, lanes, xsize, ysize, zsize = n // 2, rows // 2, lanes // 2, xsize // 2, ysize // 2, lanes // 2
     h, over = 5, 1
     xlo, xhi = swap("gx", xdev, fc[:, :h], fc[:, n - h :])
-    first_rows, last_rows = [jnp.concatenate([a[:, :, s : s + 8] for a in (xlo, fc, xhi)], 1) for s in (0, rows - 8)]
+    first_rows, last_rows = pl.pallas_call(
+        rows_kernel,
+        in_specs=[VMEM] * 3,
+        out_specs=[VMEM] * 2,
+        out_shape=[S(2, n + 2 * h, 8, lanes)] * 2,
+        compiler_params=params(24),
+        name="second_rows",
+    )(xlo, fc, xhi)
     ylo, yhi = swap("gy", ydev, first_rows, last_rows)
-    w_full, w_mean = weights(zsize, lanes, lanes)
+    both = [jnp.stack([w, jnp.roll(w, lanes // 2, 1)]) for w in weights(zsize, lanes, lanes)]
     state = (n + 2 * h, 1, rows + 16, LANES)
-    scratch = lambda s, width: [V(3, *s), V(*s), V(*s), V(2, *s), V(2, *s), V(2, *s), V(2, 1, *s[2:]), V(2, width, 16, LANES), V(width, 16, LANES)]
+    work = lambda s: [V(*s), V(*s), V(2, *s), V(2, *s), V(2, *s), V(2, 1, *s[2:])]
     width = n // 2 + 2 * over
     second_u, fc = pl.pallas_call(
         functools.partial(middle_kernel, h, over, xsize, ysize),
         in_specs=[SMEM] + [VMEM] * 7,
         out_specs=[VMEM] * 2,
-        out_shape=[S(2, n, rows, lanes), S(3, width, width, lanes)],
-        scratch_shapes=scratch(state, width),
+        out_shape=[S(2, n, rows, lanes), S(width + width // 2, width, lanes)],
+        scratch_shapes=[V(3, *state)] + work(state) + [V(2, width, 16, LANES), V(2, width // 2, 16, LANES)],
         compiler_params=params(24),
         name="second_level",
-    )(place, fc, xlo, xhi, ylo, yhi, w_full, w_mean)
+    )(place, fc, xlo, xhi, ylo, yhi, *both)
 
     n, xsize, ysize, zsize = n // 2, xsize // 2, ysize // 2, zsize // 2
-    xlo, xhi = swap("gx", xdev, fc[:, 2:], fc[:, :n])
-    first_rows, last_rows = [jnp.concatenate([a[:, :, s : s + 8] for a in (xlo, fc, xhi)], 1) for s in (2, 0)]
-    ylo, yhi = swap("gy", ydev, first_rows, last_rows)
-    w_full, w_mean = weights(zsize, lanes, lanes)
+    m = n // 2
+
+    def joined(lo, own, hi, cells):
+        f = (lo[:n], own[: n + 2], hi[:n])
+        c = (lo[n:], own[n + 2 :], hi[n:])
+        return jnp.concatenate([a[:, cells] for a in f + c], 0)
+
+    pick = lambda i, j: jnp.concatenate([fc[i : i + n], fc[n + 2 + j : n + 2 + j + m]], 0)
+    xlo, xhi = swap("gx", xdev, pick(2, 1), pick(0, 0))
+    ylo, yhi = swap("gy", ydev, joined(xlo, fc, xhi, slice(2, n + 2)), joined(xlo, fc, xhi, slice(0, n)))
     state = (n + 18, 1, 40, LANES)
-    m = n // 2
     small = (m + 6, 1, 16, LANES)
     third, coarse = pl.pallas_call(
         functools.partial(coarse_kernel, n, 4, xsize, ysize, zsize),
         in_specs=[SMEM] + [VMEM] * 7,
         out_specs=[VMEM] * 2,
         out_shape=[S(2, n, n, zsize), S(2, m, m, zsize // 2)],
-        scratch_shapes=scratch(state, m + 6) + [V(*small), V(*small), V(2, *small), V(2, 2, *small)],
+        scratch_shapes=[V(n + 18 + m + 9, 1, 40, LANES)] + work(state) + [V(2, m + 6, 16, LANES), V(m + 6, 16, LANES)]
+        + [V(*small), V(*small), V(2, *small), V(2, 2, *small)],
         compiler_params=params(24),
         name="coarse_levels",
-    )(place, fc, xlo, xhi, ylo, yhi, w_full, w_mean)
+    )(place, fc, xlo, xhi, ylo, yhi, *weights(zsize, lanes, lanes))
     return fine, second_u, third, coarse
 
 

time: 77.8 us -> 72.5 us (0.932)
  the two profiles are of different devices: /device:TPU:31 before, /device:TPU:63 now
where the time goes in v3:
time: 72.5 us; the launch traced here: 72.3 us
  waiting for transfers between devices  29.7 us (41%)
  Pallas kernels  21.1 us (29%)
  starting transfers between devices  17 us (23%)
  local copies, waits for them, and re-layouts  3.57 us (5%)
  between operations  0.82 us (1%)
    ppermute x7, waiting for transfers between devices, swap(): lax.ppermute(first, axis, [((i + 1) % devices, i) for i in range(devices)])  17.9 us
    ppermute x7, starting transfers between devices, swap(): lax.ppermute(last, axis, [(i, (i + 1) % devices) for i in range(devices)])  16.3 us
    ppermute x7, waiting for transfers between devices, swap(): lax.ppermute(last, axis, [(i, (i + 1) % devices) for i in range(devices)])  11.8 us
    pallas_call x1, Pallas kernels, body(): pl.pallas_call(inner_kernel, in_specs=[VMEM] * 4, out_specs=[VMEM] * 6, o...  5.7 us
    pallas_call x1, Pallas kernels, body(): pl.pallas_call(functools.partial(faces_kernel, xsize, ysize), in_specs=[S...  4.21 us
    pallas_call x1, Pallas kernels, body(): pl.pallas_call(pack_kernel, in_specs=[pl.BlockSpec(memory_space=pl.ANY)]...  3.58 us
    unnamed x24, local copies, waits for them, and re-layouts  3.49 us
    pallas_call x1, Pallas kernels, body(): pl.pallas_call(functools.partial(coarse_kernel, n, 4, xsize, ysize, zsize...  2.64 us
  transfers between devices with their start and end apart: 14, of which 10 were waited for; matrix products, arithmetic and copies ran while one was open for 0% of the time, Pallas kernels for 16%

profile of v3, /device:TPU:63, one launch (start us, length us, event | category | flops | bytes accessed | tf_op | source)
XLA Modules:
  0.0 72.3 jit_solution(12378302108750038136)
XLA Ops:
  0.6 1.2 %copy-done = f32[32,32,256]{2,1,0:T(8,128)S(1)} copy-done((f32[32,32,256]{2,1,0:T(8,128)S(1)}, f32[32,32,256]{2,1,0:T(8,128)}, u32[]{:S(2)}) %copy-start) | copy-done | bytes 1048600
  1.9 3.6 %pack_faces.1 = (f32[2,32,32,256]{3,2,1,0:T(8,128)S(1)}, f32[32,32,256]{2,1,0:T(8,128)S(1)}, f32[8,32,256]{2,1,0:T(8,128)}, f32[8,32,256]{2,1,0:T(8,128)}, f32[3...) custom-call(f32[2,32,32,256]{3,2,1,0:T(8,128)} %f.1, f32[32,32,256]{2,1,0:T(8,128)S(1)} %copy-done), custom_call_target="tpu_custom_call" | custom-call | tf_op jit(solution)/shard_map/pack_faces/pallas_call | solution.py:488
  6.4 1.6 %collective-permute-start = (f32[8,32,256]{2,1,0:T(8,128)}, f32[8,32,256]{2,1,0:T(8,128)S(1)}, u32[]{:S(2)}, u32[]{:S(2)}) collective-permute-start(f32[8,32,256]{2,1,0:T(8,128)} %get-tuple-element.39), channel_id=1, source_target_pairs={{0,32},{32,64},{64,96},{96,128},{128,160},{160,192},{192,224},{224... | collective-permute-start | bytes 786440 | tf_op jit(solution)/shard_map/ppermute | solution.py:479
  9.1 4.7 %collective-permute-done.xlo = f32[8,32,256]{2,1,0:T(8,128)S(1)} collective-permute-done((f32[8,32,256]{2,1,0:T(8,128)}, f32[8,32,256]{2,1,0:T(8,128)S(1)}, u32[]{:S(2)}, u32[]{:S(2)}) %collective-permute-start) | collective-permute-done | bytes 262176 | tf_op jit(solution)/shard_map/ppermute | solution.py:479
  13.8 1.7 %collective-permute-done.1.xhi = f32[8,32,256]{2,1,0:T(8,128)S(1)} collective-permute-done((f32[8,32,256]{2,1,0:T(8,128)}, f32[8,32,256]{2,1,0:T(8,128)S(1)}, u32[]{:S(2)}, u32[]{:S(2)}) %collective-permute-start.1) | collective-permute-done | bytes 262176 | tf_op jit(solution)/shard_map/ppermute | solution.py:480
  15.5 1.5 %collective-permute-start.4 = (f32[16,4,256]{2,1,0:T(4,128)S(1)}, f32[16,4,256]{2,1,0:T(4,128)S(1)}, u32[]{:S(2)}, u32[]{:S(2)}) collective-permute-start(f32[16,4,256]{2,1,0:T(4,128)S(1)} %get-tuple-element.59), channel_id=1, source_target_pairs={{0,1},{1,2},{2,3},{3,4},{4,5},{5,6},{6,7},{7,8},{8,9},{9,10},{10,1... | collective-permute-start | bytes 196616 | tf_op jit(solution)/shard_map/ppermute | solution.py:479
  17.5 1.2 %copy-done.2 = f32[32,32,256]{2,1,0:T(8,128)S(1)} copy-done((f32[32,32,256]{2,1,0:T(8,128)S(1)}, f32[32,32,256]{2,1,0:T(8,128)}, u32[]{:S(2)}) %copy-start.2) | copy-done | bytes 1048600
  18.7 5.7 %inner_cells.1 = (f32[2,38,2,48,128]{4,3,2,1,0:T(8,128)S(1)}, f32[2,38,2,48,128]{4,3,2,1,0:T(8,128)S(1)}, f32[2,38,2,48,128]{4,3,2,1,0:T(8,128)S(1)}, f32[38,2,4...) custom-call(f32[2,32,32,256]{3,2,1,0:T(8,128)S(1)} %get-tuple-element.31.f, ...), custom_call_target="tpu_custom_call" | custom-call | flops 100000000 | bytes 16000000 | tf_op jit(solution)/shard_map/inner_cells/pallas_call | solution.py:507
  24.4 4.2 %face_cells.1 = (f32[2,38,2,48,128]{4,3,2,1,0:T(8,128)S(1)}, f32[2,38,2,48,128]{4,3,2,1,0:T(8,128)S(1)}, f32[2,38,2,48,128]{4,3,2,1,0:T(8,128)S(1)}, f32[38,2,48...) custom-call(s32[2]{0:T(128)S(1)} %pad_add_fusion.place, ...), custom_call_target="tpu_custom_call", output_to_operand_aliasing={{0}: (1, {}), {1}: (2, {}), {2}: (3, {}), {3}: (4, {}), {4}... | custom-call | flops 50000000 | bytes 8000000 | tf_op jit(solution)/shard_map/face_cells/pallas_call | solution.py:518
  28.7 1.1 %corner_cells.1 = (f32[2,38,2,48,128]{4,3,2,1,0:T(8,128)S(1)}, f32[2,38,2,48,128]{4,3,2,1,0:T(8,128)S(1)}, f32[2,38,2,48,128]{4,3,2,1,0:T(8,128)S(1)}, f32[38,2,...) custom-call(s32[2]{0:T(128)S(1)} %pad_add_fusion.place, ...), custom_call_target="tpu_custom_call", output_to_operand_aliasing={{0}: (1, {}), {1}: (2, {}), {2}: (3, {}), {3}: (4, {}), {4}... | custom-call | tf_op jit(solution)/shard_map/corner_cells/pallas_call | solution.py:529
  29.8 2.9 %collective-permute-start.6 = (f32[3,5,16,128]{3,2,1,0:T(8,128)S(1)}, f32[3,5,16,128]{3,2,1,0:T(8,128)S(1)}, u32[]{:S(2)}, u32[]{:S(2)}) collective-permute-start(f32[3,5,16,128]{3,2,1,0:T(8,128)S(1)} %get-tuple-element.61), channel_id=1, source_target_pairs={{0,32},{32,64},{64,96},{96,128},{128,160},{160,192},{192,224},{224... | collective-permute-start | bytes 368648 | tf_op jit(solution)/shard_map/ppermute | solution.py:479
  32.7 1.9 %collective-permute-done.6.xlo = f32[3,5,16,128]{3,2,1,0:T(8,128)S(1)} collective-permute-done((f32[3,5,16,128]{3,2,1,0:T(8,128)S(1)}, f32[3,5,16,128]{3,2,1,0:T(8,128)S(1)}, u32[]{:S(2)}, u32[]{:S(2)}) %collective-permute-start.6) | collective-permute-done | bytes 122912 | tf_op jit(solution)/shard_map/ppermute | solution.py:479
  34.6 3.1 %collective-permute-done.7.xhi = f32[3,5,16,128]{3,2,1,0:T(8,128)S(1)} collective-permute-done((f32[3,5,16,128]{3,2,1,0:T(8,128)S(1)}, f32[3,5,16,128]{3,2,1,0:T(8,128)S(1)}, u32[]{:S(2)}, u32[]{:S(2)}) %collective-permute-start.7) | collective-permute-done | bytes 122912 | tf_op jit(solution)/shard_map/ppermute | solution.py:480
  37.7 5.9 %collective-permute-start.8 = (f32[2,26,8,128]{3,2,1,0:T(8,128)S(1)}, f32[2,26,8,128]{3,2,1,0:T(8,128)S(1)}, u32[]{:S(2)}, u32[]{:S(2)}) collective-permute-start(f32[2,26,8,128]{3,2,1,0:T(8,128)S(1)} %get-tuple-element.52), channel_id=1, source_target_pairs={{0,1},{1,2},{2,3},{3,4},{4,5},{5,6},{6,7},{7,8},{8,9},{9,10},{10,1... | collective-permute-start | bytes 638984 | tf_op jit(solution)/shard_map/ppermute | solution.py:479
  43.6 2.8 %collective-permute-done.8.ylo = f32[2,26,8,128]{3,2,1,0:T(8,128)S(1)} collective-permute-done((f32[2,26,8,128]{3,2,1,0:T(8,128)S(1)}, f32[2,26,8,128]{3,2,1,0:T(8,128)S(1)}, u32[]{:S(2)}, u32[]{:S(2)}) %collective-permute-start.8) | collective-permute-done | bytes 213024 | tf_op jit(solution)/shard_map/ppermute | solution.py:479
  46.4 5.8 %collective-permute-done.9.yhi = f32[2,26,8,128]{3,2,1,0:T(8,128)S(1)} collective-permute-done((f32[2,26,8,128]{3,2,1,0:T(8,128)S(1)}, f32[2,26,8,128]{3,2,1,0:T(8,128)S(1)}, u32[]{:S(2)}, u32[]{:S(2)}) %collective-permute-start.9) | collective-permute-done | bytes 213024 | tf_op jit(solution)/shard_map/ppermute | solution.py:480
  52.2 2.2 %second_level.1 = (f32[2,16,16,128]{3,2,1,0:T(8,128)}, f32[15,10,128]{2,1,0:T(8,128)S(1)}) custom-call(s32[2]{0:T(128)S(1)} %pad_add_fusion.place, f32[3,16,16,128]{3,2,1,0:T(8,128)S(1)} %get-tuple-element.51.fc.fc_own, f32[3,5,16,128]{3,2,1,0:T(8,128)S(1)} %collective-permute-done.6.xlo, f32[3,5,16,128]{3,2,1,0:T(8,128)S(1)} %collective-permute-done.7.xhi, ...), custom_call_target="tpu_custom_call" | custom-call | tf_op jit(solution)/shard_map/second_level/pallas_call | solution.py:565
  54.5 2.0 %collective-permute-start.10 = (f32[12,10,128]{2,1,0:T(8,128)S(1)}, f32[12,10,128]{2,1,0:T(8,128)S(1)}, u32[]{:S(2)}, u32[]{:S(2)}) collective-permute-start(f32[12,10,128]{2,1,0:T(8,128)S(1)} %pad_maximum_fusion), channel_id=1, source_target_pairs={{0,32},{32,64},{64,96},{96,128},{128,160},{160,192},{192,224},{224... | collective-permute-start | bytes 184328 | tf_op jit(solution)/shard_map/ppermute | solution.py:479
  56.6 1.9 %collective-permute-done.10.xlo = f32[12,10,128]{2,1,0:T(8,128)S(1)} collective-permute-done((f32[12,10,128]{2,1,0:T(8,128)S(1)}, f32[12,10,128]{2,1,0:T(8,128)S(1)}, u32[]{:S(2)}, u32[]{:S(2)}) %collective-permute-start.10) | collective-permute-done | bytes 61472 | tf_op jit(solution)/shard_map/ppermute | solution.py:479
  58.6 1.5 %collective-permute-done.11.xhi = f32[12,10,128]{2,1,0:T(8,128)S(1)} collective-permute-done((f32[12,10,128]{2,1,0:T(8,128)S(1)}, f32[12,10,128]{2,1,0:T(8,128)S(1)}, u32[]{:S(2)}, u32[]{:S(2)}) %collective-permute-start.11) | collective-permute-done | bytes 61472 | tf_op jit(solution)/shard_map/ppermute | solution.py:480
  60.1 1.5 %collective-permute-start.12 = (f32[39,8,128]{2,1,0:T(8,128)S(1)}, f32[39,8,128]{2,1,0:T(8,128)S(1)}, u32[]{:S(2)}, u32[]{:S(2)}) collective-permute-start(f32[39,8,128]{2,1,0:T(8,128)S(1)} %get-tuple-element.71), channel_id=1, source_target_pairs={{0,1},{1,2},{2,3},{3,4},{4,5},{5,6},{6,7},{7,8},{8,9},{9,10},{10,1... | collective-permute-start | bytes 479240 | tf_op jit(solution)/shard_map/ppermute | solution.py:479
  61.6 1.7 %fine_iterate.1 = f32[2,32,32,256]{3,2,1,0:T(8,128)} custom-call(f32[2,38,2,48,128]{4,3,2,1,0:T(8,128)S(1)} %get-tuple-element.49.u, f32[2,38,2,48,128]{4,3,2,1,0:T(8,128)S(1)} %get-tuple-element.50.e), custom_call_target="tpu_custom_call" | custom-call | flops 1000000 | bytes 8000000 | tf_op jit(solution)/shard_map/fine_iterate/pallas_call | solution.py:539
  63.9 5.8 %collective-permute-done.13.yhi = f32[39,8,128]{2,1,0:T(8,128)S(1)} collective-permute-done((f32[39,8,128]{2,1,0:T(8,128)S(1)}, f32[39,8,128]{2,1,0:T(8,128)S(1)}, u32[]{:S(2)}, u32[]{:S(2)}) %collective-permute-start.13) | collective-permute-done | bytes 159776 | tf_op jit(solution)/shard_map/ppermute | solution.py:480
  69.7 2.6 %coarse_levels.1 = (f32[2,8,8,64]{3,2,1,0:T(8,128)}, f32[2,4,4,32]{3,2,1,0:T(4,128)}) custom-call(s32[2]{0:T(128)S(1)} %pad_add_fusion.place, f32[15,10,128]{2,1,0:T(8,128)S(1)} %get-tuple-element.55.fc_own, f32[12,10,128]{2,1,0:T(8,128)S(1)} %collective-permute-done.10.xlo, f32[12,10,128]{2,1,0:T(8,128)S(1)} %collective-permute-done.11.xhi, ...), custom_call_target="tpu_custom_call" | custom-call | tf_op jit(solution)/shard_map/coarse_levels/pallas_call | solution.py:588
  (45 shorter events, 3.3 us)
Async XLA Ops:
  0.6 1.2 %copy-start = (f32[32,32,256]{2,1,0:T(8,128)S(1)}, f32[32,32,256]{2,1,0:T(8,128)}, u32[]{:S(2)}) copy-start(f32[32,32,256]{2,1,0:T(8,128)} %c.1) | copy-start | bytes 3145732
  1.9 15.6 %copy-start.3 = (bf16[256,128]{1,0:T(8,128)(2,1)S(1)}, bf16[256,128]{1,0:T(8,128)(2,1)}, u32[]{:S(2)}) copy-start(bf16[256,128]{1,0:T(8,128)(2,1)} %constant.21.clone.w_full) | copy-start | bytes 196612
  1.9 15.6 %copy-start.6 = (bf16[256,128]{1,0:T(8,128)(2,1)S(1)}, bf16[256,128]{1,0:T(8,128)(2,1)}, u32[]{:S(2)}) copy-start(bf16[256,128]{1,0:T(8,128)(2,1)} %constant.22.clone.w_mean) | copy-start | bytes 196612
  5.4 1.0 %copy-start.1 = (f32[32,32,256]{2,1,0:T(8,128)}, f32[32,32,256]{2,1,0:T(8,128)S(1)}, u32[]{:S(2)}) copy-start(f32[32,32,256]{2,1,0:T(8,128)S(1)} %get-tuple-element.32.c) | copy-start | bytes 3145732
  6.4 7.4 %collective-permute-start = (f32[8,32,256]{2,1,0:T(8,128)}, f32[8,32,256]{2,1,0:T(8,128)S(1)}, u32[]{:S(2)}, u32[]{:S(2)}) collective-permute-start(f32[8,32,256]{2,1,0:T(8,128)} %get-tuple-element.39), channel_id=1, source_target_pairs={{0,32},{32,64},{64,96},{96,128},{128,160},{160,192},{192,224},{224... | collective-permute-start | bytes 786440 | tf_op jit(solution)/shard_map/ppermute | solution.py:479
  8.1 7.4 %collective-permute-start.1 = (f32[8,32,256]{2,1,0:T(8,128)}, f32[8,32,256]{2,1,0:T(8,128)S(1)}, u32[]{:S(2)}, u32[]{:S(2)}) collective-permute-start(f32[8,32,256]{2,1,0:T(8,128)} %get-tuple-element.40), channel_id=1, source_target_pairs={{32,0},{64,32},{96,64},{128,96},{160,128},{192,160},{224,192},{0,2... | collective-permute-start | bytes 786440 | tf_op jit(solution)/shard_map/ppermute | solution.py:480
  8.1 16.3 %collective-permute-start.2 = (f32[32,8,256]{2,1,0:T(8,128)}, f32[32,8,256]{2,1,0:T(8,128)S(1)}, u32[]{:S(2)}, u32[]{:S(2)}) collective-permute-start(f32[32,8,256]{2,1,0:T(8,128)} %get-tuple-element.41), channel_id=1, source_target_pairs={{0,1},{1,2},{2,3},{3,4},{4,5},{5,6},{6,7},{7,8},{8,9},{9,10},{10,1... | collective-permute-start | bytes 786440 | tf_op jit(solution)/shard_map/ppermute | solution.py:479
  8.9 15.6 %collective-permute-start.3 = (f32[32,8,256]{2,1,0:T(8,128)S(1)}, f32[32,8,256]{2,1,0:T(8,128)S(1)}, u32[]{:S(2)}, u32[]{:S(2)}) collective-permute-start(f32[32,8,256]{2,1,0:T(8,128)S(1)} %get-tuple-element.42), channel_id=1, source_target_pairs={{1,0},{2,1},{3,2},{4,3},{5,4},{6,5},{7,6},{8,7},{9,8},{10,9},{11,1... | collective-permute-start | bytes 786440 | tf_op jit(solution)/shard_map/ppermute | solution.py:480
  15.5 13.1 %collective-permute-start.4 = (f32[16,4,256]{2,1,0:T(4,128)S(1)}, f32[16,4,256]{2,1,0:T(4,128)S(1)}, u32[]{:S(2)}, u32[]{:S(2)}) collective-permute-start(f32[16,4,256]{2,1,0:T(4,128)S(1)} %get-tuple-element.59), channel_id=1, source_target_pairs={{0,1},{1,2},{2,3},{3,4},{4,5},{5,6},{6,7},{7,8},{8,9},{9,10},{10,1... | collective-permute-start | bytes 196616 | tf_op jit(solution)/shard_map/ppermute | solution.py:479
  17.0 11.6 %collective-permute-start.5 = (f32[16,4,256]{2,1,0:T(4,128)S(1)}, f32[16,4,256]{2,1,0:T(4,128)S(1)}, u32[]{:S(2)}, u32[]{:S(2)}) collective-permute-start(f32[16,4,256]{2,1,0:T(4,128)S(1)} %get-tuple-element.58), channel_id=1, source_target_pairs={{1,0},{2,1},{3,2},{4,3},{5,4},{6,5},{7,6},{8,7},{9,8},{10,9},{11,1... | collective-permute-start | bytes 196616 | tf_op jit(solution)/shard_map/ppermute | solution.py:480
  17.5 1.2 %copy-start.2 = (f32[32,32,256]{2,1,0:T(8,128)S(1)}, f32[32,32,256]{2,1,0:T(8,128)}, u32[]{:S(2)}) copy-start(f32[32,32,256]{2,1,0:T(8,128)} %copy-done.1) | copy-start | bytes 3145732
  28.7 23.6 %copy-start.4 = (bf16[2,128,128]{2,1,0:T(8,128)(2,1)S(1)}, bf16[2,128,128]{2,1,0:T(8,128)(2,1)}, u32[]{:S(2)}) copy-start(bf16[2,128,128]{2,1,0:T(8,128)(2,1)} %constant.32.w_full) | copy-start | bytes 196612
  28.7 23.6 %copy-start.5 = (bf16[2,128,128]{2,1,0:T(8,128)(2,1)S(1)}, bf16[2,128,128]{2,1,0:T(8,128)(2,1)}, u32[]{:S(2)}) copy-start(bf16[2,128,128]{2,1,0:T(8,128)(2,1)} %constant.38.w_mean) | copy-start | bytes 196612
  29.8 4.8 %collective-permute-start.6 = (f32[3,5,16,128]{3,2,1,0:T(8,128)S(1)}, f32[3,5,16,128]{3,2,1,0:T(8,128)S(1)}, u32[]{:S(2)}, u32[]{:S(2)}) collective-permute-start(f32[3,5,16,128]{3,2,1,0:T(8,128)S(1)} %get-tuple-element.61), channel_id=1, source_target_pairs={{0,32},{32,64},{64,96},{96,128},{128,160},{160,192},{192,224},{224... | collective-permute-start | bytes 368648 | tf_op jit(solution)/shard_map/ppermute | solution.py:479
  32.7 4.9 %collective-permute-start.7 = (f32[3,5,16,128]{3,2,1,0:T(8,128)S(1)}, f32[3,5,16,128]{3,2,1,0:T(8,128)S(1)}, u32[]{:S(2)}, u32[]{:S(2)}) collective-permute-start(f32[3,5,16,128]{3,2,1,0:T(8,128)S(1)} %get-tuple-element.60), channel_id=1, source_target_pairs={{32,0},{64,32},{96,64},{128,96},{160,128},{192,160},{224,192},{0,2... | collective-permute-start | bytes 368648 | tf_op jit(solution)/shard_map/ppermute | solution.py:480
  37.7 8.7 %collective-permute-start.8 = (f32[2,26,8,128]{3,2,1,0:T(8,128)S(1)}, f32[2,26,8,128]{3,2,1,0:T(8,128)S(1)}, u32[]{:S(2)}, u32[]{:S(2)}) collective-permute-start(f32[2,26,8,128]{3,2,1,0:T(8,128)S(1)} %get-tuple-element.52), channel_id=1, source_target_pairs={{0,1},{1,2},{2,3},{3,4},{4,5},{5,6},{6,7},{7,8},{8,9},{9,10},{10,1... | collective-permute-start | bytes 638984 | tf_op jit(solution)/shard_map/ppermute | solution.py:479
  43.6 8.6 %collective-permute-start.9 = (f32[2,26,8,128]{3,2,1,0:T(8,128)S(1)}, f32[2,26,8,128]{3,2,1,0:T(8,128)S(1)}, u32[]{:S(2)}, u32[]{:S(2)}) collective-permute-start(f32[2,26,8,128]{3,2,1,0:T(8,128)S(1)} %get-tuple-element.53), channel_id=1, source_target_pairs={{1,0},{2,1},{3,2},{4,3},{5,4},{6,5},{7,6},{8,7},{9,8},{10,9},{11,1... | collective-permute-start | bytes 638984 | tf_op jit(solution)/shard_map/ppermute | solution.py:480
  54.5 4.0 %collective-permute-start.10 = (f32[12,10,128]{2,1,0:T(8,128)S(1)}, f32[12,10,128]{2,1,0:T(8,128)S(1)}, u32[]{:S(2)}, u32[]{:S(2)}) collective-permute-start(f32[12,10,128]{2,1,0:T(8,128)S(1)} %pad_maximum_fusion), channel_id=1, source_target_pairs={{0,32},{32,64},{64,96},{96,128},{128,160},{160,192},{192,224},{224... | collective-permute-start | bytes 184328 | tf_op jit(solution)/shard_map/ppermute | solution.py:479
  56.5 3.5 %collective-permute-start.11 = (f32[12,10,128]{2,1,0:T(8,128)S(1)}, f32[12,10,128]{2,1,0:T(8,128)S(1)}, u32[]{:S(2)}, u32[]{:S(2)}) collective-permute-start(f32[12,10,128]{2,1,0:T(8,128)S(1)} %pad_maximum_fusion.1), channel_id=1, source_target_pairs={{32,0},{64,32},{96,64},{128,96},{160,128},{192,160},{224,192},{0,2... | collective-permute-start | bytes 184328 | tf_op jit(solution)/shard_map/ppermute | solution.py:480
  60.1 3.7 %collective-permute-start.12 = (f32[39,8,128]{2,1,0:T(8,128)S(1)}, f32[39,8,128]{2,1,0:T(8,128)S(1)}, u32[]{:S(2)}, u32[]{:S(2)}) collective-permute-start(f32[39,8,128]{2,1,0:T(8,128)S(1)} %get-tuple-element.71), channel_id=1, source_target_pairs={{0,1},{1,2},{2,3},{3,4},{4,5},{5,6},{6,7},{7,8},{8,9},{9,10},{10,1... | collective-permute-start | bytes 479240 | tf_op jit(solution)/shard_map/ppermute | solution.py:479
  61.6 8.0 %collective-permute-start.13 = (f32[39,8,128]{2,1,0:T(8,128)S(1)}, f32[39,8,128]{2,1,0:T(8,128)S(1)}, u32[]{:S(2)}, u32[]{:S(2)}) collective-permute-start(f32[39,8,128]{2,1,0:T(8,128)S(1)} %get-tuple-element.70), channel_id=1, source_target_pairs={{1,0},{2,1},{3,2},{4,3},{5,4},{6,5},{7,6},{8,7},{9,8},{10,9},{11,1... | collective-permute-start | bytes 479240 | tf_op jit(solution)/shard_map/ppermute | solution.py:480
  61.6 8.0 %copy-start.7 = (bf16[128,128]{1,0:T(8,128)(2,1)S(1)}, bf16[128,128]{1,0:T(8,128)(2,1)}, u32[]{:S(2)}) copy-start(bf16[128,128]{1,0:T(8,128)(2,1)} %constant.25.clone.w_full) | copy-start | bytes 98308
  61.6 8.0 %copy-start.8 = (bf16[128,128]{1,0:T(8,128)(2,1)S(1)}, bf16[128,128]{1,0:T(8,128)(2,1)}, u32[]{:S(2)}) copy-start(bf16[128,128]{1,0:T(8,128)(2,1)} %constant.26.clone.w_mean) | copy-start | bytes 98308

commit v4 on v3

--- a/solution.py
+++ b/solution.py
@@ -1,7 +1,6 @@
 import functools
 import jax
 import jax.numpy as jnp
-import numpy as np
 from jax import lax
 from jax.experimental import pallas as pl
 from jax.experimental.pallas import tpu as pltpu
@@ -88,16 +87,16 @@
     out[i, pl.ds(0, rows), pl.ds(LANES * h, LANES)] = val
 
 
-def weights(zsize, lanes_in, lanes_out):
-    full = np.zeros((lanes_in, lanes_out), np.float32)
-    mean = np.zeros((lanes_in, lanes_out), np.float32)
-    for i in range(zsize // 2):
-        for j, w in enumerate((1.0, 3.0, 3.0, 1.0)):
-            z = 2 * i - 1 + j
-            if 0 <= z < zsize:
-                full[z, i] = w / 512.0
-        mean[2 * i, i] = mean[2 * i + 1, i] = 0.125
-    return jnp.asarray(full, jnp.bfloat16), jnp.asarray(mean, jnp.bfloat16)
+def weights(lanes, zsize, mean=False, shift=0):
+    z = lax.broadcasted_iota(jnp.int32, (lanes, LANES), 0)
+    i = lax.broadcasted_iota(jnp.int32, (lanes, LANES), 1) - shift
+    d = z - 2 * i
+    inner = (d == 0) | (d == 1)
+    if mean:
+        w = jnp.where(inner, 0.125, 0.0)
+    else:
+        w = jnp.where(inner, 3.0 / 512.0, jnp.where((d == -1) | (d == 2), 1.0 / 512.0, 0.0))
+    return jnp.where((z < zsize) & (i >= 0) & (i < zsize // 2), w, 0.0).astype(jnp.bfloat16)
 
 
 def exact_dot(part, w):
@@ -114,37 +113,41 @@
 PX, PY = 3, 8
 
 
-def pack_kernel(f, c, f_out, c_out, x_first, x_last, y_first, y_last, sems):
-    n, rows, lanes = c_out.shape
-    cuts = [(0, PX), (n - PX, PX)]
-    step = (n - 2 * PX + 3) // 4
-    inner = [(x, min(step, n - PX - x)) for x in range(PX, n - PX, step)]
+def pack_kernel(f, c, x_first, x_last, y_first, y_last, planes, strips, sems):
+    n, rows = c.shape[:2]
+    edges = (0, n - PX)
+    tiles = (0, rows - 8)
+    middle = pl.ds(PX, n - 2 * PX)
     copies = []
-    for x, count in cuts + inner:
-        at = pl.ds(x, count)
-        copies += [(f.at[0, at], f_out.at[0, at]), (f.at[1, at], f_out.at[1, at]), (c.at[at], c_out.at[at])]
+    for side, x in enumerate(edges):
+        at = pl.ds(x, PX)
+        copies += [(f.at[0, at], planes.at[side, 0]), (f.at[1, at], planes.at[side, 1]), (c.at[at], planes.at[side, 2])]
+    for side, row in enumerate(tiles):
+        at = pl.ds(row, 8)
+        into = [strips.at[side, k, middle] for k in range(3)]
+        copies += [(f.at[0, middle, at], into[0]), (f.at[1, middle, at], into[1]), (c.at[middle, at], into[2])]
     copies = [pltpu.make_async_copy(src, dst, sems.at[i]) for i, (src, dst) in enumerate(copies)]
     for copy in copies:
         copy.start()
     for copy in copies[:6]:
         copy.wait()
-    for out, first, c_first in ((x_first, 0, 0), (x_last, n - PX, n - 2)):
+    for side, out in enumerate((x_first, x_last)):
         for j in range(PX):
-            x = first + j
-            a, b = inverse(c_out[x], 1.0, None)
-            out[j], out[PX + j] = divided(f_out[0, x], f_out[1, x], a, b)
+            a, b = inverse(planes[side, 2, j], 1.0, None)
+            out[j], out[PX + j] = divided(planes[side, 0, j], planes[side, 1, j], a, b)
         for j in range(2):
-            out[2 * PX + j] = c_out[c_first + j]
+            out[2 * PX + j] = planes[side, 2, j + side]
+        for end, row in enumerate(tiles):
+            strips[end, :, pl.ds(edges[side], PX)] = planes[side, :, :, pl.ds(row, 8), :]
     for copy in copies[6:]:
         copy.wait()
-    row = lax.broadcasted_iota(jnp.int32, (8, lanes), 0)
+    row = lax.broadcasted_iota(jnp.int32, (8, c.shape[2]), 0)
 
     def strip(x, carry):
-        for out, start, shifts in ((y_first, 0, (0, 3, 6)), (y_last, rows - 8, (3, 6, 0))):
-            at = pl.ds(start, 8)
-            cc = c_out[x, at, :]
+        for side, out, shifts in ((0, y_first, (0, 3, 6)), (1, y_last, (3, 6, 0))):
+            cc = strips[side, 2, x]
             a, b = inverse(cc, 1.0, None)
-            re, im = divided(f_out[0, x, at, :], f_out[1, x, at, :], a, b)
+            re, im = divided(strips[side, 0, x], strips[side, 1, x], a, b)
             re, im, cc = [pltpu.roll(v, shift, 0) if shift else v for v, shift in zip((re, im, cc), shifts)]
             out[x] = jnp.where(row < 3, re, jnp.where(row < 6, im, cc))
         return carry
@@ -152,7 +155,7 @@
     lax.fori_loop(0, n, strip, 0, unroll=4)
 
 
-def inner_kernel(f, c, w_full, w_mean, u, e, r, ga, gb, fc_out, t, part):
+def inner_kernel(f, c, u, e, r, ga, gb, fc_out, t, part):
     n, rows, lanes = c.shape
     halves = lanes // LANES
     at = pl.ds(PY, rows)
@@ -199,9 +202,10 @@
         return carry
 
     lax.fori_loop(2, n // 2 - 2, coarse, 0, unroll=2)
+    w = weights(lanes, lanes)
     for k in (0, 1):
-        fc_out[k, 2 : n // 2 - 2] = exact_dot(part[k, 2 : n // 2 - 2], w_full[...])
-    fc_out[2] = exact_dot(part[2], w_mean[...])
+        fc_out[k, 2 : n // 2 - 2] = exact_dot(part[k, 2 : n // 2 - 2], w)
+    fc_out[2] = exact_dot(part[2], weights(lanes, lanes, mean=True))
 
 
 def inside(place, n, rows, xsize, ysize):
@@ -242,7 +246,7 @@
     return side[i, :, cut], side[PX + i, :, cut], cc, c_here, i == (PX - 1 if low else 0)
 
 
-def faces_kernel(xsize, ysize, place, u_in, e_in, r_in, ga_in, gb_in, fc_in, xlo, xhi, ylo, yhi, w_full, u, e, r, ga, gb, fc_out, part, q):
+def faces_kernel(xsize, ysize, place, u_in, e_in, r_in, ga_in, gb_in, fc_in, xlo, xhi, ylo, yhi, u, e, r, ga, gb, fc_out, part, q):
     n, (rows, lanes) = ylo.shape[0], xlo.shape[1:]
     halves = lanes // LANES
     cut = [pl.ds(LANES * h, LANES) for h in range(halves)]
@@ -300,14 +304,15 @@
         return carry
 
     lax.fori_loop(0, m, coarse, 0, unroll=4)
+    w = weights(lanes, lanes)
     for k in (0, 1):
-        q[k] = exact_dot(part[k], w_full[...])
+        q[k] = exact_dot(part[k], w)
         for row, start in ((0, 0), (rows // 2 - 2, 10)):
             four = [q[k, :, pl.ds(start + j, 2, 2), :] for j in range(4)]
             fc_out[k, pl.ds(2, m), pl.ds(row, 2), :] = (four[0] + four[3]) + 3.0 * (four[1] + four[2])
 
 
-def corners_kernel(xsize, ysize, n, rows, place, u_in, e_in, r_in, ga_in, gb_in, fc_in, clo, chi, w_full, u, e, r, ga, gb, fc_out, t, part):
+def corners_kernel(xsize, ysize, n, rows, place, u_in, e_in, r_in, ga_in, gb_in, fc_in, clo, chi, u, e, r, ga, gb, fc_out, t, part):
     halves = clo.shape[2] // LANES
     ok = inside(place, n, rows, xsize, ysize)
     del u_in, e_in, r_in, ga_in, gb_in, fc_in
@@ -326,10 +331,11 @@
         for row in (low, high):
             finish(e, r, x, row, 8, ok(x, row, 8))
     planes = (0, 1, n // 2 - 2, n // 2 - 1)
+    w = weights(part.shape[3], part.shape[3])
     for k in (0, 1):
         for j, i in enumerate(planes):
             restrict_xy(r, t, part, j, 2 * i + PX - 1, PY - 1, rows // 2, k, (low, rows + 8))
-        val = exact_dot(part[k], w_full[...])
+        val = exact_dot(part[k], w)
         for j, i in enumerate(planes):
             fc_out[k, i] = val[j]
 
@@ -374,7 +380,7 @@
                 out[1, base + i] = jnp.where(own, im, pltpu.roll(cc, 2, 0))
 
 
-def middle_kernel(halo, over, xsize, ysize, place, fc_own, xlo, xhi, ylo, yhi, w_full, w_mean, u_out, fc_out, fc, ga, gb, u, e, r, t, part, part_c):
+def middle_kernel(halo, over, xsize, ysize, place, fc_own, xlo, xhi, ylo, yhi, u_out, fc_out, fc, ga, gb, u, e, r, t, part, part_c):
     n, rows = fc_own.shape[1:3]
     planes = n + 2 * halo
     for k in range(3):
@@ -410,11 +416,12 @@
         for k in (0, 1):
             restrict_xy(r, t, part, i, x, row, width, k, (4, rows + 8))
         add_pairs(fc[2, x + 1, 0], fc[2, x + 2, 0], t, 0, part_c.at[i % 2], i // 2, row + 1, width)
-    fc_out[pl.ds(0, width)] = (exact_dot(part[0], w_full[0]) + exact_dot(part[1], w_full[1]))[:, :width]
-    fc_out[pl.ds(width, pairs)] = (exact_dot(part_c[0], w_mean[0]) + exact_dot(part_c[1], w_mean[1]))[:, :width]
-
-
-def coarse_kernel(n, sweeps, xsize, ysize, zsize, place, fc_own, xlo, xhi, ylo, yhi, w_full, w_mean, u_out, v_out, fc, ga, gb, u, e, r, t, part, part_c, gc, gd, v, w):
+    two = [(part.at[k], part_c.at[k], LANES // 2 * k) for k in (0, 1)]
+    fc_out[pl.ds(0, width)] = sum(exact_dot(p[...], weights(LANES, LANES, shift=s)) for p, _, s in two)[:, :width]
+    fc_out[pl.ds(width, pairs)] = sum(exact_dot(p[...], weights(LANES, LANES, True, s)) for _, p, s in two)[:, :width]
+
+
+def coarse_kernel(n, sweeps, xsize, ysize, zsize, place, fc_own, xlo, xhi, ylo, yhi, u_out, v_out, fc, ga, gb, u, e, r, t, part, part_c, gc, gd, v, w):
     m = n // 2
     planes = n + 18
     for src, x, first, count in ((xlo, 0, 0, 8), (fc_own, 8, 0, n + 2), (xhi, n + 10, 0, 8), (xlo, planes, 8, 4), (fc_own, planes + 4, n + 2, m + 1), (xhi, planes + m + 5, 8, 4)):
@@ -450,7 +457,8 @@
             restrict_xy(r, t, part, i, 2 * i + 2, 9, width, k, (8, n + 16))
         t[0, 0, every, :] = cells(2, 2 * i + 3, every) + cells(2, 2 * i + 4, every)
         part_c[i, pl.ds(0, width), :] = t[0, 0, pl.ds(10, width, 2), :] + t[0, 0, pl.ds(11, width, 2), :]
-    f = [exact_dot(part[k], w_full[...]) for k in (0, 1)] + [exact_dot(part_c[...], w_mean[...])]
+    w_full = weights(LANES, zsize)
+    f = [exact_dot(part[k], w_full) for k in (0, 1)] + [exact_dot(part_c[...], weights(LANES, zsize, True))]
     ok = inside(place[0] * m - 3, place[1] * m - 3, xsize // 2, ysize // 2, zsize // 2)
     for x in range(width):
         point(f[0][x], f[1][x], f[2][x], 64.0, ok(x, 0, 16), v, gc, gd, x, 0, 0)
@@ -485,39 +493,39 @@
     S = lambda *shape: jax.ShapeDtypeStruct(shape, f32)
     V = lambda *shape: pltpu.VMEM(shape, f32)
 
-    f, c, x_first, x_last, y_first, y_last = pl.pallas_call(
+    x_first, x_last, y_first, y_last = pl.pallas_call(
         pack_kernel,
-        in_specs=[pl.BlockSpec(memory_space=pl.ANY)] * 2,
-        out_specs=[VMEM] * 6,
-        out_shape=[S(2, n, rows, lanes), S(n, rows, lanes)] + [S(8, rows, lanes)] * 2 + [S(n, 8, lanes)] * 2,
-        scratch_shapes=[pltpu.SemaphoreType.DMA((18,))],
-        compiler_params=params(48),
+        in_specs=[pl.BlockSpec(memory_space=pltpu.HBM)] * 2,
+        out_specs=[VMEM] * 4,
+        out_shape=[S(8, rows, lanes)] * 2 + [S(n, 8, lanes)] * 2,
+        scratch_shapes=[V(2, 3, PX, rows, lanes), V(2, 3, n, 8, lanes), pltpu.SemaphoreType.DMA((12,))],
+        compiler_params=params(60),
         name="pack_faces",
     )(source, wavenumber_sq)
     xlo, xhi = swap("gx", xdev, x_first, x_last)
     ylo, yhi = swap("gy", ydev, y_first, y_last)
-    planes = jnp.concatenate([xlo, xhi], 0)
-    clo, chi = swap("gy", ydev, planes[:, :4], planes[:, rows - 4 :])
     halves = lanes // LANES
-    w_full, w_mean = weights(lanes, lanes, lanes // 2)
     state = (n + 2 * PX, halves, rows + 2 * PY, LANES)
     part = (n // 2, rows // 2, lanes)
     shapes = [S(2, *state)] * 3 + [S(*state)] * 2 + [S(3, n // 2, rows // 2, lanes // 2)]
     column = V(2, halves, rows + 2 * PY, LANES)
     held = pl.pallas_call(
         inner_kernel,
-        in_specs=[VMEM] * 4,
+        in_specs=[VMEM] * 2,
         out_specs=[VMEM] * 6,
         out_shape=shapes,
         scratch_shapes=[column, V(3, *part)],
         compiler_params=params(24),
         cost_estimate=pl.CostEstimate(flops=100_000_000, bytes_accessed=16_000_000, transcendentals=0),
         name="inner_cells",
-    )(f, c, w_full, w_mean)
+    )(source, wavenumber_sq)
+    xlo, xhi, held = lax.optimization_barrier((xlo, xhi, held))
+    planes = jnp.concatenate([xlo, xhi], 0)
+    clo, chi = swap("gy", ydev, planes[:, :4], planes[:, rows - 4 :])
     in_place = {i + 1: i for i in range(6)}
     held = pl.pallas_call(
         functools.partial(faces_kernel, xsize, ysize),
-        in_specs=[SMEM] + [VMEM] * 11,
+        in_specs=[SMEM] + [VMEM] * 10,
         out_specs=[VMEM] * 6,
         out_shape=shapes,
         input_output_aliases=in_place,
@@ -525,17 +533,17 @@
         compiler_params=params(24),
         cost_estimate=pl.CostEstimate(flops=50_000_000, bytes_accessed=8_000_000, transcendentals=0),
         name="face_cells",
-    )(place, *held, xlo, xhi, ylo, yhi, w_full)
+    )(place, *held, xlo, xhi, ylo, yhi)
     u, e, _, _, _, fc = pl.pallas_call(
         functools.partial(corners_kernel, xsize, ysize, n, rows),
-        in_specs=[SMEM] + [VMEM] * 9,
+        in_specs=[SMEM] + [VMEM] * 8,
         out_specs=[VMEM] * 6,
         out_shape=shapes,
         input_output_aliases=in_place,
         scratch_shapes=[column, V(2, 4, rows // 2, lanes)],
         compiler_params=params(24),
         name="corner_cells",
-    )(place, *held, clo, chi, w_full)
+    )(place, *held, clo, chi)
     fine = pl.pallas_call(
         iterate_kernel,
         in_specs=[VMEM] * 2,
@@ -558,19 +566,18 @@
         name="second_rows",
     )(xlo, fc, xhi)
     ylo, yhi = swap("gy", ydev, first_rows, last_rows)
-    both = [jnp.stack([w, jnp.roll(w, lanes // 2, 1)]) for w in weights(zsize, lanes, lanes)]
     state = (n + 2 * h, 1, rows + 16, LANES)
     work = lambda s: [V(*s), V(*s), V(2, *s), V(2, *s), V(2, *s), V(2, 1, *s[2:])]
     width = n // 2 + 2 * over
     second_u, fc = pl.pallas_call(
         functools.partial(middle_kernel, h, over, xsize, ysize),
-        in_specs=[SMEM] + [VMEM] * 7,
+        in_specs=[SMEM] + [VMEM] * 5,
         out_specs=[VMEM] * 2,
         out_shape=[S(2, n, rows, lanes), S(width + width // 2, width, lanes)],
         scratch_shapes=[V(3, *state)] + work(state) + [V(2, width, 16, LANES), V(2, width // 2, 16, LANES)],
         compiler_params=params(24),
         name="second_level",
-    )(place, fc, xlo, xhi, ylo, yhi, *both)
+    )(place, fc, xlo, xhi, ylo, yhi)
 
     n, xsize, ysize, zsize = n // 2, xsize // 2, ysize // 2, zsize // 2
     m = n // 2
@@ -587,14 +594,14 @@
     small = (m + 6, 1, 16, LANES)
     third, coarse = pl.pallas_call(
         functools.partial(coarse_kernel, n, 4, xsize, ysize, zsize),
-        in_specs=[SMEM] + [VMEM] * 7,
+        in_specs=[SMEM] + [VMEM] * 5,
         out_specs=[VMEM] * 2,
         out_shape=[S(2, n, n, zsize), S(2, m, m, zsize // 2)],
         scratch_shapes=[V(n + 18 + m + 9, 1, 40, LANES)] + work(state) + [V(2, m + 6, 16, LANES), V(m + 6, 16, LANES)]
         + [V(*small), V(*small), V(2, *small), V(2, 2, *small)],
         compiler_params=params(24),
         name="coarse_levels",
-    )(place, fc, xlo, xhi, ylo, yhi, *weights(zsize, lanes, lanes))
+    )(place, fc, xlo, xhi, ylo, yhi)
     return fine, second_u, third, coarse
 
 

time: 72.5 us -> 69.8 us (0.963)
  the two profiles are of different devices: /device:TPU:63 before, /device:TPU:96 now
where the time goes in v4:
time: 69.8 us; the launch traced here: 69.7 us
  starting transfers between devices  26 us (37%)
  Pallas kernels  21 us (30%)
  waiting for transfers between devices  20.7 us (30%)
  local copies, waits for them, and re-layouts  1.1 us (2%)
  between operations  0.81 us (1%)
    ppermute x7, starting transfers between devices, swap(): lax.ppermute(first, axis, [((i + 1) % devices, i) for i in range(devices)])  16 us
    ppermute x7, waiting for transfers between devices, swap(): lax.ppermute(last, axis, [(i, (i + 1) % devices) for i in range(devices)])  13 us
    ppermute x7, starting transfers between devices, swap(): lax.ppermute(last, axis, [(i, (i + 1) % devices) for i in range(devices)])  10 us
    ppermute x7, waiting for transfers between devices, swap(): lax.ppermute(first, axis, [((i + 1) % devices, i) for i in range(devices)])  7.69 us
    pallas_call x1, Pallas kernels, body(): pl.pallas_call(inner_kernel, in_specs=[VMEM] * 2, out_specs=[VMEM] * 6, o...  5.74 us
    pallas_call x1, Pallas kernels, body(): pl.pallas_call(functools.partial(faces_kernel, xsize, ysize), in_specs=[S...  4.8 us
    pallas_call x1, Pallas kernels, body(): pl.pallas_call(pack_kernel, in_specs=[pl.BlockSpec(memory_space=pltpu.HBM...  3.11 us
    pallas_call x1, Pallas kernels, body(): pl.pallas_call(functools.partial(coarse_kernel, n, 4, xsize, ysize, zsize...  2.62 us
  transfers between devices with their start and end apart: 14, of which 7 were waited for; matrix products, arithmetic and copies ran while one was open for 2% of the time, Pallas kernels for 17%

profile of v4, /device:TPU:96, one launch (start us, length us, event | category | flops | bytes accessed | tf_op | source)
XLA Modules:
  0.0 69.7 jit_solution(9525049907024567292)
XLA Ops:
  0.7 3.1 %pack_faces.1 = (f32[8,32,256]{2,1,0:T(8,128)}, f32[8,32,256]{2,1,0:T(8,128)}, f32[32,8,256]{2,1,0:T(8,128)}, f32[32,8,256]{2,1,0:T(8,128)}) custom-call(f32[2,32,32,256]{3,2,1,0:T(8,128)} %f.3, f32[32,32,256]{2,1,0:T(8,128)} %c.3), custom_call_target="tpu_custom_call" | custom-call | tf_op jit(solution)/shard_map/pack_faces/pallas_call | solution.py:496
  3.8 3.2 %collective-permute-start = (f32[8,32,256]{2,1,0:T(8,128)}, f32[8,32,256]{2,1,0:T(8,128)S(1)}, u32[]{:S(2)}, u32[]{:S(2)}) collective-permute-start(f32[8,32,256]{2,1,0:T(8,128)} %get-tuple-element.37), channel_id=1, source_target_pairs={{0,32},{32,64},{64,96},{96,128},{128,160},{160,192},{192,224},{224... | collective-permute-start | bytes 786440 | tf_op jit(solution)/shard_map/ppermute | solution.py:487
  7.0 5.1 %collective-permute-start.3 = (f32[32,8,256]{2,1,0:T(8,128)}, f32[32,8,256]{2,1,0:T(8,128)}, u32[]{:S(2)}, u32[]{:S(2)}) collective-permute-start(f32[32,8,256]{2,1,0:T(8,128)} %get-tuple-element.54), channel_id=1, source_target_pairs={{1,0},{2,1},{3,2},{4,3},{5,4},{6,5},{7,6},{8,7},{9,8},{10,9},{11,1... | collective-permute-start | bytes 786440 | tf_op jit(solution)/shard_map/ppermute | solution.py:488
  12.0 5.7 %inner_cells.1 = (f32[2,38,2,48,128]{4,3,2,1,0:T(8,128)S(1)}, f32[2,38,2,48,128]{4,3,2,1,0:T(8,128)S(1)}, f32[2,38,2,48,128]{4,3,2,1,0:T(8,128)S(1)}, f32[38,2,4...) custom-call(f32[2,32,32,256]{3,2,1,0:T(8,128)S(1)} %copy-done, ...), custom_call_target="tpu_custom_call" | custom-call | flops 100000000 | bytes 16000000 | tf_op jit(solution)/shard_map/inner_cells/pallas_call | solution.py:512
  17.8 1.0 %constant_dynamic-update-slice_fusion = f32[16,32,256]{2,1,0:T(8,128)S(1)} fusion(f32[16,32,256]{2,1,0:T(8,128)S(1)} %constant_dynamic-update-slice_fusion.1, f32[8,32,256]{2,1,0:T(8,128)} %collective-permute-done.1.xhi), kind=kLoop, calls=%fused_computation.8 | loop fusion | bytes 524288 | tf_op jit(solution)/shard_map/concatenate | solution.py:523
  18.8 2.0 %collective-permute-start.5 = (f32[16,4,256]{2,1,0:T(4,128)S(1)}, f32[16,4,256]{2,1,0:T(4,128)S(1)}, u32[]{:S(2)}, u32[]{:S(2)}) collective-permute-start(f32[16,4,256]{2,1,0:T(4,128)S(1)} %get-tuple-element.70), channel_id=1, source_target_pairs={{1,0},{2,1},{3,2},{4,3},{5,4},{6,5},{7,6},{8,7},{9,8},{10,9},{11,1... | collective-permute-start | bytes 196616 | tf_op jit(solution)/shard_map/ppermute | solution.py:488
  20.9 4.8 %face_cells.1 = (f32[2,38,2,48,128]{4,3,2,1,0:T(8,128)S(1)}, f32[2,38,2,48,128]{4,3,2,1,0:T(8,128)S(1)}, f32[2,38,2,48,128]{4,3,2,1,0:T(8,128)S(1)}, f32[38,2,48...) custom-call(s32[2]{0:T(128)S(1)} %pad_add_fusion.place, ...), custom_call_target="tpu_custom_call", output_to_operand_aliasing={{0}: (1, {}), {1}: (2, {}), {2}: (3, {}), {3}: (4, {}), {4}... | custom-call | flops 50000000 | bytes 8000000 | tf_op jit(solution)/shard_map/face_cells/pallas_call | solution.py:526
  25.7 2.1 %collective-permute-done.4.clo = f32[16,4,256]{2,1,0:T(4,128)S(1)} collective-permute-done((f32[16,4,256]{2,1,0:T(4,128)S(1)}, f32[16,4,256]{2,1,0:T(4,128)S(1)}, u32[]{:S(2)}, u32[]{:S(2)}) %collective-permute-start.4) | collective-permute-done | bytes 65568 | tf_op jit(solution)/shard_map/ppermute | solution.py:487
  27.8 1.1 %corner_cells.1 = (f32[2,38,2,48,128]{4,3,2,1,0:T(8,128)S(1)}, f32[2,38,2,48,128]{4,3,2,1,0:T(8,128)S(1)}, f32[2,38,2,48,128]{4,3,2,1,0:T(8,128)S(1)}, f32[38,2,...) custom-call(s32[2]{0:T(128)S(1)} %pad_add_fusion.place, ...), custom_call_target="tpu_custom_call", output_to_operand_aliasing={{0}: (1, {}), {1}: (2, {}), {2}: (3, {}), {3}: (4, {}), {4}... | custom-call | tf_op jit(solution)/shard_map/corner_cells/pallas_call | solution.py:537
  29.1 3.2 %collective-permute-start.6 = (f32[3,5,16,128]{3,2,1,0:T(8,128)S(1)}, f32[3,5,16,128]{3,2,1,0:T(8,128)S(1)}, u32[]{:S(2)}, u32[]{:S(2)}) collective-permute-start(f32[3,5,16,128]{3,2,1,0:T(8,128)S(1)} %get-tuple-element.73), channel_id=1, source_target_pairs={{0,32},{32,64},{64,96},{96,128},{128,160},{160,192},{192,224},{224... | collective-permute-start | bytes 368648 | tf_op jit(solution)/shard_map/ppermute | solution.py:487
  32.3 2.9 %collective-permute-done.7.xhi = f32[3,5,16,128]{3,2,1,0:T(8,128)S(1)} collective-permute-done((f32[3,5,16,128]{3,2,1,0:T(8,128)S(1)}, f32[3,5,16,128]{3,2,1,0:T(8,128)S(1)}, u32[]{:S(2)}, u32[]{:S(2)}) %collective-permute-start.7) | collective-permute-done | bytes 122912 | tf_op jit(solution)/shard_map/ppermute | solution.py:488
  35.2 0.1 collective-permute-start.8
  35.3 5.1 %collective-permute-start.9 = (f32[2,26,8,128]{3,2,1,0:T(8,128)S(1)}, f32[2,26,8,128]{3,2,1,0:T(8,128)S(1)}, u32[]{:S(2)}, u32[]{:S(2)}) collective-permute-start(f32[2,26,8,128]{3,2,1,0:T(8,128)S(1)} %get-tuple-element.65), channel_id=1, source_target_pairs={{1,0},{2,1},{3,2},{4,3},{5,4},{6,5},{7,6},{8,7},{9,8},{10,9},{11,1... | collective-permute-start | bytes 638984 | tf_op jit(solution)/shard_map/ppermute | solution.py:488
  40.3 3.5 %collective-permute-done.8.ylo = f32[2,26,8,128]{3,2,1,0:T(8,128)S(1)} collective-permute-done((f32[2,26,8,128]{3,2,1,0:T(8,128)S(1)}, f32[2,26,8,128]{3,2,1,0:T(8,128)S(1)}, u32[]{:S(2)}, u32[]{:S(2)}) %collective-permute-start.8) | collective-permute-done | bytes 213024 | tf_op jit(solution)/shard_map/ppermute | solution.py:487
  43.9 2.0 %second_level.1 = (f32[2,16,16,128]{3,2,1,0:T(8,128)}, f32[15,10,128]{2,1,0:T(8,128)S(1)}) custom-call(s32[2]{0:T(128)S(1)} %pad_add_fusion.place, f32[3,16,16,128]{3,2,1,0:T(8,128)S(1)} %get-tuple-element.63.fc.fc_own, f32[3,5,16,128]{3,2,1,0:T(8,128)S(1)} %collective-permute-done.6.xlo, f32[3,5,16,128]{3,2,1,0:T(8,128)S(1)} %collective-permute-done.7.xhi, ...), custom_call_target="tpu_custom_call" | custom-call | tf_op jit(solution)/shard_map/second_level/pallas_call | solution.py:572
  45.9 3.5 %collective-permute-start.10 = (f32[12,10,128]{2,1,0:T(8,128)S(1)}, f32[12,10,128]{2,1,0:T(8,128)S(1)}, u32[]{:S(2)}, u32[]{:S(2)}) collective-permute-start(f32[12,10,128]{2,1,0:T(8,128)S(1)} %pad_maximum_fusion), channel_id=1, source_target_pairs={{0,32},{32,64},{64,96},{96,128},{128,160},{160,192},{192,224},{224... | collective-permute-start | bytes 184328 | tf_op jit(solution)/shard_map/ppermute | solution.py:487
  49.4 0.1 collective-permute-start.11
  49.5 2.1 %collective-permute-done.10.xlo = f32[12,10,128]{2,1,0:T(8,128)S(1)} collective-permute-done((f32[12,10,128]{2,1,0:T(8,128)S(1)}, f32[12,10,128]{2,1,0:T(8,128)S(1)}, u32[]{:S(2)}, u32[]{:S(2)}) %collective-permute-start.10) | collective-permute-done | bytes 61472 | tf_op jit(solution)/shard_map/ppermute | solution.py:487
  51.6 3.7 %collective-permute-done.11.xhi = f32[12,10,128]{2,1,0:T(8,128)S(1)} collective-permute-done((f32[12,10,128]{2,1,0:T(8,128)S(1)}, f32[12,10,128]{2,1,0:T(8,128)S(1)}, u32[]{:S(2)}, u32[]{:S(2)}) %collective-permute-start.11) | collective-permute-done | bytes 61472 | tf_op jit(solution)/shard_map/ppermute | solution.py:488
  55.3 3.7 %collective-permute-start.13 = (f32[39,8,128]{2,1,0:T(8,128)S(1)}, f32[39,8,128]{2,1,0:T(8,128)S(1)}, u32[]{:S(2)}, u32[]{:S(2)}) collective-permute-start(f32[39,8,128]{2,1,0:T(8,128)S(1)} %get-tuple-element.82), channel_id=1, source_target_pairs={{1,0},{2,1},{3,2},{4,3},{5,4},{6,5},{7,6},{8,7},{9,8},{10,9},{11,1... | collective-permute-start | bytes 479240 | tf_op jit(solution)/shard_map/ppermute | solution.py:488
  59.0 1.6 %fine_iterate.1 = f32[2,32,32,256]{3,2,1,0:T(8,128)} custom-call(f32[2,38,2,48,128]{4,3,2,1,0:T(8,128)S(1)} %get-tuple-element.61.u, f32[2,38,2,48,128]{4,3,2,1,0:T(8,128)S(1)} %get-tuple-element.62.e), custom_call_target="tpu_custom_call" | custom-call | flops 1000000 | bytes 8000000 | tf_op jit(solution)/shard_map/fine_iterate/pallas_call | solution.py:547
  60.7 1.1 %collective-permute-done.13.yhi = f32[39,8,128]{2,1,0:T(8,128)S(1)} collective-permute-done((f32[39,8,128]{2,1,0:T(8,128)S(1)}, f32[39,8,128]{2,1,0:T(8,128)S(1)}, u32[]{:S(2)}, u32[]{:S(2)}) %collective-permute-start.13) | collective-permute-done | bytes 159776 | tf_op jit(solution)/shard_map/ppermute | solution.py:488
  61.8 5.2 %collective-permute-done.12.ylo = f32[39,8,128]{2,1,0:T(8,128)S(1)} collective-permute-done((f32[39,8,128]{2,1,0:T(8,128)S(1)}, f32[39,8,128]{2,1,0:T(8,128)S(1)}, u32[]{:S(2)}, u32[]{:S(2)}) %collective-permute-start.12) | collective-permute-done | bytes 159776 | tf_op jit(solution)/shard_map/ppermute | solution.py:487
  67.1 2.6 %coarse_levels.1 = (f32[2,8,8,64]{3,2,1,0:T(8,128)}, f32[2,4,4,32]{3,2,1,0:T(4,128)}) custom-call(s32[2]{0:T(128)S(1)} %pad_add_fusion.place, f32[15,10,128]{2,1,0:T(8,128)S(1)} %get-tuple-element.67.fc_own, f32[12,10,128]{2,1,0:T(8,128)S(1)} %collective-permute-done.10.xlo, f32[12,10,128]{2,1,0:T(8,128)S(1)} %collective-permute-done.11.xhi, ...), custom_call_target="tpu_custom_call" | custom-call | tf_op jit(solution)/shard_map/coarse_levels/pallas_call | solution.py:595
  (31 shorter events, 0.4 us)
Async XLA Ops:
  0.6 11.4 %copy-start.1 = (f32[32,32,256]{2,1,0:T(8,128)S(1)}, f32[32,32,256]{2,1,0:T(8,128)}, u32[]{:S(2)}) copy-start(f32[32,32,256]{2,1,0:T(8,128)} %c.3) | copy-start | bytes 3145732
  0.6 11.4 %copy-start = (f32[2,32,32,256]{3,2,1,0:T(8,128)S(1)}, f32[2,32,32,256]{3,2,1,0:T(8,128)}, u32[]{:S(2)}) copy-start(f32[2,32,32,256]{3,2,1,0:T(8,128)} %f.3) | copy-start | bytes 6291460
  3.8 14.0 %collective-permute-start = (f32[8,32,256]{2,1,0:T(8,128)}, f32[8,32,256]{2,1,0:T(8,128)S(1)}, u32[]{:S(2)}, u32[]{:S(2)}) collective-permute-start(f32[8,32,256]{2,1,0:T(8,128)} %get-tuple-element.37), channel_id=1, source_target_pairs={{0,32},{32,64},{64,96},{96,128},{128,160},{160,192},{192,224},{224... | collective-permute-start | bytes 786440 | tf_op jit(solution)/shard_map/ppermute | solution.py:487
  7.0 10.8 %collective-permute-start.1 = (f32[8,32,256]{2,1,0:T(8,128)}, f32[8,32,256]{2,1,0:T(8,128)}, u32[]{:S(2)}, u32[]{:S(2)}) collective-permute-start(f32[8,32,256]{2,1,0:T(8,128)} %get-tuple-element.38), channel_id=1, source_target_pairs={{32,0},{64,32},{96,64},{128,96},{160,128},{192,160},{224,192},{0,2... | collective-permute-start | bytes 786440 | tf_op jit(solution)/shard_map/ppermute | solution.py:488
  7.0 13.9 %collective-permute-start.2 = (f32[32,8,256]{2,1,0:T(8,128)}, f32[32,8,256]{2,1,0:T(8,128)}, u32[]{:S(2)}, u32[]{:S(2)}) collective-permute-start(f32[32,8,256]{2,1,0:T(8,128)} %get-tuple-element.53), channel_id=1, source_target_pairs={{0,1},{1,2},{2,3},{3,4},{4,5},{5,6},{6,7},{7,8},{8,9},{9,10},{10,1... | collective-permute-start | bytes 786440 | tf_op jit(solution)/shard_map/ppermute | solution.py:487
  7.0 13.9 %collective-permute-start.3 = (f32[32,8,256]{2,1,0:T(8,128)}, f32[32,8,256]{2,1,0:T(8,128)}, u32[]{:S(2)}, u32[]{:S(2)}) collective-permute-start(f32[32,8,256]{2,1,0:T(8,128)} %get-tuple-element.54), channel_id=1, source_target_pairs={{1,0},{2,1},{3,2},{4,3},{5,4},{6,5},{7,6},{8,7},{9,8},{10,9},{11,1... | collective-permute-start | bytes 786440 | tf_op jit(solution)/shard_map/ppermute | solution.py:488
  18.8 6.9 %collective-permute-start.5 = (f32[16,4,256]{2,1,0:T(4,128)S(1)}, f32[16,4,256]{2,1,0:T(4,128)S(1)}, u32[]{:S(2)}, u32[]{:S(2)}) collective-permute-start(f32[16,4,256]{2,1,0:T(4,128)S(1)} %get-tuple-element.70), channel_id=1, source_target_pairs={{1,0},{2,1},{3,2},{4,3},{5,4},{6,5},{7,6},{8,7},{9,8},{10,9},{11,1... | collective-permute-start | bytes 196616 | tf_op jit(solution)/shard_map/ppermute | solution.py:488
  20.8 7.0 %collective-permute-start.4 = (f32[16,4,256]{2,1,0:T(4,128)S(1)}, f32[16,4,256]{2,1,0:T(4,128)S(1)}, u32[]{:S(2)}, u32[]{:S(2)}) collective-permute-start(f32[16,4,256]{2,1,0:T(4,128)S(1)} %get-tuple-element.71), channel_id=1, source_target_pairs={{0,1},{1,2},{2,3},{3,4},{4,5},{5,6},{6,7},{7,8},{8,9},{9,10},{10,1... | collective-permute-start | bytes 196616 | tf_op jit(solution)/shard_map/ppermute | solution.py:487
  29.0 6.2 %collective-permute-start.7 = (f32[3,5,16,128]{3,2,1,0:T(8,128)S(1)}, f32[3,5,16,128]{3,2,1,0:T(8,128)S(1)}, u32[]{:S(2)}, u32[]{:S(2)}) collective-permute-start(f32[3,5,16,128]{3,2,1,0:T(8,128)S(1)} %get-tuple-element.72), channel_id=1, source_target_pairs={{32,0},{64,32},{96,64},{128,96},{160,128},{192,160},{224,192},{0,2... | collective-permute-start | bytes 368648 | tf_op jit(solution)/shard_map/ppermute | solution.py:488
  29.1 6.1 %collective-permute-start.6 = (f32[3,5,16,128]{3,2,1,0:T(8,128)S(1)}, f32[3,5,16,128]{3,2,1,0:T(8,128)S(1)}, u32[]{:S(2)}, u32[]{:S(2)}) collective-permute-start(f32[3,5,16,128]{3,2,1,0:T(8,128)S(1)} %get-tuple-element.73), channel_id=1, source_target_pairs={{0,32},{32,64},{64,96},{96,128},{128,160},{160,192},{192,224},{224... | collective-permute-start | bytes 368648 | tf_op jit(solution)/shard_map/ppermute | solution.py:487
  35.2 8.7 %collective-permute-start.8 = (f32[2,26,8,128]{3,2,1,0:T(8,128)S(1)}, f32[2,26,8,128]{3,2,1,0:T(8,128)S(1)}, u32[]{:S(2)}, u32[]{:S(2)}) collective-permute-start(f32[2,26,8,128]{3,2,1,0:T(8,128)S(1)} %get-tuple-element.64), channel_id=1, source_target_pairs={{0,1},{1,2},{2,3},{3,4},{4,5},{5,6},{6,7},{7,8},{8,9},{9,10},{10,1... | collective-permute-start | bytes 638984 | tf_op jit(solution)/shard_map/ppermute | solution.py:487
  35.3 8.6 %collective-permute-start.9 = (f32[2,26,8,128]{3,2,1,0:T(8,128)S(1)}, f32[2,26,8,128]{3,2,1,0:T(8,128)S(1)}, u32[]{:S(2)}, u32[]{:S(2)}) collective-permute-start(f32[2,26,8,128]{3,2,1,0:T(8,128)S(1)} %get-tuple-element.65), channel_id=1, source_target_pairs={{1,0},{2,1},{3,2},{4,3},{5,4},{6,5},{7,6},{8,7},{9,8},{10,9},{11,1... | collective-permute-start | bytes 638984 | tf_op jit(solution)/shard_map/ppermute | solution.py:488
  45.9 5.7 %collective-permute-start.10 = (f32[12,10,128]{2,1,0:T(8,128)S(1)}, f32[12,10,128]{2,1,0:T(8,128)S(1)}, u32[]{:S(2)}, u32[]{:S(2)}) collective-permute-start(f32[12,10,128]{2,1,0:T(8,128)S(1)} %pad_maximum_fusion), channel_id=1, source_target_pairs={{0,32},{32,64},{64,96},{96,128},{128,160},{160,192},{192,224},{224... | collective-permute-start | bytes 184328 | tf_op jit(solution)/shard_map/ppermute | solution.py:487
  49.4 5.9 %collective-permute-start.11 = (f32[12,10,128]{2,1,0:T(8,128)S(1)}, f32[12,10,128]{2,1,0:T(8,128)S(1)}, u32[]{:S(2)}, u32[]{:S(2)}) collective-permute-start(f32[12,10,128]{2,1,0:T(8,128)S(1)} %pad_maximum_fusion.1), channel_id=1, source_target_pairs={{32,0},{64,32},{96,64},{128,96},{160,128},{192,160},{224,192},{0,2... | collective-permute-start | bytes 184328 | tf_op jit(solution)/shard_map/ppermute | solution.py:488
  55.3 6.5 %collective-permute-start.13 = (f32[39,8,128]{2,1,0:T(8,128)S(1)}, f32[39,8,128]{2,1,0:T(8,128)S(1)}, u32[]{:S(2)}, u32[]{:S(2)}) collective-permute-start(f32[39,8,128]{2,1,0:T(8,128)S(1)} %get-tuple-element.82), channel_id=1, source_target_pairs={{1,0},{2,1},{3,2},{4,3},{5,4},{6,5},{7,6},{8,7},{9,8},{10,9},{11,1... | collective-permute-start | bytes 479240 | tf_op jit(solution)/shard_map/ppermute | solution.py:488
  59.0 8.0 %collective-permute-start.12 = (f32[39,8,128]{2,1,0:T(8,128)S(1)}, f32[39,8,128]{2,1,0:T(8,128)S(1)}, u32[]{:S(2)}, u32[]{:S(2)}) collective-permute-start(f32[39,8,128]{2,1,0:T(8,128)S(1)} %get-tuple-element.83), channel_id=1, source_target_pairs={{0,1},{1,2},{2,3},{3,4},{4,5},{5,6},{6,7},{7,8},{8,9},{9,10},{10,1... | collective-permute-start | bytes 479240 | tf_op jit(solution)/shard_map/ppermute | solution.py:487

commit v5 on v4

--- a/solution.py
+++ b/solution.py
@@ -67,6 +67,10 @@
             e[k, x, h, at, :] = 0.4 * u[k, x, h, at, :] + d[k]
 
 
+def is_even(place, shape):
+    return jnp.full(shape, lax.rem(place[1], 2)) == 0
+
+
 def rows_inside(shape, y0, ysize):
     row = lax.broadcasted_iota(jnp.int32, shape, 0) + y0
     return (row >= 0) & (row < ysize)
@@ -113,7 +117,7 @@
 PX, PY = 3, 8
 
 
-def pack_kernel(f, c, x_first, x_last, y_first, y_last, planes, strips, sems):
+def pack_kernel(place, f, c, x_first, x_last, y_chip, y_next, planes, strips, sems):
     n, rows = c.shape[:2]
     edges = (0, n - PX)
     tiles = (0, rows - 8)
@@ -141,15 +145,19 @@
             strips[end, :, pl.ds(edges[side], PX)] = planes[side, :, :, pl.ds(row, 8), :]
     for copy in copies[6:]:
         copy.wait()
-    row = lax.broadcasted_iota(jnp.int32, (8, c.shape[2]), 0)
+    shape = (8, c.shape[2])
+    row = lax.broadcasted_iota(jnp.int32, shape, 0)
+    even = is_even(place, shape)
 
     def strip(x, carry):
-        for side, out, shifts in ((0, y_first, (0, 3, 6)), (1, y_last, (3, 6, 0))):
+        made = []
+        for side, shifts in ((0, (0, 3, 6)), (1, (3, 6, 0))):
             cc = strips[side, 2, x]
             a, b = inverse(cc, 1.0, None)
             re, im = divided(strips[side, 0, x], strips[side, 1, x], a, b)
             re, im, cc = [pltpu.roll(v, shift, 0) if shift else v for v, shift in zip((re, im, cc), shifts)]
-            out[x] = jnp.where(row < 3, re, jnp.where(row < 6, im, cc))
+            made.append(jnp.where(row < 3, re, jnp.where(row < 6, im, cc)))
+        y_chip[x], y_next[x] = jnp.where(even, made[1], made[0]), jnp.where(even, made[0], made[1])
         return carry
 
     lax.fori_loop(0, n, strip, 0, unroll=4)
@@ -246,8 +254,8 @@
     return side[i, :, cut], side[PX + i, :, cut], cc, c_here, i == (PX - 1 if low else 0)
 
 
-def faces_kernel(xsize, ysize, place, u_in, e_in, r_in, ga_in, gb_in, fc_in, xlo, xhi, ylo, yhi, u, e, r, ga, gb, fc_out, part, q):
-    n, (rows, lanes) = ylo.shape[0], xlo.shape[1:]
+def faces_kernel(xsize, ysize, place, u_in, e_in, r_in, ga_in, gb_in, fc_in, xlo, xhi, y_chip, y_next, u, e, r, ga, gb, fc_out, part, q):
+    n, (rows, lanes) = y_chip.shape[0], xlo.shape[1:]
     halves = lanes // LANES
     cut = [pl.ds(LANES * h, LANES) for h in range(halves)]
     ok = inside(place, n, rows, xsize, ysize)
@@ -260,11 +268,13 @@
                 halo(re, im, cc, good, u, ga, gb, r, base + i, h, PY, c_here, r_here)
     low, high = PY - 4, PY + rows - 4
     good_lo, good_hi = ok(PX, 0, 8), ok(PX, PY + rows, 8)
+    even = is_even(place, (8, LANES))
 
     def strips(x, carry):
-        for side, good, row, shifts in ((ylo, good_lo, 0, (5, 2, 0)), (yhi, good_hi, PY + rows, (0, 5, 2))):
-            for h in range(halves):
-                tile = side[x, :, cut[h]]
+        for h in range(halves):
+            chip, other = y_chip[x, :, cut[h]], y_next[x, :, cut[h]]
+            lo, hi = jnp.where(even, other, chip), jnp.where(even, chip, other)
+            for tile, good, row, shifts in ((lo, good_lo, 0, (5, 2, 0)), (hi, good_hi, PY + rows, (0, 5, 2))):
                 re, im, cc = [pltpu.roll(tile, shift, 0) if shift else tile for shift in shifts]
                 halo(re, im, cc, good, u, ga, gb, r, x + PX, h, row, True, True)
         return carry
@@ -312,18 +322,29 @@
             fc_out[k, pl.ds(2, m), pl.ds(row, 2), :] = (four[0] + four[3]) + 3.0 * (four[1] + four[2])
 
 
-def corners_kernel(xsize, ysize, n, rows, place, u_in, e_in, r_in, ga_in, gb_in, fc_in, clo, chi, u, e, r, ga, gb, fc_out, t, part):
-    halves = clo.shape[2] // LANES
+def pack_corners_kernel(place, xlo, xhi, chip, other):
+    rows = xlo.shape[1]
+    even = is_even(place, (4, xlo.shape[2]))
+    for side, base in ((xlo, 0), (xhi, 8)):
+        for j in range(8):
+            first, last = side[j, pl.ds(0, 4), :], side[j, pl.ds(rows - 4, 4), :]
+            chip[base + j], other[base + j] = jnp.where(even, last, first), jnp.where(even, first, last)
+
+
+def corners_kernel(xsize, ysize, n, rows, place, u_in, e_in, r_in, ga_in, gb_in, fc_in, c_chip, c_next, u, e, r, ga, gb, fc_out, t, part):
+    halves = c_chip.shape[2] // LANES
+    even = is_even(place, (4, LANES))
     ok = inside(place, n, rows, xsize, ysize)
     del u_in, e_in, r_in, ga_in, gb_in, fc_in
     low, high = PY - 4, PY + rows - 4
-    for side, row in ((clo, PY - 4), (chi, PY + rows)):
-        for planes, is_low, base in ((side.at[pl.ds(0, 8)], True, 0), (side.at[pl.ds(8, 8)], False, n + PX)):
-            for i in range(PX):
-                good = ok(base + i, row, 4)
-                for h in range(halves):
-                    re, im, cc, c_here, r_here = plane_cells(planes, is_low, i, h)
-                    halo(re, im, cc, good, u, ga, gb, r, base + i, h, row, c_here, r_here)
+    for first, low_planes, base in ((0, True, 0), (8, False, n + PX)):
+        chip, other = c_chip.at[pl.ds(first, 8)], c_next.at[pl.ds(first, 8)]
+        for i in range(PX):
+            for h in range(halves):
+                one, two = plane_cells(chip, low_planes, i, h), plane_cells(other, low_planes, i, h)
+                for row, (p, q) in ((PY - 4, (two, one)), (PY + rows, (one, two))):
+                    re, im, cc = [None if v is None else jnp.where(even, v, w) for v, w in zip(p[:3], q[:3])]
+                    halo(re, im, cc, ok(base + i, row, 4), u, ga, gb, r, base + i, h, row, *one[3:])
     for x in (PX - 2, PX - 1, PX, n + PX - 1, n + PX, n + PX + 1):
         for row in (low, high):
             second(u, ga, gb, e, x, row, 8, 1.0, True)
@@ -369,28 +390,33 @@
             r[k, x, 0, at, :] = jnp.where(good, 0.04 * cells(k, x, at) + s, 0.0)
 
 
-def rows_kernel(xlo, fc, xhi, first, last):
+def rows_kernel(place, xlo, fc, xhi, chip, other):
     halo, n, rows = xlo.shape[1], fc.shape[1], fc.shape[2]
     row = lax.broadcasted_iota(jnp.int32, (8, LANES), 0)
+    even = is_even(place, (8, LANES))
     for src, base, count in ((xlo, 0, halo), (fc, halo, n), (xhi, n + halo, halo)):
         for i in range(count):
-            for out, start, own in ((first, 0, row < 5), (last, rows - 8, row >= 3)):
+            made = []
+            for start, own in ((0, row < 5), (rows - 8, row >= 3)):
                 re, im, cc = [src[k, i, pl.ds(start, 8), :] for k in range(3)]
-                out[0, base + i] = jnp.where(own, re, pltpu.roll(cc, 5, 0))
-                out[1, base + i] = jnp.where(own, im, pltpu.roll(cc, 2, 0))
-
-
-def middle_kernel(halo, over, xsize, ysize, place, fc_own, xlo, xhi, ylo, yhi, u_out, fc_out, fc, ga, gb, u, e, r, t, part, part_c):
+                made.append((jnp.where(own, re, pltpu.roll(cc, 5, 0)), jnp.where(own, im, pltpu.roll(cc, 2, 0))))
+            for k, (first, last) in enumerate(zip(*made)):
+                chip[k, base + i], other[k, base + i] = jnp.where(even, last, first), jnp.where(even, first, last)
+
+
+def middle_kernel(halo, over, xsize, ysize, place, fc_own, xlo, xhi, y_chip, y_next, u_out, fc_out, fc, ga, gb, u, e, r, t, part, part_c):
     n, rows = fc_own.shape[1:3]
     planes = n + 2 * halo
     for k in range(3):
         for src, x, count in ((xlo, 0, halo), (fc_own, halo, n), (xhi, n + halo, halo)):
             fc[k, pl.ds(x, count), 0, pl.ds(8, rows), :] = src[k]
     row = lax.broadcasted_iota(jnp.int32, (8, LANES), 0)
-    for side, start, split in ((ylo, 0, 6), (yhi, 8 + rows, 3)):
-        at = pl.ds(start, 8)
-        for x in range(planes):
-            one, two = side[0, x], side[1, x]
+    even = is_even(place, (8, LANES))
+    for x in range(planes):
+        chip, other = [y_chip[k, x] for k in (0, 1)], [y_next[k, x] for k in (0, 1)]
+        for start, split, p, q in ((0, 6, other, chip), (8 + rows, 3, chip, other)):
+            at = pl.ds(start, 8)
+            one, two = [jnp.where(even, v, w) for v, w in zip(p, q)]
             fc[0, x, 0, at, :], fc[1, x, 0, at, :] = one, two
             fc[2, x, 0, at, :] = jnp.where(row < split, pltpu.roll(one, 3, 0), pltpu.roll(two, 6, 0))
     x0, y0 = place[0] * n - halo, place[1] * rows - 8
@@ -421,13 +447,15 @@
     fc_out[pl.ds(width, pairs)] = sum(exact_dot(p[...], weights(LANES, LANES, True, s)) for _, p, s in two)[:, :width]
 
 
-def coarse_kernel(n, sweeps, xsize, ysize, zsize, place, fc_own, xlo, xhi, ylo, yhi, u_out, v_out, fc, ga, gb, u, e, r, t, part, part_c, gc, gd, v, w):
+def coarse_kernel(n, sweeps, xsize, ysize, zsize, place, fc_own, xlo, xhi, y_chip, y_next, u_out, v_out, fc, ga, gb, u, e, r, t, part, part_c, gc, gd, v, w):
     m = n // 2
     planes = n + 18
     for src, x, first, count in ((xlo, 0, 0, 8), (fc_own, 8, 0, n + 2), (xhi, n + 10, 0, 8), (xlo, planes, 8, 4), (fc_own, planes + 4, n + 2, m + 1), (xhi, planes + m + 5, 8, 4)):
         fc[pl.ds(x, count), 0, pl.ds(15, n + 2), :] = src[pl.ds(first, count)]
-    fc[:, 0, pl.ds(7, 8), :] = ylo[...]
-    fc[:, 0, pl.ds(n + 17, 8), :] = yhi[...]
+    even = is_even(place, (8, LANES))
+    for x in range(fc.shape[0]):
+        chip, other = y_chip[x], y_next[x]
+        fc[x, 0, pl.ds(7, 8), :], fc[x, 0, pl.ds(n + 17, 8), :] = jnp.where(even, other, chip), jnp.where(even, chip, other)
     lane = lax.broadcasted_iota(jnp.int32, (1, LANES), 1)
 
     def cells(k, x, at):
@@ -483,27 +511,35 @@
     xdev, ydev = lax.axis_size("gx"), lax.axis_size("gy")
     place = jnp.stack([lax.axis_index("gx"), lax.axis_index("gy")]).astype(jnp.int32)
 
-    def swap(axis, devices, first, last):
-        before = lax.ppermute(last, axis, [(i, (i + 1) % devices) for i in range(devices)])
-        after = lax.ppermute(first, axis, [((i + 1) % devices, i) for i in range(devices)])
+    def planes_step(first, last):
+        before = lax.ppermute(last, "gx", [(i, (i + 1) % xdev) for i in range(xdev)])
+        after = lax.ppermute(first, "gx", [((i + 1) % xdev, i) for i in range(xdev)])
         return before, after
+
+    every = [(i, j) for i in range(xdev) for j in range(ydev)]
+    number = lambda i, j: i * ydev + j
+    on_chip = [(number(i, j), number(i, j ^ 1)) for i, j in every]
+    next_chip = [(number(i, j), number(i ^ 1, j) if j in (0, ydev - 1) else number(i, ((j - 1) ^ 1) + 1)) for i, j in every]
+
+    def rows_step(chip, other):
+        return lax.ppermute(chip, ("gx", "gy"), on_chip), lax.ppermute(other, ("gx", "gy"), next_chip)
 
     _, n, rows, lanes = source.shape
     xsize, ysize = n * xdev, rows * ydev
     S = lambda *shape: jax.ShapeDtypeStruct(shape, f32)
     V = lambda *shape: pltpu.VMEM(shape, f32)
 
-    x_first, x_last, y_first, y_last = pl.pallas_call(
+    x_first, x_last, y_chip, y_next = pl.pallas_call(
         pack_kernel,
-        in_specs=[pl.BlockSpec(memory_space=pltpu.HBM)] * 2,
+        in_specs=[SMEM] + [pl.BlockSpec(memory_space=pltpu.HBM)] * 2,
         out_specs=[VMEM] * 4,
         out_shape=[S(8, rows, lanes)] * 2 + [S(n, 8, lanes)] * 2,
         scratch_shapes=[V(2, 3, PX, rows, lanes), V(2, 3, n, 8, lanes), pltpu.SemaphoreType.DMA((12,))],
         compiler_params=params(60),
         name="pack_faces",
-    )(source, wavenumber_sq)
-    xlo, xhi = swap("gx", xdev, x_first, x_last)
-    ylo, yhi = swap("gy", ydev, y_first, y_last)
+    )(place, source, wavenumber_sq)
+    xlo, xhi = planes_step(x_first, x_last)
+    y_chip, y_next = rows_step(y_chip, y_next)
     halves = lanes // LANES
     state = (n + 2 * PX, halves, rows + 2 * PY, LANES)
     part = (n // 2, rows // 2, lanes)
@@ -520,8 +556,16 @@
         name="inner_cells",
     )(source, wavenumber_sq)
     xlo, xhi, held = lax.optimization_barrier((xlo, xhi, held))
-    planes = jnp.concatenate([xlo, xhi], 0)
-    clo, chi = swap("gy", ydev, planes[:, :4], planes[:, rows - 4 :])
+    c_chip, c_next = rows_step(
+        *pl.pallas_call(
+            pack_corners_kernel,
+            in_specs=[SMEM] + [VMEM] * 2,
+            out_specs=[VMEM] * 2,
+            out_shape=[S(16, 4, lanes)] * 2,
+            compiler_params=params(24),
+            name="pack_corners",
+        )(place, xlo, xhi)
+    )
     in_place = {i + 1: i for i in range(6)}
     held = pl.pallas_call(
         functools.partial(faces_kernel, xsize, ysize),
@@ -533,7 +577,7 @@
         compiler_params=params(24),
         cost_estimate=pl.CostEstimate(flops=50_000_000, bytes_accessed=8_000_000, transcendentals=0),
         name="face_cells",
-    )(place, *held, xlo, xhi, ylo, yhi)
+    )(place, *held, xlo, xhi, y_chip, y_next)
     u, e, _, _, _, fc = pl.pallas_call(
         functools.partial(corners_kernel, xsize, ysize, n, rows),
         in_specs=[SMEM] + [VMEM] * 8,
@@ -543,7 +587,7 @@
         scratch_shapes=[column, V(2, 4, rows // 2, lanes)],
         compiler_params=params(24),
         name="corner_cells",
-    )(place, *held, clo, chi)
+    )(place, *held, c_chip, c_next)
     fine = pl.pallas_call(
         iterate_kernel,
         in_specs=[VMEM] * 2,
@@ -556,16 +600,16 @@
 
     n, rows, lanes, xsize, ysize, zsize = n // 2, rows // 2, lanes // 2, xsize // 2, ysize // 2, lanes // 2
     h, over = 5, 1
-    xlo, xhi = swap("gx", xdev, fc[:, :h], fc[:, n - h :])
-    first_rows, last_rows = pl.pallas_call(
+    xlo, xhi = planes_step(fc[:, :h], fc[:, n - h :])
+    chip, other = pl.pallas_call(
         rows_kernel,
-        in_specs=[VMEM] * 3,
+        in_specs=[SMEM] + [VMEM] * 3,
         out_specs=[VMEM] * 2,
         out_shape=[S(2, n + 2 * h, 8, lanes)] * 2,
         compiler_params=params(24),
         name="second_rows",
-    )(xlo, fc, xhi)
-    ylo, yhi = swap("gy", ydev, first_rows, last_rows)
+    )(place, xlo, fc, xhi)
+    chip, other = rows_step(chip, other)
     state = (n + 2 * h, 1, rows + 16, LANES)
     work = lambda s: [V(*s), V(*s), V(2, *s), V(2, *s), V(2, *s), V(2, 1, *s[2:])]
     width = n // 2 + 2 * over
@@ -577,7 +621,7 @@
         scratch_shapes=[V(3, *state)] + work(state) + [V(2, width, 16, LANES), V(2, width // 2, 16, LANES)],
         compiler_params=params(24),
         name="second_level",
-    )(place, fc, xlo, xhi, ylo, yhi)
+    )(place, fc, xlo, xhi, chip, other)
 
     n, xsize, ysize, zsize = n // 2, xsize // 2, ysize // 2, zsize // 2
     m = n // 2
@@ -588,8 +632,10 @@
         return jnp.concatenate([a[:, cells] for a in f + c], 0)
 
     pick = lambda i, j: jnp.concatenate([fc[i : i + n], fc[n + 2 + j : n + 2 + j + m]], 0)
-    xlo, xhi = swap("gx", xdev, pick(2, 1), pick(0, 0))
-    ylo, yhi = swap("gy", ydev, joined(xlo, fc, xhi, slice(2, n + 2)), joined(xlo, fc, xhi, slice(0, n)))
+    xlo, xhi = planes_step(pick(2, 1), pick(0, 0))
+    first, last = joined(xlo, fc, xhi, slice(2, n + 2)), joined(xlo, fc, xhi, slice(0, n))
+    even = place[1] % 2 == 0
+    chip, other = rows_step(jnp.where(even, last, first), jnp.where(even, first, last))
     state = (n + 18, 1, 40, LANES)
     small = (m + 6, 1, 16, LANES)
     third, coarse = pl.pallas_call(
@@ -601,7 +647,7 @@
         + [V(*small), V(*small), V(2, *small), V(2, 2, *small)],
         compiler_params=params(24),
         name="coarse_levels",
-    )(place, fc, xlo, xhi, ylo, yhi)
+    )(place, fc, xlo, xhi, chip, other)
     return fine, second_u, third, coarse
 
 

time: 69.8 us -> 66.2 us (0.948)
  the two profiles are of different devices: /device:TPU:96 before, /device:TPU:120 now
where the time goes in v5:
time: 66.2 us; the launch traced here: 65.5 us
  Pallas kernels  22.5 us (34%)
  starting transfers between devices  19 us (29%)
  waiting for transfers between devices  14.8 us (22%)
  local copies, waits for them, and re-layouts  7.82 us (12%)
  between operations  0.82 us (1%)
    ppermute x3, starting transfers between devices, planes_step(): lax.ppermute(last, 'gx', [(i, (i + 1) % xdev) for i in range(xdev)])  9.74 us
    ppermute x4, starting transfers between devices, rows_step(): lax.ppermute(other, ('gx', 'gy'), next_chip)  8.86 us
    unnamed x19, local copies, waits for them, and re-layouts  7.78 us
    ppermute x3, waiting for transfers between devices, planes_step(): lax.ppermute(first, 'gx', [((i + 1) % xdev, i) for i in range(xdev)])  6.87 us
    ppermute x4, waiting for transfers between devices, rows_step(): lax.ppermute(other, ('gx', 'gy'), next_chip)  5.82 us
    pallas_call x1, Pallas kernels, body(): pl.pallas_call(inner_kernel, in_specs=[VMEM] * 2, out_specs=[VMEM] * 6, o...  5.77 us
    pallas_call x1, Pallas kernels, body(): pl.pallas_call(functools.partial(faces_kernel, xsize, ysize), in_specs=[S...  4.28 us
    pallas_call x1, Pallas kernels, body(): pl.pallas_call(pack_kernel, in_specs=[SMEM] + [pl.BlockSpec(memory_space=...  3.76 us
  transfers between devices with their start and end apart: 14, of which 6 were waited for; matrix products, arithmetic and copies ran while one was open for 0% of the time, Pallas kernels for 19%

profile of v5, /device:TPU:120, one launch (start us, length us, event | category | flops | bytes accessed | tf_op | source)
XLA Modules:
  0.0 65.5 jit_solution(6539554007791962403)
XLA Ops:
  0.7 0.6 pad_add_fusion.place
  1.3 3.8 %pack_faces.1 = (f32[8,32,256]{2,1,0:T(8,128)}, f32[8,32,256]{2,1,0:T(8,128)}, f32[32,8,256]{2,1,0:T(8,128)}, f32[32,8,256]{2,1,0:T(8,128)}) custom-call(s32[2]{0:T(128)} %pad_add_fusion.place, f32[2,32,32,256]{3,2,1,0:T(8,128)} %f.3, f32[32,32,256]{2,1,0:T(8,128)} %c.3), custom_call_target="tpu_custom_call" | custom-call | tf_op jit(solution)/shard_map/pack_faces/pallas_call | solution.py:532
  5.0 3.2 %collective-permute-start = (f32[8,32,256]{2,1,0:T(8,128)}, f32[8,32,256]{2,1,0:T(8,128)S(1)}, u32[]{:S(2)}, u32[]{:S(2)}) collective-permute-start(f32[8,32,256]{2,1,0:T(8,128)} %get-tuple-element.39), channel_id=1, source_target_pairs={{0,32},{32,64},{64,96},{96,128},{128,160},{160,192},{192,224},{224... | collective-permute-start | bytes 786440 | tf_op jit(solution)/shard_map/ppermute | solution.py:515
  8.3 3.0 %collective-permute-start.3 = (f32[32,8,256]{2,1,0:T(8,128)}, f32[32,8,256]{2,1,0:T(8,128)S(1)}, u32[]{:S(2)}, u32[]{:S(2)}) collective-permute-start(f32[32,8,256]{2,1,0:T(8,128)} %get-tuple-element.56), channel_id=1, source_target_pairs={{0,32},{1,2},{2,1},{3,4},{4,3},{5,6},{6,5},{7,8},{8,7},{9,10},{10,... | collective-permute-start | bytes 786440 | tf_op jit(solution)/shard_map/ppermute | solution.py:525
  11.3 5.8 %inner_cells.1 = (f32[2,38,2,48,128]{4,3,2,1,0:T(8,128)S(1)}, f32[2,38,2,48,128]{4,3,2,1,0:T(8,128)S(1)}, f32[2,38,2,48,128]{4,3,2,1,0:T(8,128)S(1)}, f32[38,2,4...) custom-call(f32[2,32,32,256]{3,2,1,0:T(8,128)S(1)} %copy-done.4, ...), custom_call_target="tpu_custom_call" | custom-call | flops 100000000 | bytes 16000000 | tf_op jit(solution)/shard_map/inner_cells/pallas_call | solution.py:548
  18.1 3.0 %collective-permute-start.5 = (f32[16,4,256]{2,1,0:T(4,128)S(1)}, f32[16,4,256]{2,1,0:T(4,128)S(1)}, u32[]{:S(2)}, u32[]{:S(2)}) collective-permute-start(f32[16,4,256]{2,1,0:T(4,128)S(1)} %get-tuple-element.64), channel_id=1, source_target_pairs={{0,32},{1,2},{2,1},{3,4},{4,3},{5,6},{6,5},{7,8},{8,7},{9,10},{10,... | collective-permute-start | bytes 196616 | tf_op jit(solution)/shard_map/ppermute | solution.py:525
  21.2 4.3 %face_cells.1 = (f32[2,38,2,48,128]{4,3,2,1,0:T(8,128)S(1)}, f32[2,38,2,48,128]{4,3,2,1,0:T(8,128)S(1)}, f32[2,38,2,48,128]{4,3,2,1,0:T(8,128)S(1)}, f32[38,2,48...) custom-call(s32[2]{0:T(128)S(1)} %copy-done.6, ...), custom_call_target="tpu_custom_call", output_to_operand_aliasing={{0}: (1, {}), {1}: (2, {}), {2}: (3, {}), {3}: (4, {}), {4}... | custom-call | flops 50000000 | bytes 8000000 | tf_op jit(solution)/shard_map/face_cells/pallas_call | solution.py:570
  25.5 1.1 %corner_cells.1 = (f32[2,38,2,48,128]{4,3,2,1,0:T(8,128)S(1)}, f32[2,38,2,48,128]{4,3,2,1,0:T(8,128)S(1)}, f32[2,38,2,48,128]{4,3,2,1,0:T(8,128)S(1)}, f32[38,2,...) custom-call(s32[2]{0:T(128)S(1)} %copy-done.6, ...), custom_call_target="tpu_custom_call", output_to_operand_aliasing={{0}: (1, {}), {1}: (2, {}), {2}: (3, {}), {3}: (4, {}), {4}... | custom-call | tf_op jit(solution)/shard_map/corner_cells/pallas_call | solution.py:581
  26.6 1.8 %copy-done = f32[2,38,2,48,128]{4,3,2,1,0:T(8,128)} copy-done((f32[2,38,2,48,128]{4,3,2,1,0:T(8,128)}, f32[2,38,2,48,128]{4,3,2,1,0:T(8,128)S(1)}, u32[]{:S(2)}) %copy-start) | copy-done | bytes 3735576
  28.4 1.8 %copy-done.2 = f32[2,38,2,48,128]{4,3,2,1,0:T(8,128)} copy-done((f32[2,38,2,48,128]{4,3,2,1,0:T(8,128)}, f32[2,38,2,48,128]{4,3,2,1,0:T(8,128)S(1)}, u32[]{:S(2)}) %copy-start.2) | copy-done | bytes 3735576
  30.3 3.2 %collective-permute-start.6 = (f32[3,5,16,128]{3,2,1,0:T(8,128)S(1)}, f32[3,5,16,128]{3,2,1,0:T(8,128)S(1)}, u32[]{:S(2)}, u32[]{:S(2)}) collective-permute-start(f32[3,5,16,128]{3,2,1,0:T(8,128)S(1)} %get-tuple-element.75), channel_id=1, source_target_pairs={{0,32},{32,64},{64,96},{96,128},{128,160},{160,192},{192,224},{224... | collective-permute-start | bytes 368648 | tf_op jit(solution)/shard_map/ppermute | solution.py:515
  33.5 2.9 %collective-permute-done.7.xhi = f32[3,5,16,128]{3,2,1,0:T(8,128)S(1)} collective-permute-done((f32[3,5,16,128]{3,2,1,0:T(8,128)S(1)}, f32[3,5,16,128]{3,2,1,0:T(8,128)S(1)}, u32[]{:S(2)}, u32[]{:S(2)}) %collective-permute-start.7) | collective-permute-done | bytes 122912 | tf_op jit(solution)/shard_map/ppermute | solution.py:516
  36.4 0.6 second_rows.1
  37.1 2.1 %collective-permute-start.9 = (f32[2,26,8,128]{3,2,1,0:T(8,128)S(1)}, f32[2,26,8,128]{3,2,1,0:T(8,128)S(1)}, u32[]{:S(2)}, u32[]{:S(2)}) collective-permute-start(f32[2,26,8,128]{3,2,1,0:T(8,128)S(1)} %get-tuple-element.69), channel_id=1, source_target_pairs={{0,32},{1,2},{2,1},{3,4},{4,3},{5,6},{6,5},{7,8},{8,7},{9,10},{10,... | collective-permute-start | bytes 638984 | tf_op jit(solution)/shard_map/ppermute | solution.py:525
  39.2 5.3 %collective-permute-done.9.y_next = f32[2,26,8,128]{3,2,1,0:T(8,128)S(1)} collective-permute-done((f32[2,26,8,128]{3,2,1,0:T(8,128)S(1)}, f32[2,26,8,128]{3,2,1,0:T(8,128)S(1)}, u32[]{:S(2)}, u32[]{:S(2)}) %collective-permute-start.9) | collective-permute-done | bytes 213024 | tf_op jit(solution)/shard_map/ppermute | solution.py:525
  44.6 2.1 %second_level.1 = (f32[2,16,16,128]{3,2,1,0:T(8,128)}, f32[15,10,128]{2,1,0:T(8,128)S(1)}) custom-call(s32[2]{0:T(128)S(1)} %copy-done.6, f32[3,16,16,128]{3,2,1,0:T(8,128)S(1)} %get-tuple-element.67.fc.fc_own, f32[3,5,16,128]{3,2,1,0:T(8,128)S(1)} %collective-permute-done.6.xlo, f32[3,5,16,128]{3,2,1,0:T(8,128)S(1)} %collective-permute-done.7.xhi, ...), custom_call_target="tpu_custom_call" | custom-call | tf_op jit(solution)/shard_map/second_level/pallas_call | solution.py:616
  46.7 3.3 %collective-permute-start.10 = (f32[12,10,128]{2,1,0:T(8,128)S(1)}, f32[12,10,128]{2,1,0:T(8,128)S(1)}, u32[]{:S(2)}, u32[]{:S(2)}) collective-permute-start(f32[12,10,128]{2,1,0:T(8,128)S(1)} %pad_maximum_fusion), channel_id=1, source_target_pairs={{0,32},{32,64},{64,96},{96,128},{128,160},{160,192},{192,224},{224... | collective-permute-start | bytes 184328 | tf_op jit(solution)/shard_map/ppermute | solution.py:515
  50.1 2.1 %collective-permute-done.10.xlo = f32[12,10,128]{2,1,0:T(8,128)S(1)} collective-permute-done((f32[12,10,128]{2,1,0:T(8,128)S(1)}, f32[12,10,128]{2,1,0:T(8,128)S(1)}, u32[]{:S(2)}, u32[]{:S(2)}) %collective-permute-start.10) | collective-permute-done | bytes 61472 | tf_op jit(solution)/shard_map/ppermute | solution.py:515
  52.2 3.7 %collective-permute-done.11.xhi = f32[12,10,128]{2,1,0:T(8,128)S(1)} collective-permute-done((f32[12,10,128]{2,1,0:T(8,128)S(1)}, f32[12,10,128]{2,1,0:T(8,128)S(1)}, u32[]{:S(2)}, u32[]{:S(2)}) %collective-permute-start.11) | collective-permute-done | bytes 61472 | tf_op jit(solution)/shard_map/ppermute | solution.py:516
  56.0 0.6 collective-permute-start.13
  56.6 2.1 %copy-done.1 = f32[2,38,2,48,128]{4,3,2,1,0:T(8,128)S(1)} copy-done((f32[2,38,2,48,128]{4,3,2,1,0:T(8,128)S(1)}, f32[2,38,2,48,128]{4,3,2,1,0:T(8,128)}, u32[]{:S(2)}) %copy-start.1) | copy-done | bytes 3735576
  58.7 2.1 %copy-done.3 = f32[2,38,2,48,128]{4,3,2,1,0:T(8,128)S(1)} copy-done((f32[2,38,2,48,128]{4,3,2,1,0:T(8,128)S(1)}, f32[2,38,2,48,128]{4,3,2,1,0:T(8,128)}, u32[]{:S(2)}) %copy-start.3) | copy-done | bytes 3735576
  60.7 1.6 %fine_iterate.1 = f32[2,32,32,256]{3,2,1,0:T(8,128)} custom-call(f32[2,38,2,48,128]{4,3,2,1,0:T(8,128)S(1)} %copy-done.1, f32[2,38,2,48,128]{4,3,2,1,0:T(8,128)S(1)} %copy-done.3), custom_call_target="tpu_custom_call" | custom-call | flops 1000000 | bytes 8000000 | tf_op jit(solution)/shard_map/fine_iterate/pallas_call | solution.py:591
  62.9 2.7 %coarse_levels.1 = (f32[2,8,8,64]{3,2,1,0:T(8,128)}, f32[2,4,4,32]{3,2,1,0:T(4,128)}) custom-call(s32[2]{0:T(128)S(1)} %copy-done.6, f32[15,10,128]{2,1,0:T(8,128)S(1)} %get-tuple-element.71.fc_own, f32[12,10,128]{2,1,0:T(8,128)S(1)} %collective-permute-done.10.xlo, f32[12,10,128]{2,1,0:T(8,128)S(1)} %collective-permute-done.11.xhi, ...), custom_call_target="tpu_custom_call" | custom-call | tf_op jit(solution)/shard_map/coarse_levels/pallas_call | solution.py:641
  (40 shorter events, 1.9 us)
Async XLA Ops:
  0.6 10.7 %copy-start.5 = (f32[32,32,256]{2,1,0:T(8,128)S(1)}, f32[32,32,256]{2,1,0:T(8,128)}, u32[]{:S(2)}) copy-start(f32[32,32,256]{2,1,0:T(8,128)} %c.3) | copy-start | bytes 3145732
  0.6 10.7 %copy-start.4 = (f32[2,32,32,256]{3,2,1,0:T(8,128)S(1)}, f32[2,32,32,256]{3,2,1,0:T(8,128)}, u32[]{:S(2)}) copy-start(f32[2,32,32,256]{3,2,1,0:T(8,128)} %f.3) | copy-start | bytes 6291460
  1.3 16.2 %copy-start.6 = (s32[2]{0:T(128)S(1)}, s32[2]{0:T(128)}, u32[]{:S(2)}) copy-start(s32[2]{0:T(128)} %pad_add_fusion.place) | copy-start | bytes 28
  5.0 12.0 %collective-permute-start = (f32[8,32,256]{2,1,0:T(8,128)}, f32[8,32,256]{2,1,0:T(8,128)S(1)}, u32[]{:S(2)}, u32[]{:S(2)}) collective-permute-start(f32[8,32,256]{2,1,0:T(8,128)} %get-tuple-element.39), channel_id=1, source_target_pairs={{0,32},{32,64},{64,96},{96,128},{128,160},{160,192},{192,224},{224... | collective-permute-start | bytes 786440 | tf_op jit(solution)/shard_map/ppermute | solution.py:515
  8.2 9.2 %collective-permute-start.1 = (f32[8,32,256]{2,1,0:T(8,128)}, f32[8,32,256]{2,1,0:T(8,128)S(1)}, u32[]{:S(2)}, u32[]{:S(2)}) collective-permute-start(f32[8,32,256]{2,1,0:T(8,128)} %get-tuple-element.40), channel_id=1, source_target_pairs={{32,0},{64,32},{96,64},{128,96},{160,128},{192,160},{224,192},{0,2... | collective-permute-start | bytes 786440 | tf_op jit(solution)/shard_map/ppermute | solution.py:516
  8.2 12.9 %collective-permute-start.2 = (f32[32,8,256]{2,1,0:T(8,128)}, f32[32,8,256]{2,1,0:T(8,128)S(1)}, u32[]{:S(2)}, u32[]{:S(2)}) collective-permute-start(f32[32,8,256]{2,1,0:T(8,128)} %get-tuple-element.55), channel_id=1, source_target_pairs={{0,1},{1,0},{2,3},{3,2},{4,5},{5,4},{6,7},{7,6},{8,9},{9,8},{10,11... | collective-permute-start | bytes 786440 | tf_op jit(solution)/shard_map/ppermute | solution.py:525
  8.3 12.9 %collective-permute-start.3 = (f32[32,8,256]{2,1,0:T(8,128)}, f32[32,8,256]{2,1,0:T(8,128)S(1)}, u32[]{:S(2)}, u32[]{:S(2)}) collective-permute-start(f32[32,8,256]{2,1,0:T(8,128)} %get-tuple-element.56), channel_id=1, source_target_pairs={{0,32},{1,2},{2,1},{3,4},{4,3},{5,6},{6,5},{7,8},{8,7},{9,10},{10,... | collective-permute-start | bytes 786440 | tf_op jit(solution)/shard_map/ppermute | solution.py:525
  18.0 7.4 %collective-permute-start.4 = (f32[16,4,256]{2,1,0:T(4,128)S(1)}, f32[16,4,256]{2,1,0:T(4,128)S(1)}, u32[]{:S(2)}, u32[]{:S(2)}) collective-permute-start(f32[16,4,256]{2,1,0:T(4,128)S(1)} %get-tuple-element.63), channel_id=1, source_target_pairs={{0,1},{1,0},{2,3},{3,2},{4,5},{5,4},{6,7},{7,6},{8,9},{9,8},{10,11... | collective-permute-start | bytes 196616 | tf_op jit(solution)/shard_map/ppermute | solution.py:525
  18.1 7.3 %collective-permute-start.5 = (f32[16,4,256]{2,1,0:T(4,128)S(1)}, f32[16,4,256]{2,1,0:T(4,128)S(1)}, u32[]{:S(2)}, u32[]{:S(2)}) collective-permute-start(f32[16,4,256]{2,1,0:T(4,128)S(1)} %get-tuple-element.64), channel_id=1, source_target_pairs={{0,32},{1,2},{2,1},{3,4},{4,3},{5,6},{6,5},{7,8},{8,7},{9,10},{10,... | collective-permute-start | bytes 196616 | tf_op jit(solution)/shard_map/ppermute | solution.py:525
  26.6 1.8 %copy-start = (f32[2,38,2,48,128]{4,3,2,1,0:T(8,128)}, f32[2,38,2,48,128]{4,3,2,1,0:T(8,128)S(1)}, u32[]{:S(2)}) copy-start(f32[2,38,2,48,128]{4,3,2,1,0:T(8,128)S(1)} %get-tuple-element.65.u) | copy-start | bytes 11206660
  28.4 1.8 %copy-start.2 = (f32[2,38,2,48,128]{4,3,2,1,0:T(8,128)}, f32[2,38,2,48,128]{4,3,2,1,0:T(8,128)S(1)}, u32[]{:S(2)}) copy-start(f32[2,38,2,48,128]{4,3,2,1,0:T(8,128)S(1)} %get-tuple-element.66.e) | copy-start | bytes 11206660
  30.2 6.2 %collective-permute-start.7 = (f32[3,5,16,128]{3,2,1,0:T(8,128)S(1)}, f32[3,5,16,128]{3,2,1,0:T(8,128)S(1)}, u32[]{:S(2)}, u32[]{:S(2)}) collective-permute-start(f32[3,5,16,128]{3,2,1,0:T(8,128)S(1)} %get-tuple-element.74), channel_id=1, source_target_pairs={{32,0},{64,32},{96,64},{128,96},{160,128},{192,160},{224,192},{0,2... | collective-permute-start | bytes 368648 | tf_op jit(solution)/shard_map/ppermute | solution.py:516
  30.3 6.1 %collective-permute-start.6 = (f32[3,5,16,128]{3,2,1,0:T(8,128)S(1)}, f32[3,5,16,128]{3,2,1,0:T(8,128)S(1)}, u32[]{:S(2)}, u32[]{:S(2)}) collective-permute-start(f32[3,5,16,128]{3,2,1,0:T(8,128)S(1)} %get-tuple-element.75), channel_id=1, source_target_pairs={{0,32},{32,64},{64,96},{96,128},{128,160},{160,192},{192,224},{224... | collective-permute-start | bytes 368648 | tf_op jit(solution)/shard_map/ppermute | solution.py:515
  37.0 2.3 %collective-permute-start.8 = (f32[2,26,8,128]{3,2,1,0:T(8,128)S(1)}, f32[2,26,8,128]{3,2,1,0:T(8,128)S(1)}, u32[]{:S(2)}, u32[]{:S(2)}) collective-permute-start(f32[2,26,8,128]{3,2,1,0:T(8,128)S(1)} %get-tuple-element.68), channel_id=1, source_target_pairs={{0,1},{1,0},{2,3},{3,2},{4,5},{5,4},{6,7},{7,6},{8,9},{9,8},{10,11... | collective-permute-start | bytes 638984 | tf_op jit(solution)/shard_map/ppermute | solution.py:525
  37.1 7.5 %collective-permute-start.9 = (f32[2,26,8,128]{3,2,1,0:T(8,128)S(1)}, f32[2,26,8,128]{3,2,1,0:T(8,128)S(1)}, u32[]{:S(2)}, u32[]{:S(2)}) collective-permute-start(f32[2,26,8,128]{3,2,1,0:T(8,128)S(1)} %get-tuple-element.69), channel_id=1, source_target_pairs={{0,32},{1,2},{2,1},{3,4},{4,3},{5,6},{6,5},{7,8},{8,7},{9,10},{10,... | collective-permute-start | bytes 638984 | tf_op jit(solution)/shard_map/ppermute | solution.py:525
  46.7 5.5 %collective-permute-start.10 = (f32[12,10,128]{2,1,0:T(8,128)S(1)}, f32[12,10,128]{2,1,0:T(8,128)S(1)}, u32[]{:S(2)}, u32[]{:S(2)}) collective-permute-start(f32[12,10,128]{2,1,0:T(8,128)S(1)} %pad_maximum_fusion), channel_id=1, source_target_pairs={{0,32},{32,64},{64,96},{96,128},{128,160},{160,192},{192,224},{224... | collective-permute-start | bytes 184328 | tf_op jit(solution)/shard_map/ppermute | solution.py:515
  50.0 5.9 %collective-permute-start.11 = (f32[12,10,128]{2,1,0:T(8,128)S(1)}, f32[12,10,128]{2,1,0:T(8,128)S(1)}, u32[]{:S(2)}, u32[]{:S(2)}) collective-permute-start(f32[12,10,128]{2,1,0:T(8,128)S(1)} %pad_maximum_fusion.1), channel_id=1, source_target_pairs={{32,0},{64,32},{96,64},{128,96},{160,128},{192,160},{224,192},{0,2... | collective-permute-start | bytes 184328 | tf_op jit(solution)/shard_map/ppermute | solution.py:516
  56.0 6.9 %collective-permute-start.13 = (f32[39,8,128]{2,1,0:T(8,128)S(1)}, f32[39,8,128]{2,1,0:T(8,128)S(1)}, u32[]{:S(2)}, u32[]{:S(2)}) collective-permute-start(f32[39,8,128]{2,1,0:T(8,128)S(1)} %get-tuple-element.76), channel_id=1, source_target_pairs={{0,32},{1,2},{2,1},{3,4},{4,3},{5,6},{6,5},{7,8},{8,7},{9,10},{10,... | collective-permute-start | bytes 479240 | tf_op jit(solution)/shard_map/ppermute | solution.py:525
  56.6 6.3 %collective-permute-start.12 = (f32[39,8,128]{2,1,0:T(8,128)S(1)}, f32[39,8,128]{2,1,0:T(8,128)S(1)}, u32[]{:S(2)}, u32[]{:S(2)}) collective-permute-start(f32[39,8,128]{2,1,0:T(8,128)S(1)} %get-tuple-element.77), channel_id=1, source_target_pairs={{0,1},{1,0},{2,3},{3,2},{4,5},{5,4},{6,7},{7,6},{8,9},{9,8},{10,11... | collective-permute-start | bytes 479240 | tf_op jit(solution)/shard_map/ppermute | solution.py:525
  56.6 2.1 %copy-start.1 = (f32[2,38,2,48,128]{4,3,2,1,0:T(8,128)S(1)}, f32[2,38,2,48,128]{4,3,2,1,0:T(8,128)}, u32[]{:S(2)}) copy-start(f32[2,38,2,48,128]{4,3,2,1,0:T(8,128)} %copy-done) | copy-start | bytes 11206660
  58.7 2.1 %copy-start.3 = (f32[2,38,2,48,128]{4,3,2,1,0:T(8,128)S(1)}, f32[2,38,2,48,128]{4,3,2,1,0:T(8,128)}, u32[]{:S(2)}) copy-start(f32[2,38,2,48,128]{4,3,2,1,0:T(8,128)} %copy-done.2) | copy-start | bytes 11206660

commit v6 on v5

--- a/solution.py
+++ b/solution.py
@@ -117,64 +117,50 @@
 PX, PY = 3, 8
 
 
-def pack_kernel(place, f, c, x_first, x_last, y_chip, y_next, planes, strips, sems):
-    n, rows = c.shape[:2]
-    edges = (0, n - PX)
-    tiles = (0, rows - 8)
-    middle = pl.ds(PX, n - 2 * PX)
+def planes_kernel(f, c, x_first, x_last, planes, sems):
+    n = c.shape[0]
     copies = []
-    for side, x in enumerate(edges):
+    for side, x in enumerate((0, n - PX)):
         at = pl.ds(x, PX)
-        copies += [(f.at[0, at], planes.at[side, 0]), (f.at[1, at], planes.at[side, 1]), (c.at[at], planes.at[side, 2])]
-    for side, row in enumerate(tiles):
-        at = pl.ds(row, 8)
-        into = [strips.at[side, k, middle] for k in range(3)]
-        copies += [(f.at[0, middle, at], into[0]), (f.at[1, middle, at], into[1]), (c.at[middle, at], into[2])]
+        copies += [(c.at[at], planes.at[side, 2]), (f.at[0, at], planes.at[side, 0]), (f.at[1, at], planes.at[side, 1])]
     copies = [pltpu.make_async_copy(src, dst, sems.at[i]) for i, (src, dst) in enumerate(copies)]
     for copy in copies:
         copy.start()
-    for copy in copies[:6]:
-        copy.wait()
     for side, out in enumerate((x_first, x_last)):
+        for copy in copies[3 * side : 3 * side + 3]:
+            copy.wait()
         for j in range(PX):
             a, b = inverse(planes[side, 2, j], 1.0, None)
             out[j], out[PX + j] = divided(planes[side, 0, j], planes[side, 1, j], a, b)
         for j in range(2):
             out[2 * PX + j] = planes[side, 2, j + side]
-        for end, row in enumerate(tiles):
-            strips[end, :, pl.ds(edges[side], PX)] = planes[side, :, :, pl.ds(row, 8), :]
-    for copy in copies[6:]:
-        copy.wait()
-    shape = (8, c.shape[2])
-    row = lax.broadcasted_iota(jnp.int32, shape, 0)
-    even = is_even(place, shape)
-
-    def strip(x, carry):
-        made = []
-        for side, shifts in ((0, (0, 3, 6)), (1, (3, 6, 0))):
-            cc = strips[side, 2, x]
-            a, b = inverse(cc, 1.0, None)
-            re, im = divided(strips[side, 0, x], strips[side, 1, x], a, b)
-            re, im, cc = [pltpu.roll(v, shift, 0) if shift else v for v, shift in zip((re, im, cc), shifts)]
-            made.append(jnp.where(row < 3, re, jnp.where(row < 6, im, cc)))
-        y_chip[x], y_next[x] = jnp.where(even, made[1], made[0]), jnp.where(even, made[0], made[1])
-        return carry
-
-    lax.fori_loop(0, n, strip, 0, unroll=4)
-
-
-def inner_kernel(f, c, u, e, r, ga, gb, fc_out, t, part):
+
+
+def first_kernel(place, f, c, u, ga, gb, y_chip, y_next):
+    n, rows, lanes = c.shape
+    cut = [pl.ds(LANES * h, LANES) for h in range(lanes // LANES)]
+    row = lax.broadcasted_iota(jnp.int32, (8, LANES), 0)
+    even = is_even(place, (8, LANES))
+
+    def step(x, carry):
+        for h, lane in enumerate(cut):
+            point(f[0, x, :, lane], f[1, x, :, lane], c[x, :, lane], 1.0, None, u, ga, gb, x + PX, h, PY)
+            made = []
+            for start, shifts in ((0, (0, 3, 6)), (rows - 8, (3, 6, 0))):
+                tiles = [u[k, x + PX, h, pl.ds(PY + start, 8), :] for k in (0, 1)] + [c[x, pl.ds(start, 8), lane]]
+                re, im, cc = [pltpu.roll(v, shift, 0) if shift else v for v, shift in zip(tiles, shifts)]
+                made.append(jnp.where(row < 3, re, jnp.where(row < 6, im, cc)))
+            y_chip[x, :, lane], y_next[x, :, lane] = jnp.where(even, made[1], made[0]), jnp.where(even, made[0], made[1])
+        return carry
+
+    lax.fori_loop(0, n, step, 0, unroll=2)
+
+
+def inner_kernel(f, c, u, ga, gb, e, r, fc_out, t, part):
     n, rows, lanes = c.shape
     halves = lanes // LANES
     at = pl.ds(PY, rows)
     cut = [pl.ds(LANES * h, LANES) for h in range(halves)]
-
-    def first(x, carry):
-        for h in range(halves):
-            point(f[0, x, :, cut[h]], f[1, x, :, cut[h]], c[x, :, cut[h]], 1.0, None, u, ga, gb, x + PX, h, PY)
-        return carry
-
-    lax.fori_loop(0, n, first, 0, unroll=2)
 
     def middle(x, carry):
         second(u, ga, gb, e, x + PX, PY, rows, 1.0, True)
@@ -529,32 +515,44 @@
     S = lambda *shape: jax.ShapeDtypeStruct(shape, f32)
     V = lambda *shape: pltpu.VMEM(shape, f32)
 
-    x_first, x_last, y_chip, y_next = pl.pallas_call(
-        pack_kernel,
-        in_specs=[SMEM] + [pl.BlockSpec(memory_space=pltpu.HBM)] * 2,
-        out_specs=[VMEM] * 4,
-        out_shape=[S(8, rows, lanes)] * 2 + [S(n, 8, lanes)] * 2,
-        scratch_shapes=[V(2, 3, PX, rows, lanes), V(2, 3, n, 8, lanes), pltpu.SemaphoreType.DMA((12,))],
-        compiler_params=params(60),
-        name="pack_faces",
-    )(place, source, wavenumber_sq)
-    xlo, xhi = planes_step(x_first, x_last)
-    y_chip, y_next = rows_step(y_chip, y_next)
     halves = lanes // LANES
     state = (n + 2 * PX, halves, rows + 2 * PY, LANES)
     part = (n // 2, rows // 2, lanes)
-    shapes = [S(2, *state)] * 3 + [S(*state)] * 2 + [S(3, n // 2, rows // 2, lanes // 2)]
+    two, one, coarser = S(2, *state), S(*state), S(3, n // 2, rows // 2, lanes // 2)
     column = V(2, halves, rows + 2 * PY, LANES)
-    held = pl.pallas_call(
+    x_first, x_last = pl.pallas_call(
+        planes_kernel,
+        in_specs=[pl.BlockSpec(memory_space=pltpu.HBM)] * 2,
+        out_specs=[VMEM] * 2,
+        out_shape=[S(8, rows, lanes)] * 2,
+        scratch_shapes=[V(2, 3, PX, rows, lanes), pltpu.SemaphoreType.DMA((6,))],
+        compiler_params=params(60),
+        name="pack_planes",
+    )(source, wavenumber_sq)
+    source, wavenumber_sq, x_first, x_last = lax.optimization_barrier((source, wavenumber_sq, x_first, x_last))
+    xlo, xhi = planes_step(x_first, x_last)
+    u, ga, gb, y_chip, y_next = pl.pallas_call(
+        first_kernel,
+        in_specs=[SMEM] + [VMEM] * 2,
+        out_specs=[VMEM] * 5,
+        out_shape=[two, one, one] + [S(n, 8, lanes)] * 2,
+        compiler_params=params(24),
+        cost_estimate=pl.CostEstimate(flops=30_000_000, bytes_accessed=8_000_000, transcendentals=0),
+        name="first_iterate",
+    )(place, source, wavenumber_sq)
+    y_chip, y_next = rows_step(y_chip, y_next)
+    e, r, fc = pl.pallas_call(
         inner_kernel,
-        in_specs=[VMEM] * 2,
-        out_specs=[VMEM] * 6,
-        out_shape=shapes,
+        in_specs=[VMEM] * 5,
+        out_specs=[VMEM] * 3,
+        out_shape=[two, two, coarser],
         scratch_shapes=[column, V(3, *part)],
         compiler_params=params(24),
-        cost_estimate=pl.CostEstimate(flops=100_000_000, bytes_accessed=16_000_000, transcendentals=0),
+        cost_estimate=pl.CostEstimate(flops=70_000_000, bytes_accessed=16_000_000, transcendentals=0),
         name="inner_cells",
-    )(source, wavenumber_sq)
+    )(source, wavenumber_sq, u, ga, gb)
+    held = (u, e, r, ga, gb, fc)
+    shapes = [two] * 3 + [one] * 2 + [coarser]
     xlo, xhi, held = lax.optimization_barrier((xlo, xhi, held))
     c_chip, c_next = rows_step(
         *pl.pallas_call(
@@ -588,19 +586,20 @@
         compiler_params=params(24),
         name="corner_cells",
     )(place, *held, c_chip, c_next)
+    fine_shape = S(2, n, rows, lanes)
+    n, rows, lanes, xsize, ysize, zsize = n // 2, rows // 2, lanes // 2, xsize // 2, ysize // 2, lanes // 2
+    h, over = 5, 1
+    xlo, xhi = planes_step(fc[:, :h], fc[:, n - h :])
     fine = pl.pallas_call(
         iterate_kernel,
         in_specs=[VMEM] * 2,
         out_specs=VMEM,
-        out_shape=S(2, n, rows, lanes),
+        out_shape=fine_shape,
         compiler_params=params(24),
         cost_estimate=pl.CostEstimate(flops=1_000_000, bytes_accessed=8_000_000, transcendentals=0),
         name="fine_iterate",
     )(u, e)
-
-    n, rows, lanes, xsize, ysize, zsize = n // 2, rows // 2, lanes // 2, xsize // 2, ysize // 2, lanes // 2
-    h, over = 5, 1
-    xlo, xhi = planes_step(fc[:, :h], fc[:, n - h :])
+    xlo, xhi, fine = lax.optimization_barrier((xlo, xhi, fine))
     chip, other = pl.pallas_call(
         rows_kernel,
         in_specs=[SMEM] + [VMEM] * 3,

time: 66.2 us -> 60.9 us (0.920)
  local copies, waits for them, and re-layouts: 7.82 us -> 0.08 us
  waiting for transfers between devices: 14.8 us -> 18.5 us
    unnamed x19 -> x9, local copies, waits for them, and re-layouts: 7.78 us -> 0.04 us
    ppermute x4, waiting for transfers between devices: 5.82 us -> 11.5 us  [rows_step(): lax.ppermute(other, ('gx', 'gy'), next_chip)]
    ppermute x3, waiting for transfers between devices: 6.87 us -> 4.89 us  [planes_step(): lax.ppermute(first, 'gx', [((i + 1) % xdev, i) for i in range(xdev)])]
    pallas_call x2 -> x3, Pallas kernels: 9.53 us -> 8.54 us  [the longest x1 5.12 us: body(): pl.pallas_call(inner_kernel, in_specs=[VMEM] * 5, out_specs=[VMEM] * 3, o...]
  transfers between devices with their start and end apart: 14 -> 14, of which waited for: 6 -> 5; matrix products, arithmetic and copies ran while one was open for 0% -> 0% of each run, Pallas kernels for 19% -> 23%
where the time goes in v6:
time: 60.9 us; the launch traced here: 60.8 us
  Pallas kernels  22.5 us (37%)
  starting transfers between devices  18.7 us (31%)
  waiting for transfers between devices  18.5 us (30%)
  between operations  0.83 us (1%)
    ppermute x4, waiting for transfers between devices, rows_step(): lax.ppermute(other, ('gx', 'gy'), next_chip)  11.5 us
    ppermute x3, starting transfers between devices, planes_step(): lax.ppermute(last, 'gx', [(i, (i + 1) % xdev) for i in range(xdev)])  9.74 us
    ppermute x4, starting transfers between devices, rows_step(): lax.ppermute(other, ('gx', 'gy'), next_chip)  8.56 us
    pallas_call x1, Pallas kernels, body(): pl.pallas_call(inner_kernel, in_specs=[VMEM] * 5, out_specs=[VMEM] * 3, o...  5.12 us
    ppermute x3, waiting for transfers between devices, planes_step(): lax.ppermute(first, 'gx', [((i + 1) % xdev, i) for i in range(xdev)])  4.89 us
    pallas_call x1, Pallas kernels, body(): pl.pallas_call(functools.partial(faces_kernel, xsize, ysize), in_specs=[S...  4.78 us
    pallas_call x1, Pallas kernels, body(): pl.pallas_call(functools.partial(coarse_kernel, n, 4, xsize, ysize, zsize...  2.66 us
    pallas_call x1, Pallas kernels, body(): pl.pallas_call(planes_kernel, in_specs=[pl.BlockSpec(memory_space=pltpu.H...  2.12 us
  transfers between devices with their start and end apart: 14, of which 5 were waited for; matrix products, arithmetic and copies ran while one was open for 0% of the time, Pallas kernels for 23%

profile of v6, /device:TPU:120, one launch (start us, length us, event | category | flops | bytes accessed | tf_op | source)
XLA Modules:
  0.0 60.8 jit_solution(2830158454317323989)
XLA Ops:
  0.7 2.1 %pack_planes.1 = (f32[8,32,256]{2,1,0:T(8,128)}, f32[8,32,256]{2,1,0:T(8,128)}) custom-call(f32[2,32,32,256]{3,2,1,0:T(8,128)} %f.3, f32[32,32,256]{2,1,0:T(8,128)} %c.3), custom_call_target="tpu_custom_call" | custom-call | tf_op jit(solution)/shard_map/pack_planes/pallas_call | solution.py:523
  2.8 3.2 %collective-permute-start = (f32[8,32,256]{2,1,0:T(8,128)}, f32[8,32,256]{2,1,0:T(8,128)}, u32[]{:S(2)}, u32[]{:S(2)}) collective-permute-start(f32[8,32,256]{2,1,0:T(8,128)} %get-tuple-element.48), channel_id=1, source_target_pairs={{0,32},{32,64},{64,96},{96,128},{128,160},{160,192},{192,224},{224... | collective-permute-start | bytes 786440 | tf_op jit(solution)/shard_map/ppermute | solution.py:501
  6.1 1.3 %first_iterate.1 = (f32[2,38,2,48,128]{4,3,2,1,0:T(8,128)S(1)}, f32[38,2,48,128]{3,2,1,0:T(8,128)S(1)}, f32[38,2,48,128]{3,2,1,0:T(8,128)S(1)}, f32[32,8,256]{2,1,0:T(8,128)S(1)}, f32[32,8,256]{2,1,0:T(8,128)S(1)}) custom-call(s32[2]{0:T(128)S(1)} %pad_add_fusion.place, f32[2,32,32,256]{3,2,1,0:T(8,128)S(1)} %copy-done, f32[32,32,256]{2,1,0:T(8,128)S(1)} %copy-done.1), custom_call_target="tpu_custom_call" | custom-call | flops 30000000 | bytes 8000000 | tf_op jit(solution)/shard_map/first_iterate/pallas_call | solution.py:534
  7.4 0.1 collective-permute-start.2
  7.5 3.0 %collective-permute-start.3 = (f32[32,8,256]{2,1,0:T(8,128)S(1)}, f32[32,8,256]{2,1,0:T(8,128)S(1)}, u32[]{:S(2)}, u32[]{:S(2)}) collective-permute-start(f32[32,8,256]{2,1,0:T(8,128)S(1)} %get-tuple-element.67), channel_id=1, source_target_pairs={{0,32},{1,2},{2,1},{3,4},{4,3},{5,6},{6,5},{7,8},{8,7},{9,10},{10,... | collective-permute-start | bytes 786440 | tf_op jit(solution)/shard_map/ppermute | solution.py:511
  10.5 5.1 %inner_cells.1 = (f32[2,38,2,48,128]{4,3,2,1,0:T(8,128)S(1)}, f32[2,38,2,48,128]{4,3,2,1,0:T(8,128)S(1)}, f32[3,16,16,128]{3,2,1,0:T(8,128)S(1)}) custom-call(f32[2,32,32,256]{3,2,1,0:T(8,128)S(1)} %copy-done, f32[32,32,256]{2,1,0:T(8,128)S(1)} %copy-done.1, f32[2,38,2,48,128]{4,3,2,1,0:T(8,128)S(1)} %get-tuple-element.58.u.u_in, ...), custom_call_target="tpu_custom_call" | custom-call | flops 70000000 | bytes 16000000 | tf_op jit(solution)/shard_map/inner_cells/pallas_call | solution.py:544
  15.7 1.1 %pack_corners.1 = (f32[16,4,256]{2,1,0:T(4,128)S(1)}, f32[16,4,256]{2,1,0:T(4,128)S(1)}) custom-call(s32[2]{0:T(128)S(1)} %pad_add_fusion.place, f32[8,32,256]{2,1,0:T(8,128)} %collective-permute-done.xlo, f32[8,32,256]{2,1,0:T(8,128)} %collective-permute-done.1.xhi), custom_call_target="tpu_custom_call" | custom-call | tf_op jit(solution)/shard_map/pack_corners/pallas_call | solution.py:558
  16.7 0.1 collective-permute-start.4
  16.8 2.7 %collective-permute-start.5 = (f32[16,4,256]{2,1,0:T(4,128)S(1)}, f32[16,4,256]{2,1,0:T(4,128)S(1)}, u32[]{:S(2)}, u32[]{:S(2)}) collective-permute-start(f32[16,4,256]{2,1,0:T(4,128)S(1)} %get-tuple-element.75), channel_id=1, source_target_pairs={{0,32},{1,2},{2,1},{3,4},{4,3},{5,6},{6,5},{7,8},{8,7},{9,10},{10,... | collective-permute-start | bytes 196616 | tf_op jit(solution)/shard_map/ppermute | solution.py:511
  19.5 4.8 %face_cells.1 = (f32[2,38,2,48,128]{4,3,2,1,0:T(8,128)S(1)}, f32[2,38,2,48,128]{4,3,2,1,0:T(8,128)S(1)}, f32[2,38,2,48,128]{4,3,2,1,0:T(8,128)S(1)}, f32[38,2,48...) custom-call(s32[2]{0:T(128)S(1)} %pad_add_fusion.place, ...), custom_call_target="tpu_custom_call", output_to_operand_aliasing={{0}: (1, {}), {1}: (2, {}), {2}: (3, {}), {3}: (4, {}), {4}... | custom-call | flops 50000000 | bytes 8000000 | tf_op jit(solution)/shard_map/face_cells/pallas_call | solution.py:568
  24.3 1.1 %corner_cells.1 = (f32[2,38,2,48,128]{4,3,2,1,0:T(8,128)S(1)}, f32[2,38,2,48,128]{4,3,2,1,0:T(8,128)S(1)}, f32[2,38,2,48,128]{4,3,2,1,0:T(8,128)S(1)}, f32[38,2,...) custom-call(s32[2]{0:T(128)S(1)} %pad_add_fusion.place, ...), custom_call_target="tpu_custom_call", output_to_operand_aliasing={{0}: (1, {}), {1}: (2, {}), {2}: (3, {}), {3}: (4, {}), {4}... | custom-call | tf_op jit(solution)/shard_map/corner_cells/pallas_call | solution.py:579
  25.6 3.2 %collective-permute-start.6 = (f32[3,5,16,128]{3,2,1,0:T(8,128)S(1)}, f32[3,5,16,128]{3,2,1,0:T(8,128)S(1)}, u32[]{:S(2)}, u32[]{:S(2)}) collective-permute-start(f32[3,5,16,128]{3,2,1,0:T(8,128)S(1)} %get-tuple-element.89), channel_id=1, source_target_pairs={{0,32},{32,64},{64,96},{96,128},{128,160},{160,192},{192,224},{224... | collective-permute-start | bytes 368648 | tf_op jit(solution)/shard_map/ppermute | solution.py:501
  28.8 1.6 %fine_iterate.1 = f32[2,32,32,256]{3,2,1,0:T(8,128)} custom-call(f32[2,38,2,48,128]{4,3,2,1,0:T(8,128)S(1)} %get-tuple-element.77.u, f32[2,38,2,48,128]{4,3,2,1,0:T(8,128)S(1)} %get-tuple-element.78.e), custom_call_target="tpu_custom_call" | custom-call | flops 1000000 | bytes 8000000 | tf_op jit(solution)/shard_map/fine_iterate/pallas_call | solution.py:593
  30.4 1.2 %collective-permute-done.7.xhi = f32[3,5,16,128]{3,2,1,0:T(8,128)S(1)} collective-permute-done((f32[3,5,16,128]{3,2,1,0:T(8,128)S(1)}, f32[3,5,16,128]{3,2,1,0:T(8,128)S(1)}, u32[]{:S(2)}, u32[]{:S(2)}) %collective-permute-start.7) | collective-permute-done | bytes 122912 | tf_op jit(solution)/shard_map/ppermute | solution.py:502
  31.6 0.6 second_rows.1
  32.3 2.1 %collective-permute-start.9 = (f32[2,26,8,128]{3,2,1,0:T(8,128)S(1)}, f32[2,26,8,128]{3,2,1,0:T(8,128)S(1)}, u32[]{:S(2)}, u32[]{:S(2)}) collective-permute-start(f32[2,26,8,128]{3,2,1,0:T(8,128)S(1)} %get-tuple-element.83), channel_id=1, source_target_pairs={{0,32},{1,2},{2,1},{3,4},{4,3},{5,6},{6,5},{7,8},{8,7},{9,10},{10,... | collective-permute-start | bytes 638984 | tf_op jit(solution)/shard_map/ppermute | solution.py:511
  34.4 5.4 %collective-permute-done.9.y_next = f32[2,26,8,128]{3,2,1,0:T(8,128)S(1)} collective-permute-done((f32[2,26,8,128]{3,2,1,0:T(8,128)S(1)}, f32[2,26,8,128]{3,2,1,0:T(8,128)S(1)}, u32[]{:S(2)}, u32[]{:S(2)}) %collective-permute-start.9) | collective-permute-done | bytes 213024 | tf_op jit(solution)/shard_map/ppermute | solution.py:511
  39.8 2.1 %second_level.1 = (f32[2,16,16,128]{3,2,1,0:T(8,128)}, f32[15,10,128]{2,1,0:T(8,128)S(1)}) custom-call(s32[2]{0:T(128)S(1)} %pad_add_fusion.place, f32[3,16,16,128]{3,2,1,0:T(8,128)S(1)} %get-tuple-element.76.fc.fc_own, f32[3,5,16,128]{3,2,1,0:T(8,128)S(1)} %collective-permute-done.6.xlo, f32[3,5,16,128]{3,2,1,0:T(8,128)S(1)} %collective-permute-done.7.xhi, ...), custom_call_target="tpu_custom_call" | custom-call | tf_op jit(solution)/shard_map/second_level/pallas_call | solution.py:615
  41.9 3.3 %collective-permute-start.10 = (f32[12,10,128]{2,1,0:T(8,128)S(1)}, f32[12,10,128]{2,1,0:T(8,128)S(1)}, u32[]{:S(2)}, u32[]{:S(2)}) collective-permute-start(f32[12,10,128]{2,1,0:T(8,128)S(1)} %pad_maximum_fusion), channel_id=1, source_target_pairs={{0,32},{32,64},{64,96},{96,128},{128,160},{160,192},{192,224},{224... | collective-permute-start | bytes 184328 | tf_op jit(solution)/shard_map/ppermute | solution.py:501
  45.3 2.1 %collective-permute-done.10.xlo = f32[12,10,128]{2,1,0:T(8,128)S(1)} collective-permute-done((f32[12,10,128]{2,1,0:T(8,128)S(1)}, f32[12,10,128]{2,1,0:T(8,128)S(1)}, u32[]{:S(2)}, u32[]{:S(2)}) %collective-permute-start.10) | collective-permute-done | bytes 61472 | tf_op jit(solution)/shard_map/ppermute | solution.py:501
  47.5 3.7 %collective-permute-done.11.xhi = f32[12,10,128]{2,1,0:T(8,128)S(1)} collective-permute-done((f32[12,10,128]{2,1,0:T(8,128)S(1)}, f32[12,10,128]{2,1,0:T(8,128)S(1)}, u32[]{:S(2)}, u32[]{:S(2)}) %collective-permute-start.11) | collective-permute-done | bytes 61472 | tf_op jit(solution)/shard_map/ppermute | solution.py:502
  51.2 0.8 %collective-permute-start.13 = (f32[39,8,128]{2,1,0:T(8,128)S(1)}, f32[39,8,128]{2,1,0:T(8,128)S(1)}, u32[]{:S(2)}, u32[]{:S(2)}) collective-permute-start(f32[39,8,128]{2,1,0:T(8,128)S(1)} %get-tuple-element.90), channel_id=1, source_target_pairs={{0,32},{1,2},{2,1},{3,4},{4,3},{5,6},{6,5},{7,8},{8,7},{9,10},{10,... | collective-permute-start | bytes 479240 | tf_op jit(solution)/shard_map/ppermute | solution.py:511
  52.0 6.1 %collective-permute-done.13.y_next = f32[39,8,128]{2,1,0:T(8,128)S(1)} collective-permute-done((f32[39,8,128]{2,1,0:T(8,128)S(1)}, f32[39,8,128]{2,1,0:T(8,128)S(1)}, u32[]{:S(2)}, u32[]{:S(2)}) %collective-permute-start.13) | collective-permute-done | bytes 159776 | tf_op jit(solution)/shard_map/ppermute | solution.py:511
  58.1 2.7 %coarse_levels.1 = (f32[2,8,8,64]{3,2,1,0:T(8,128)}, f32[2,4,4,32]{3,2,1,0:T(4,128)}) custom-call(s32[2]{0:T(128)S(1)} %pad_add_fusion.place, f32[15,10,128]{2,1,0:T(8,128)S(1)} %get-tuple-element.85.fc_own, f32[12,10,128]{2,1,0:T(8,128)S(1)} %collective-permute-done.10.xlo, f32[12,10,128]{2,1,0:T(8,128)S(1)} %collective-permute-done.11.xhi, ...), custom_call_target="tpu_custom_call" | custom-call | tf_op jit(solution)/shard_map/coarse_levels/pallas_call | solution.py:640
  (31 shorter events, 0.5 us)
Async XLA Ops:
  0.6 5.4 %copy-start.1 = (f32[32,32,256]{2,1,0:T(8,128)S(1)}, f32[32,32,256]{2,1,0:T(8,128)}, u32[]{:S(2)}) copy-start(f32[32,32,256]{2,1,0:T(8,128)} %c.3) | copy-start | bytes 3145732
  0.6 5.4 %copy-start = (f32[2,32,32,256]{3,2,1,0:T(8,128)S(1)}, f32[2,32,32,256]{3,2,1,0:T(8,128)}, u32[]{:S(2)}) copy-start(f32[2,32,32,256]{3,2,1,0:T(8,128)} %f.3) | copy-start | bytes 6291460
  2.8 12.9 %collective-permute-start = (f32[8,32,256]{2,1,0:T(8,128)}, f32[8,32,256]{2,1,0:T(8,128)}, u32[]{:S(2)}, u32[]{:S(2)}) collective-permute-start(f32[8,32,256]{2,1,0:T(8,128)} %get-tuple-element.48), channel_id=1, source_target_pairs={{0,32},{32,64},{64,96},{96,128},{128,160},{160,192},{192,224},{224... | collective-permute-start | bytes 786440 | tf_op jit(solution)/shard_map/ppermute | solution.py:501
  6.0 9.7 %collective-permute-start.1 = (f32[8,32,256]{2,1,0:T(8,128)}, f32[8,32,256]{2,1,0:T(8,128)}, u32[]{:S(2)}, u32[]{:S(2)}) collective-permute-start(f32[8,32,256]{2,1,0:T(8,128)} %get-tuple-element.49), channel_id=1, source_target_pairs={{32,0},{64,32},{96,64},{128,96},{160,128},{192,160},{224,192},{0,2... | collective-permute-start | bytes 786440 | tf_op jit(solution)/shard_map/ppermute | solution.py:502
  7.4 12.1 %collective-permute-start.2 = (f32[32,8,256]{2,1,0:T(8,128)S(1)}, f32[32,8,256]{2,1,0:T(8,128)S(1)}, u32[]{:S(2)}, u32[]{:S(2)}) collective-permute-start(f32[32,8,256]{2,1,0:T(8,128)S(1)} %get-tuple-element.66), channel_id=1, source_target_pairs={{0,1},{1,0},{2,3},{3,2},{4,5},{5,4},{6,7},{7,6},{8,9},{9,8},{10,11... | collective-permute-start | bytes 786440 | tf_op jit(solution)/shard_map/ppermute | solution.py:511
  7.5 12.0 %collective-permute-start.3 = (f32[32,8,256]{2,1,0:T(8,128)S(1)}, f32[32,8,256]{2,1,0:T(8,128)S(1)}, u32[]{:S(2)}, u32[]{:S(2)}) collective-permute-start(f32[32,8,256]{2,1,0:T(8,128)S(1)} %get-tuple-element.67), channel_id=1, source_target_pairs={{0,32},{1,2},{2,1},{3,4},{4,3},{5,6},{6,5},{7,8},{8,7},{9,10},{10,... | collective-permute-start | bytes 786440 | tf_op jit(solution)/shard_map/ppermute | solution.py:511
  16.7 7.6 %collective-permute-start.4 = (f32[16,4,256]{2,1,0:T(4,128)S(1)}, f32[16,4,256]{2,1,0:T(4,128)S(1)}, u32[]{:S(2)}, u32[]{:S(2)}) collective-permute-start(f32[16,4,256]{2,1,0:T(4,128)S(1)} %get-tuple-element.74), channel_id=1, source_target_pairs={{0,1},{1,0},{2,3},{3,2},{4,5},{5,4},{6,7},{7,6},{8,9},{9,8},{10,11... | collective-permute-start | bytes 196616 | tf_op jit(solution)/shard_map/ppermute | solution.py:511
  16.8 7.5 %collective-permute-start.5 = (f32[16,4,256]{2,1,0:T(4,128)S(1)}, f32[16,4,256]{2,1,0:T(4,128)S(1)}, u32[]{:S(2)}, u32[]{:S(2)}) collective-permute-start(f32[16,4,256]{2,1,0:T(4,128)S(1)} %get-tuple-element.75), channel_id=1, source_target_pairs={{0,32},{1,2},{2,1},{3,4},{4,3},{5,6},{6,5},{7,8},{8,7},{9,10},{10,... | collective-permute-start | bytes 196616 | tf_op jit(solution)/shard_map/ppermute | solution.py:511
  25.5 6.2 %collective-permute-start.7 = (f32[3,5,16,128]{3,2,1,0:T(8,128)S(1)}, f32[3,5,16,128]{3,2,1,0:T(8,128)S(1)}, u32[]{:S(2)}, u32[]{:S(2)}) collective-permute-start(f32[3,5,16,128]{3,2,1,0:T(8,128)S(1)} %get-tuple-element.88), channel_id=1, source_target_pairs={{32,0},{64,32},{96,64},{128,96},{160,128},{192,160},{224,192},{0,2... | collective-permute-start | bytes 368648 | tf_op jit(solution)/shard_map/ppermute | solution.py:502
  25.6 6.1 %collective-permute-start.6 = (f32[3,5,16,128]{3,2,1,0:T(8,128)S(1)}, f32[3,5,16,128]{3,2,1,0:T(8,128)S(1)}, u32[]{:S(2)}, u32[]{:S(2)}) collective-permute-start(f32[3,5,16,128]{3,2,1,0:T(8,128)S(1)} %get-tuple-element.89), channel_id=1, source_target_pairs={{0,32},{32,64},{64,96},{96,128},{128,160},{160,192},{192,224},{224... | collective-permute-start | bytes 368648 | tf_op jit(solution)/shard_map/ppermute | solution.py:501
  32.2 2.2 %collective-permute-start.8 = (f32[2,26,8,128]{3,2,1,0:T(8,128)S(1)}, f32[2,26,8,128]{3,2,1,0:T(8,128)S(1)}, u32[]{:S(2)}, u32[]{:S(2)}) collective-permute-start(f32[2,26,8,128]{3,2,1,0:T(8,128)S(1)} %get-tuple-element.82), channel_id=1, source_target_pairs={{0,1},{1,0},{2,3},{3,2},{4,5},{5,4},{6,7},{7,6},{8,9},{9,8},{10,11... | collective-permute-start | bytes 638984 | tf_op jit(solution)/shard_map/ppermute | solution.py:511
  32.3 7.5 %collective-permute-start.9 = (f32[2,26,8,128]{3,2,1,0:T(8,128)S(1)}, f32[2,26,8,128]{3,2,1,0:T(8,128)S(1)}, u32[]{:S(2)}, u32[]{:S(2)}) collective-permute-start(f32[2,26,8,128]{3,2,1,0:T(8,128)S(1)} %get-tuple-element.83), channel_id=1, source_target_pairs={{0,32},{1,2},{2,1},{3,4},{4,3},{5,6},{6,5},{7,8},{8,7},{9,10},{10,... | collective-permute-start | bytes 638984 | tf_op jit(solution)/shard_map/ppermute | solution.py:511
  41.9 5.5 %collective-permute-start.10 = (f32[12,10,128]{2,1,0:T(8,128)S(1)}, f32[12,10,128]{2,1,0:T(8,128)S(1)}, u32[]{:S(2)}, u32[]{:S(2)}) collective-permute-start(f32[12,10,128]{2,1,0:T(8,128)S(1)} %pad_maximum_fusion), channel_id=1, source_target_pairs={{0,32},{32,64},{64,96},{96,128},{128,160},{160,192},{192,224},{224... | collective-permute-start | bytes 184328 | tf_op jit(solution)/shard_map/ppermute | solution.py:501
  45.3 5.9 %collective-permute-start.11 = (f32[12,10,128]{2,1,0:T(8,128)S(1)}, f32[12,10,128]{2,1,0:T(8,128)S(1)}, u32[]{:S(2)}, u32[]{:S(2)}) collective-permute-start(f32[12,10,128]{2,1,0:T(8,128)S(1)} %pad_maximum_fusion.1), channel_id=1, source_target_pairs={{32,0},{64,32},{96,64},{128,96},{160,128},{192,160},{224,192},{0,2... | collective-permute-start | bytes 184328 | tf_op jit(solution)/shard_map/ppermute | solution.py:502
  51.2 6.9 %collective-permute-start.13 = (f32[39,8,128]{2,1,0:T(8,128)S(1)}, f32[39,8,128]{2,1,0:T(8,128)S(1)}, u32[]{:S(2)}, u32[]{:S(2)}) collective-permute-start(f32[39,8,128]{2,1,0:T(8,128)S(1)} %get-tuple-element.90), channel_id=1, source_target_pairs={{0,32},{1,2},{2,1},{3,4},{4,3},{5,6},{6,5},{7,8},{8,7},{9,10},{10,... | collective-permute-start | bytes 479240 | tf_op jit(solution)/shard_map/ppermute | solution.py:511
  52.0 6.1 %collective-permute-start.12 = (f32[39,8,128]{2,1,0:T(8,128)S(1)}, f32[39,8,128]{2,1,0:T(8,128)S(1)}, u32[]{:S(2)}, u32[]{:S(2)}) collective-permute-start(f32[39,8,128]{2,1,0:T(8,128)S(1)} %get-tuple-element.91), channel_id=1, source_target_pairs={{0,1},{1,0},{2,3},{3,2},{4,5},{5,4},{6,7},{7,6},{8,9},{9,8},{10,11... | collective-permute-start | bytes 479240 | tf_op jit(solution)/shard_map/ppermute | solution.py:511

commit v7 on v6

--- a/solution.py
+++ b/solution.py
@@ -11,6 +11,7 @@
 LANES = 128
 VMEM = pl.BlockSpec(memory_space=pltpu.VMEM)
 SMEM = pl.BlockSpec(memory_space=pltpu.SMEM)
+ANY = pl.BlockSpec(memory_space=pl.ANY)
 
 
 def params(mib):
@@ -153,7 +154,7 @@
             y_chip[x, :, lane], y_next[x, :, lane] = jnp.where(even, made[1], made[0]), jnp.where(even, made[0], made[1])
         return carry
 
-    lax.fori_loop(0, n, step, 0, unroll=2)
+    lax.fori_loop(0, n, step, 0, unroll=True)
 
 
 def inner_kernel(f, c, u, ga, gb, e, r, fc_out, t, part):
@@ -166,7 +167,7 @@
         second(u, ga, gb, e, x + PX, PY, rows, 1.0, True)
         return carry
 
-    lax.fori_loop(1, n - 1, middle, 0, unroll=2)
+    lax.fori_loop(1, n - 1, middle, 0, unroll=True)
     row = lax.broadcasted_iota(jnp.int32, (rows, LANES), 0)
     full = (row >= 2) & (row < rows - 2)
 
@@ -177,7 +178,7 @@
                 r[k, x + PX, h, at, :] = 0.04 * f[k, x, :, cut[h]] + jnp.where(full, s[h], 0.0)
         return carry
 
-    lax.fori_loop(2, n - 2, last, 0, unroll=2)
+    lax.fori_loop(2, n - 2, last, 0, unroll=True)
     for x in (0, 1, n - 2, n - 1):
         for k in (0, 1):
             for h in range(halves):
@@ -188,14 +189,14 @@
             add_pairs(c[2 * i, :, cut[h]], c[2 * i + 1, :, cut[h]], t, h, part.at[2], i, 0, rows // 2)
         return carry
 
-    lax.fori_loop(0, n // 2, pairs, 0, unroll=2)
+    lax.fori_loop(0, n // 2, pairs, 0, unroll=True)
 
     def coarse(i, carry):
         for k in (0, 1):
             restrict_xy(r, t, part, i, 2 * i + PX - 1, PY - 1, rows // 2, k, (PY, rows))
         return carry
 
-    lax.fori_loop(2, n // 2 - 2, coarse, 0, unroll=2)
+    lax.fori_loop(2, n // 2 - 2, coarse, 0, unroll=True)
     w = weights(lanes, lanes)
     for k in (0, 1):
         fc_out[k, 2 : n // 2 - 2] = exact_dot(part[k, 2 : n // 2 - 2], w)
@@ -240,18 +241,15 @@
     return side[i, :, cut], side[PX + i, :, cut], cc, c_here, i == (PX - 1 if low else 0)
 
 
-def faces_kernel(xsize, ysize, place, u_in, e_in, r_in, ga_in, gb_in, fc_in, xlo, xhi, y_chip, y_next, u, e, r, ga, gb, fc_out, part, q):
+def faces_kernel(xsize, ysize, place, u_in, e_in, r_in, ga_in, gb_in, fc_in, xlo, xhi, y_chip, y_next, u, e, r, ga, gb, fc_out, part, q, sides, sems):
     n, (rows, lanes) = y_chip.shape[0], xlo.shape[1:]
     halves = lanes // LANES
     cut = [pl.ds(LANES * h, LANES) for h in range(halves)]
     ok = inside(place, n, rows, xsize, ysize)
     del u_in, e_in, r_in, ga_in, gb_in, fc_in
-    for side, low, base in ((xlo, True, 0), (xhi, False, n + PX)):
-        for i in range(PX):
-            good = ok(base + i, PY, rows)
-            for h in range(halves):
-                re, im, cc, c_here, r_here = plane_cells(side, low, i, h)
-                halo(re, im, cc, good, u, ga, gb, r, base + i, h, PY, c_here, r_here)
+    copies = [pltpu.make_async_copy(src, sides.at[i], sems.at[i]) for i, src in enumerate((xlo, xhi))]
+    for copy in copies:
+        copy.start()
     low, high = PY - 4, PY + rows - 4
     good_lo, good_hi = ok(PX, 0, 8), ok(PX, PY + rows, 8)
     even = is_even(place, (8, LANES))
@@ -265,7 +263,15 @@
                 halo(re, im, cc, good, u, ga, gb, r, x + PX, h, row, True, True)
         return carry
 
-    lax.fori_loop(0, n, strips, 0, unroll=4)
+    lax.fori_loop(0, n, strips, 0, unroll=True)
+    for copy in copies:
+        copy.wait()
+    for side, is_low, base in ((sides.at[0], True, 0), (sides.at[1], False, n + PX)):
+        for i in range(PX):
+            good = ok(base + i, PY, rows)
+            for h in range(halves):
+                re, im, cc, c_here, r_here = plane_cells(side, is_low, i, h)
+                halo(re, im, cc, good, u, ga, gb, r, base + i, h, PY, c_here, r_here)
     for x in (PX - 2, PX - 1, PX, n + PX - 1, n + PX, n + PX + 1):
         second(u, ga, gb, e, x, PY, rows, 1.0, True)
 
@@ -274,7 +280,7 @@
             second(u, ga, gb, e, x, row, 8, 1.0, True)
         return carry
 
-    lax.fori_loop(PX + 1, n + PX - 1, middle, 0, unroll=3)
+    lax.fori_loop(PX + 1, n + PX - 1, middle, 0, unroll=True)
     for x in (PX - 1, PX, PX + 1, n + PX - 2, n + PX - 1, n + PX):
         finish(e, r, x, PY + 4, rows - 8, ok(x, PY + 4, rows - 8))
     row = lax.broadcasted_iota(jnp.int32, (8, LANES), 0)
@@ -285,7 +291,7 @@
         finish(e, r, x, high, 8, good_high)
         return carry
 
-    lax.fori_loop(PX + 2, n + PX - 2, last, 0, unroll=4)
+    lax.fori_loop(PX + 2, n + PX - 2, last, 0, unroll=True)
     m = n // 2 - 4
 
     def coarse(i, carry):
@@ -299,7 +305,7 @@
                     )
         return carry
 
-    lax.fori_loop(0, m, coarse, 0, unroll=4)
+    lax.fori_loop(0, m, coarse, 0, unroll=True)
     w = weights(lanes, lanes)
     for k in (0, 1):
         q[k] = exact_dot(part[k], w)
@@ -308,13 +314,20 @@
             fc_out[k, pl.ds(2, m), pl.ds(row, 2), :] = (four[0] + four[3]) + 3.0 * (four[1] + four[2])
 
 
-def pack_corners_kernel(place, xlo, xhi, chip, other):
+def pack_corners_kernel(place, xlo, xhi, chip, other, tiles, sems):
     rows = xlo.shape[1]
+    copies = []
+    for i, side in enumerate((xlo, xhi)):
+        for j, row in enumerate((0, rows - 8)):
+            copies.append(pltpu.make_async_copy(side.at[:, pl.ds(row, 8)], tiles.at[j, pl.ds(8 * i, 8)], sems.at[2 * i + j]))
+    for copy in copies:
+        copy.start()
     even = is_even(place, (4, xlo.shape[2]))
-    for side, base in ((xlo, 0), (xhi, 8)):
-        for j in range(8):
-            first, last = side[j, pl.ds(0, 4), :], side[j, pl.ds(rows - 4, 4), :]
-            chip[base + j], other[base + j] = jnp.where(even, last, first), jnp.where(even, first, last)
+    for copy in copies:
+        copy.wait()
+    for j in range(16):
+        first, last = tiles[0, j, pl.ds(0, 4), :], tiles[1, j, pl.ds(4, 4), :]
+        chip[j], other[j] = jnp.where(even, last, first), jnp.where(even, first, last)
 
 
 def corners_kernel(xsize, ysize, n, rows, place, u_in, e_in, r_in, ga_in, gb_in, fc_in, c_chip, c_next, u, e, r, ga, gb, fc_out, t, part):
@@ -526,9 +539,9 @@
         out_specs=[VMEM] * 2,
         out_shape=[S(8, rows, lanes)] * 2,
         scratch_shapes=[V(2, 3, PX, rows, lanes), pltpu.SemaphoreType.DMA((6,))],
-        compiler_params=params(60),
+        compiler_params=params(24),
         name="pack_planes",
-    )(source, wavenumber_sq)
+    )(*[pltpu.with_memory_space_constraint(x, pltpu.HBM) for x in (source, wavenumber_sq)])
     source, wavenumber_sq, x_first, x_last = lax.optimization_barrier((source, wavenumber_sq, x_first, x_last))
     xlo, xhi = planes_step(x_first, x_last)
     u, ga, gb, y_chip, y_next = pl.pallas_call(
@@ -557,9 +570,10 @@
     c_chip, c_next = rows_step(
         *pl.pallas_call(
             pack_corners_kernel,
-            in_specs=[SMEM] + [VMEM] * 2,
+            in_specs=[SMEM] + [ANY] * 2,
             out_specs=[VMEM] * 2,
             out_shape=[S(16, 4, lanes)] * 2,
+            scratch_shapes=[V(2, 16, 8, lanes), pltpu.SemaphoreType.DMA((4,))],
             compiler_params=params(24),
             name="pack_corners",
         )(place, xlo, xhi)
@@ -567,11 +581,11 @@
     in_place = {i + 1: i for i in range(6)}
     held = pl.pallas_call(
         functools.partial(faces_kernel, xsize, ysize),
-        in_specs=[SMEM] + [VMEM] * 10,
+        in_specs=[SMEM] + [VMEM] * 6 + [ANY] * 2 + [VMEM] * 2,
         out_specs=[VMEM] * 6,
         out_shape=shapes,
         input_output_aliases=in_place,
-        scratch_shapes=[V(2, n // 2 - 4, 16, lanes), V(2, n // 2 - 4, 16, lanes // 2)],
+        scratch_shapes=[V(2, n // 2 - 4, 16, lanes), V(2, n // 2 - 4, 16, lanes // 2), V(2, 8, rows, lanes), pltpu.SemaphoreType.DMA((2,))],
         compiler_params=params(24),
         cost_estimate=pl.CostEstimate(flops=50_000_000, bytes_accessed=8_000_000, transcendentals=0),
         name="face_cells",

time: 60.9 us -> 60.2 us (0.989)
  Pallas kernels: 22.5 us -> 19 us
  waiting for transfers between devices: 18.5 us -> 21.6 us
    pallas_call x1, Pallas kernels: 5.12 us -> 2.68 us  [body(): pl.pallas_call(inner_kernel, in_specs=[VMEM] * 5, out_specs=[VMEM] * 3, o...]
    ppermute x3, waiting for transfers between devices: 4.89 us -> 7.08 us  [planes_step(): lax.ppermute(first, 'gx', [((i + 1) % xdev, i) for i in range(xdev)])]
    pallas_call x1, Pallas kernels: 4.78 us -> 3.39 us  [body(): pl.pallas_call(functools.partial(faces_kernel, xsize, ysize), in_specs=[S...]
    ppermute x4, waiting for transfers between devices: 11.5 us -> 12.4 us  [rows_step(): lax.ppermute(other, ('gx', 'gy'), next_chip)]
  transfers between devices with their start and end apart: 14 -> 14, of which waited for: 5 -> 6; matrix products, arithmetic and copies ran while one was open for 0% -> 0% of each run, Pallas kernels for 23% -> 17%
where the time goes in v7:
time: 60.2 us; the launch traced here: 60 us
  waiting for transfers between devices  21.6 us (36%)
  Pallas kernels  19 us (32%)
  starting transfers between devices  18.4 us (31%)
  between operations  0.83 us (1%)
    ppermute x4, waiting for transfers between devices, rows_step(): lax.ppermute(other, ('gx', 'gy'), next_chip)  12.4 us
    ppermute x3, starting transfers between devices, planes_step(): lax.ppermute(last, 'gx', [(i, (i + 1) % xdev) for i in range(xdev)])  9.74 us
    ppermute x4, starting transfers between devices, rows_step(): lax.ppermute(other, ('gx', 'gy'), next_chip)  8.06 us
    ppermute x3, waiting for transfers between devices, planes_step(): lax.ppermute(first, 'gx', [((i + 1) % xdev, i) for i in range(xdev)])  7.08 us
    pallas_call x1, Pallas kernels, body(): pl.pallas_call(functools.partial(faces_kernel, xsize, ysize), in_specs=[S...  3.39 us
    pallas_call x1, Pallas kernels, body(): pl.pallas_call(inner_kernel, in_specs=[VMEM] * 5, out_specs=[VMEM] * 3, o...  2.68 us
    pallas_call x1, Pallas kernels, body(): pl.pallas_call(functools.partial(coarse_kernel, n, 4, xsize, ysize, zsize...  2.66 us
    pallas_call x1, Pallas kernels, body(): pl.pallas_call(planes_kernel, in_specs=[pl.BlockSpec(memory_space=pltpu.H...  2.12 us
  transfers between devices with their start and end apart: 14, of which 6 were waited for; matrix products, arithmetic and copies ran while one was open for 0% of the time, Pallas kernels for 17%

profile of v7, /device:TPU:120, one launch (start us, length us, event | category | flops | bytes accessed | tf_op | source)
XLA Modules:
  0.0 60.0 jit_solution(15775296704501444102)
XLA Ops:
  0.7 2.1 %pack_planes.1 = (f32[8,32,256]{2,1,0:T(8,128)}, f32[8,32,256]{2,1,0:T(8,128)}) custom-call(f32[2,32,32,256]{3,2,1,0:T(8,128)} %f.3, f32[32,32,256]{2,1,0:T(8,128)} %c.3), custom_call_target="tpu_custom_call" | custom-call | tf_op jit(solution)/shard_map/pack_planes/pallas_call | solution.py:536
  2.8 3.2 %collective-permute-start = (f32[8,32,256]{2,1,0:T(8,128)}, f32[8,32,256]{2,1,0:T(8,128)}, u32[]{:S(2)}, u32[]{:S(2)}) collective-permute-start(f32[8,32,256]{2,1,0:T(8,128)} %get-tuple-element.48), channel_id=1, source_target_pairs={{0,32},{32,64},{64,96},{96,128},{128,160},{160,192},{192,224},{224... | collective-permute-start | bytes 786440 | tf_op jit(solution)/shard_map/ppermute | solution.py:514
  6.1 1.2 %first_iterate.1 = (f32[2,38,2,48,128]{4,3,2,1,0:T(8,128)S(1)}, f32[38,2,48,128]{3,2,1,0:T(8,128)S(1)}, f32[38,2,48,128]{3,2,1,0:T(8,128)S(1)}, f32[32,8,256]{2,1,0:T(8,128)S(1)}, f32[32,8,256]{2,1,0:T(8,128)S(1)}) custom-call(s32[2]{0:T(128)S(1)} %pad_add_fusion.place, f32[2,32,32,256]{3,2,1,0:T(8,128)S(1)} %copy-done, f32[32,32,256]{2,1,0:T(8,128)S(1)} %copy-done.1), custom_call_target="tpu_custom_call" | custom-call | flops 30000000 | bytes 8000000 | tf_op jit(solution)/shard_map/first_iterate/pallas_call | solution.py:547
  7.3 3.0 %collective-permute-start.3 = (f32[32,8,256]{2,1,0:T(8,128)S(1)}, f32[32,8,256]{2,1,0:T(8,128)S(1)}, u32[]{:S(2)}, u32[]{:S(2)}) collective-permute-start(f32[32,8,256]{2,1,0:T(8,128)S(1)} %get-tuple-element.67), channel_id=1, source_target_pairs={{0,32},{1,2},{2,1},{3,4},{4,3},{5,6},{6,5},{7,8},{8,7},{9,10},{10,... | collective-permute-start | bytes 786440 | tf_op jit(solution)/shard_map/ppermute | solution.py:524
  10.4 2.7 %inner_cells.1 = (f32[2,38,2,48,128]{4,3,2,1,0:T(8,128)S(1)}, f32[2,38,2,48,128]{4,3,2,1,0:T(8,128)S(1)}, f32[3,16,16,128]{3,2,1,0:T(8,128)S(1)}) custom-call(f32[2,32,32,256]{3,2,1,0:T(8,128)S(1)} %copy-done, f32[32,32,256]{2,1,0:T(8,128)S(1)} %copy-done.1, f32[2,38,2,48,128]{4,3,2,1,0:T(8,128)S(1)} %get-tuple-element.58.u.u_in, ...), custom_call_target="tpu_custom_call" | custom-call | flops 70000000 | bytes 16000000 | tf_op jit(solution)/shard_map/inner_cells/pallas_call | solution.py:557
  13.1 2.2 %collective-permute-done.1.xhi = f32[8,32,256]{2,1,0:T(8,128)} collective-permute-done((f32[8,32,256]{2,1,0:T(8,128)}, f32[8,32,256]{2,1,0:T(8,128)}, u32[]{:S(2)}, u32[]{:S(2)}) %collective-permute-start.1) | collective-permute-done | bytes 262176 | tf_op jit(solution)/shard_map/ppermute | solution.py:515
  15.3 1.5 %pack_corners.1 = (f32[16,4,256]{2,1,0:T(4,128)S(1)}, f32[16,4,256]{2,1,0:T(4,128)S(1)}) custom-call(s32[2]{0:T(128)S(1)} %pad_add_fusion.place, f32[8,32,256]{2,1,0:T(8,128)} %collective-permute-done.xlo, f32[8,32,256]{2,1,0:T(8,128)} %collective-permute-done.1.xhi), custom_call_target="tpu_custom_call" | custom-call | tf_op jit(solution)/shard_map/pack_corners/pallas_call | solution.py:571
  16.9 3.0 %collective-permute-start.5 = (f32[16,4,256]{2,1,0:T(4,128)S(1)}, f32[16,4,256]{2,1,0:T(4,128)S(1)}, u32[]{:S(2)}, u32[]{:S(2)}) collective-permute-start(f32[16,4,256]{2,1,0:T(4,128)S(1)} %get-tuple-element.75), channel_id=1, source_target_pairs={{0,32},{1,2},{2,1},{3,4},{4,3},{5,6},{6,5},{7,8},{8,7},{9,10},{10,... | collective-permute-start | bytes 196616 | tf_op jit(solution)/shard_map/ppermute | solution.py:524
  20.0 3.4 %face_cells.1 = (f32[2,38,2,48,128]{4,3,2,1,0:T(8,128)S(1)}, f32[2,38,2,48,128]{4,3,2,1,0:T(8,128)S(1)}, f32[2,38,2,48,128]{4,3,2,1,0:T(8,128)S(1)}, f32[38,2,48...) custom-call(s32[2]{0:T(128)S(1)} %pad_add_fusion.place, ...), custom_call_target="tpu_custom_call", output_to_operand_aliasing={{0}: (1, {}), {1}: (2, {}), {2}: (3, {}), {3}: (4, {}), {4}... | custom-call | flops 50000000 | bytes 8000000 | tf_op jit(solution)/shard_map/face_cells/pallas_call | solution.py:582
  23.4 1.1 %corner_cells.1 = (f32[2,38,2,48,128]{4,3,2,1,0:T(8,128)S(1)}, f32[2,38,2,48,128]{4,3,2,1,0:T(8,128)S(1)}, f32[2,38,2,48,128]{4,3,2,1,0:T(8,128)S(1)}, f32[38,2,...) custom-call(s32[2]{0:T(128)S(1)} %pad_add_fusion.place, ...), custom_call_target="tpu_custom_call", output_to_operand_aliasing={{0}: (1, {}), {1}: (2, {}), {2}: (3, {}), {3}: (4, {}), {4}... | custom-call | tf_op jit(solution)/shard_map/corner_cells/pallas_call | solution.py:593
  24.6 3.2 %collective-permute-start.6 = (f32[3,5,16,128]{3,2,1,0:T(8,128)S(1)}, f32[3,5,16,128]{3,2,1,0:T(8,128)S(1)}, u32[]{:S(2)}, u32[]{:S(2)}) collective-permute-start(f32[3,5,16,128]{3,2,1,0:T(8,128)S(1)} %get-tuple-element.89), channel_id=1, source_target_pairs={{0,32},{32,64},{64,96},{96,128},{128,160},{160,192},{192,224},{224... | collective-permute-start | bytes 368648 | tf_op jit(solution)/shard_map/ppermute | solution.py:514
  27.9 1.6 %fine_iterate.1 = f32[2,32,32,256]{3,2,1,0:T(8,128)} custom-call(f32[2,38,2,48,128]{4,3,2,1,0:T(8,128)S(1)} %get-tuple-element.77.u, f32[2,38,2,48,128]{4,3,2,1,0:T(8,128)S(1)} %get-tuple-element.78.e), custom_call_target="tpu_custom_call" | custom-call | flops 1000000 | bytes 8000000 | tf_op jit(solution)/shard_map/fine_iterate/pallas_call | solution.py:607
  29.5 1.2 %collective-permute-done.7.xhi = f32[3,5,16,128]{3,2,1,0:T(8,128)S(1)} collective-permute-done((f32[3,5,16,128]{3,2,1,0:T(8,128)S(1)}, f32[3,5,16,128]{3,2,1,0:T(8,128)S(1)}, u32[]{:S(2)}, u32[]{:S(2)}) %collective-permute-start.7) | collective-permute-done | bytes 122912 | tf_op jit(solution)/shard_map/ppermute | solution.py:515
  30.7 0.6 second_rows.1
  31.3 0.3 collective-permute-start.8
  31.6 1.7 %collective-permute-start.9 = (f32[2,26,8,128]{3,2,1,0:T(8,128)S(1)}, f32[2,26,8,128]{3,2,1,0:T(8,128)S(1)}, u32[]{:S(2)}, u32[]{:S(2)}) collective-permute-start(f32[2,26,8,128]{3,2,1,0:T(8,128)S(1)} %get-tuple-element.83), channel_id=1, source_target_pairs={{0,32},{1,2},{2,1},{3,4},{4,3},{5,6},{6,5},{7,8},{8,7},{9,10},{10,... | collective-permute-start | bytes 638984 | tf_op jit(solution)/shard_map/ppermute | solution.py:524
  33.2 5.8 %collective-permute-done.9.y_next = f32[2,26,8,128]{3,2,1,0:T(8,128)S(1)} collective-permute-done((f32[2,26,8,128]{3,2,1,0:T(8,128)S(1)}, f32[2,26,8,128]{3,2,1,0:T(8,128)S(1)}, u32[]{:S(2)}, u32[]{:S(2)}) %collective-permute-start.9) | collective-permute-done | bytes 213024 | tf_op jit(solution)/shard_map/ppermute | solution.py:524
  39.1 2.1 %second_level.1 = (f32[2,16,16,128]{3,2,1,0:T(8,128)}, f32[15,10,128]{2,1,0:T(8,128)S(1)}) custom-call(s32[2]{0:T(128)S(1)} %pad_add_fusion.place, f32[3,16,16,128]{3,2,1,0:T(8,128)S(1)} %get-tuple-element.76.fc.fc_own, f32[3,5,16,128]{3,2,1,0:T(8,128)S(1)} %collective-permute-done.6.xlo, f32[3,5,16,128]{3,2,1,0:T(8,128)S(1)} %collective-permute-done.7.xhi, ...), custom_call_target="tpu_custom_call" | custom-call | tf_op jit(solution)/shard_map/second_level/pallas_call | solution.py:629
  41.2 3.3 %collective-permute-start.10 = (f32[12,10,128]{2,1,0:T(8,128)S(1)}, f32[12,10,128]{2,1,0:T(8,128)S(1)}, u32[]{:S(2)}, u32[]{:S(2)}) collective-permute-start(f32[12,10,128]{2,1,0:T(8,128)S(1)} %pad_maximum_fusion), channel_id=1, source_target_pairs={{0,32},{32,64},{64,96},{96,128},{128,160},{160,192},{192,224},{224... | collective-permute-start | bytes 184328 | tf_op jit(solution)/shard_map/ppermute | solution.py:514
  44.6 2.1 %collective-permute-done.10.xlo = f32[12,10,128]{2,1,0:T(8,128)S(1)} collective-permute-done((f32[12,10,128]{2,1,0:T(8,128)S(1)}, f32[12,10,128]{2,1,0:T(8,128)S(1)}, u32[]{:S(2)}, u32[]{:S(2)}) %collective-permute-start.10) | collective-permute-done | bytes 61472 | tf_op jit(solution)/shard_map/ppermute | solution.py:514
  46.7 3.7 %collective-permute-done.11.xhi = f32[12,10,128]{2,1,0:T(8,128)S(1)} collective-permute-done((f32[12,10,128]{2,1,0:T(8,128)S(1)}, f32[12,10,128]{2,1,0:T(8,128)S(1)}, u32[]{:S(2)}, u32[]{:S(2)}) %collective-permute-start.11) | collective-permute-done | bytes 61472 | tf_op jit(solution)/shard_map/ppermute | solution.py:515
  50.5 0.3 collective-permute-start.13
  50.8 6.6 %collective-permute-done.13.y_next = f32[39,8,128]{2,1,0:T(8,128)S(1)} collective-permute-done((f32[39,8,128]{2,1,0:T(8,128)S(1)}, f32[39,8,128]{2,1,0:T(8,128)S(1)}, u32[]{:S(2)}, u32[]{:S(2)}) %collective-permute-start.13) | collective-permute-done | bytes 159776 | tf_op jit(solution)/shard_map/ppermute | solution.py:524
  57.4 2.7 %coarse_levels.1 = (f32[2,8,8,64]{3,2,1,0:T(8,128)}, f32[2,4,4,32]{3,2,1,0:T(4,128)}) custom-call(s32[2]{0:T(128)S(1)} %pad_add_fusion.place, f32[15,10,128]{2,1,0:T(8,128)S(1)} %get-tuple-element.85.fc_own, f32[12,10,128]{2,1,0:T(8,128)S(1)} %collective-permute-done.10.xlo, f32[12,10,128]{2,1,0:T(8,128)S(1)} %collective-permute-done.11.xhi, ...), custom_call_target="tpu_custom_call" | custom-call | tf_op jit(solution)/shard_map/coarse_levels/pallas_call | solution.py:654
  (31 shorter events, 0.6 us)
Async XLA Ops:
  0.6 5.4 %copy-start.1 = (f32[32,32,256]{2,1,0:T(8,128)S(1)}, f32[32,32,256]{2,1,0:T(8,128)}, u32[]{:S(2)}) copy-start(f32[32,32,256]{2,1,0:T(8,128)} %c.3) | copy-start | bytes 3145732
  0.6 5.4 %copy-start = (f32[2,32,32,256]{3,2,1,0:T(8,128)S(1)}, f32[2,32,32,256]{3,2,1,0:T(8,128)}, u32[]{:S(2)}) copy-start(f32[2,32,32,256]{3,2,1,0:T(8,128)} %f.3) | copy-start | bytes 6291460
  2.8 10.3 %collective-permute-start = (f32[8,32,256]{2,1,0:T(8,128)}, f32[8,32,256]{2,1,0:T(8,128)}, u32[]{:S(2)}, u32[]{:S(2)}) collective-permute-start(f32[8,32,256]{2,1,0:T(8,128)} %get-tuple-element.48), channel_id=1, source_target_pairs={{0,32},{32,64},{64,96},{96,128},{128,160},{160,192},{192,224},{224... | collective-permute-start | bytes 786440 | tf_op jit(solution)/shard_map/ppermute | solution.py:514
  6.0 9.3 %collective-permute-start.1 = (f32[8,32,256]{2,1,0:T(8,128)}, f32[8,32,256]{2,1,0:T(8,128)}, u32[]{:S(2)}, u32[]{:S(2)}) collective-permute-start(f32[8,32,256]{2,1,0:T(8,128)} %get-tuple-element.49), channel_id=1, source_target_pairs={{32,0},{64,32},{96,64},{128,96},{160,128},{192,160},{224,192},{0,2... | collective-permute-start | bytes 786440 | tf_op jit(solution)/shard_map/ppermute | solution.py:515
  7.2 12.7 %collective-permute-start.2 = (f32[32,8,256]{2,1,0:T(8,128)S(1)}, f32[32,8,256]{2,1,0:T(8,128)S(1)}, u32[]{:S(2)}, u32[]{:S(2)}) collective-permute-start(f32[32,8,256]{2,1,0:T(8,128)S(1)} %get-tuple-element.66), channel_id=1, source_target_pairs={{0,1},{1,0},{2,3},{3,2},{4,5},{5,4},{6,7},{7,6},{8,9},{9,8},{10,11... | collective-permute-start | bytes 786440 | tf_op jit(solution)/shard_map/ppermute | solution.py:524
  7.3 12.6 %collective-permute-start.3 = (f32[32,8,256]{2,1,0:T(8,128)S(1)}, f32[32,8,256]{2,1,0:T(8,128)S(1)}, u32[]{:S(2)}, u32[]{:S(2)}) collective-permute-start(f32[32,8,256]{2,1,0:T(8,128)S(1)} %get-tuple-element.67), channel_id=1, source_target_pairs={{0,32},{1,2},{2,1},{3,4},{4,3},{5,6},{6,5},{7,8},{8,7},{9,10},{10,... | collective-permute-start | bytes 786440 | tf_op jit(solution)/shard_map/ppermute | solution.py:524
  16.8 6.5 %collective-permute-start.4 = (f32[16,4,256]{2,1,0:T(4,128)S(1)}, f32[16,4,256]{2,1,0:T(4,128)S(1)}, u32[]{:S(2)}, u32[]{:S(2)}) collective-permute-start(f32[16,4,256]{2,1,0:T(4,128)S(1)} %get-tuple-element.74), channel_id=1, source_target_pairs={{0,1},{1,0},{2,3},{3,2},{4,5},{5,4},{6,7},{7,6},{8,9},{9,8},{10,11... | collective-permute-start | bytes 196616 | tf_op jit(solution)/shard_map/ppermute | solution.py:524
  16.9 6.5 %collective-permute-start.5 = (f32[16,4,256]{2,1,0:T(4,128)S(1)}, f32[16,4,256]{2,1,0:T(4,128)S(1)}, u32[]{:S(2)}, u32[]{:S(2)}) collective-permute-start(f32[16,4,256]{2,1,0:T(4,128)S(1)} %get-tuple-element.75), channel_id=1, source_target_pairs={{0,32},{1,2},{2,1},{3,4},{4,3},{5,6},{6,5},{7,8},{8,7},{9,10},{10,... | collective-permute-start | bytes 196616 | tf_op jit(solution)/shard_map/ppermute | solution.py:524
  24.5 6.2 %collective-permute-start.7 = (f32[3,5,16,128]{3,2,1,0:T(8,128)S(1)}, f32[3,5,16,128]{3,2,1,0:T(8,128)S(1)}, u32[]{:S(2)}, u32[]{:S(2)}) collective-permute-start(f32[3,5,16,128]{3,2,1,0:T(8,128)S(1)} %get-tuple-element.88), channel_id=1, source_target_pairs={{32,0},{64,32},{96,64},{128,96},{160,128},{192,160},{224,192},{0,2... | collective-permute-start | bytes 368648 | tf_op jit(solution)/shard_map/ppermute | solution.py:515
  24.6 6.1 %collective-permute-start.6 = (f32[3,5,16,128]{3,2,1,0:T(8,128)S(1)}, f32[3,5,16,128]{3,2,1,0:T(8,128)S(1)}, u32[]{:S(2)}, u32[]{:S(2)}) collective-permute-start(f32[3,5,16,128]{3,2,1,0:T(8,128)S(1)} %get-tuple-element.89), channel_id=1, source_target_pairs={{0,32},{32,64},{64,96},{96,128},{128,160},{160,192},{192,224},{224... | collective-permute-start | bytes 368648 | tf_op jit(solution)/shard_map/ppermute | solution.py:514
  31.3 1.9 %collective-permute-start.8 = (f32[2,26,8,128]{3,2,1,0:T(8,128)S(1)}, f32[2,26,8,128]{3,2,1,0:T(8,128)S(1)}, u32[]{:S(2)}, u32[]{:S(2)}) collective-permute-start(f32[2,26,8,128]{3,2,1,0:T(8,128)S(1)} %get-tuple-element.82), channel_id=1, source_target_pairs={{0,1},{1,0},{2,3},{3,2},{4,5},{5,4},{6,7},{7,6},{8,9},{9,8},{10,11... | collective-permute-start | bytes 638984 | tf_op jit(solution)/shard_map/ppermute | solution.py:524
  31.6 7.5 %collective-permute-start.9 = (f32[2,26,8,128]{3,2,1,0:T(8,128)S(1)}, f32[2,26,8,128]{3,2,1,0:T(8,128)S(1)}, u32[]{:S(2)}, u32[]{:S(2)}) collective-permute-start(f32[2,26,8,128]{3,2,1,0:T(8,128)S(1)} %get-tuple-element.83), channel_id=1, source_target_pairs={{0,32},{1,2},{2,1},{3,4},{4,3},{5,6},{6,5},{7,8},{8,7},{9,10},{10,... | collective-permute-start | bytes 638984 | tf_op jit(solution)/shard_map/ppermute | solution.py:524
  41.2 5.5 %collective-permute-start.10 = (f32[12,10,128]{2,1,0:T(8,128)S(1)}, f32[12,10,128]{2,1,0:T(8,128)S(1)}, u32[]{:S(2)}, u32[]{:S(2)}) collective-permute-start(f32[12,10,128]{2,1,0:T(8,128)S(1)} %pad_maximum_fusion), channel_id=1, source_target_pairs={{0,32},{32,64},{64,96},{96,128},{128,160},{160,192},{192,224},{224... | collective-permute-start | bytes 184328 | tf_op jit(solution)/shard_map/ppermute | solution.py:514
  44.5 5.9 %collective-permute-start.11 = (f32[12,10,128]{2,1,0:T(8,128)S(1)}, f32[12,10,128]{2,1,0:T(8,128)S(1)}, u32[]{:S(2)}, u32[]{:S(2)}) collective-permute-start(f32[12,10,128]{2,1,0:T(8,128)S(1)} %pad_maximum_fusion.1), channel_id=1, source_target_pairs={{32,0},{64,32},{96,64},{128,96},{160,128},{192,160},{224,192},{0,2... | collective-permute-start | bytes 184328 | tf_op jit(solution)/shard_map/ppermute | solution.py:515
  50.5 6.9 %collective-permute-start.13 = (f32[39,8,128]{2,1,0:T(8,128)S(1)}, f32[39,8,128]{2,1,0:T(8,128)S(1)}, u32[]{:S(2)}, u32[]{:S(2)}) collective-permute-start(f32[39,8,128]{2,1,0:T(8,128)S(1)} %get-tuple-element.90), channel_id=1, source_target_pairs={{0,32},{1,2},{2,1},{3,4},{4,3},{5,6},{6,5},{7,8},{8,7},{9,10},{10,... | collective-permute-start | bytes 479240 | tf_op jit(solution)/shard_map/ppermute | solution.py:524
  50.8 6.6 %collective-permute-start.12 = (f32[39,8,128]{2,1,0:T(8,128)S(1)}, f32[39,8,128]{2,1,0:T(8,128)S(1)}, u32[]{:S(2)}, u32[]{:S(2)}) collective-permute-start(f32[39,8,128]{2,1,0:T(8,128)S(1)} %get-tuple-element.91), channel_id=1, source_target_pairs={{0,1},{1,0},{2,3},{3,2},{4,5},{5,4},{6,7},{7,6},{8,9},{9,8},{10,11... | collective-permute-start | bytes 479240 | tf_op jit(solution)/shard_map/ppermute | solution.py:524

commit v8 on v7

--- a/solution.py
+++ b/solution.py
@@ -77,13 +77,20 @@
     return (row >= 0) & (row < ysize)
 
 
+def restrict_rows(vals, t, out, to, row, rows, k, start):
+    for h, val in enumerate(vals):
+        t[k, h, pl.ds(start, val.shape[0]), :] = val
+        part = [t[k, h, pl.ds(row + j, rows, 2), :] for j in range(4)]
+        out[k, to, pl.ds(0, rows), pl.ds(LANES * h, LANES)] = (part[0] + part[3]) + 3.0 * (part[1] + part[2])
+
+
 def restrict_xy(r, t, out, to, plane, row, rows, k, window):
     at = pl.ds(*window)
+    vals = []
     for h in range(r.shape[2]):
-        val = (r[k, plane, h, at, :] + r[k, plane + 3, h, at, :]) + 3.0 * (r[k, plane + 1, h, at, :] + r[k, plane + 2, h, at, :])
-        t[k, h, at, :] = val
-        part = [t[k, h, pl.ds(row + j, rows, 2), :] for j in range(4)]
-        out[k, to, pl.ds(0, rows), pl.ds(LANES * h, LANES)] = (part[0] + part[3]) + 3.0 * (part[1] + part[2])
+        four = [r[k, plane + j, h, at, :] for j in range(4)]
+        vals.append((four[0] + four[3]) + 3.0 * (four[1] + four[2]))
+    restrict_rows(vals, t, out, to, row, rows, k, window[0])
 
 
 def add_pairs(c0, c1, t, h, out, i, row, rows):
@@ -115,7 +122,7 @@
     return (dot(hi, w) + (dot(mid, w) + dot(low, w))).reshape(planes, rows, w.shape[1])
 
 
-PX, PY = 3, 8
+PX, PY = 2, 8
 
 
 def planes_kernel(f, c, x_first, x_last, planes, sems):
@@ -133,8 +140,7 @@
         for j in range(PX):
             a, b = inverse(planes[side, 2, j], 1.0, None)
             out[j], out[PX + j] = divided(planes[side, 0, j], planes[side, 1, j], a, b)
-        for j in range(2):
-            out[2 * PX + j] = planes[side, 2, j + side]
+        out[2 * PX] = planes[side, 2, (PX - 1) * side]
 
 
 def first_kernel(place, f, c, u, ga, gb, y_chip, y_next):
@@ -183,6 +189,8 @@
         for k in (0, 1):
             for h in range(halves):
                 r[k, x + PX, h, at, :] = 0.04 * f[k, x, :, cut[h]]
+    for x in (PX - 1, n + PX):
+        r[:, x] = jnp.zeros((2,) + r.shape[2:], jnp.float32)
 
     def pairs(i, carry):
         for h in range(halves):
@@ -235,10 +243,8 @@
 
 def plane_cells(side, low, i, h):
     cut = pl.ds(LANES * h, LANES)
-    j = i - 1 if low else i
-    c_here = 0 <= j < 2
-    cc = side[2 * PX + j, :, cut] if c_here else None
-    return side[i, :, cut], side[PX + i, :, cut], cc, c_here, i == (PX - 1 if low else 0)
+    c_here = i == (PX - 1 if low else 0)
+    return side[i, :, cut], side[PX + i, :, cut], side[2 * PX, :, cut] if c_here else None, c_here
 
 
 def faces_kernel(xsize, ysize, place, u_in, e_in, r_in, ga_in, gb_in, fc_in, xlo, xhi, y_chip, y_next, u, e, r, ga, gb, fc_out, part, q, sides, sems):
@@ -270,9 +276,9 @@
         for i in range(PX):
             good = ok(base + i, PY, rows)
             for h in range(halves):
-                re, im, cc, c_here, r_here = plane_cells(side, is_low, i, h)
-                halo(re, im, cc, good, u, ga, gb, r, base + i, h, PY, c_here, r_here)
-    for x in (PX - 2, PX - 1, PX, n + PX - 1, n + PX, n + PX + 1):
+                re, im, cc, c_here = plane_cells(side, is_low, i, h)
+                halo(re, im, cc, good, u, ga, gb, r, base + i, h, PY, c_here, False)
+    for x in (PX - 1, PX, n + PX - 1, n + PX):
         second(u, ga, gb, e, x, PY, rows, 1.0, True)
 
     def middle(x, carry):
@@ -281,7 +287,7 @@
         return carry
 
     lax.fori_loop(PX + 1, n + PX - 1, middle, 0, unroll=True)
-    for x in (PX - 1, PX, PX + 1, n + PX - 2, n + PX - 1, n + PX):
+    for x in (PX, PX + 1, n + PX - 2, n + PX - 1):
         finish(e, r, x, PY + 4, rows - 8, ok(x, PY + 4, rows - 8))
     row = lax.broadcasted_iota(jnp.int32, (8, LANES), 0)
     good_low, good_high = ok(PX, low, 8) & (row < 6), ok(PX, high, 8) & (row >= 2)
@@ -315,39 +321,40 @@
 
 
 def pack_corners_kernel(place, xlo, xhi, chip, other, tiles, sems):
-    rows = xlo.shape[1]
+    count, rows = xlo.shape[:2]
     copies = []
     for i, side in enumerate((xlo, xhi)):
         for j, row in enumerate((0, rows - 8)):
-            copies.append(pltpu.make_async_copy(side.at[:, pl.ds(row, 8)], tiles.at[j, pl.ds(8 * i, 8)], sems.at[2 * i + j]))
+            copies.append(pltpu.make_async_copy(side.at[:, pl.ds(row, 8)], tiles.at[j, pl.ds(count * i, count)], sems.at[2 * i + j]))
     for copy in copies:
         copy.start()
     even = is_even(place, (4, xlo.shape[2]))
     for copy in copies:
         copy.wait()
-    for j in range(16):
+    for j in range(2 * count):
         first, last = tiles[0, j, pl.ds(0, 4), :], tiles[1, j, pl.ds(4, 4), :]
         chip[j], other[j] = jnp.where(even, last, first), jnp.where(even, first, last)
 
 
-def corners_kernel(xsize, ysize, n, rows, place, u_in, e_in, r_in, ga_in, gb_in, fc_in, c_chip, c_next, u, e, r, ga, gb, fc_out, t, part):
+def corners_kernel(xsize, ysize, n, rows, place, u_in, e_in, r_in, ga_in, gb_in, fc_in, c_chip, c_next, u, e, r, ga, gb, fc_out, edge_out, t, part):
     halves = c_chip.shape[2] // LANES
     even = is_even(place, (4, LANES))
     ok = inside(place, n, rows, xsize, ysize)
     del u_in, e_in, r_in, ga_in, gb_in, fc_in
     low, high = PY - 4, PY + rows - 4
-    for first, low_planes, base in ((0, True, 0), (8, False, n + PX)):
-        chip, other = c_chip.at[pl.ds(first, 8)], c_next.at[pl.ds(first, 8)]
+    held = 2 * PX + 1
+    for first, low_planes, base in ((0, True, 0), (held, False, n + PX)):
+        chip, other = c_chip.at[pl.ds(first, held)], c_next.at[pl.ds(first, held)]
         for i in range(PX):
             for h in range(halves):
                 one, two = plane_cells(chip, low_planes, i, h), plane_cells(other, low_planes, i, h)
                 for row, (p, q) in ((PY - 4, (two, one)), (PY + rows, (one, two))):
                     re, im, cc = [None if v is None else jnp.where(even, v, w) for v, w in zip(p[:3], q[:3])]
-                    halo(re, im, cc, ok(base + i, row, 4), u, ga, gb, r, base + i, h, row, *one[3:])
-    for x in (PX - 2, PX - 1, PX, n + PX - 1, n + PX, n + PX + 1):
+                    halo(re, im, cc, ok(base + i, row, 4), u, ga, gb, r, base + i, h, row, one[3], False)
+    for x in (PX - 1, PX, n + PX - 1, n + PX):
         for row in (low, high):
             second(u, ga, gb, e, x, row, 8, 1.0, True)
-    for x in (PX - 1, PX, PX + 1, n + PX - 2, n + PX - 1, n + PX):
+    for x in (PX, PX + 1, n + PX - 2, n + PX - 1):
         for row in (low, high):
             finish(e, r, x, row, 8, ok(x, row, 8))
     planes = (0, 1, n // 2 - 2, n // 2 - 1)
@@ -355,9 +362,12 @@
     for k in (0, 1):
         for j, i in enumerate(planes):
             restrict_xy(r, t, part, j, 2 * i + PX - 1, PY - 1, rows // 2, k, (low, rows + 8))
+        for j, x in ((4, PX), (5, n + PX - 1)):
+            restrict_rows([r[k, x, h, pl.ds(low, rows + 8), :] for h in range(halves)], t, part, j, PY - 1, rows // 2, k, low)
         val = exact_dot(part[k], w)
         for j, i in enumerate(planes):
             fc_out[k, i] = val[j]
+        edge_out[0, k], edge_out[1, k] = val[4], val[5]
 
 
 def iterate_kernel(u, e, out):
@@ -389,26 +399,34 @@
             r[k, x, 0, at, :] = jnp.where(good, 0.04 * cells(k, x, at) + s, 0.0)
 
 
-def rows_kernel(place, xlo, fc, xhi, chip, other):
-    halo, n, rows = xlo.shape[1], fc.shape[1], fc.shape[2]
+def rows_kernel(xdev, halo, place, xlo, fc, xhi, edges, chip, other, window):
+    n, rows = fc.shape[1:3]
     row = lax.broadcasted_iota(jnp.int32, (8, LANES), 0)
     even = is_even(place, (8, LANES))
-    for src, base, count in ((xlo, 0, halo), (fc, halo, n), (xhi, n + halo, halo)):
-        for i in range(count):
-            made = []
-            for start, own in ((0, row < 5), (rows - 8, row >= 3)):
-                re, im, cc = [src[k, i, pl.ds(start, 8), :] for k in range(3)]
-                made.append((jnp.where(own, re, pltpu.roll(cc, 5, 0)), jnp.where(own, im, pltpu.roll(cc, 2, 0))))
-            for k, (first, last) in enumerate(zip(*made)):
-                chip[k, base + i], other[k, base + i] = jnp.where(even, last, first), jnp.where(even, first, last)
-
-
-def middle_kernel(halo, over, xsize, ysize, place, fc_own, xlo, xhi, y_chip, y_next, u_out, fc_out, fc, ga, gb, u, e, r, t, part, part_c):
-    n, rows = fc_own.shape[1:3]
-    planes = n + 2 * halo
+    here = jnp.full((rows, LANES), place[0])
     for k in range(3):
-        for src, x, count in ((xlo, 0, halo), (fc_own, halo, n), (xhi, n + halo, halo)):
-            fc[k, pl.ds(x, count), 0, pl.ds(8, rows), :] = src[k]
+        window[k, pl.ds(0, halo)] = xlo[pl.ds(k * halo, halo)]
+        window[k, pl.ds(halo, n)] = fc[k]
+        window[k, pl.ds(n + halo, halo)] = xhi[pl.ds(k * halo, halo)]
+    for k in (0, 1):
+        window[k, halo - 1] += edges[0, k]
+        window[k, halo] += jnp.where(here > 0, xlo[3 * halo + k], 0.0)
+        window[k, n + halo - 1] += jnp.where(here < xdev - 1, xhi[3 * halo + k], 0.0)
+        window[k, n + halo] += edges[1, k]
+    for x in range(n + 2 * halo):
+        made = []
+        for start, own in ((0, row < 5), (rows - 8, row >= 3)):
+            re, im, cc = [window[k, x, pl.ds(start, 8), :] for k in range(3)]
+            made.append((jnp.where(own, re, pltpu.roll(cc, 5, 0)), jnp.where(own, im, pltpu.roll(cc, 2, 0))))
+        for k, (first, last) in enumerate(zip(*made)):
+            chip[k, x], other[k, x] = jnp.where(even, last, first), jnp.where(even, first, last)
+
+
+def middle_kernel(halo, over, xsize, ysize, place, window, y_chip, y_next, u_out, fc_out, fc, ga, gb, u, e, r, t, part, part_c):
+    planes, rows = window.shape[1:3]
+    n = planes - 2 * halo
+    for k in range(3):
+        fc[k, :, 0, pl.ds(8, rows), :] = window[k]
     row = lax.broadcasted_iota(jnp.int32, (8, LANES), 0)
     even = is_even(place, (8, LANES))
     for x in range(planes):
@@ -533,11 +551,12 @@
     part = (n // 2, rows // 2, lanes)
     two, one, coarser = S(2, *state), S(*state), S(3, n // 2, rows // 2, lanes // 2)
     column = V(2, halves, rows + 2 * PY, LANES)
+    held_planes = 2 * PX + 1
     x_first, x_last = pl.pallas_call(
         planes_kernel,
         in_specs=[pl.BlockSpec(memory_space=pltpu.HBM)] * 2,
         out_specs=[VMEM] * 2,
-        out_shape=[S(8, rows, lanes)] * 2,
+        out_shape=[S(held_planes, rows, lanes)] * 2,
         scratch_shapes=[V(2, 3, PX, rows, lanes), pltpu.SemaphoreType.DMA((6,))],
         compiler_params=params(24),
         name="pack_planes",
@@ -572,8 +591,8 @@
             pack_corners_kernel,
             in_specs=[SMEM] + [ANY] * 2,
             out_specs=[VMEM] * 2,
-            out_shape=[S(16, 4, lanes)] * 2,
-            scratch_shapes=[V(2, 16, 8, lanes), pltpu.SemaphoreType.DMA((4,))],
+            out_shape=[S(2 * held_planes, 4, lanes)] * 2,
+            scratch_shapes=[V(2, 2 * held_planes, 8, lanes), pltpu.SemaphoreType.DMA((4,))],
             compiler_params=params(24),
             name="pack_corners",
         )(place, xlo, xhi)
@@ -585,25 +604,26 @@
         out_specs=[VMEM] * 6,
         out_shape=shapes,
         input_output_aliases=in_place,
-        scratch_shapes=[V(2, n // 2 - 4, 16, lanes), V(2, n // 2 - 4, 16, lanes // 2), V(2, 8, rows, lanes), pltpu.SemaphoreType.DMA((2,))],
+        scratch_shapes=[V(2, n // 2 - 4, 16, lanes), V(2, n // 2 - 4, 16, lanes // 2), V(2, held_planes, rows, lanes), pltpu.SemaphoreType.DMA((2,))],
         compiler_params=params(24),
         cost_estimate=pl.CostEstimate(flops=50_000_000, bytes_accessed=8_000_000, transcendentals=0),
         name="face_cells",
     )(place, *held, xlo, xhi, y_chip, y_next)
-    u, e, _, _, _, fc = pl.pallas_call(
+    u, e, _, _, _, fc, edges = pl.pallas_call(
         functools.partial(corners_kernel, xsize, ysize, n, rows),
         in_specs=[SMEM] + [VMEM] * 8,
-        out_specs=[VMEM] * 6,
-        out_shape=shapes,
+        out_specs=[VMEM] * 7,
+        out_shape=shapes + [S(2, 2, rows // 2, lanes // 2)],
         input_output_aliases=in_place,
-        scratch_shapes=[column, V(2, 4, rows // 2, lanes)],
+        scratch_shapes=[column, V(2, 6, rows // 2, lanes)],
         compiler_params=params(24),
         name="corner_cells",
     )(place, *held, c_chip, c_next)
     fine_shape = S(2, n, rows, lanes)
     n, rows, lanes, xsize, ysize, zsize = n // 2, rows // 2, lanes // 2, xsize // 2, ysize // 2, lanes // 2
     h, over = 5, 1
-    xlo, xhi = planes_step(fc[:, :h], fc[:, n - h :])
+    slab = lambda x, edge: jnp.concatenate([fc[:, x : x + h].reshape(3 * h, rows, lanes), edge], 0)
+    xlo, xhi = planes_step(slab(0, edges[0]), slab(n - h, edges[1]))
     fine = pl.pallas_call(
         iterate_kernel,
         in_specs=[VMEM] * 2,
@@ -614,27 +634,27 @@
         name="fine_iterate",
     )(u, e)
     xlo, xhi, fine = lax.optimization_barrier((xlo, xhi, fine))
-    chip, other = pl.pallas_call(
-        rows_kernel,
-        in_specs=[SMEM] + [VMEM] * 3,
-        out_specs=[VMEM] * 2,
-        out_shape=[S(2, n + 2 * h, 8, lanes)] * 2,
+    chip, other, window = pl.pallas_call(
+        functools.partial(rows_kernel, xdev, h),
+        in_specs=[SMEM] + [VMEM] * 4,
+        out_specs=[VMEM] * 3,
+        out_shape=[S(2, n + 2 * h, 8, lanes)] * 2 + [S(3, n + 2 * h, rows, lanes)],
         compiler_params=params(24),
         name="second_rows",
-    )(place, xlo, fc, xhi)
+    )(place, xlo, fc, xhi, edges)
     chip, other = rows_step(chip, other)
     state = (n + 2 * h, 1, rows + 16, LANES)
     work = lambda s: [V(*s), V(*s), V(2, *s), V(2, *s), V(2, *s), V(2, 1, *s[2:])]
     width = n // 2 + 2 * over
     second_u, fc = pl.pallas_call(
         functools.partial(middle_kernel, h, over, xsize, ysize),
-        in_specs=[SMEM] + [VMEM] * 5,
+        in_specs=[SMEM] + [VMEM] * 3,
         out_specs=[VMEM] * 2,
         out_shape=[S(2, n, rows, lanes), S(width + width // 2, width, lanes)],
         scratch_shapes=[V(3, *state)] + work(state) + [V(2, width, 16, LANES), V(2, width // 2, 16, LANES)],
         compiler_params=params(24),
         name="second_level",
-    )(place, fc, xlo, xhi, chip, other)
+    )(place, window, chip, other)
 
     n, xsize, ysize, zsize = n // 2, xsize // 2, ysize // 2, zsize // 2
     m = n // 2

time: 60.2 us -> 58.3 us (0.968)
  the two profiles are of different devices: /device:TPU:120 before, /device:TPU:56 now
where the time goes in v8:
time: 58.3 us; the launch traced here: 58.2 us
  waiting for transfers between devices  25.1 us (43%)
  Pallas kernels  16.9 us (29%)
  starting transfers between devices  14.3 us (25%)
  between operations  0.85 us (1%)
  local copies, waits for them, and re-layouts  0.84 us (1%)
    ppermute x4, waiting for transfers between devices, rows_step(): lax.ppermute(other, ('gx', 'gy'), next_chip)  13.4 us
    ppermute x3, waiting for transfers between devices, planes_step(): lax.ppermute(first, 'gx', [((i + 1) % xdev, i) for i in range(xdev)])  7.76 us
    ppermute x3, starting transfers between devices, planes_step(): lax.ppermute(last, 'gx', [(i, (i + 1) % xdev) for i in range(xdev)])  7.11 us
    ppermute x4, starting transfers between devices, rows_step(): lax.ppermute(other, ('gx', 'gy'), next_chip)  6.59 us
    ppermute x3, waiting for transfers between devices, planes_step(): lax.ppermute(last, 'gx', [(i, (i + 1) % xdev) for i in range(xdev)])  3.91 us
    pallas_call x1, Pallas kernels, body(): pl.pallas_call(functools.partial(faces_kernel, xsize, ysize), in_specs=[S...  3.04 us
    pallas_call x1, Pallas kernels, body(): pl.pallas_call(inner_kernel, in_specs=[VMEM] * 5, out_specs=[VMEM] * 3, o...  2.71 us
    pallas_call x1, Pallas kernels, body(): pl.pallas_call(functools.partial(coarse_kernel, n, 4, xsize, ysize, zsize...  2.65 us
  transfers between devices with their start and end apart: 14, of which 10 were waited for; matrix products, arithmetic and copies ran while one was open for 0% of the time, Pallas kernels for 14%

profile of v8, /device:TPU:56, one launch (start us, length us, event | category | flops | bytes accessed | tf_op | source)
XLA Modules:
  0.0 58.2 jit_solution(10118241217686842077)
XLA Ops:
  0.7 1.2 %pack_planes.1 = (f32[5,32,256]{2,1,0:T(8,128)S(1)}, f32[5,32,256]{2,1,0:T(8,128)S(1)}) custom-call(f32[2,32,32,256]{3,2,1,0:T(8,128)} %f.3, f32[32,32,256]{2,1,0:T(8,128)} %c.3), custom_call_target="tpu_custom_call" | custom-call | tf_op jit(solution)/shard_map/pack_planes/pallas_call | solution.py:555
  2.0 0.7 %copy-done = f32[2,32,32,256]{3,2,1,0:T(8,128)S(1)} copy-done((f32[2,32,32,256]{3,2,1,0:T(8,128)S(1)}, f32[2,32,32,256]{3,2,1,0:T(8,128)}, u32[]{:S(2)}) %copy-start) | copy-done | bytes 2097176
  2.7 1.2 %first_iterate.1 = (f32[2,36,2,48,128]{4,3,2,1,0:T(8,128)S(1)}, f32[36,2,48,128]{3,2,1,0:T(8,128)S(1)}, f32[36,2,48,128]{3,2,1,0:T(8,128)S(1)}, f32[32,8,256]{2,1,0:T(8,128)S(1)}, f32[32,8,256]{2,1,0:T(8,128)S(1)}) custom-call(s32[2]{0:T(128)S(1)} %pad_add_fusion.place, f32[2,32,32,256]{3,2,1,0:T(8,128)S(1)} %copy-done, f32[32,32,256]{2,1,0:T(8,128)S(1)} %copy-done.1), custom_call_target="tpu_custom_call" | custom-call | flops 30000000 | bytes 8000000 | tf_op jit(solution)/shard_map/first_iterate/pallas_call | solution.py:566
  4.0 3.0 %collective-permute-start.3 = (f32[32,8,256]{2,1,0:T(8,128)S(1)}, f32[32,8,256]{2,1,0:T(8,128)S(1)}, u32[]{:S(2)}, u32[]{:S(2)}) collective-permute-start(f32[32,8,256]{2,1,0:T(8,128)S(1)} %get-tuple-element.69), channel_id=1, source_target_pairs={{0,32},{1,2},{2,1},{3,4},{4,3},{5,6},{6,5},{7,8},{8,7},{9,10},{10,... | collective-permute-start | bytes 786440 | tf_op jit(solution)/shard_map/ppermute | solution.py:542
  7.1 1.9 %collective-permute-start = (f32[5,32,256]{2,1,0:T(8,128)S(1)}, f32[5,32,256]{2,1,0:T(8,128)S(1)}, u32[]{:S(2)}, u32[]{:S(2)}) collective-permute-start(f32[5,32,256]{2,1,0:T(8,128)S(1)} %get-tuple-element.50), channel_id=1, source_target_pairs={{0,32},{32,64},{64,96},{96,128},{128,160},{160,192},{192,224},{224... | collective-permute-start | bytes 491528 | tf_op jit(solution)/shard_map/ppermute | solution.py:532
  9.1 2.7 %inner_cells.1 = (f32[2,36,2,48,128]{4,3,2,1,0:T(8,128)S(1)}, f32[2,36,2,48,128]{4,3,2,1,0:T(8,128)S(1)}, f32[3,16,16,128]{3,2,1,0:T(8,128)S(1)}) custom-call(f32[2,32,32,256]{3,2,1,0:T(8,128)S(1)} %copy-done, f32[32,32,256]{2,1,0:T(8,128)S(1)} %copy-done.1, f32[2,36,2,48,128]{4,3,2,1,0:T(8,128)S(1)} %get-tuple-element.60.u.u_in, ...), custom_call_target="tpu_custom_call" | custom-call | flops 70000000 | bytes 16000000 | tf_op jit(solution)/shard_map/inner_cells/pallas_call | solution.py:576
  12.4 1.9 %collective-permute-done.1.xhi = f32[5,32,256]{2,1,0:T(8,128)S(1)} collective-permute-done((f32[5,32,256]{2,1,0:T(8,128)S(1)}, f32[5,32,256]{2,1,0:T(8,128)S(1)}, u32[]{:S(2)}, u32[]{:S(2)}) %collective-permute-start.1) | collective-permute-done | bytes 163872 | tf_op jit(solution)/shard_map/ppermute | solution.py:533
  14.3 0.6 %pack_corners.1 = (f32[10,4,256]{2,1,0:T(4,128)S(1)}, f32[10,4,256]{2,1,0:T(4,128)S(1)}) custom-call(s32[2]{0:T(128)S(1)} %pad_add_fusion.place, f32[5,32,256]{2,1,0:T(8,128)S(1)} %collective-permute-done.xlo, f32[5,32,256]{2,1,0:T(8,128)S(1)} %collective-permute-done.1.xhi), custom_call_target="tpu_custom_call" | custom-call | tf_op jit(solution)/shard_map/pack_corners/pallas_call | solution.py:590
  15.0 2.1 %collective-permute-start.5 = (f32[10,4,256]{2,1,0:T(4,128)S(1)}, f32[10,4,256]{2,1,0:T(4,128)S(1)}, u32[]{:S(2)}, u32[]{:S(2)}) collective-permute-start(f32[10,4,256]{2,1,0:T(4,128)S(1)} %get-tuple-element.77), channel_id=1, source_target_pairs={{0,32},{1,2},{2,1},{3,4},{4,3},{5,6},{6,5},{7,8},{8,7},{9,10},{10,... | collective-permute-start | bytes 122888 | tf_op jit(solution)/shard_map/ppermute | solution.py:542
  17.1 3.0 %face_cells.1 = (f32[2,36,2,48,128]{4,3,2,1,0:T(8,128)S(1)}, f32[2,36,2,48,128]{4,3,2,1,0:T(8,128)S(1)}, f32[2,36,2,48,128]{4,3,2,1,0:T(8,128)S(1)}, f32[36,2,48...) custom-call(s32[2]{0:T(128)S(1)} %pad_add_fusion.place, ...), custom_call_target="tpu_custom_call", output_to_operand_aliasing={{0}: (1, {}), {1}: (2, {}), {2}: (3, {}), {3}: (4, {}), {4}... | custom-call | flops 50000000 | bytes 8000000 | tf_op jit(solution)/shard_map/face_cells/pallas_call | solution.py:601
  20.7 1.1 %corner_cells.1 = (f32[2,36,2,48,128]{4,3,2,1,0:T(8,128)S(1)}, f32[2,36,2,48,128]{4,3,2,1,0:T(8,128)S(1)}, f32[2,36,2,48,128]{4,3,2,1,0:T(8,128)S(1)}, f32[36,2,...) custom-call(s32[2]{0:T(128)S(1)} %pad_add_fusion.place, ...), custom_call_target="tpu_custom_call", output_to_operand_aliasing={{0}: (1, {}), {1}: (2, {}), {2}: (3, {}), {3}: (4, {}), {4}... | custom-call | tf_op jit(solution)/shard_map/corner_cells/pallas_call | solution.py:612
  21.8 3.1 %collective-permute-start.6 = (f32[17,16,128]{2,1,0:T(8,128)S(1)}, f32[17,16,128]{2,1,0:T(8,128)S(1)}, u32[]{:S(2)}, u32[]{:S(2)}) collective-permute-start(f32[17,16,128]{2,1,0:T(8,128)S(1)} %pad_maximum_fusion), channel_id=1, source_target_pairs={{0,32},{32,64},{64,96},{96,128},{128,160},{160,192},{192,224},{224... | collective-permute-start | bytes 417800 | tf_op jit(solution)/shard_map/ppermute | solution.py:532
  25.0 1.7 %fine_iterate.1 = f32[2,32,32,256]{3,2,1,0:T(8,128)} custom-call(f32[2,36,2,48,128]{4,3,2,1,0:T(8,128)S(1)} %get-tuple-element.80.u, f32[2,36,2,48,128]{4,3,2,1,0:T(8,128)S(1)} %get-tuple-element.81.e), custom_call_target="tpu_custom_call" | custom-call | flops 1000000 | bytes 8000000 | tf_op jit(solution)/shard_map/fine_iterate/pallas_call | solution.py:627
  26.7 0.8 %collective-permute-done.6.xlo = f32[17,16,128]{2,1,0:T(8,128)S(1)} collective-permute-done((f32[17,16,128]{2,1,0:T(8,128)S(1)}, f32[17,16,128]{2,1,0:T(8,128)S(1)}, u32[]{:S(2)}, u32[]{:S(2)}) %collective-permute-start.6) | collective-permute-done | bytes 139296 | tf_op jit(solution)/shard_map/ppermute | solution.py:532
  27.5 3.8 %collective-permute-done.7.xhi = f32[17,16,128]{2,1,0:T(8,128)S(1)} collective-permute-done((f32[17,16,128]{2,1,0:T(8,128)S(1)}, f32[17,16,128]{2,1,0:T(8,128)S(1)}, u32[]{:S(2)}, u32[]{:S(2)}) %collective-permute-start.7) | collective-permute-done | bytes 139296 | tf_op jit(solution)/shard_map/ppermute | solution.py:533
  31.3 0.6 %second_rows.1 = (f32[2,26,8,128]{3,2,1,0:T(8,128)S(1)}, f32[2,26,8,128]{3,2,1,0:T(8,128)S(1)}, f32[3,26,16,128]{3,2,1,0:T(8,128)S(1)}) custom-call(s32[2]{0:T(128)S(1)} %pad_add_fusion.place, f32[17,16,128]{2,1,0:T(8,128)S(1)} %collective-permute-done.6.xlo, f32[3,16,16,128]{3,2,1,0:T(8,128)S(1)} %get-tuple-element.78.fc, ...), custom_call_target="tpu_custom_call" | custom-call | tf_op jit(solution)/shard_map/second_rows/pallas_call | solution.py:637
  32.0 1.4 %collective-permute-start.9 = (f32[2,26,8,128]{3,2,1,0:T(8,128)S(1)}, f32[2,26,8,128]{3,2,1,0:T(8,128)S(1)}, u32[]{:S(2)}, u32[]{:S(2)}) collective-permute-start(f32[2,26,8,128]{3,2,1,0:T(8,128)S(1)} %get-tuple-element.87), channel_id=1, source_target_pairs={{0,32},{1,2},{2,1},{3,4},{4,3},{5,6},{6,5},{7,8},{8,7},{9,10},{10,... | collective-permute-start | bytes 638984 | tf_op jit(solution)/shard_map/ppermute | solution.py:542
  33.5 6.2 %collective-permute-done.9.y_next = f32[2,26,8,128]{3,2,1,0:T(8,128)S(1)} collective-permute-done((f32[2,26,8,128]{3,2,1,0:T(8,128)S(1)}, f32[2,26,8,128]{3,2,1,0:T(8,128)S(1)}, u32[]{:S(2)}, u32[]{:S(2)}) %collective-permute-start.9) | collective-permute-done | bytes 213024 | tf_op jit(solution)/shard_map/ppermute | solution.py:542
  39.6 2.1 %second_level.1 = (f32[2,16,16,128]{3,2,1,0:T(8,128)}, f32[15,10,128]{2,1,0:T(8,128)S(1)}) custom-call(s32[2]{0:T(128)S(1)} %pad_add_fusion.place, f32[3,26,16,128]{3,2,1,0:T(8,128)S(1)} %get-tuple-element.85.window, f32[2,26,8,128]{3,2,1,0:T(8,128)S(1)} %collective-permute-done.8.y_chip, f32[2,26,8,128]{3,2,1,0:T(8,128)S(1)} %collective-permute-done.9.y_next), custom_call_target="tpu_custom_call" | custom-call | tf_op jit(solution)/shard_map/second_level/pallas_call | solution.py:649
  41.8 2.1 %collective-permute-start.10 = (f32[12,10,128]{2,1,0:T(8,128)S(1)}, f32[12,10,128]{2,1,0:T(8,128)S(1)}, u32[]{:S(2)}, u32[]{:S(2)}) collective-permute-start(f32[12,10,128]{2,1,0:T(8,128)S(1)} %pad_maximum_fusion.2), channel_id=1, source_target_pairs={{0,32},{32,64},{64,96},{96,128},{128,160},{160,192},{192,224},{224... | collective-permute-start | bytes 184328 | tf_op jit(solution)/shard_map/ppermute | solution.py:532
  44.0 2.5 %collective-permute-done.10.xlo = f32[12,10,128]{2,1,0:T(8,128)S(1)} collective-permute-done((f32[12,10,128]{2,1,0:T(8,128)S(1)}, f32[12,10,128]{2,1,0:T(8,128)S(1)}, u32[]{:S(2)}, u32[]{:S(2)}) %collective-permute-start.10) | collective-permute-done | bytes 61472 | tf_op jit(solution)/shard_map/ppermute | solution.py:532
  46.5 2.1 %collective-permute-done.11.xhi = f32[12,10,128]{2,1,0:T(8,128)S(1)} collective-permute-done((f32[12,10,128]{2,1,0:T(8,128)S(1)}, f32[12,10,128]{2,1,0:T(8,128)S(1)}, u32[]{:S(2)}, u32[]{:S(2)}) %collective-permute-start.11) | collective-permute-done | bytes 61472 | tf_op jit(solution)/shard_map/ppermute | solution.py:533
  48.9 6.7 %collective-permute-done.13.y_next = f32[39,8,128]{2,1,0:T(8,128)S(1)} collective-permute-done((f32[39,8,128]{2,1,0:T(8,128)S(1)}, f32[39,8,128]{2,1,0:T(8,128)S(1)}, u32[]{:S(2)}, u32[]{:S(2)}) %collective-permute-start.13) | collective-permute-done | bytes 159776 | tf_op jit(solution)/shard_map/ppermute | solution.py:542
  55.6 2.7 %coarse_levels.1 = (f32[2,8,8,64]{3,2,1,0:T(8,128)}, f32[2,4,4,32]{3,2,1,0:T(4,128)}) custom-call(s32[2]{0:T(128)S(1)} %pad_add_fusion.place, f32[15,10,128]{2,1,0:T(8,128)S(1)} %get-tuple-element.89.fc_own, f32[12,10,128]{2,1,0:T(8,128)S(1)} %collective-permute-done.10.xlo, f32[12,10,128]{2,1,0:T(8,128)S(1)} %collective-permute-done.11.xhi, ...), custom_call_target="tpu_custom_call" | custom-call | tf_op jit(solution)/shard_map/coarse_levels/pallas_call | solution.py:674
  (34 shorter events, 2.2 us)
Async XLA Ops:
  0.6 1.4 %copy-start.1 = (f32[32,32,256]{2,1,0:T(8,128)S(1)}, f32[32,32,256]{2,1,0:T(8,128)}, u32[]{:S(2)}) copy-start(f32[32,32,256]{2,1,0:T(8,128)} %c.3) | copy-start | bytes 3145732
  0.6 2.1 %copy-start = (f32[2,32,32,256]{3,2,1,0:T(8,128)S(1)}, f32[2,32,32,256]{3,2,1,0:T(8,128)}, u32[]{:S(2)}) copy-start(f32[2,32,32,256]{3,2,1,0:T(8,128)} %f.3) | copy-start | bytes 6291460
  3.9 13.2 %collective-permute-start.2 = (f32[32,8,256]{2,1,0:T(8,128)S(1)}, f32[32,8,256]{2,1,0:T(8,128)S(1)}, u32[]{:S(2)}, u32[]{:S(2)}) collective-permute-start(f32[32,8,256]{2,1,0:T(8,128)S(1)} %get-tuple-element.68), channel_id=1, source_target_pairs={{0,1},{1,0},{2,3},{3,2},{4,5},{5,4},{6,7},{7,6},{8,9},{9,8},{10,11... | collective-permute-start | bytes 786440 | tf_op jit(solution)/shard_map/ppermute | solution.py:542
  4.0 13.1 %collective-permute-start.3 = (f32[32,8,256]{2,1,0:T(8,128)S(1)}, f32[32,8,256]{2,1,0:T(8,128)S(1)}, u32[]{:S(2)}, u32[]{:S(2)}) collective-permute-start(f32[32,8,256]{2,1,0:T(8,128)S(1)} %get-tuple-element.69), channel_id=1, source_target_pairs={{0,32},{1,2},{2,1},{3,4},{4,3},{5,6},{6,5},{7,8},{8,7},{9,10},{10,... | collective-permute-start | bytes 786440 | tf_op jit(solution)/shard_map/ppermute | solution.py:542
  7.1 5.3 %collective-permute-start = (f32[5,32,256]{2,1,0:T(8,128)S(1)}, f32[5,32,256]{2,1,0:T(8,128)S(1)}, u32[]{:S(2)}, u32[]{:S(2)}) collective-permute-start(f32[5,32,256]{2,1,0:T(8,128)S(1)} %get-tuple-element.50), channel_id=1, source_target_pairs={{0,32},{32,64},{64,96},{96,128},{128,160},{160,192},{192,224},{224... | collective-permute-start | bytes 491528 | tf_op jit(solution)/shard_map/ppermute | solution.py:532
  9.0 5.3 %collective-permute-start.1 = (f32[5,32,256]{2,1,0:T(8,128)S(1)}, f32[5,32,256]{2,1,0:T(8,128)S(1)}, u32[]{:S(2)}, u32[]{:S(2)}) collective-permute-start(f32[5,32,256]{2,1,0:T(8,128)S(1)} %get-tuple-element.51), channel_id=1, source_target_pairs={{32,0},{64,32},{96,64},{128,96},{160,128},{192,160},{224,192},{0,2... | collective-permute-start | bytes 491528 | tf_op jit(solution)/shard_map/ppermute | solution.py:533
  14.9 5.2 %collective-permute-start.4 = (f32[10,4,256]{2,1,0:T(4,128)S(1)}, f32[10,4,256]{2,1,0:T(4,128)S(1)}, u32[]{:S(2)}, u32[]{:S(2)}) collective-permute-start(f32[10,4,256]{2,1,0:T(4,128)S(1)} %get-tuple-element.76), channel_id=1, source_target_pairs={{0,1},{1,0},{2,3},{3,2},{4,5},{5,4},{6,7},{7,6},{8,9},{9,8},{10,11... | collective-permute-start | bytes 122888 | tf_op jit(solution)/shard_map/ppermute | solution.py:542
  15.0 5.6 %collective-permute-start.5 = (f32[10,4,256]{2,1,0:T(4,128)S(1)}, f32[10,4,256]{2,1,0:T(4,128)S(1)}, u32[]{:S(2)}, u32[]{:S(2)}) collective-permute-start(f32[10,4,256]{2,1,0:T(4,128)S(1)} %get-tuple-element.77), channel_id=1, source_target_pairs={{0,32},{1,2},{2,1},{3,4},{4,3},{5,6},{6,5},{7,8},{8,7},{9,10},{10,... | collective-permute-start | bytes 122888 | tf_op jit(solution)/shard_map/ppermute | solution.py:542
  21.8 5.7 %collective-permute-start.6 = (f32[17,16,128]{2,1,0:T(8,128)S(1)}, f32[17,16,128]{2,1,0:T(8,128)S(1)}, u32[]{:S(2)}, u32[]{:S(2)}) collective-permute-start(f32[17,16,128]{2,1,0:T(8,128)S(1)} %pad_maximum_fusion), channel_id=1, source_target_pairs={{0,32},{32,64},{64,96},{96,128},{128,160},{160,192},{192,224},{224... | collective-permute-start | bytes 417800 | tf_op jit(solution)/shard_map/ppermute | solution.py:532
  24.9 6.3 %collective-permute-start.7 = (f32[17,16,128]{2,1,0:T(8,128)S(1)}, f32[17,16,128]{2,1,0:T(8,128)S(1)}, u32[]{:S(2)}, u32[]{:S(2)}) collective-permute-start(f32[17,16,128]{2,1,0:T(8,128)S(1)} %pad_maximum_fusion.1), channel_id=1, source_target_pairs={{32,0},{64,32},{96,64},{128,96},{160,128},{192,160},{224,192},{0,2... | collective-permute-start | bytes 417800 | tf_op jit(solution)/shard_map/ppermute | solution.py:533
  31.9 1.6 %collective-permute-start.8 = (f32[2,26,8,128]{3,2,1,0:T(8,128)S(1)}, f32[2,26,8,128]{3,2,1,0:T(8,128)S(1)}, u32[]{:S(2)}, u32[]{:S(2)}) collective-permute-start(f32[2,26,8,128]{3,2,1,0:T(8,128)S(1)} %get-tuple-element.86), channel_id=1, source_target_pairs={{0,1},{1,0},{2,3},{3,2},{4,5},{5,4},{6,7},{7,6},{8,9},{9,8},{10,11... | collective-permute-start | bytes 638984 | tf_op jit(solution)/shard_map/ppermute | solution.py:542
  32.0 7.6 %collective-permute-start.9 = (f32[2,26,8,128]{3,2,1,0:T(8,128)S(1)}, f32[2,26,8,128]{3,2,1,0:T(8,128)S(1)}, u32[]{:S(2)}, u32[]{:S(2)}) collective-permute-start(f32[2,26,8,128]{3,2,1,0:T(8,128)S(1)} %get-tuple-element.87), channel_id=1, source_target_pairs={{0,32},{1,2},{2,1},{3,4},{4,3},{5,6},{6,5},{7,8},{8,7},{9,10},{10,... | collective-permute-start | bytes 638984 | tf_op jit(solution)/shard_map/ppermute | solution.py:542
  41.8 4.7 %collective-permute-start.10 = (f32[12,10,128]{2,1,0:T(8,128)S(1)}, f32[12,10,128]{2,1,0:T(8,128)S(1)}, u32[]{:S(2)}, u32[]{:S(2)}) collective-permute-start(f32[12,10,128]{2,1,0:T(8,128)S(1)} %pad_maximum_fusion.2), channel_id=1, source_target_pairs={{0,32},{32,64},{64,96},{96,128},{128,160},{160,192},{192,224},{224... | collective-permute-start | bytes 184328 | tf_op jit(solution)/shard_map/ppermute | solution.py:532
  43.9 4.7 %collective-permute-start.11 = (f32[12,10,128]{2,1,0:T(8,128)S(1)}, f32[12,10,128]{2,1,0:T(8,128)S(1)}, u32[]{:S(2)}, u32[]{:S(2)}) collective-permute-start(f32[12,10,128]{2,1,0:T(8,128)S(1)} %pad_maximum_fusion.3), channel_id=1, source_target_pairs={{32,0},{64,32},{96,64},{128,96},{160,128},{192,160},{224,192},{0,2... | collective-permute-start | bytes 184328 | tf_op jit(solution)/shard_map/ppermute | solution.py:533
  48.7 6.9 %collective-permute-start.13 = (f32[39,8,128]{2,1,0:T(8,128)S(1)}, f32[39,8,128]{2,1,0:T(8,128)S(1)}, u32[]{:S(2)}, u32[]{:S(2)}) collective-permute-start(f32[39,8,128]{2,1,0:T(8,128)S(1)} %get-tuple-element.94), channel_id=1, source_target_pairs={{0,32},{1,2},{2,1},{3,4},{4,3},{5,6},{6,5},{7,8},{8,7},{9,10},{10,... | collective-permute-start | bytes 479240 | tf_op jit(solution)/shard_map/ppermute | solution.py:542
  48.8 6.8 %collective-permute-start.12 = (f32[39,8,128]{2,1,0:T(8,128)S(1)}, f32[39,8,128]{2,1,0:T(8,128)S(1)}, u32[]{:S(2)}, u32[]{:S(2)}) collective-permute-start(f32[39,8,128]{2,1,0:T(8,128)S(1)} %get-tuple-element.95), channel_id=1, source_target_pairs={{0,1},{1,0},{2,3},{3,2},{4,5},{5,4},{6,7},{7,6},{8,9},{9,8},{10,11... | collective-permute-start | bytes 479240 | tf_op jit(solution)/shard_map/ppermute | solution.py:542

commit v9 on v8

--- a/solution.py
+++ b/solution.py
@@ -556,7 +556,7 @@
         planes_kernel,
         in_specs=[pl.BlockSpec(memory_space=pltpu.HBM)] * 2,
         out_specs=[VMEM] * 2,
-        out_shape=[S(held_planes, rows, lanes)] * 2,
+        out_shape=[S(held_planes + 2, rows, lanes)] * 2,
         scratch_shapes=[V(2, 3, PX, rows, lanes), pltpu.SemaphoreType.DMA((6,))],
         compiler_params=params(24),
         name="pack_planes",
@@ -586,6 +586,7 @@
     held = (u, e, r, ga, gb, fc)
     shapes = [two] * 3 + [one] * 2 + [coarser]
     xlo, xhi, held = lax.optimization_barrier((xlo, xhi, held))
+    xlo, xhi = xlo[:held_planes], xhi[:held_planes]
     c_chip, c_next = rows_step(
         *pl.pallas_call(
             pack_corners_kernel,

time: 58.3 us -> 59 us (1.012)
  the two profiles are of different devices: /device:TPU:56 before, /device:TPU:120 now
where the time goes in v9:
time: 59 us; the launch traced here: 58.1 us
  waiting for transfers between devices  22.5 us (38%)
  Pallas kernels  17.6 us (30%)
  starting transfers between devices  15.1 us (26%)
  local copies, waits for them, and re-layouts  1.94 us (3%)
  between operations  0.87 us (1%)
    ppermute x4, waiting for transfers between devices, rows_step(): lax.ppermute(other, ('gx', 'gy'), next_chip)  12.9 us
    ppermute x4, starting transfers between devices, rows_step(): lax.ppermute(other, ('gx', 'gy'), next_chip)  7.18 us
    ppermute x3, waiting for transfers between devices, planes_step(): lax.ppermute(first, 'gx', [((i + 1) % xdev, i) for i in range(xdev)])  5.34 us
    ppermute x3, starting transfers between devices, planes_step(): lax.ppermute(last, 'gx', [(i, (i + 1) % xdev) for i in range(xdev)])  4.86 us
    ppermute x3, waiting for transfers between devices, planes_step(): lax.ppermute(last, 'gx', [(i, (i + 1) % xdev) for i in range(xdev)])  3.79 us
    pallas_call x1, Pallas kernels, body(): pl.pallas_call(functools.partial(faces_kernel, xsize, ysize), in_specs=[S...  3.04 us
    pallas_call x1, Pallas kernels, body(): pl.pallas_call(inner_kernel, in_specs=[VMEM] * 5, out_specs=[VMEM] * 3, o...  2.71 us
    ppermute x3, starting transfers between devices, planes_step(): lax.ppermute(first, 'gx', [((i + 1) % xdev, i) for i in range(xdev)])  2.69 us
  transfers between devices with their start and end apart: 14, of which 8 were waited for; matrix products, arithmetic and copies ran while one was open for 3% of the time, Pallas kernels for 16%

profile of v9, /device:TPU:120, one launch (start us, length us, event | category | flops | bytes accessed | tf_op | source)
XLA Modules:
  0.0 58.1 jit_solution(9596347421629374648)
XLA Ops:
  0.7 1.9 %pack_planes.1 = (f32[7,32,256]{2,1,0:T(8,128)S(1)}, f32[7,32,256]{2,1,0:T(8,128)}) custom-call(f32[2,32,32,256]{3,2,1,0:T(8,128)} %f.3, f32[32,32,256]{2,1,0:T(8,128)} %c.3), custom_call_target="tpu_custom_call" | custom-call | tf_op jit(solution)/shard_map/pack_planes/pallas_call | solution.py:555
  2.6 3.2 %collective-permute-start = (f32[7,32,256]{2,1,0:T(8,128)}, f32[7,32,256]{2,1,0:T(8,128)}, u32[]{:S(2)}, u32[]{:S(2)}) collective-permute-start(f32[7,32,256]{2,1,0:T(8,128)} %get-tuple-element.50), channel_id=1, source_target_pairs={{0,32},{32,64},{64,96},{96,128},{128,160},{160,192},{192,224},{224... | collective-permute-start | bytes 688136 | tf_op jit(solution)/shard_map/ppermute | solution.py:532
  5.9 1.2 %first_iterate.1 = (f32[2,36,2,48,128]{4,3,2,1,0:T(8,128)S(1)}, f32[36,2,48,128]{3,2,1,0:T(8,128)S(1)}, f32[36,2,48,128]{3,2,1,0:T(8,128)S(1)}, f32[32,8,256]{2,1,0:T(8,128)S(1)}, f32[32,8,256]{2,1,0:T(8,128)S(1)}) custom-call(s32[2]{0:T(128)S(1)} %pad_add_fusion.place, f32[2,32,32,256]{3,2,1,0:T(8,128)S(1)} %copy-done, f32[32,32,256]{2,1,0:T(8,128)S(1)} %copy-done.1), custom_call_target="tpu_custom_call" | custom-call | flops 30000000 | bytes 8000000 | tf_op jit(solution)/shard_map/first_iterate/pallas_call | solution.py:566
  7.1 3.0 %collective-permute-start.3 = (f32[32,8,256]{2,1,0:T(8,128)S(1)}, f32[32,8,256]{2,1,0:T(8,128)S(1)}, u32[]{:S(2)}, u32[]{:S(2)}) collective-permute-start(f32[32,8,256]{2,1,0:T(8,128)S(1)} %get-tuple-element.69), channel_id=1, source_target_pairs={{0,32},{1,2},{2,1},{3,4},{4,3},{5,6},{6,5},{7,8},{8,7},{9,10},{10,... | collective-permute-start | bytes 786440 | tf_op jit(solution)/shard_map/ppermute | solution.py:542
  10.2 2.7 %inner_cells.1 = (f32[2,36,2,48,128]{4,3,2,1,0:T(8,128)S(1)}, f32[2,36,2,48,128]{4,3,2,1,0:T(8,128)S(1)}, f32[3,16,16,128]{3,2,1,0:T(8,128)S(1)}) custom-call(f32[2,32,32,256]{3,2,1,0:T(8,128)S(1)} %copy-done, f32[32,32,256]{2,1,0:T(8,128)S(1)} %copy-done.1, f32[2,36,2,48,128]{4,3,2,1,0:T(8,128)S(1)} %get-tuple-element.60.u.u_in, ...), custom_call_target="tpu_custom_call" | custom-call | flops 70000000 | bytes 16000000 | tf_op jit(solution)/shard_map/inner_cells/pallas_call | solution.py:576
  12.9 1.2 %collective-permute-done.1 = f32[7,32,256]{2,1,0:T(8,128)} collective-permute-done((f32[7,32,256]{2,1,0:T(8,128)S(1)}, f32[7,32,256]{2,1,0:T(8,128)}, u32[]{:S(2)}, u32[]{:S(2)}) %collective-permute-start.1) | collective-permute-done | bytes 229408 | tf_op jit(solution)/shard_map/ppermute | solution.py:533
  14.2 0.9 %slice.90.xlo = f32[5,32,256]{2,1,0:T(8,128)S(1)} slice(f32[7,32,256]{2,1,0:T(8,128)} %collective-permute-done), slice={[0:5], [0:32], [0:256]} | slice | bytes 327680 | tf_op jit(solution)/shard_map/slice | solution.py:589
  15.1 0.9 %slice.91.xhi = f32[5,32,256]{2,1,0:T(8,128)S(1)} slice(f32[7,32,256]{2,1,0:T(8,128)} %collective-permute-done.1), slice={[0:5], [0:32], [0:256]} | slice | bytes 327680 | tf_op jit(solution)/shard_map/slice | solution.py:589
  16.0 0.6 %pack_corners.1 = (f32[10,4,256]{2,1,0:T(4,128)S(1)}, f32[10,4,256]{2,1,0:T(4,128)S(1)}) custom-call(s32[2]{0:T(128)S(1)} %pad_add_fusion.place, f32[5,32,256]{2,1,0:T(8,128)S(1)} %slice.90.xlo, f32[5,32,256]{2,1,0:T(8,128)S(1)} %slice.91.xhi), custom_call_target="tpu_custom_call" | custom-call | tf_op jit(solution)/shard_map/pack_corners/pallas_call | solution.py:591
  16.8 3.0 %collective-permute-start.5 = (f32[10,4,256]{2,1,0:T(4,128)S(1)}, f32[10,4,256]{2,1,0:T(4,128)S(1)}, u32[]{:S(2)}, u32[]{:S(2)}) collective-permute-start(f32[10,4,256]{2,1,0:T(4,128)S(1)} %get-tuple-element.77), channel_id=1, source_target_pairs={{0,32},{1,2},{2,1},{3,4},{4,3},{5,6},{6,5},{7,8},{8,7},{9,10},{10,... | collective-permute-start | bytes 122888 | tf_op jit(solution)/shard_map/ppermute | solution.py:542
  19.8 3.0 %face_cells.1 = (f32[2,36,2,48,128]{4,3,2,1,0:T(8,128)S(1)}, f32[2,36,2,48,128]{4,3,2,1,0:T(8,128)S(1)}, f32[2,36,2,48,128]{4,3,2,1,0:T(8,128)S(1)}, f32[36,2,48...) custom-call(s32[2]{0:T(128)S(1)} %pad_add_fusion.place, ...), custom_call_target="tpu_custom_call", output_to_operand_aliasing={{0}: (1, {}), {1}: (2, {}), {2}: (3, {}), {3}: (4, {}), {4}... | custom-call | flops 50000000 | bytes 8000000 | tf_op jit(solution)/shard_map/face_cells/pallas_call | solution.py:602
  22.9 1.1 %corner_cells.1 = (f32[2,36,2,48,128]{4,3,2,1,0:T(8,128)S(1)}, f32[2,36,2,48,128]{4,3,2,1,0:T(8,128)S(1)}, f32[2,36,2,48,128]{4,3,2,1,0:T(8,128)S(1)}, f32[36,2,...) custom-call(s32[2]{0:T(128)S(1)} %pad_add_fusion.place, ...), custom_call_target="tpu_custom_call", output_to_operand_aliasing={{0}: (1, {}), {1}: (2, {}), {2}: (3, {}), {3}: (4, {}), {4}... | custom-call | tf_op jit(solution)/shard_map/corner_cells/pallas_call | solution.py:613
  24.0 1.6 %collective-permute-start.6 = (f32[17,16,128]{2,1,0:T(8,128)S(1)}, f32[17,16,128]{2,1,0:T(8,128)S(1)}, u32[]{:S(2)}, u32[]{:S(2)}) collective-permute-start(f32[17,16,128]{2,1,0:T(8,128)S(1)} %pad_maximum_fusion), channel_id=1, source_target_pairs={{0,32},{32,64},{64,96},{96,128},{128,160},{160,192},{192,224},{224... | collective-permute-start | bytes 417800 | tf_op jit(solution)/shard_map/ppermute | solution.py:532
  26.2 1.6 %fine_iterate.1 = f32[2,32,32,256]{3,2,1,0:T(8,128)} custom-call(f32[2,36,2,48,128]{4,3,2,1,0:T(8,128)S(1)} %get-tuple-element.80.u, f32[2,36,2,48,128]{4,3,2,1,0:T(8,128)S(1)} %get-tuple-element.81.e), custom_call_target="tpu_custom_call" | custom-call | flops 1000000 | bytes 8000000 | tf_op jit(solution)/shard_map/fine_iterate/pallas_call | solution.py:628
  27.9 1.3 %collective-permute-done.6.xlo = f32[17,16,128]{2,1,0:T(8,128)S(1)} collective-permute-done((f32[17,16,128]{2,1,0:T(8,128)S(1)}, f32[17,16,128]{2,1,0:T(8,128)S(1)}, u32[]{:S(2)}, u32[]{:S(2)}) %collective-permute-start.6) | collective-permute-done | bytes 139296 | tf_op jit(solution)/shard_map/ppermute | solution.py:532
  29.2 2.8 %collective-permute-done.7.xhi = f32[17,16,128]{2,1,0:T(8,128)S(1)} collective-permute-done((f32[17,16,128]{2,1,0:T(8,128)S(1)}, f32[17,16,128]{2,1,0:T(8,128)S(1)}, u32[]{:S(2)}, u32[]{:S(2)}) %collective-permute-start.7) | collective-permute-done | bytes 139296 | tf_op jit(solution)/shard_map/ppermute | solution.py:533
  32.7 1.0 %collective-permute-start.9 = (f32[2,26,8,128]{3,2,1,0:T(8,128)S(1)}, f32[2,26,8,128]{3,2,1,0:T(8,128)S(1)}, u32[]{:S(2)}, u32[]{:S(2)}) collective-permute-start(f32[2,26,8,128]{3,2,1,0:T(8,128)S(1)} %get-tuple-element.87), channel_id=1, source_target_pairs={{0,32},{1,2},{2,1},{3,4},{4,3},{5,6},{6,5},{7,8},{8,7},{9,10},{10,... | collective-permute-start | bytes 638984 | tf_op jit(solution)/shard_map/ppermute | solution.py:542
  34.2 6.2 %collective-permute-done.9.y_next = f32[2,26,8,128]{3,2,1,0:T(8,128)S(1)} collective-permute-done((f32[2,26,8,128]{3,2,1,0:T(8,128)S(1)}, f32[2,26,8,128]{3,2,1,0:T(8,128)S(1)}, u32[]{:S(2)}, u32[]{:S(2)}) %collective-permute-start.9) | collective-permute-done | bytes 213024 | tf_op jit(solution)/shard_map/ppermute | solution.py:542
  40.4 2.1 %second_level.1 = (f32[2,16,16,128]{3,2,1,0:T(8,128)}, f32[15,10,128]{2,1,0:T(8,128)S(1)}) custom-call(s32[2]{0:T(128)S(1)} %pad_add_fusion.place, f32[3,26,16,128]{3,2,1,0:T(8,128)S(1)} %get-tuple-element.85.window, f32[2,26,8,128]{3,2,1,0:T(8,128)S(1)} %collective-permute-done.8.y_chip, f32[2,26,8,128]{3,2,1,0:T(8,128)S(1)} %collective-permute-done.9.y_next), custom_call_target="tpu_custom_call" | custom-call | tf_op jit(solution)/shard_map/second_level/pallas_call | solution.py:650
  42.6 2.1 %collective-permute-start.11 = (f32[12,10,128]{2,1,0:T(8,128)S(1)}, f32[12,10,128]{2,1,0:T(8,128)S(1)}, u32[]{:S(2)}, u32[]{:S(2)}) collective-permute-start(f32[12,10,128]{2,1,0:T(8,128)S(1)} %pad_maximum_fusion.3), channel_id=1, source_target_pairs={{32,0},{64,32},{96,64},{128,96},{160,128},{192,160},{224,192},{0,2... | collective-permute-start | bytes 184328 | tf_op jit(solution)/shard_map/ppermute | solution.py:533
  44.7 2.5 %collective-permute-done.10.xlo = f32[12,10,128]{2,1,0:T(8,128)S(1)} collective-permute-done((f32[12,10,128]{2,1,0:T(8,128)S(1)}, f32[12,10,128]{2,1,0:T(8,128)S(1)}, u32[]{:S(2)}, u32[]{:S(2)}) %collective-permute-start.10) | collective-permute-done | bytes 61472 | tf_op jit(solution)/shard_map/ppermute | solution.py:532
  47.2 1.3 %collective-permute-done.11.xhi = f32[12,10,128]{2,1,0:T(8,128)S(1)} collective-permute-done((f32[12,10,128]{2,1,0:T(8,128)S(1)}, f32[12,10,128]{2,1,0:T(8,128)S(1)}, u32[]{:S(2)}, u32[]{:S(2)}) %collective-permute-start.11) | collective-permute-done | bytes 61472 | tf_op jit(solution)/shard_map/ppermute | solution.py:533
  48.8 6.7 %collective-permute-done.13.y_next = f32[39,8,128]{2,1,0:T(8,128)S(1)} collective-permute-done((f32[39,8,128]{2,1,0:T(8,128)S(1)}, f32[39,8,128]{2,1,0:T(8,128)S(1)}, u32[]{:S(2)}, u32[]{:S(2)}) %collective-permute-start.13) | collective-permute-done | bytes 159776 | tf_op jit(solution)/shard_map/ppermute | solution.py:542
  55.5 2.7 %coarse_levels.1 = (f32[2,8,8,64]{3,2,1,0:T(8,128)}, f32[2,4,4,32]{3,2,1,0:T(4,128)}) custom-call(s32[2]{0:T(128)S(1)} %pad_add_fusion.place, f32[15,10,128]{2,1,0:T(8,128)S(1)} %get-tuple-element.89.fc_own, f32[12,10,128]{2,1,0:T(8,128)S(1)} %collective-permute-done.10.xlo, f32[12,10,128]{2,1,0:T(8,128)S(1)} %collective-permute-done.11.xhi, ...), custom_call_target="tpu_custom_call" | custom-call | tf_op jit(solution)/shard_map/coarse_levels/pallas_call | solution.py:675
  (36 shorter events, 2.5 us)
Async XLA Ops:
  0.6 5.2 %copy-start.1 = (f32[32,32,256]{2,1,0:T(8,128)S(1)}, f32[32,32,256]{2,1,0:T(8,128)}, u32[]{:S(2)}) copy-start(f32[32,32,256]{2,1,0:T(8,128)} %c.3) | copy-start | bytes 3145732
  0.6 5.2 %copy-start = (f32[2,32,32,256]{3,2,1,0:T(8,128)S(1)}, f32[2,32,32,256]{3,2,1,0:T(8,128)}, u32[]{:S(2)}) copy-start(f32[2,32,32,256]{3,2,1,0:T(8,128)} %f.3) | copy-start | bytes 6291460
  2.6 10.3 %collective-permute-start = (f32[7,32,256]{2,1,0:T(8,128)}, f32[7,32,256]{2,1,0:T(8,128)}, u32[]{:S(2)}, u32[]{:S(2)}) collective-permute-start(f32[7,32,256]{2,1,0:T(8,128)} %get-tuple-element.50), channel_id=1, source_target_pairs={{0,32},{32,64},{64,96},{96,128},{128,160},{160,192},{192,224},{224... | collective-permute-start | bytes 688136 | tf_op jit(solution)/shard_map/ppermute | solution.py:532
  5.8 8.4 %collective-permute-start.1 = (f32[7,32,256]{2,1,0:T(8,128)S(1)}, f32[7,32,256]{2,1,0:T(8,128)}, u32[]{:S(2)}, u32[]{:S(2)}) collective-permute-start(f32[7,32,256]{2,1,0:T(8,128)S(1)} %get-tuple-element.51), channel_id=1, source_target_pairs={{32,0},{64,32},{96,64},{128,96},{160,128},{192,160},{224,192},{0,2... | collective-permute-start | bytes 688136 | tf_op jit(solution)/shard_map/ppermute | solution.py:533
  7.0 12.8 %collective-permute-start.2 = (f32[32,8,256]{2,1,0:T(8,128)S(1)}, f32[32,8,256]{2,1,0:T(8,128)S(1)}, u32[]{:S(2)}, u32[]{:S(2)}) collective-permute-start(f32[32,8,256]{2,1,0:T(8,128)S(1)} %get-tuple-element.68), channel_id=1, source_target_pairs={{0,1},{1,0},{2,3},{3,2},{4,5},{5,4},{6,7},{7,6},{8,9},{9,8},{10,11... | collective-permute-start | bytes 786440 | tf_op jit(solution)/shard_map/ppermute | solution.py:542
  7.1 12.7 %collective-permute-start.3 = (f32[32,8,256]{2,1,0:T(8,128)S(1)}, f32[32,8,256]{2,1,0:T(8,128)S(1)}, u32[]{:S(2)}, u32[]{:S(2)}) collective-permute-start(f32[32,8,256]{2,1,0:T(8,128)S(1)} %get-tuple-element.69), channel_id=1, source_target_pairs={{0,32},{1,2},{2,1},{3,4},{4,3},{5,6},{6,5},{7,8},{8,7},{9,10},{10,... | collective-permute-start | bytes 786440 | tf_op jit(solution)/shard_map/ppermute | solution.py:542
  16.7 6.2 %collective-permute-start.4 = (f32[10,4,256]{2,1,0:T(4,128)S(1)}, f32[10,4,256]{2,1,0:T(4,128)S(1)}, u32[]{:S(2)}, u32[]{:S(2)}) collective-permute-start(f32[10,4,256]{2,1,0:T(4,128)S(1)} %get-tuple-element.76), channel_id=1, source_target_pairs={{0,1},{1,0},{2,3},{3,2},{4,5},{5,4},{6,7},{7,6},{8,9},{9,8},{10,11... | collective-permute-start | bytes 122888 | tf_op jit(solution)/shard_map/ppermute | solution.py:542
  16.8 6.1 %collective-permute-start.5 = (f32[10,4,256]{2,1,0:T(4,128)S(1)}, f32[10,4,256]{2,1,0:T(4,128)S(1)}, u32[]{:S(2)}, u32[]{:S(2)}) collective-permute-start(f32[10,4,256]{2,1,0:T(4,128)S(1)} %get-tuple-element.77), channel_id=1, source_target_pairs={{0,32},{1,2},{2,1},{3,4},{4,3},{5,6},{6,5},{7,8},{8,7},{9,10},{10,... | collective-permute-start | bytes 122888 | tf_op jit(solution)/shard_map/ppermute | solution.py:542
  24.0 5.1 %collective-permute-start.6 = (f32[17,16,128]{2,1,0:T(8,128)S(1)}, f32[17,16,128]{2,1,0:T(8,128)S(1)}, u32[]{:S(2)}, u32[]{:S(2)}) collective-permute-start(f32[17,16,128]{2,1,0:T(8,128)S(1)} %pad_maximum_fusion), channel_id=1, source_target_pairs={{0,32},{32,64},{64,96},{96,128},{128,160},{160,192},{192,224},{224... | collective-permute-start | bytes 417800 | tf_op jit(solution)/shard_map/ppermute | solution.py:532
  25.6 6.3 %collective-permute-start.7 = (f32[17,16,128]{2,1,0:T(8,128)S(1)}, f32[17,16,128]{2,1,0:T(8,128)S(1)}, u32[]{:S(2)}, u32[]{:S(2)}) collective-permute-start(f32[17,16,128]{2,1,0:T(8,128)S(1)} %pad_maximum_fusion.1), channel_id=1, source_target_pairs={{32,0},{64,32},{96,64},{128,96},{160,128},{192,160},{224,192},{0,2... | collective-permute-start | bytes 417800 | tf_op jit(solution)/shard_map/ppermute | solution.py:533
  32.6 1.6 %collective-permute-start.8 = (f32[2,26,8,128]{3,2,1,0:T(8,128)S(1)}, f32[2,26,8,128]{3,2,1,0:T(8,128)S(1)}, u32[]{:S(2)}, u32[]{:S(2)}) collective-permute-start(f32[2,26,8,128]{3,2,1,0:T(8,128)S(1)} %get-tuple-element.86), channel_id=1, source_target_pairs={{0,1},{1,0},{2,3},{3,2},{4,5},{5,4},{6,7},{7,6},{8,9},{9,8},{10,11... | collective-permute-start | bytes 638984 | tf_op jit(solution)/shard_map/ppermute | solution.py:542
  32.7 7.6 %collective-permute-start.9 = (f32[2,26,8,128]{3,2,1,0:T(8,128)S(1)}, f32[2,26,8,128]{3,2,1,0:T(8,128)S(1)}, u32[]{:S(2)}, u32[]{:S(2)}) collective-permute-start(f32[2,26,8,128]{3,2,1,0:T(8,128)S(1)} %get-tuple-element.87), channel_id=1, source_target_pairs={{0,32},{1,2},{2,1},{3,4},{4,3},{5,6},{6,5},{7,8},{8,7},{9,10},{10,... | collective-permute-start | bytes 638984 | tf_op jit(solution)/shard_map/ppermute | solution.py:542
  42.5 4.7 %collective-permute-start.10 = (f32[12,10,128]{2,1,0:T(8,128)S(1)}, f32[12,10,128]{2,1,0:T(8,128)S(1)}, u32[]{:S(2)}, u32[]{:S(2)}) collective-permute-start(f32[12,10,128]{2,1,0:T(8,128)S(1)} %pad_maximum_fusion.2), channel_id=1, source_target_pairs={{0,32},{32,64},{64,96},{96,128},{128,160},{160,192},{192,224},{224... | collective-permute-start | bytes 184328 | tf_op jit(solution)/shard_map/ppermute | solution.py:532
  42.6 5.9 %collective-permute-start.11 = (f32[12,10,128]{2,1,0:T(8,128)S(1)}, f32[12,10,128]{2,1,0:T(8,128)S(1)}, u32[]{:S(2)}, u32[]{:S(2)}) collective-permute-start(f32[12,10,128]{2,1,0:T(8,128)S(1)} %pad_maximum_fusion.3), channel_id=1, source_target_pairs={{32,0},{64,32},{96,64},{128,96},{160,128},{192,160},{224,192},{0,2... | collective-permute-start | bytes 184328 | tf_op jit(solution)/shard_map/ppermute | solution.py:533
  48.6 6.9 %collective-permute-start.13 = (f32[39,8,128]{2,1,0:T(8,128)S(1)}, f32[39,8,128]{2,1,0:T(8,128)S(1)}, u32[]{:S(2)}, u32[]{:S(2)}) collective-permute-start(f32[39,8,128]{2,1,0:T(8,128)S(1)} %get-tuple-element.94), channel_id=1, source_target_pairs={{0,32},{1,2},{2,1},{3,4},{4,3},{5,6},{6,5},{7,8},{8,7},{9,10},{10,... | collective-permute-start | bytes 479240 | tf_op jit(solution)/shard_map/ppermute | solution.py:542
  48.7 6.8 %collective-permute-start.12 = (f32[39,8,128]{2,1,0:T(8,128)S(1)}, f32[39,8,128]{2,1,0:T(8,128)S(1)}, u32[]{:S(2)}, u32[]{:S(2)}) collective-permute-start(f32[39,8,128]{2,1,0:T(8,128)S(1)} %get-tuple-element.95), channel_id=1, source_target_pairs={{0,1},{1,0},{2,3},{3,2},{4,5},{5,4},{6,7},{7,6},{8,9},{9,8},{10,11... | collective-permute-start | bytes 479240 | tf_op jit(solution)/shard_map/ppermute | solution.py:542

commit v10 on v9

--- a/solution.py
+++ b/solution.py
@@ -253,7 +253,8 @@
     cut = [pl.ds(LANES * h, LANES) for h in range(halves)]
     ok = inside(place, n, rows, xsize, ysize)
     del u_in, e_in, r_in, ga_in, gb_in, fc_in
-    copies = [pltpu.make_async_copy(src, sides.at[i], sems.at[i]) for i, src in enumerate((xlo, xhi))]
+    used = pl.ds(0, 2 * PX + 1)
+    copies = [pltpu.make_async_copy(src.at[used], sides.at[i], sems.at[i]) for i, src in enumerate((xlo, xhi))]
     for copy in copies:
         copy.start()
     low, high = PY - 4, PY + rows - 4
@@ -321,11 +322,11 @@
 
 
 def pack_corners_kernel(place, xlo, xhi, chip, other, tiles, sems):
-    count, rows = xlo.shape[:2]
+    count, rows = 2 * PX + 1, xlo.shape[1]
     copies = []
     for i, side in enumerate((xlo, xhi)):
         for j, row in enumerate((0, rows - 8)):
-            copies.append(pltpu.make_async_copy(side.at[:, pl.ds(row, 8)], tiles.at[j, pl.ds(count * i, count)], sems.at[2 * i + j]))
+            copies.append(pltpu.make_async_copy(side.at[pl.ds(0, count), pl.ds(row, 8)], tiles.at[j, pl.ds(count * i, count)], sems.at[2 * i + j]))
     for copy in copies:
         copy.start()
     even = is_even(place, (4, xlo.shape[2]))
@@ -586,7 +587,6 @@
     held = (u, e, r, ga, gb, fc)
     shapes = [two] * 3 + [one] * 2 + [coarser]
     xlo, xhi, held = lax.optimization_barrier((xlo, xhi, held))
-    xlo, xhi = xlo[:held_planes], xhi[:held_planes]
     c_chip, c_next = rows_step(
         *pl.pallas_call(
             pack_corners_kernel,

time: 59 us -> 57.9 us (0.981)
  local copies, waits for them, and re-layouts: 1.94 us -> 0.09 us
  Pallas kernels: 17.6 us -> 18.7 us
    slice x2 -> x0, local copies, waits for them, and re-layouts: 1.86 us -> none  [body(): xlo, xhi = (xlo[:held_planes], xhi[:held_planes])]
    pallas_call x1, Pallas kernels: 0.65 us -> 1.41 us  [body(): pl.pallas_call(pack_corners_kernel, in_specs=[SMEM] + [ANY] * 2, out_spec...]
  transfers between devices with their start and end apart: 14 -> 14, of which waited for: 8 -> 8; matrix products, arithmetic and copies ran while one was open for 3% -> 0% of each run, Pallas kernels for 16% -> 18%
where the time goes in v10:
time: 57.9 us; the launch traced here: 57.1 us
  waiting for transfers between devices  22 us (38%)
  Pallas kernels  18.7 us (32%)
  starting transfers between devices  15.3 us (26%)
  between operations  0.86 us (1%)
    ppermute x4, waiting for transfers between devices, rows_step(): lax.ppermute(other, ('gx', 'gy'), next_chip)  12.9 us
    ppermute x4, starting transfers between devices, rows_step(): lax.ppermute(other, ('gx', 'gy'), next_chip)  7.37 us
    ppermute x3, waiting for transfers between devices, planes_step(): lax.ppermute(first, 'gx', [((i + 1) % xdev, i) for i in range(xdev)])  5.05 us
    ppermute x3, starting transfers between devices, planes_step(): lax.ppermute(last, 'gx', [(i, (i + 1) % xdev) for i in range(xdev)])  4.36 us
    ppermute x3, waiting for transfers between devices, planes_step(): lax.ppermute(last, 'gx', [(i, (i + 1) % xdev) for i in range(xdev)])  3.79 us
    pallas_call x1, Pallas kernels, body(): pl.pallas_call(functools.partial(faces_kernel, xsize, ysize), in_specs=[S...  3.34 us
    ppermute x3, starting transfers between devices, planes_step(): lax.ppermute(first, 'gx', [((i + 1) % xdev, i) for i in range(xdev)])  3.19 us
    pallas_call x1, Pallas kernels, body(): pl.pallas_call(inner_kernel, in_specs=[VMEM] * 5, out_specs=[VMEM] * 3, o...  2.71 us
  transfers between devices with their start and end apart: 14, of which 8 were waited for; matrix products, arithmetic and copies ran while one was open for 0% of the time, Pallas kernels for 18%

profile of v10, /device:TPU:120, one launch (start us, length us, event | category | flops | bytes accessed | tf_op | source)
XLA Modules:
  0.0 57.1 jit_solution(8303497200327896719)
XLA Ops:
  0.7 2.0 %pack_planes.1 = (f32[7,32,256]{2,1,0:T(8,128)}, f32[7,32,256]{2,1,0:T(8,128)}) custom-call(f32[2,32,32,256]{3,2,1,0:T(8,128)} %f.3, f32[32,32,256]{2,1,0:T(8,128)} %c.3), custom_call_target="tpu_custom_call" | custom-call | tf_op jit(solution)/shard_map/pack_planes/pallas_call | solution.py:556
  2.6 3.2 %collective-permute-start = (f32[7,32,256]{2,1,0:T(8,128)}, f32[7,32,256]{2,1,0:T(8,128)S(1)}, u32[]{:S(2)}, u32[]{:S(2)}) collective-permute-start(f32[7,32,256]{2,1,0:T(8,128)} %get-tuple-element.50), channel_id=1, source_target_pairs={{0,32},{32,64},{64,96},{96,128},{128,160},{160,192},{192,224},{224... | collective-permute-start | bytes 688136 | tf_op jit(solution)/shard_map/ppermute | solution.py:533
  5.9 1.2 %first_iterate.1 = (f32[2,36,2,48,128]{4,3,2,1,0:T(8,128)S(1)}, f32[36,2,48,128]{3,2,1,0:T(8,128)S(1)}, f32[36,2,48,128]{3,2,1,0:T(8,128)S(1)}, f32[32,8,256]{2,1,0:T(8,128)S(1)}, f32[32,8,256]{2,1,0:T(8,128)S(1)}) custom-call(s32[2]{0:T(128)S(1)} %pad_add_fusion.place, f32[2,32,32,256]{3,2,1,0:T(8,128)S(1)} %copy-done, f32[32,32,256]{2,1,0:T(8,128)S(1)} %copy-done.1), custom_call_target="tpu_custom_call" | custom-call | flops 30000000 | bytes 8000000 | tf_op jit(solution)/shard_map/first_iterate/pallas_call | solution.py:567
  7.2 3.0 %collective-permute-start.3 = (f32[32,8,256]{2,1,0:T(8,128)S(1)}, f32[32,8,256]{2,1,0:T(8,128)S(1)}, u32[]{:S(2)}, u32[]{:S(2)}) collective-permute-start(f32[32,8,256]{2,1,0:T(8,128)S(1)} %get-tuple-element.69), channel_id=1, source_target_pairs={{0,32},{1,2},{2,1},{3,4},{4,3},{5,6},{6,5},{7,8},{8,7},{9,10},{10,... | collective-permute-start | bytes 786440 | tf_op jit(solution)/shard_map/ppermute | solution.py:543
  10.2 2.7 %inner_cells.1 = (f32[2,36,2,48,128]{4,3,2,1,0:T(8,128)S(1)}, f32[2,36,2,48,128]{4,3,2,1,0:T(8,128)S(1)}, f32[3,16,16,128]{3,2,1,0:T(8,128)S(1)}) custom-call(f32[2,32,32,256]{3,2,1,0:T(8,128)S(1)} %copy-done, f32[32,32,256]{2,1,0:T(8,128)S(1)} %copy-done.1, f32[2,36,2,48,128]{4,3,2,1,0:T(8,128)S(1)} %get-tuple-element.60.u.u_in, ...), custom_call_target="tpu_custom_call" | custom-call | flops 70000000 | bytes 16000000 | tf_op jit(solution)/shard_map/inner_cells/pallas_call | solution.py:577
  13.0 1.5 %collective-permute-done.1.xhi = f32[7,32,256]{2,1,0:T(8,128)} collective-permute-done((f32[7,32,256]{2,1,0:T(8,128)}, f32[7,32,256]{2,1,0:T(8,128)}, u32[]{:S(2)}, u32[]{:S(2)}) %collective-permute-start.1) | collective-permute-done | bytes 229408 | tf_op jit(solution)/shard_map/ppermute | solution.py:534
  14.4 1.4 %pack_corners.1 = (f32[10,4,256]{2,1,0:T(4,128)S(1)}, f32[10,4,256]{2,1,0:T(4,128)S(1)}) custom-call(s32[2]{0:T(128)S(1)} %pad_add_fusion.place, f32[7,32,256]{2,1,0:T(8,128)S(1)} %collective-permute-done.xlo, f32[7,32,256]{2,1,0:T(8,128)} %collective-permute-done.1.xhi), custom_call_target="tpu_custom_call" | custom-call | tf_op jit(solution)/shard_map/pack_corners/pallas_call | solution.py:591
  15.9 3.0 %collective-permute-start.5 = (f32[10,4,256]{2,1,0:T(4,128)S(1)}, f32[10,4,256]{2,1,0:T(4,128)S(1)}, u32[]{:S(2)}, u32[]{:S(2)}) collective-permute-start(f32[10,4,256]{2,1,0:T(4,128)S(1)} %get-tuple-element.77), channel_id=1, source_target_pairs={{0,32},{1,2},{2,1},{3,4},{4,3},{5,6},{6,5},{7,8},{8,7},{9,10},{10,... | collective-permute-start | bytes 122888 | tf_op jit(solution)/shard_map/ppermute | solution.py:543
  19.0 3.3 %face_cells.1 = (f32[2,36,2,48,128]{4,3,2,1,0:T(8,128)S(1)}, f32[2,36,2,48,128]{4,3,2,1,0:T(8,128)S(1)}, f32[2,36,2,48,128]{4,3,2,1,0:T(8,128)S(1)}, f32[36,2,48...) custom-call(s32[2]{0:T(128)S(1)} %pad_add_fusion.place, ...), custom_call_target="tpu_custom_call", output_to_operand_aliasing={{0}: (1, {}), {1}: (2, {}), {2}: (3, {}), {3}: (4, {}), {4}... | custom-call | flops 50000000 | bytes 8000000 | tf_op jit(solution)/shard_map/face_cells/pallas_call | solution.py:602
  22.3 1.1 %corner_cells.1 = (f32[2,36,2,48,128]{4,3,2,1,0:T(8,128)S(1)}, f32[2,36,2,48,128]{4,3,2,1,0:T(8,128)S(1)}, f32[2,36,2,48,128]{4,3,2,1,0:T(8,128)S(1)}, f32[36,2,...) custom-call(s32[2]{0:T(128)S(1)} %pad_add_fusion.place, ...), custom_call_target="tpu_custom_call", output_to_operand_aliasing={{0}: (1, {}), {1}: (2, {}), {2}: (3, {}), {3}: (4, {}), {4}... | custom-call | tf_op jit(solution)/shard_map/corner_cells/pallas_call | solution.py:613
  23.5 1.1 %collective-permute-start.6 = (f32[17,16,128]{2,1,0:T(8,128)S(1)}, f32[17,16,128]{2,1,0:T(8,128)S(1)}, u32[]{:S(2)}, u32[]{:S(2)}) collective-permute-start(f32[17,16,128]{2,1,0:T(8,128)S(1)} %pad_maximum_fusion), channel_id=1, source_target_pairs={{0,32},{32,64},{64,96},{96,128},{128,160},{160,192},{192,224},{224... | collective-permute-start | bytes 417800 | tf_op jit(solution)/shard_map/ppermute | solution.py:533
  24.6 1.1 %collective-permute-start.7 = (f32[17,16,128]{2,1,0:T(8,128)S(1)}, f32[17,16,128]{2,1,0:T(8,128)S(1)}, u32[]{:S(2)}, u32[]{:S(2)}) collective-permute-start(f32[17,16,128]{2,1,0:T(8,128)S(1)} %pad_maximum_fusion.1), channel_id=1, source_target_pairs={{32,0},{64,32},{96,64},{128,96},{160,128},{192,160},{224,192},{0,2... | collective-permute-start | bytes 417800 | tf_op jit(solution)/shard_map/ppermute | solution.py:534
  25.7 1.6 %fine_iterate.1 = f32[2,32,32,256]{3,2,1,0:T(8,128)} custom-call(f32[2,36,2,48,128]{4,3,2,1,0:T(8,128)S(1)} %get-tuple-element.80.u, f32[2,36,2,48,128]{4,3,2,1,0:T(8,128)S(1)} %get-tuple-element.81.e), custom_call_target="tpu_custom_call" | custom-call | flops 1000000 | bytes 8000000 | tf_op jit(solution)/shard_map/fine_iterate/pallas_call | solution.py:628
  27.3 1.3 %collective-permute-done.6.xlo = f32[17,16,128]{2,1,0:T(8,128)S(1)} collective-permute-done((f32[17,16,128]{2,1,0:T(8,128)S(1)}, f32[17,16,128]{2,1,0:T(8,128)S(1)}, u32[]{:S(2)}, u32[]{:S(2)}) %collective-permute-start.6) | collective-permute-done | bytes 139296 | tf_op jit(solution)/shard_map/ppermute | solution.py:533
  28.6 2.3 %collective-permute-done.7.xhi = f32[17,16,128]{2,1,0:T(8,128)S(1)} collective-permute-done((f32[17,16,128]{2,1,0:T(8,128)S(1)}, f32[17,16,128]{2,1,0:T(8,128)S(1)}, u32[]{:S(2)}, u32[]{:S(2)}) %collective-permute-start.7) | collective-permute-done | bytes 139296 | tf_op jit(solution)/shard_map/ppermute | solution.py:534
  30.9 0.6 %second_rows.1 = (f32[2,26,8,128]{3,2,1,0:T(8,128)S(1)}, f32[2,26,8,128]{3,2,1,0:T(8,128)S(1)}, f32[3,26,16,128]{3,2,1,0:T(8,128)S(1)}) custom-call(s32[2]{0:T(128)S(1)} %pad_add_fusion.place, f32[17,16,128]{2,1,0:T(8,128)S(1)} %collective-permute-done.6.xlo, f32[3,16,16,128]{3,2,1,0:T(8,128)S(1)} %get-tuple-element.78.fc, ...), custom_call_target="tpu_custom_call" | custom-call | tf_op jit(solution)/shard_map/second_rows/pallas_call | solution.py:638
  31.6 1.2 %collective-permute-start.9 = (f32[2,26,8,128]{3,2,1,0:T(8,128)S(1)}, f32[2,26,8,128]{3,2,1,0:T(8,128)S(1)}, u32[]{:S(2)}, u32[]{:S(2)}) collective-permute-start(f32[2,26,8,128]{3,2,1,0:T(8,128)S(1)} %get-tuple-element.87), channel_id=1, source_target_pairs={{0,32},{1,2},{2,1},{3,4},{4,3},{5,6},{6,5},{7,8},{8,7},{9,10},{10,... | collective-permute-start | bytes 638984 | tf_op jit(solution)/shard_map/ppermute | solution.py:543
  33.1 6.2 %collective-permute-done.9.y_next = f32[2,26,8,128]{3,2,1,0:T(8,128)S(1)} collective-permute-done((f32[2,26,8,128]{3,2,1,0:T(8,128)S(1)}, f32[2,26,8,128]{3,2,1,0:T(8,128)S(1)}, u32[]{:S(2)}, u32[]{:S(2)}) %collective-permute-start.9) | collective-permute-done | bytes 213024 | tf_op jit(solution)/shard_map/ppermute | solution.py:543
  39.3 2.1 %second_level.1 = (f32[2,16,16,128]{3,2,1,0:T(8,128)}, f32[15,10,128]{2,1,0:T(8,128)S(1)}) custom-call(s32[2]{0:T(128)S(1)} %pad_add_fusion.place, f32[3,26,16,128]{3,2,1,0:T(8,128)S(1)} %get-tuple-element.85.window, f32[2,26,8,128]{3,2,1,0:T(8,128)S(1)} %collective-permute-done.8.y_chip, f32[2,26,8,128]{3,2,1,0:T(8,128)S(1)} %collective-permute-done.9.y_next), custom_call_target="tpu_custom_call" | custom-call | tf_op jit(solution)/shard_map/second_level/pallas_call | solution.py:650
  41.5 2.1 %collective-permute-start.11 = (f32[12,10,128]{2,1,0:T(8,128)S(1)}, f32[12,10,128]{2,1,0:T(8,128)S(1)}, u32[]{:S(2)}, u32[]{:S(2)}) collective-permute-start(f32[12,10,128]{2,1,0:T(8,128)S(1)} %pad_maximum_fusion.3), channel_id=1, source_target_pairs={{32,0},{64,32},{96,64},{128,96},{160,128},{192,160},{224,192},{0,2... | collective-permute-start | bytes 184328 | tf_op jit(solution)/shard_map/ppermute | solution.py:534
  43.6 2.5 %collective-permute-done.10.xlo = f32[12,10,128]{2,1,0:T(8,128)S(1)} collective-permute-done((f32[12,10,128]{2,1,0:T(8,128)S(1)}, f32[12,10,128]{2,1,0:T(8,128)S(1)}, u32[]{:S(2)}, u32[]{:S(2)}) %collective-permute-start.10) | collective-permute-done | bytes 61472 | tf_op jit(solution)/shard_map/ppermute | solution.py:533
  46.1 1.3 %collective-permute-done.11.xhi = f32[12,10,128]{2,1,0:T(8,128)S(1)} collective-permute-done((f32[12,10,128]{2,1,0:T(8,128)S(1)}, f32[12,10,128]{2,1,0:T(8,128)S(1)}, u32[]{:S(2)}, u32[]{:S(2)}) %collective-permute-start.11) | collective-permute-done | bytes 61472 | tf_op jit(solution)/shard_map/ppermute | solution.py:534
  47.7 6.7 %collective-permute-done.13.y_next = f32[39,8,128]{2,1,0:T(8,128)S(1)} collective-permute-done((f32[39,8,128]{2,1,0:T(8,128)S(1)}, f32[39,8,128]{2,1,0:T(8,128)S(1)}, u32[]{:S(2)}, u32[]{:S(2)}) %collective-permute-start.13) | collective-permute-done | bytes 159776 | tf_op jit(solution)/shard_map/ppermute | solution.py:543
  54.4 2.7 %coarse_levels.1 = (f32[2,8,8,64]{3,2,1,0:T(8,128)}, f32[2,4,4,32]{3,2,1,0:T(4,128)}) custom-call(s32[2]{0:T(128)S(1)} %pad_add_fusion.place, f32[15,10,128]{2,1,0:T(8,128)S(1)} %get-tuple-element.89.fc_own, f32[12,10,128]{2,1,0:T(8,128)S(1)} %collective-permute-done.10.xlo, f32[12,10,128]{2,1,0:T(8,128)S(1)} %collective-permute-done.11.xhi, ...), custom_call_target="tpu_custom_call" | custom-call | tf_op jit(solution)/shard_map/coarse_levels/pallas_call | solution.py:675
  (34 shorter events, 1.0 us)
Async XLA Ops:
  0.6 5.3 %copy-start.1 = (f32[32,32,256]{2,1,0:T(8,128)S(1)}, f32[32,32,256]{2,1,0:T(8,128)}, u32[]{:S(2)}) copy-start(f32[32,32,256]{2,1,0:T(8,128)} %c.3) | copy-start | bytes 3145732
  0.6 5.3 %copy-start = (f32[2,32,32,256]{3,2,1,0:T(8,128)S(1)}, f32[2,32,32,256]{3,2,1,0:T(8,128)}, u32[]{:S(2)}) copy-start(f32[2,32,32,256]{3,2,1,0:T(8,128)} %f.3) | copy-start | bytes 6291460
  2.6 10.3 %collective-permute-start = (f32[7,32,256]{2,1,0:T(8,128)}, f32[7,32,256]{2,1,0:T(8,128)S(1)}, u32[]{:S(2)}, u32[]{:S(2)}) collective-permute-start(f32[7,32,256]{2,1,0:T(8,128)} %get-tuple-element.50), channel_id=1, source_target_pairs={{0,32},{32,64},{64,96},{96,128},{128,160},{160,192},{192,224},{224... | collective-permute-start | bytes 688136 | tf_op jit(solution)/shard_map/ppermute | solution.py:533
  5.8 8.6 %collective-permute-start.1 = (f32[7,32,256]{2,1,0:T(8,128)}, f32[7,32,256]{2,1,0:T(8,128)}, u32[]{:S(2)}, u32[]{:S(2)}) collective-permute-start(f32[7,32,256]{2,1,0:T(8,128)} %get-tuple-element.51), channel_id=1, source_target_pairs={{32,0},{64,32},{96,64},{128,96},{160,128},{192,160},{224,192},{0,2... | collective-permute-start | bytes 688136 | tf_op jit(solution)/shard_map/ppermute | solution.py:534
  7.1 11.9 %collective-permute-start.2 = (f32[32,8,256]{2,1,0:T(8,128)S(1)}, f32[32,8,256]{2,1,0:T(8,128)S(1)}, u32[]{:S(2)}, u32[]{:S(2)}) collective-permute-start(f32[32,8,256]{2,1,0:T(8,128)S(1)} %get-tuple-element.68), channel_id=1, source_target_pairs={{0,1},{1,0},{2,3},{3,2},{4,5},{5,4},{6,7},{7,6},{8,9},{9,8},{10,11... | collective-permute-start | bytes 786440 | tf_op jit(solution)/shard_map/ppermute | solution.py:543
  7.2 11.8 %collective-permute-start.3 = (f32[32,8,256]{2,1,0:T(8,128)S(1)}, f32[32,8,256]{2,1,0:T(8,128)S(1)}, u32[]{:S(2)}, u32[]{:S(2)}) collective-permute-start(f32[32,8,256]{2,1,0:T(8,128)S(1)} %get-tuple-element.69), channel_id=1, source_target_pairs={{0,32},{1,2},{2,1},{3,4},{4,3},{5,6},{6,5},{7,8},{8,7},{9,10},{10,... | collective-permute-start | bytes 786440 | tf_op jit(solution)/shard_map/ppermute | solution.py:543
  15.8 6.5 %collective-permute-start.4 = (f32[10,4,256]{2,1,0:T(4,128)S(1)}, f32[10,4,256]{2,1,0:T(4,128)S(1)}, u32[]{:S(2)}, u32[]{:S(2)}) collective-permute-start(f32[10,4,256]{2,1,0:T(4,128)S(1)} %get-tuple-element.76), channel_id=1, source_target_pairs={{0,1},{1,0},{2,3},{3,2},{4,5},{5,4},{6,7},{7,6},{8,9},{9,8},{10,11... | collective-permute-start | bytes 122888 | tf_op jit(solution)/shard_map/ppermute | solution.py:543
  15.9 6.4 %collective-permute-start.5 = (f32[10,4,256]{2,1,0:T(4,128)S(1)}, f32[10,4,256]{2,1,0:T(4,128)S(1)}, u32[]{:S(2)}, u32[]{:S(2)}) collective-permute-start(f32[10,4,256]{2,1,0:T(4,128)S(1)} %get-tuple-element.77), channel_id=1, source_target_pairs={{0,32},{1,2},{2,1},{3,4},{4,3},{5,6},{6,5},{7,8},{8,7},{9,10},{10,... | collective-permute-start | bytes 122888 | tf_op jit(solution)/shard_map/ppermute | solution.py:543
  23.5 5.1 %collective-permute-start.6 = (f32[17,16,128]{2,1,0:T(8,128)S(1)}, f32[17,16,128]{2,1,0:T(8,128)S(1)}, u32[]{:S(2)}, u32[]{:S(2)}) collective-permute-start(f32[17,16,128]{2,1,0:T(8,128)S(1)} %pad_maximum_fusion), channel_id=1, source_target_pairs={{0,32},{32,64},{64,96},{96,128},{128,160},{160,192},{192,224},{224... | collective-permute-start | bytes 417800 | tf_op jit(solution)/shard_map/ppermute | solution.py:533
  24.6 6.3 %collective-permute-start.7 = (f32[17,16,128]{2,1,0:T(8,128)S(1)}, f32[17,16,128]{2,1,0:T(8,128)S(1)}, u32[]{:S(2)}, u32[]{:S(2)}) collective-permute-start(f32[17,16,128]{2,1,0:T(8,128)S(1)} %pad_maximum_fusion.1), channel_id=1, source_target_pairs={{32,0},{64,32},{96,64},{128,96},{160,128},{192,160},{224,192},{0,2... | collective-permute-start | bytes 417800 | tf_op jit(solution)/shard_map/ppermute | solution.py:534
  31.5 1.6 %collective-permute-start.8 = (f32[2,26,8,128]{3,2,1,0:T(8,128)S(1)}, f32[2,26,8,128]{3,2,1,0:T(8,128)S(1)}, u32[]{:S(2)}, u32[]{:S(2)}) collective-permute-start(f32[2,26,8,128]{3,2,1,0:T(8,128)S(1)} %get-tuple-element.86), channel_id=1, source_target_pairs={{0,1},{1,0},{2,3},{3,2},{4,5},{5,4},{6,7},{7,6},{8,9},{9,8},{10,11... | collective-permute-start | bytes 638984 | tf_op jit(solution)/shard_map/ppermute | solution.py:543
  31.6 7.6 %collective-permute-start.9 = (f32[2,26,8,128]{3,2,1,0:T(8,128)S(1)}, f32[2,26,8,128]{3,2,1,0:T(8,128)S(1)}, u32[]{:S(2)}, u32[]{:S(2)}) collective-permute-start(f32[2,26,8,128]{3,2,1,0:T(8,128)S(1)} %get-tuple-element.87), channel_id=1, source_target_pairs={{0,32},{1,2},{2,1},{3,4},{4,3},{5,6},{6,5},{7,8},{8,7},{9,10},{10,... | collective-permute-start | bytes 638984 | tf_op jit(solution)/shard_map/ppermute | solution.py:543
  41.4 4.7 %collective-permute-start.10 = (f32[12,10,128]{2,1,0:T(8,128)S(1)}, f32[12,10,128]{2,1,0:T(8,128)S(1)}, u32[]{:S(2)}, u32[]{:S(2)}) collective-permute-start(f32[12,10,128]{2,1,0:T(8,128)S(1)} %pad_maximum_fusion.2), channel_id=1, source_target_pairs={{0,32},{32,64},{64,96},{96,128},{128,160},{160,192},{192,224},{224... | collective-permute-start | bytes 184328 | tf_op jit(solution)/shard_map/ppermute | solution.py:533
  41.5 5.9 %collective-permute-start.11 = (f32[12,10,128]{2,1,0:T(8,128)S(1)}, f32[12,10,128]{2,1,0:T(8,128)S(1)}, u32[]{:S(2)}, u32[]{:S(2)}) collective-permute-start(f32[12,10,128]{2,1,0:T(8,128)S(1)} %pad_maximum_fusion.3), channel_id=1, source_target_pairs={{32,0},{64,32},{96,64},{128,96},{160,128},{192,160},{224,192},{0,2... | collective-permute-start | bytes 184328 | tf_op jit(solution)/shard_map/ppermute | solution.py:534
  47.5 6.9 %collective-permute-start.13 = (f32[39,8,128]{2,1,0:T(8,128)S(1)}, f32[39,8,128]{2,1,0:T(8,128)S(1)}, u32[]{:S(2)}, u32[]{:S(2)}) collective-permute-start(f32[39,8,128]{2,1,0:T(8,128)S(1)} %get-tuple-element.94), channel_id=1, source_target_pairs={{0,32},{1,2},{2,1},{3,4},{4,3},{5,6},{6,5},{7,8},{8,7},{9,10},{10,... | collective-permute-start | bytes 479240 | tf_op jit(solution)/shard_map/ppermute | solution.py:543
  47.6 6.8 %collective-permute-start.12 = (f32[39,8,128]{2,1,0:T(8,128)S(1)}, f32[39,8,128]{2,1,0:T(8,128)S(1)}, u32[]{:S(2)}, u32[]{:S(2)}) collective-permute-start(f32[39,8,128]{2,1,0:T(8,128)S(1)} %get-tuple-element.95), channel_id=1, source_target_pairs={{0,1},{1,0},{2,3},{3,2},{4,5},{5,4},{6,7},{7,6},{8,9},{9,8},{10,11... | collective-permute-start | bytes 479240 | tf_op jit(solution)/shard_map/ppermute | solution.py:543

commit v11 on v10

--- a/solution.py
+++ b/solution.py
@@ -111,15 +111,13 @@
     return jnp.where((z < zsize) & (i >= 0) & (i < zsize // 2), w, 0.0).astype(jnp.bfloat16)
 
 
-def exact_dot(part, w):
+def split_dot(part, w):
     planes, rows, lanes = part.shape
     x = part.reshape(planes * rows, lanes)
     hi = x.astype(jnp.bfloat16)
-    rest = x - hi.astype(jnp.float32)
-    mid = rest.astype(jnp.bfloat16)
-    low = (rest - mid.astype(jnp.float32)).astype(jnp.bfloat16)
+    low = (x - hi.astype(jnp.float32)).astype(jnp.bfloat16)
     dot = functools.partial(jnp.dot, preferred_element_type=jnp.float32)
-    return (dot(hi, w) + (dot(mid, w) + dot(low, w))).reshape(planes, rows, w.shape[1])
+    return (dot(hi, w) + dot(low, w)).reshape(planes, rows, w.shape[1])
 
 
 PX, PY = 2, 8
@@ -207,8 +205,8 @@
     lax.fori_loop(2, n // 2 - 2, coarse, 0, unroll=True)
     w = weights(lanes, lanes)
     for k in (0, 1):
-        fc_out[k, 2 : n // 2 - 2] = exact_dot(part[k, 2 : n // 2 - 2], w)
-    fc_out[2] = exact_dot(part[2], weights(lanes, lanes, mean=True))
+        fc_out[k, 2 : n // 2 - 2] = split_dot(part[k, 2 : n // 2 - 2], w)
+    fc_out[2] = split_dot(part[2], weights(lanes, lanes, mean=True))
 
 
 def inside(place, n, rows, xsize, ysize):
@@ -315,7 +313,7 @@
     lax.fori_loop(0, m, coarse, 0, unroll=True)
     w = weights(lanes, lanes)
     for k in (0, 1):
-        q[k] = exact_dot(part[k], w)
+        q[k] = split_dot(part[k], w)
         for row, start in ((0, 0), (rows // 2 - 2, 10)):
             four = [q[k, :, pl.ds(start + j, 2, 2), :] for j in range(4)]
             fc_out[k, pl.ds(2, m), pl.ds(row, 2), :] = (four[0] + four[3]) + 3.0 * (four[1] + four[2])
@@ -365,7 +363,7 @@
             restrict_xy(r, t, part, j, 2 * i + PX - 1, PY - 1, rows // 2, k, (low, rows + 8))
         for j, x in ((4, PX), (5, n + PX - 1)):
             restrict_rows([r[k, x, h, pl.ds(low, rows + 8), :] for h in range(halves)], t, part, j, PY - 1, rows // 2, k, low)
-        val = exact_dot(part[k], w)
+        val = split_dot(part[k], w)
         for j, i in enumerate(planes):
             fc_out[k, i] = val[j]
         edge_out[0, k], edge_out[1, k] = val[4], val[5]
@@ -461,19 +459,24 @@
             restrict_xy(r, t, part, i, x, row, width, k, (4, rows + 8))
         add_pairs(fc[2, x + 1, 0], fc[2, x + 2, 0], t, 0, part_c.at[i % 2], i // 2, row + 1, width)
     two = [(part.at[k], part_c.at[k], LANES // 2 * k) for k in (0, 1)]
-    fc_out[pl.ds(0, width)] = sum(exact_dot(p[...], weights(LANES, LANES, shift=s)) for p, _, s in two)[:, :width]
-    fc_out[pl.ds(width, pairs)] = sum(exact_dot(p[...], weights(LANES, LANES, True, s)) for _, p, s in two)[:, :width]
+    fc_out[pl.ds(0, width)] = sum(split_dot(p[...], weights(LANES, LANES, shift=s)) for p, _, s in two)[:, :width]
+    fc_out[pl.ds(width, pairs)] = sum(split_dot(p[...], weights(LANES, LANES, True, s)) for _, p, s in two)[:, :width]
 
 
 def coarse_kernel(n, sweeps, xsize, ysize, zsize, place, fc_own, xlo, xhi, y_chip, y_next, u_out, v_out, fc, ga, gb, u, e, r, t, part, part_c, gc, gd, v, w):
     m = n // 2
     planes = n + 18
-    for src, x, first, count in ((xlo, 0, 0, 8), (fc_own, 8, 0, n + 2), (xhi, n + 10, 0, 8), (xlo, planes, 8, 4), (fc_own, planes + 4, n + 2, m + 1), (xhi, planes + m + 5, 8, 4)):
-        fc[pl.ds(x, count), 0, pl.ds(15, n + 2), :] = src[pl.ds(first, count)]
+    own, own_c = range(8, n + 10), range(planes + 4, planes + m + 5)
+    for src, x, first, count in ((xlo, 0, 0, 8), (xhi, n + 10, 0, 8), (xlo, planes, 8, 4), (xhi, planes + m + 5, 8, 4)):
+        fc[pl.ds(x, count), 0, pl.ds(16, n), :] = src[pl.ds(first, count)]
+    fc[pl.ds(8, n + 2), 0, pl.ds(15, n + 2), :] = fc_own[pl.ds(0, n + 2)]
+    fc[pl.ds(planes + 4, m + 1), 0, pl.ds(15, n + 2), :] = fc_own[pl.ds(n + 2, m + 1)]
     even = is_even(place, (8, LANES))
     for x in range(fc.shape[0]):
+        out = 1 if x in own or x in own_c else 0
         chip, other = y_chip[x], y_next[x]
-        fc[x, 0, pl.ds(7, 8), :], fc[x, 0, pl.ds(n + 17, 8), :] = jnp.where(even, other, chip), jnp.where(even, chip, other)
+        fc[x, 0, pl.ds(8 - out, 8), :] = jnp.where(even, other, chip)
+        fc[x, 0, pl.ds(n + 16 + out, 8), :] = jnp.where(even, chip, other)
     lane = lax.broadcasted_iota(jnp.int32, (1, LANES), 1)
 
     def cells(k, x, at):
@@ -504,7 +507,7 @@
         t[0, 0, every, :] = cells(2, 2 * i + 3, every) + cells(2, 2 * i + 4, every)
         part_c[i, pl.ds(0, width), :] = t[0, 0, pl.ds(10, width, 2), :] + t[0, 0, pl.ds(11, width, 2), :]
     w_full = weights(LANES, zsize)
-    f = [exact_dot(part[k], w_full) for k in (0, 1)] + [exact_dot(part_c[...], weights(LANES, zsize, True))]
+    f = [split_dot(part[k], w_full) for k in (0, 1)] + [split_dot(part_c[...], weights(LANES, zsize, True))]
     ok = inside(place[0] * m - 3, place[1] * m - 3, xsize // 2, ysize // 2, zsize // 2)
     for x in range(width):
         point(f[0][x], f[1][x], f[2][x], 64.0, ok(x, 0, 16), v, gc, gd, x, 0, 0)
@@ -660,14 +663,13 @@
     n, xsize, ysize, zsize = n // 2, xsize // 2, ysize // 2, zsize // 2
     m = n // 2
 
-    def joined(lo, own, hi, cells):
-        f = (lo[:n], own[: n + 2], hi[:n])
-        c = (lo[n:], own[n + 2 :], hi[n:])
-        return jnp.concatenate([a[:, cells] for a in f + c], 0)
-
-    pick = lambda i, j: jnp.concatenate([fc[i : i + n], fc[n + 2 + j : n + 2 + j + m]], 0)
+    def joined(start):
+        own = fc[:, start : start + n]
+        return jnp.concatenate([xlo[:n], own[: n + 2], xhi[:n], xlo[n:], own[n + 2 :], xhi[n:]], 0)
+
+    pick = lambda i, j: jnp.concatenate([fc[i : i + n, 1 : n + 1], fc[n + 2 + j : n + 2 + j + m, 1 : n + 1]], 0)
     xlo, xhi = planes_step(pick(2, 1), pick(0, 0))
-    first, last = joined(xlo, fc, xhi, slice(2, n + 2)), joined(xlo, fc, xhi, slice(0, n))
+    first, last = joined(2), joined(0)
     even = place[1] % 2 == 0
     chip, other = rows_step(jnp.where(even, last, first), jnp.where(even, first, last))
     state = (n + 18, 1, 40, LANES)

time: 57.9 us -> 56.9 us (0.983)
  no operation moved by 1% of the time
where the time goes in v11:
time: 56.9 us; the launch traced here: 56.2 us
  waiting for transfers between devices  21.6 us (38%)
  Pallas kernels  18.2 us (32%)
  starting transfers between devices  15.2 us (27%)
  between operations  0.88 us (2%)
    ppermute x4, waiting for transfers between devices, rows_step(): lax.ppermute(other, ('gx', 'gy'), next_chip)  12.9 us
    ppermute x4, starting transfers between devices, rows_step(): lax.ppermute(other, ('gx', 'gy'), next_chip)  7.37 us
    ppermute x3, waiting for transfers between devices, planes_step(): lax.ppermute(first, 'gx', [((i + 1) % xdev, i) for i in range(xdev)])  5.1 us
    ppermute x3, starting transfers between devices, planes_step(): lax.ppermute(last, 'gx', [(i, (i + 1) % xdev) for i in range(xdev)])  4.36 us
    ppermute x3, waiting for transfers between devices, planes_step(): lax.ppermute(last, 'gx', [(i, (i + 1) % xdev) for i in range(xdev)])  3.35 us
    pallas_call x1, Pallas kernels, body(): pl.pallas_call(functools.partial(faces_kernel, xsize, ysize), in_specs=[S...  3.26 us
    ppermute x3, starting transfers between devices, planes_step(): lax.ppermute(first, 'gx', [((i + 1) % xdev, i) for i in range(xdev)])  3.12 us
    pallas_call x1, Pallas kernels, body(): pl.pallas_call(inner_kernel, in_specs=[VMEM] * 5, out_specs=[VMEM] * 3, o...  2.63 us
  transfers between devices with their start and end apart: 14, of which 8 were waited for; matrix products, arithmetic and copies ran while one was open for 0% of the time, Pallas kernels for 18%

profile of v11, /device:TPU:120, one launch (start us, length us, event | category | flops | bytes accessed | tf_op | source)
XLA Modules:
  0.0 56.2 jit_solution(5703302773585809938)
XLA Ops:
  0.7 2.0 %pack_planes.1 = (f32[7,32,256]{2,1,0:T(8,128)}, f32[7,32,256]{2,1,0:T(8,128)}) custom-call(f32[2,32,32,256]{3,2,1,0:T(8,128)} %f.3, f32[32,32,256]{2,1,0:T(8,128)} %c.3), custom_call_target="tpu_custom_call" | custom-call | tf_op jit(solution)/shard_map/pack_planes/pallas_call | solution.py:559
  2.6 3.2 %collective-permute-start = (f32[7,32,256]{2,1,0:T(8,128)}, f32[7,32,256]{2,1,0:T(8,128)S(1)}, u32[]{:S(2)}, u32[]{:S(2)}) collective-permute-start(f32[7,32,256]{2,1,0:T(8,128)} %get-tuple-element.50), channel_id=1, source_target_pairs={{0,32},{32,64},{64,96},{96,128},{128,160},{160,192},{192,224},{224... | collective-permute-start | bytes 688136 | tf_op jit(solution)/shard_map/ppermute | solution.py:536
  5.9 1.2 %first_iterate.1 = (f32[2,36,2,48,128]{4,3,2,1,0:T(8,128)S(1)}, f32[36,2,48,128]{3,2,1,0:T(8,128)S(1)}, f32[36,2,48,128]{3,2,1,0:T(8,128)S(1)}, f32[32,8,256]{2,1,0:T(8,128)S(1)}, f32[32,8,256]{2,1,0:T(8,128)S(1)}) custom-call(s32[2]{0:T(128)S(1)} %pad_add_fusion.place, f32[2,32,32,256]{3,2,1,0:T(8,128)S(1)} %copy-done, f32[32,32,256]{2,1,0:T(8,128)S(1)} %copy-done.1), custom_call_target="tpu_custom_call" | custom-call | flops 30000000 | bytes 8000000 | tf_op jit(solution)/shard_map/first_iterate/pallas_call | solution.py:570
  7.2 3.0 %collective-permute-start.3 = (f32[32,8,256]{2,1,0:T(8,128)S(1)}, f32[32,8,256]{2,1,0:T(8,128)S(1)}, u32[]{:S(2)}, u32[]{:S(2)}) collective-permute-start(f32[32,8,256]{2,1,0:T(8,128)S(1)} %get-tuple-element.69), channel_id=1, source_target_pairs={{0,32},{1,2},{2,1},{3,4},{4,3},{5,6},{6,5},{7,8},{8,7},{9,10},{10,... | collective-permute-start | bytes 786440 | tf_op jit(solution)/shard_map/ppermute | solution.py:546
  10.2 2.6 %inner_cells.1 = (f32[2,36,2,48,128]{4,3,2,1,0:T(8,128)S(1)}, f32[2,36,2,48,128]{4,3,2,1,0:T(8,128)S(1)}, f32[3,16,16,128]{3,2,1,0:T(8,128)S(1)}) custom-call(f32[2,32,32,256]{3,2,1,0:T(8,128)S(1)} %copy-done, f32[32,32,256]{2,1,0:T(8,128)S(1)} %copy-done.1, f32[2,36,2,48,128]{4,3,2,1,0:T(8,128)S(1)} %get-tuple-element.60.u.u_in, ...), custom_call_target="tpu_custom_call" | custom-call | flops 70000000 | bytes 16000000 | tf_op jit(solution)/shard_map/inner_cells/pallas_call | solution.py:580
  12.9 1.5 %collective-permute-done.1.xhi = f32[7,32,256]{2,1,0:T(8,128)} collective-permute-done((f32[7,32,256]{2,1,0:T(8,128)}, f32[7,32,256]{2,1,0:T(8,128)}, u32[]{:S(2)}, u32[]{:S(2)}) %collective-permute-start.1) | collective-permute-done | bytes 229408 | tf_op jit(solution)/shard_map/ppermute | solution.py:537
  14.4 1.4 %pack_corners.1 = (f32[10,4,256]{2,1,0:T(4,128)S(1)}, f32[10,4,256]{2,1,0:T(4,128)S(1)}) custom-call(s32[2]{0:T(128)S(1)} %pad_add_fusion.place, f32[7,32,256]{2,1,0:T(8,128)S(1)} %collective-permute-done.xlo, f32[7,32,256]{2,1,0:T(8,128)} %collective-permute-done.1.xhi), custom_call_target="tpu_custom_call" | custom-call | tf_op jit(solution)/shard_map/pack_corners/pallas_call | solution.py:594
  15.9 3.0 %collective-permute-start.5 = (f32[10,4,256]{2,1,0:T(4,128)S(1)}, f32[10,4,256]{2,1,0:T(4,128)S(1)}, u32[]{:S(2)}, u32[]{:S(2)}) collective-permute-start(f32[10,4,256]{2,1,0:T(4,128)S(1)} %get-tuple-element.77), channel_id=1, source_target_pairs={{0,32},{1,2},{2,1},{3,4},{4,3},{5,6},{6,5},{7,8},{8,7},{9,10},{10,... | collective-permute-start | bytes 122888 | tf_op jit(solution)/shard_map/ppermute | solution.py:546
  19.0 3.3 %face_cells.1 = (f32[2,36,2,48,128]{4,3,2,1,0:T(8,128)S(1)}, f32[2,36,2,48,128]{4,3,2,1,0:T(8,128)S(1)}, f32[2,36,2,48,128]{4,3,2,1,0:T(8,128)S(1)}, f32[36,2,48...) custom-call(s32[2]{0:T(128)S(1)} %pad_add_fusion.place, ...), custom_call_target="tpu_custom_call", output_to_operand_aliasing={{0}: (1, {}), {1}: (2, {}), {2}: (3, {}), {3}: (4, {}), {4}... | custom-call | flops 50000000 | bytes 8000000 | tf_op jit(solution)/shard_map/face_cells/pallas_call | solution.py:605
  22.3 1.0 %corner_cells.1 = (f32[2,36,2,48,128]{4,3,2,1,0:T(8,128)S(1)}, f32[2,36,2,48,128]{4,3,2,1,0:T(8,128)S(1)}, f32[2,36,2,48,128]{4,3,2,1,0:T(8,128)S(1)}, f32[36,2,...) custom-call(s32[2]{0:T(128)S(1)} %pad_add_fusion.place, ...), custom_call_target="tpu_custom_call", output_to_operand_aliasing={{0}: (1, {}), {1}: (2, {}), {2}: (3, {}), {3}: (4, {}), {4}... | custom-call | tf_op jit(solution)/shard_map/corner_cells/pallas_call | solution.py:616
  23.4 1.1 %collective-permute-start.6 = (f32[17,16,128]{2,1,0:T(8,128)S(1)}, f32[17,16,128]{2,1,0:T(8,128)S(1)}, u32[]{:S(2)}, u32[]{:S(2)}) collective-permute-start(f32[17,16,128]{2,1,0:T(8,128)S(1)} %pad_maximum_fusion), channel_id=1, source_target_pairs={{0,32},{32,64},{64,96},{96,128},{128,160},{160,192},{192,224},{224... | collective-permute-start | bytes 417800 | tf_op jit(solution)/shard_map/ppermute | solution.py:536
  24.5 1.1 %collective-permute-start.7 = (f32[17,16,128]{2,1,0:T(8,128)S(1)}, f32[17,16,128]{2,1,0:T(8,128)S(1)}, u32[]{:S(2)}, u32[]{:S(2)}) collective-permute-start(f32[17,16,128]{2,1,0:T(8,128)S(1)} %pad_maximum_fusion.1), channel_id=1, source_target_pairs={{32,0},{64,32},{96,64},{128,96},{160,128},{192,160},{224,192},{0,2... | collective-permute-start | bytes 417800 | tf_op jit(solution)/shard_map/ppermute | solution.py:537
  25.6 1.6 %fine_iterate.1 = f32[2,32,32,256]{3,2,1,0:T(8,128)} custom-call(f32[2,36,2,48,128]{4,3,2,1,0:T(8,128)S(1)} %get-tuple-element.80.u, f32[2,36,2,48,128]{4,3,2,1,0:T(8,128)S(1)} %get-tuple-element.81.e), custom_call_target="tpu_custom_call" | custom-call | flops 1000000 | bytes 8000000 | tf_op jit(solution)/shard_map/fine_iterate/pallas_call | solution.py:631
  27.2 1.3 %collective-permute-done.6.xlo = f32[17,16,128]{2,1,0:T(8,128)S(1)} collective-permute-done((f32[17,16,128]{2,1,0:T(8,128)S(1)}, f32[17,16,128]{2,1,0:T(8,128)S(1)}, u32[]{:S(2)}, u32[]{:S(2)}) %collective-permute-start.6) | collective-permute-done | bytes 139296 | tf_op jit(solution)/shard_map/ppermute | solution.py:536
  28.5 2.3 %collective-permute-done.7.xhi = f32[17,16,128]{2,1,0:T(8,128)S(1)} collective-permute-done((f32[17,16,128]{2,1,0:T(8,128)S(1)}, f32[17,16,128]{2,1,0:T(8,128)S(1)}, u32[]{:S(2)}, u32[]{:S(2)}) %collective-permute-start.7) | collective-permute-done | bytes 139296 | tf_op jit(solution)/shard_map/ppermute | solution.py:537
  30.8 0.6 %second_rows.1 = (f32[2,26,8,128]{3,2,1,0:T(8,128)S(1)}, f32[2,26,8,128]{3,2,1,0:T(8,128)S(1)}, f32[3,26,16,128]{3,2,1,0:T(8,128)S(1)}) custom-call(s32[2]{0:T(128)S(1)} %pad_add_fusion.place, f32[17,16,128]{2,1,0:T(8,128)S(1)} %collective-permute-done.6.xlo, f32[3,16,16,128]{3,2,1,0:T(8,128)S(1)} %get-tuple-element.78.fc, ...), custom_call_target="tpu_custom_call" | custom-call | tf_op jit(solution)/shard_map/second_rows/pallas_call | solution.py:641
  31.5 1.2 %collective-permute-start.9 = (f32[2,26,8,128]{3,2,1,0:T(8,128)S(1)}, f32[2,26,8,128]{3,2,1,0:T(8,128)S(1)}, u32[]{:S(2)}, u32[]{:S(2)}) collective-permute-start(f32[2,26,8,128]{3,2,1,0:T(8,128)S(1)} %get-tuple-element.87), channel_id=1, source_target_pairs={{0,32},{1,2},{2,1},{3,4},{4,3},{5,6},{6,5},{7,8},{8,7},{9,10},{10,... | collective-permute-start | bytes 638984 | tf_op jit(solution)/shard_map/ppermute | solution.py:546
  33.0 6.2 %collective-permute-done.9.y_next = f32[2,26,8,128]{3,2,1,0:T(8,128)S(1)} collective-permute-done((f32[2,26,8,128]{3,2,1,0:T(8,128)S(1)}, f32[2,26,8,128]{3,2,1,0:T(8,128)S(1)}, u32[]{:S(2)}, u32[]{:S(2)}) %collective-permute-start.9) | collective-permute-done | bytes 213024 | tf_op jit(solution)/shard_map/ppermute | solution.py:546
  39.2 1.9 %second_level.1 = (f32[2,16,16,128]{3,2,1,0:T(8,128)}, f32[15,10,128]{2,1,0:T(8,128)S(1)}) custom-call(s32[2]{0:T(128)S(1)} %pad_add_fusion.place, f32[3,26,16,128]{3,2,1,0:T(8,128)S(1)} %get-tuple-element.85.window, f32[2,26,8,128]{3,2,1,0:T(8,128)S(1)} %collective-permute-done.8.y_chip, f32[2,26,8,128]{3,2,1,0:T(8,128)S(1)} %collective-permute-done.9.y_next), custom_call_target="tpu_custom_call" | custom-call | tf_op jit(solution)/shard_map/second_level/pallas_call | solution.py:653
  41.2 2.0 %collective-permute-start.11 = (f32[12,8,128]{2,1,0:T(8,128)S(1)}, f32[12,8,128]{2,1,0:T(8,128)S(1)}, u32[]{:S(2)}, u32[]{:S(2)}) collective-permute-start(f32[12,8,128]{2,1,0:T(8,128)S(1)} %pad_maximum_fusion.3), channel_id=1, source_target_pairs={{32,0},{64,32},{96,64},{128,96},{160,128},{192,160},{224,192},{0,2... | collective-permute-start | bytes 147464 | tf_op jit(solution)/shard_map/ppermute | solution.py:537
  43.2 2.1 %collective-permute-done.10.xlo = f32[12,8,128]{2,1,0:T(8,128)S(1)} collective-permute-done((f32[12,8,128]{2,1,0:T(8,128)S(1)}, f32[12,8,128]{2,1,0:T(8,128)S(1)}, u32[]{:S(2)}, u32[]{:S(2)}) %collective-permute-start.10) | collective-permute-done | bytes 49184 | tf_op jit(solution)/shard_map/ppermute | solution.py:536
  45.3 1.3 %collective-permute-done.11.xhi = f32[12,8,128]{2,1,0:T(8,128)S(1)} collective-permute-done((f32[12,8,128]{2,1,0:T(8,128)S(1)}, f32[12,8,128]{2,1,0:T(8,128)S(1)}, u32[]{:S(2)}, u32[]{:S(2)}) %collective-permute-start.11) | collective-permute-done | bytes 49184 | tf_op jit(solution)/shard_map/ppermute | solution.py:537
  46.9 6.7 %collective-permute-done.13.y_next = f32[39,8,128]{2,1,0:T(8,128)S(1)} collective-permute-done((f32[39,8,128]{2,1,0:T(8,128)S(1)}, f32[39,8,128]{2,1,0:T(8,128)S(1)}, u32[]{:S(2)}, u32[]{:S(2)}) %collective-permute-start.13) | collective-permute-done | bytes 159776 | tf_op jit(solution)/shard_map/ppermute | solution.py:546
  53.6 2.6 %coarse_levels.1 = (f32[2,8,8,64]{3,2,1,0:T(8,128)}, f32[2,4,4,32]{3,2,1,0:T(4,128)}) custom-call(s32[2]{0:T(128)S(1)} %pad_add_fusion.place, f32[15,10,128]{2,1,0:T(8,128)S(1)} %get-tuple-element.89.fc_own, f32[12,8,128]{2,1,0:T(8,128)S(1)} %collective-permute-done.10.xlo, f32[12,8,128]{2,1,0:T(8,128)S(1)} %collective-permute-done.11.xhi, ...), custom_call_target="tpu_custom_call" | custom-call | tf_op jit(solution)/shard_map/coarse_levels/pallas_call | solution.py:677
  (36 shorter events, 1.0 us)
Async XLA Ops:
  0.6 5.3 %copy-start.1 = (f32[32,32,256]{2,1,0:T(8,128)S(1)}, f32[32,32,256]{2,1,0:T(8,128)}, u32[]{:S(2)}) copy-start(f32[32,32,256]{2,1,0:T(8,128)} %c.3) | copy-start | bytes 3145732
  0.6 5.3 %copy-start = (f32[2,32,32,256]{3,2,1,0:T(8,128)S(1)}, f32[2,32,32,256]{3,2,1,0:T(8,128)}, u32[]{:S(2)}) copy-start(f32[2,32,32,256]{3,2,1,0:T(8,128)} %f.3) | copy-start | bytes 6291460
  2.6 10.2 %collective-permute-start = (f32[7,32,256]{2,1,0:T(8,128)}, f32[7,32,256]{2,1,0:T(8,128)S(1)}, u32[]{:S(2)}, u32[]{:S(2)}) collective-permute-start(f32[7,32,256]{2,1,0:T(8,128)} %get-tuple-element.50), channel_id=1, source_target_pairs={{0,32},{32,64},{64,96},{96,128},{128,160},{160,192},{192,224},{224... | collective-permute-start | bytes 688136 | tf_op jit(solution)/shard_map/ppermute | solution.py:536
  5.8 8.6 %collective-permute-start.1 = (f32[7,32,256]{2,1,0:T(8,128)}, f32[7,32,256]{2,1,0:T(8,128)}, u32[]{:S(2)}, u32[]{:S(2)}) collective-permute-start(f32[7,32,256]{2,1,0:T(8,128)} %get-tuple-element.51), channel_id=1, source_target_pairs={{32,0},{64,32},{96,64},{128,96},{160,128},{192,160},{224,192},{0,2... | collective-permute-start | bytes 688136 | tf_op jit(solution)/shard_map/ppermute | solution.py:537
  7.1 11.9 %collective-permute-start.2 = (f32[32,8,256]{2,1,0:T(8,128)S(1)}, f32[32,8,256]{2,1,0:T(8,128)S(1)}, u32[]{:S(2)}, u32[]{:S(2)}) collective-permute-start(f32[32,8,256]{2,1,0:T(8,128)S(1)} %get-tuple-element.68), channel_id=1, source_target_pairs={{0,1},{1,0},{2,3},{3,2},{4,5},{5,4},{6,7},{7,6},{8,9},{9,8},{10,11... | collective-permute-start | bytes 786440 | tf_op jit(solution)/shard_map/ppermute | solution.py:546
  7.2 11.8 %collective-permute-start.3 = (f32[32,8,256]{2,1,0:T(8,128)S(1)}, f32[32,8,256]{2,1,0:T(8,128)S(1)}, u32[]{:S(2)}, u32[]{:S(2)}) collective-permute-start(f32[32,8,256]{2,1,0:T(8,128)S(1)} %get-tuple-element.69), channel_id=1, source_target_pairs={{0,32},{1,2},{2,1},{3,4},{4,3},{5,6},{6,5},{7,8},{8,7},{9,10},{10,... | collective-permute-start | bytes 786440 | tf_op jit(solution)/shard_map/ppermute | solution.py:546
  15.8 6.4 %collective-permute-start.4 = (f32[10,4,256]{2,1,0:T(4,128)S(1)}, f32[10,4,256]{2,1,0:T(4,128)S(1)}, u32[]{:S(2)}, u32[]{:S(2)}) collective-permute-start(f32[10,4,256]{2,1,0:T(4,128)S(1)} %get-tuple-element.76), channel_id=1, source_target_pairs={{0,1},{1,0},{2,3},{3,2},{4,5},{5,4},{6,7},{7,6},{8,9},{9,8},{10,11... | collective-permute-start | bytes 122888 | tf_op jit(solution)/shard_map/ppermute | solution.py:546
  15.9 6.3 %collective-permute-start.5 = (f32[10,4,256]{2,1,0:T(4,128)S(1)}, f32[10,4,256]{2,1,0:T(4,128)S(1)}, u32[]{:S(2)}, u32[]{:S(2)}) collective-permute-start(f32[10,4,256]{2,1,0:T(4,128)S(1)} %get-tuple-element.77), channel_id=1, source_target_pairs={{0,32},{1,2},{2,1},{3,4},{4,3},{5,6},{6,5},{7,8},{8,7},{9,10},{10,... | collective-permute-start | bytes 122888 | tf_op jit(solution)/shard_map/ppermute | solution.py:546
  23.4 5.1 %collective-permute-start.6 = (f32[17,16,128]{2,1,0:T(8,128)S(1)}, f32[17,16,128]{2,1,0:T(8,128)S(1)}, u32[]{:S(2)}, u32[]{:S(2)}) collective-permute-start(f32[17,16,128]{2,1,0:T(8,128)S(1)} %pad_maximum_fusion), channel_id=1, source_target_pairs={{0,32},{32,64},{64,96},{96,128},{128,160},{160,192},{192,224},{224... | collective-permute-start | bytes 417800 | tf_op jit(solution)/shard_map/ppermute | solution.py:536
  24.5 6.3 %collective-permute-start.7 = (f32[17,16,128]{2,1,0:T(8,128)S(1)}, f32[17,16,128]{2,1,0:T(8,128)S(1)}, u32[]{:S(2)}, u32[]{:S(2)}) collective-permute-start(f32[17,16,128]{2,1,0:T(8,128)S(1)} %pad_maximum_fusion.1), channel_id=1, source_target_pairs={{32,0},{64,32},{96,64},{128,96},{160,128},{192,160},{224,192},{0,2... | collective-permute-start | bytes 417800 | tf_op jit(solution)/shard_map/ppermute | solution.py:537
  31.4 1.6 %collective-permute-start.8 = (f32[2,26,8,128]{3,2,1,0:T(8,128)S(1)}, f32[2,26,8,128]{3,2,1,0:T(8,128)S(1)}, u32[]{:S(2)}, u32[]{:S(2)}) collective-permute-start(f32[2,26,8,128]{3,2,1,0:T(8,128)S(1)} %get-tuple-element.86), channel_id=1, source_target_pairs={{0,1},{1,0},{2,3},{3,2},{4,5},{5,4},{6,7},{7,6},{8,9},{9,8},{10,11... | collective-permute-start | bytes 638984 | tf_op jit(solution)/shard_map/ppermute | solution.py:546
  31.5 7.6 %collective-permute-start.9 = (f32[2,26,8,128]{3,2,1,0:T(8,128)S(1)}, f32[2,26,8,128]{3,2,1,0:T(8,128)S(1)}, u32[]{:S(2)}, u32[]{:S(2)}) collective-permute-start(f32[2,26,8,128]{3,2,1,0:T(8,128)S(1)} %get-tuple-element.87), channel_id=1, source_target_pairs={{0,32},{1,2},{2,1},{3,4},{4,3},{5,6},{6,5},{7,8},{8,7},{9,10},{10,... | collective-permute-start | bytes 638984 | tf_op jit(solution)/shard_map/ppermute | solution.py:546
  41.1 4.2 %collective-permute-start.10 = (f32[12,8,128]{2,1,0:T(8,128)S(1)}, f32[12,8,128]{2,1,0:T(8,128)S(1)}, u32[]{:S(2)}, u32[]{:S(2)}) collective-permute-start(f32[12,8,128]{2,1,0:T(8,128)S(1)} %pad_maximum_fusion.2), channel_id=1, source_target_pairs={{0,32},{32,64},{64,96},{96,128},{128,160},{160,192},{192,224},{224... | collective-permute-start | bytes 147464 | tf_op jit(solution)/shard_map/ppermute | solution.py:536
  41.2 5.4 %collective-permute-start.11 = (f32[12,8,128]{2,1,0:T(8,128)S(1)}, f32[12,8,128]{2,1,0:T(8,128)S(1)}, u32[]{:S(2)}, u32[]{:S(2)}) collective-permute-start(f32[12,8,128]{2,1,0:T(8,128)S(1)} %pad_maximum_fusion.3), channel_id=1, source_target_pairs={{32,0},{64,32},{96,64},{128,96},{160,128},{192,160},{224,192},{0,2... | collective-permute-start | bytes 147464 | tf_op jit(solution)/shard_map/ppermute | solution.py:537
  46.7 6.9 %collective-permute-start.13 = (f32[39,8,128]{2,1,0:T(8,128)S(1)}, f32[39,8,128]{2,1,0:T(8,128)S(1)}, u32[]{:S(2)}, u32[]{:S(2)}) collective-permute-start(f32[39,8,128]{2,1,0:T(8,128)S(1)} %get-tuple-element.94), channel_id=1, source_target_pairs={{0,32},{1,2},{2,1},{3,4},{4,3},{5,6},{6,5},{7,8},{8,7},{9,10},{10,... | collective-permute-start | bytes 479240 | tf_op jit(solution)/shard_map/ppermute | solution.py:546
  46.8 6.8 %collective-permute-start.12 = (f32[39,8,128]{2,1,0:T(8,128)S(1)}, f32[39,8,128]{2,1,0:T(8,128)S(1)}, u32[]{:S(2)}, u32[]{:S(2)}) collective-permute-start(f32[39,8,128]{2,1,0:T(8,128)S(1)} %get-tuple-element.95), channel_id=1, source_target_pairs={{0,1},{1,0},{2,3},{3,2},{4,5},{5,4},{6,7},{7,6},{8,9},{9,8},{10,11... | collective-permute-start | bytes 479240 | tf_op jit(solution)/shard_map/ppermute | solution.py:546

commit v12 on v11

--- a/solution.py
+++ b/solution.py
@@ -161,7 +161,12 @@
     lax.fori_loop(0, n, step, 0, unroll=True)
 
 
-def inner_kernel(f, c, u, ga, gb, e, r, fc_out, t, part):
+def both_ends(ranges, step):
+    for first, last in ranges:
+        lax.fori_loop(first, last, step, 0, unroll=True)
+
+
+def inner_kernel(late, f, c, u, ga, gb, e, r, fc_out, t, part):
     n, rows, lanes = c.shape
     halves = lanes // LANES
     at = pl.ds(PY, rows)
@@ -171,7 +176,8 @@
         second(u, ga, gb, e, x + PX, PY, rows, 1.0, True)
         return carry
 
-    lax.fori_loop(1, n - 1, middle, 0, unroll=True)
+    lo, hi = late
+    both_ends(((1, 2 * lo + 2), (2 * hi - 2, n - 1)), middle)
     row = lax.broadcasted_iota(jnp.int32, (rows, LANES), 0)
     full = (row >= 2) & (row < rows - 2)
 
@@ -182,8 +188,8 @@
                 r[k, x + PX, h, at, :] = 0.04 * f[k, x, :, cut[h]] + jnp.where(full, s[h], 0.0)
         return carry
 
-    lax.fori_loop(2, n - 2, last, 0, unroll=True)
-    for x in (0, 1, n - 2, n - 1):
+    both_ends(((2, 2 * lo + 1), (2 * hi - 1, n - 2)), last)
+    for x in (0, 1, *range(2 * lo + 1, 2 * hi - 1), n - 2, n - 1):
         for k in (0, 1):
             for h in range(halves):
                 r[k, x + PX, h, at, :] = 0.04 * f[k, x, :, cut[h]]
@@ -202,10 +208,12 @@
             restrict_xy(r, t, part, i, 2 * i + PX - 1, PY - 1, rows // 2, k, (PY, rows))
         return carry
 
-    lax.fori_loop(2, n // 2 - 2, coarse, 0, unroll=True)
+    early = ((2, lo), (hi, n // 2 - 2))
+    both_ends(early, coarse)
     w = weights(lanes, lanes)
     for k in (0, 1):
-        fc_out[k, 2 : n // 2 - 2] = split_dot(part[k, 2 : n // 2 - 2], w)
+        for i, j in early:
+            fc_out[k, i:j] = split_dot(part[k, i:j], w)
     fc_out[2] = split_dot(part[2], weights(lanes, lanes, mean=True))
 
 
@@ -245,7 +253,7 @@
     return side[i, :, cut], side[PX + i, :, cut], side[2 * PX, :, cut] if c_here else None, c_here
 
 
-def faces_kernel(xsize, ysize, place, u_in, e_in, r_in, ga_in, gb_in, fc_in, xlo, xhi, y_chip, y_next, u, e, r, ga, gb, fc_out, part, q, sides, sems):
+def faces_kernel(late, xsize, ysize, place, u_in, e_in, r_in, ga_in, gb_in, fc_in, xlo, xhi, y_chip, y_next, u, e, r, ga, gb, fc_out, part, q, sides, sems):
     n, (rows, lanes) = y_chip.shape[0], xlo.shape[1:]
     halves = lanes // LANES
     cut = [pl.ds(LANES * h, LANES) for h in range(halves)]
@@ -285,7 +293,8 @@
             second(u, ga, gb, e, x, row, 8, 1.0, True)
         return carry
 
-    lax.fori_loop(PX + 1, n + PX - 1, middle, 0, unroll=True)
+    lo, hi = late
+    both_ends(((PX + 1, PX + 2 * lo + 2), (PX + 2 * hi - 2, n + PX - 1)), middle)
     for x in (PX, PX + 1, n + PX - 2, n + PX - 1):
         finish(e, r, x, PY + 4, rows - 8, ok(x, PY + 4, rows - 8))
     row = lax.broadcasted_iota(jnp.int32, (8, LANES), 0)
@@ -296,7 +305,7 @@
         finish(e, r, x, high, 8, good_high)
         return carry
 
-    lax.fori_loop(PX + 2, n + PX - 2, last, 0, unroll=True)
+    both_ends(((PX + 2, PX + 2 * lo + 1), (PX + 2 * hi - 1, n + PX - 2)), last)
     m = n // 2 - 4
 
     def coarse(i, carry):
@@ -310,7 +319,7 @@
                     )
         return carry
 
-    lax.fori_loop(0, m, coarse, 0, unroll=True)
+    both_ends(((0, lo - 2), (hi - 2, m)), coarse)
     w = weights(lanes, lanes)
     for k in (0, 1):
         q[k] = split_dot(part[k], w)
@@ -369,6 +378,24 @@
         edge_out[0, k], edge_out[1, k] = val[4], val[5]
 
 
+def late_kernel(late, xsize, ysize, n, rows, place, u, e_in, r_in, ga, gb, e, r, out, t, part):
+    halves = u.shape[2]
+    ok = inside(place, n, rows, xsize, ysize)
+    del e_in, r_in
+    lo, hi = late
+    low = PY - 4
+    for x in range(PX + 2 * lo + 2, PX + 2 * hi - 2):
+        second(u, ga, gb, e, x, low, rows + 8, 1.0, True)
+    good = ok(PX, low, rows + 8)
+    for x in range(PX + 2 * lo + 1, PX + 2 * hi - 1):
+        finish(e, r, x, low, rows + 8, good)
+    w = weights(LANES * halves, LANES * halves)
+    for k in (0, 1):
+        for i in range(lo, hi):
+            restrict_xy(r, t, part, i - lo, 2 * i + PX - 1, PY - 1, rows // 2, k, (low, rows + 8))
+        out[k] = split_dot(part[k], w)
+
+
 def iterate_kernel(u, e, out):
     n, rows = out.shape[1:3]
     at = pl.ds(PY, rows)
@@ -379,7 +406,7 @@
                 out[k, x, :, pl.ds(LANES * h, LANES)] = e[k, x + PX, h, at, :] + 0.8 * u[k, x + PX, h, at, :]
         return carry
 
-    lax.fori_loop(0, n, step, 0, unroll=2)
+    lax.fori_loop(0, n, step, 0, unroll=8)
 
 
 def whole_level(cells, u, e, r, ga, gb, planes, used, row, rows, scale, full, ok, u_put):
@@ -398,7 +425,7 @@
             r[k, x, 0, at, :] = jnp.where(good, 0.04 * cells(k, x, at) + s, 0.0)
 
 
-def rows_kernel(xdev, halo, place, xlo, fc, xhi, edges, chip, other, window):
+def rows_kernel(xdev, halo, place, xlo, fc, fc_late, xhi, edges, chip, other, window):
     n, rows = fc.shape[1:3]
     row = lax.broadcasted_iota(jnp.int32, (8, LANES), 0)
     even = is_even(place, (8, LANES))
@@ -406,6 +433,8 @@
     for k in range(3):
         window[k, pl.ds(0, halo)] = xlo[pl.ds(k * halo, halo)]
         window[k, pl.ds(halo, n)] = fc[k]
+        if k < 2:
+            window[k, pl.ds(2 * halo, n - 2 * halo)] = fc_late[k]
         window[k, pl.ds(n + halo, halo)] = xhi[pl.ds(k * halo, halo)]
     for k in (0, 1):
         window[k, halo - 1] += edges[0, k]
@@ -550,6 +579,8 @@
     S = lambda *shape: jax.ShapeDtypeStruct(shape, f32)
     V = lambda *shape: pltpu.VMEM(shape, f32)
 
+    halo_next = 5
+    late = (halo_next, n // 2 - halo_next)
     halves = lanes // LANES
     state = (n + 2 * PX, halves, rows + 2 * PY, LANES)
     part = (n // 2, rows // 2, lanes)
@@ -578,7 +609,7 @@
     )(place, source, wavenumber_sq)
     y_chip, y_next = rows_step(y_chip, y_next)
     e, r, fc = pl.pallas_call(
-        inner_kernel,
+        functools.partial(inner_kernel, late),
         in_specs=[VMEM] * 5,
         out_specs=[VMEM] * 3,
         out_shape=[two, two, coarser],
@@ -603,7 +634,7 @@
     )
     in_place = {i + 1: i for i in range(6)}
     held = pl.pallas_call(
-        functools.partial(faces_kernel, xsize, ysize),
+        functools.partial(faces_kernel, late, xsize, ysize),
         in_specs=[SMEM] + [VMEM] * 6 + [ANY] * 2 + [VMEM] * 2,
         out_specs=[VMEM] * 6,
         out_shape=shapes,
@@ -613,7 +644,7 @@
         cost_estimate=pl.CostEstimate(flops=50_000_000, bytes_accessed=8_000_000, transcendentals=0),
         name="face_cells",
     )(place, *held, xlo, xhi, y_chip, y_next)
-    u, e, _, _, _, fc, edges = pl.pallas_call(
+    u, e, r, ga, gb, fc, edges = pl.pallas_call(
         functools.partial(corners_kernel, xsize, ysize, n, rows),
         in_specs=[SMEM] + [VMEM] * 8,
         out_specs=[VMEM] * 7,
@@ -625,9 +656,20 @@
     )(place, *held, c_chip, c_next)
     fine_shape = S(2, n, rows, lanes)
     n, rows, lanes, xsize, ysize, zsize = n // 2, rows // 2, lanes // 2, xsize // 2, ysize // 2, lanes // 2
-    h, over = 5, 1
+    h, over = halo_next, 1
     slab = lambda x, edge: jnp.concatenate([fc[:, x : x + h].reshape(3 * h, rows, lanes), edge], 0)
     xlo, xhi = planes_step(slab(0, edges[0]), slab(n - h, edges[1]))
+    e, _, fc_late = pl.pallas_call(
+        functools.partial(late_kernel, late, 2 * xsize, 2 * ysize, 2 * n, 2 * rows),
+        in_specs=[SMEM] + [VMEM] * 5,
+        out_specs=[VMEM] * 3,
+        out_shape=[two, two, S(2, late[1] - late[0], rows, lanes)],
+        input_output_aliases={2: 0, 3: 1},
+        scratch_shapes=[column, V(2, late[1] - late[0], rows, 2 * lanes)],
+        compiler_params=params(24),
+        cost_estimate=pl.CostEstimate(flops=30_000_000, bytes_accessed=8_000_000, transcendentals=0),
+        name="late_cells",
+    )(place, u, e, r, ga, gb)
     fine = pl.pallas_call(
         iterate_kernel,
         in_specs=[VMEM] * 2,
@@ -637,15 +679,15 @@
         cost_estimate=pl.CostEstimate(flops=1_000_000, bytes_accessed=8_000_000, transcendentals=0),
         name="fine_iterate",
     )(u, e)
-    xlo, xhi, fine = lax.optimization_barrier((xlo, xhi, fine))
+    xlo, xhi, fine, fc_late = lax.optimization_barrier((xlo, xhi, fine, fc_late))
     chip, other, window = pl.pallas_call(
         functools.partial(rows_kernel, xdev, h),
-        in_specs=[SMEM] + [VMEM] * 4,
+        in_specs=[SMEM] + [VMEM] * 5,
         out_specs=[VMEM] * 3,
         out_shape=[S(2, n + 2 * h, 8, lanes)] * 2 + [S(3, n + 2 * h, rows, lanes)],
         compiler_params=params(24),
         name="second_rows",
-    )(place, xlo, fc, xhi, edges)
+    )(place, xlo, fc, fc_late, xhi, edges)
     chip, other = rows_step(chip, other)
     state = (n + 2 * h, 1, rows + 16, LANES)
     work = lambda s: [V(*s), V(*s), V(2, *s), V(2, *s), V(2, *s), V(2, 1, *s[2:])]

time: 56.9 us -> 56.3 us (0.989)
  waiting for transfers between devices: 21.6 us -> 20 us
  Pallas kernels: 18.2 us -> 18.8 us
    ppermute x3, waiting for transfers between devices: 3.35 us -> 2.06 us  [planes_step(): lax.ppermute(last, 'gx', [(i, (i + 1) % xdev) for i in range(xdev)])]
    pallas_call x2 -> x3, Pallas kernels: 5.89 us -> 6.52 us  [the longest x1 2.92 us: body(): pl.pallas_call(functools.partial(faces_kernel, late, xsize, ysize), in_sp...]
    ppermute x4, starting transfers between devices: 7.37 us -> 7.96 us  [rows_step(): lax.ppermute(other, ('gx', 'gy'), next_chip)]
  transfers between devices with their start and end apart: 14 -> 14, of which waited for: 8 -> 6; matrix products, arithmetic and copies ran while one was open for 0% -> 0% of each run, Pallas kernels for 18% -> 19%
where the time goes in v12:
time: 56.3 us; the launch traced here: 55.6 us
  waiting for transfers between devices  20 us (36%)
  Pallas kernels  18.8 us (33%)
  starting transfers between devices  15.7 us (28%)
  between operations  0.86 us (2%)
    ppermute x4, waiting for transfers between devices, rows_step(): lax.ppermute(other, ('gx', 'gy'), next_chip)  12.7 us
    ppermute x4, starting transfers between devices, rows_step(): lax.ppermute(other, ('gx', 'gy'), next_chip)  7.96 us
    ppermute x3, waiting for transfers between devices, planes_step(): lax.ppermute(first, 'gx', [((i + 1) % xdev, i) for i in range(xdev)])  5.25 us
    ppermute x3, starting transfers between devices, planes_step(): lax.ppermute(last, 'gx', [(i, (i + 1) % xdev) for i in range(xdev)])  4.23 us
    ppermute x3, starting transfers between devices, planes_step(): lax.ppermute(first, 'gx', [((i + 1) % xdev, i) for i in range(xdev)])  3.26 us
    pallas_call x1, Pallas kernels, body(): pl.pallas_call(functools.partial(faces_kernel, late, xsize, ysize), in_sp...  2.92 us
    pallas_call x1, Pallas kernels, body(): pl.pallas_call(functools.partial(coarse_kernel, n, 4, xsize, ysize, zsize...  2.61 us
    ppermute x3, waiting for transfers between devices, planes_step(): lax.ppermute(last, 'gx', [(i, (i + 1) % xdev) for i in range(xdev)])  2.06 us
  transfers between devices with their start and end apart: 14, of which 6 were waited for; matrix products, arithmetic and copies ran while one was open for 0% of the time, Pallas kernels for 19%

profile of v12, /device:TPU:120, one launch (start us, length us, event | category | flops | bytes accessed | tf_op | source)
XLA Modules:
  0.0 55.6 jit_solution(13803998247616467428)
XLA Ops:
  0.7 2.0 %pack_planes.1 = (f32[7,32,256]{2,1,0:T(8,128)}, f32[7,32,256]{2,1,0:T(8,128)}) custom-call(f32[2,32,32,256]{3,2,1,0:T(8,128)} %f.3, f32[32,32,256]{2,1,0:T(8,128)} %c.3), custom_call_target="tpu_custom_call" | custom-call | tf_op jit(solution)/shard_map/pack_planes/pallas_call | solution.py:590
  2.6 3.2 %collective-permute-start = (f32[7,32,256]{2,1,0:T(8,128)}, f32[7,32,256]{2,1,0:T(8,128)S(1)}, u32[]{:S(2)}, u32[]{:S(2)}) collective-permute-start(f32[7,32,256]{2,1,0:T(8,128)} %get-tuple-element.56), channel_id=1, source_target_pairs={{0,32},{32,64},{64,96},{96,128},{128,160},{160,192},{192,224},{224... | collective-permute-start | bytes 688136 | tf_op jit(solution)/shard_map/ppermute | solution.py:565
  5.9 1.2 %first_iterate.1 = (f32[2,36,2,48,128]{4,3,2,1,0:T(8,128)S(1)}, f32[36,2,48,128]{3,2,1,0:T(8,128)S(1)}, f32[36,2,48,128]{3,2,1,0:T(8,128)S(1)}, f32[32,8,256]{2,1,0:T(8,128)S(1)}, f32[32,8,256]{2,1,0:T(8,128)S(1)}) custom-call(s32[2]{0:T(128)S(1)} %pad_add_fusion.place, f32[2,32,32,256]{3,2,1,0:T(8,128)S(1)} %copy-done, f32[32,32,256]{2,1,0:T(8,128)S(1)} %copy-done.1), custom_call_target="tpu_custom_call" | custom-call | flops 30000000 | bytes 8000000 | tf_op jit(solution)/shard_map/first_iterate/pallas_call | solution.py:601
  7.2 3.0 %collective-permute-start.3 = (f32[32,8,256]{2,1,0:T(8,128)S(1)}, f32[32,8,256]{2,1,0:T(8,128)S(1)}, u32[]{:S(2)}, u32[]{:S(2)}) collective-permute-start(f32[32,8,256]{2,1,0:T(8,128)S(1)} %get-tuple-element.75), channel_id=1, source_target_pairs={{0,32},{1,2},{2,1},{3,4},{4,3},{5,6},{6,5},{7,8},{8,7},{9,10},{10,... | collective-permute-start | bytes 786440 | tf_op jit(solution)/shard_map/ppermute | solution.py:575
  10.2 1.9 %inner_cells.1 = (f32[2,36,2,48,128]{4,3,2,1,0:T(8,128)S(1)}, f32[2,36,2,48,128]{4,3,2,1,0:T(8,128)S(1)}, f32[3,16,16,128]{3,2,1,0:T(8,128)S(1)}) custom-call(f32[2,32,32,256]{3,2,1,0:T(8,128)S(1)} %copy-done, f32[32,32,256]{2,1,0:T(8,128)S(1)} %copy-done.1, f32[2,36,2,48,128]{4,3,2,1,0:T(8,128)S(1)} %get-tuple-element.66.u.u_in, ...), custom_call_target="tpu_custom_call" | custom-call | flops 70000000 | bytes 16000000 | tf_op jit(solution)/shard_map/inner_cells/pallas_call | solution.py:611
  12.2 2.2 %collective-permute-done.1.xhi = f32[7,32,256]{2,1,0:T(8,128)} collective-permute-done((f32[7,32,256]{2,1,0:T(8,128)}, f32[7,32,256]{2,1,0:T(8,128)}, u32[]{:S(2)}, u32[]{:S(2)}) %collective-permute-start.1) | collective-permute-done | bytes 229408 | tf_op jit(solution)/shard_map/ppermute | solution.py:566
  14.4 1.4 %pack_corners.1 = (f32[10,4,256]{2,1,0:T(4,128)S(1)}, f32[10,4,256]{2,1,0:T(4,128)S(1)}) custom-call(s32[2]{0:T(128)S(1)} %pad_add_fusion.place, f32[7,32,256]{2,1,0:T(8,128)S(1)} %collective-permute-done.xlo, f32[7,32,256]{2,1,0:T(8,128)} %collective-permute-done.1.xhi), custom_call_target="tpu_custom_call" | custom-call | tf_op jit(solution)/shard_map/pack_corners/pallas_call | solution.py:625
  15.9 3.0 %collective-permute-start.5 = (f32[10,4,256]{2,1,0:T(4,128)S(1)}, f32[10,4,256]{2,1,0:T(4,128)S(1)}, u32[]{:S(2)}, u32[]{:S(2)}) collective-permute-start(f32[10,4,256]{2,1,0:T(4,128)S(1)} %get-tuple-element.83), channel_id=1, source_target_pairs={{0,32},{1,2},{2,1},{3,4},{4,3},{5,6},{6,5},{7,8},{8,7},{9,10},{10,... | collective-permute-start | bytes 122888 | tf_op jit(solution)/shard_map/ppermute | solution.py:575
  19.0 2.9 %face_cells.1 = (f32[2,36,2,48,128]{4,3,2,1,0:T(8,128)S(1)}, f32[2,36,2,48,128]{4,3,2,1,0:T(8,128)S(1)}, f32[2,36,2,48,128]{4,3,2,1,0:T(8,128)S(1)}, f32[36,2,48...) custom-call(s32[2]{0:T(128)S(1)} %pad_add_fusion.place, ...), custom_call_target="tpu_custom_call", output_to_operand_aliasing={{0}: (1, {}), {1}: (2, {}), {2}: (3, {}), {3}: (4, {}), {4}... | custom-call | flops 50000000 | bytes 8000000 | tf_op jit(solution)/shard_map/face_cells/pallas_call | solution.py:636
  21.9 1.0 %corner_cells.1 = (f32[2,36,2,48,128]{4,3,2,1,0:T(8,128)S(1)}, f32[2,36,2,48,128]{4,3,2,1,0:T(8,128)S(1)}, f32[2,36,2,48,128]{4,3,2,1,0:T(8,128)S(1)}, f32[36,2,...) custom-call(s32[2]{0:T(128)S(1)} %pad_add_fusion.place, ...), custom_call_target="tpu_custom_call", output_to_operand_aliasing={{0}: (1, {}), {1}: (2, {}), {2}: (3, {}), {3}: (4, {}), {4}... | custom-call | tf_op jit(solution)/shard_map/corner_cells/pallas_call | solution.py:647
  23.0 0.7 %collective-permute-start.6 = (f32[17,16,128]{2,1,0:T(8,128)S(1)}, f32[17,16,128]{2,1,0:T(8,128)S(1)}, u32[]{:S(2)}, u32[]{:S(2)}) collective-permute-start(f32[17,16,128]{2,1,0:T(8,128)S(1)} %pad_maximum_fusion), channel_id=1, source_target_pairs={{0,32},{32,64},{64,96},{96,128},{128,160},{160,192},{192,224},{224... | collective-permute-start | bytes 417800 | tf_op jit(solution)/shard_map/ppermute | solution.py:565
  23.8 1.5 %collective-permute-start.7 = (f32[17,16,128]{2,1,0:T(8,128)S(1)}, f32[17,16,128]{2,1,0:T(8,128)S(1)}, u32[]{:S(2)}, u32[]{:S(2)}) collective-permute-start(f32[17,16,128]{2,1,0:T(8,128)S(1)} %pad_maximum_fusion.1), channel_id=1, source_target_pairs={{32,0},{64,32},{96,64},{128,96},{160,128},{192,160},{224,192},{0,2... | collective-permute-start | bytes 417800 | tf_op jit(solution)/shard_map/ppermute | solution.py:566
  25.2 1.7 %late_cells.1 = (f32[2,36,2,48,128]{4,3,2,1,0:T(8,128)S(1)}, f32[2,36,2,48,128]{4,3,2,1,0:T(8,128)S(1)}, f32[2,6,16,128]{3,2,1,0:T(8,128)S(1)}) custom-call(s32[2]{0:T(128)S(1)} %pad_add_fusion.place, f32[2,36,2,48,128]{4,3,2,1,0:T(8,128)S(1)} %get-tuple-element.86.u, ...), custom_call_target="tpu_custom_call", output_to_operand_aliasing={{0}: (2, {}), {1}: (3, {})} | custom-call | flops 30000000 | bytes 8000000 | tf_op jit(solution)/shard_map/late_cells/pallas_call | solution.py:662
  26.9 1.6 %fine_iterate.1 = f32[2,32,32,256]{3,2,1,0:T(8,128)} custom-call(f32[2,36,2,48,128]{4,3,2,1,0:T(8,128)S(1)} %get-tuple-element.86.u, f32[2,36,2,48,128]{4,3,2,1,0:T(8,128)S(1)} %get-tuple-element.91.e), custom_call_target="tpu_custom_call" | custom-call | flops 1000000 | bytes 8000000 | tf_op jit(solution)/shard_map/fine_iterate/pallas_call | solution.py:673
  28.5 1.6 %collective-permute-done.7.xhi = f32[17,16,128]{2,1,0:T(8,128)S(1)} collective-permute-done((f32[17,16,128]{2,1,0:T(8,128)S(1)}, f32[17,16,128]{2,1,0:T(8,128)S(1)}, u32[]{:S(2)}, u32[]{:S(2)}) %collective-permute-start.7) | collective-permute-done | bytes 139296 | tf_op jit(solution)/shard_map/ppermute | solution.py:566
  30.1 0.6 %second_rows.1 = (f32[2,26,8,128]{3,2,1,0:T(8,128)S(1)}, f32[2,26,8,128]{3,2,1,0:T(8,128)S(1)}, f32[3,26,16,128]{3,2,1,0:T(8,128)S(1)}) custom-call(s32[2]{0:T(128)S(1)} %pad_add_fusion.place, f32[17,16,128]{2,1,0:T(8,128)S(1)} %collective-permute-done.6.xlo, f32[3,16,16,128]{3,2,1,0:T(8,128)S(1)} %get-tuple-element.84.fc, ...), custom_call_target="tpu_custom_call" | custom-call | tf_op jit(solution)/shard_map/second_rows/pallas_call | solution.py:683
  30.8 1.5 %collective-permute-start.9 = (f32[2,26,8,128]{3,2,1,0:T(8,128)S(1)}, f32[2,26,8,128]{3,2,1,0:T(8,128)S(1)}, u32[]{:S(2)}, u32[]{:S(2)}) collective-permute-start(f32[2,26,8,128]{3,2,1,0:T(8,128)S(1)} %get-tuple-element.99), channel_id=1, source_target_pairs={{0,32},{1,2},{2,1},{3,4},{4,3},{5,6},{6,5},{7,8},{8,7},{9,10},{10,... | collective-permute-start | bytes 638984 | tf_op jit(solution)/shard_map/ppermute | solution.py:575
  32.4 6.1 %collective-permute-done.9.y_next = f32[2,26,8,128]{3,2,1,0:T(8,128)S(1)} collective-permute-done((f32[2,26,8,128]{3,2,1,0:T(8,128)S(1)}, f32[2,26,8,128]{3,2,1,0:T(8,128)S(1)}, u32[]{:S(2)}, u32[]{:S(2)}) %collective-permute-start.9) | collective-permute-done | bytes 213024 | tf_op jit(solution)/shard_map/ppermute | solution.py:575
  38.5 1.9 %second_level.1 = (f32[2,16,16,128]{3,2,1,0:T(8,128)}, f32[15,10,128]{2,1,0:T(8,128)S(1)}) custom-call(s32[2]{0:T(128)S(1)} %pad_add_fusion.place, f32[3,26,16,128]{3,2,1,0:T(8,128)S(1)} %get-tuple-element.97.window, f32[2,26,8,128]{3,2,1,0:T(8,128)S(1)} %collective-permute-done.8.y_chip, f32[2,26,8,128]{3,2,1,0:T(8,128)S(1)} %collective-permute-done.9.y_next), custom_call_target="tpu_custom_call" | custom-call | tf_op jit(solution)/shard_map/second_level/pallas_call | solution.py:695
  40.7 1.8 %collective-permute-start.11 = (f32[12,8,128]{2,1,0:T(8,128)S(1)}, f32[12,8,128]{2,1,0:T(8,128)S(1)}, u32[]{:S(2)}, u32[]{:S(2)}) collective-permute-start(f32[12,8,128]{2,1,0:T(8,128)S(1)} %pad_maximum_fusion.3), channel_id=1, source_target_pairs={{32,0},{64,32},{96,64},{128,96},{160,128},{192,160},{224,192},{0,2... | collective-permute-start | bytes 147464 | tf_op jit(solution)/shard_map/ppermute | solution.py:566
  42.5 2.1 %collective-permute-done.10.xlo = f32[12,8,128]{2,1,0:T(8,128)S(1)} collective-permute-done((f32[12,8,128]{2,1,0:T(8,128)S(1)}, f32[12,8,128]{2,1,0:T(8,128)S(1)}, u32[]{:S(2)}, u32[]{:S(2)}) %collective-permute-start.10) | collective-permute-done | bytes 49184 | tf_op jit(solution)/shard_map/ppermute | solution.py:565
  44.6 1.4 %collective-permute-done.11.xhi = f32[12,8,128]{2,1,0:T(8,128)S(1)} collective-permute-done((f32[12,8,128]{2,1,0:T(8,128)S(1)}, f32[12,8,128]{2,1,0:T(8,128)S(1)}, u32[]{:S(2)}, u32[]{:S(2)}) %collective-permute-start.11) | collective-permute-done | bytes 49184 | tf_op jit(solution)/shard_map/ppermute | solution.py:566
  46.4 6.6 %collective-permute-done.13.y_next = f32[39,8,128]{2,1,0:T(8,128)S(1)} collective-permute-done((f32[39,8,128]{2,1,0:T(8,128)S(1)}, f32[39,8,128]{2,1,0:T(8,128)S(1)}, u32[]{:S(2)}, u32[]{:S(2)}) %collective-permute-start.13) | collective-permute-done | bytes 159776 | tf_op jit(solution)/shard_map/ppermute | solution.py:575
  53.0 2.6 %coarse_levels.1 = (f32[2,8,8,64]{3,2,1,0:T(8,128)}, f32[2,4,4,32]{3,2,1,0:T(4,128)}) custom-call(s32[2]{0:T(128)S(1)} %pad_add_fusion.place, f32[15,10,128]{2,1,0:T(8,128)S(1)} %get-tuple-element.101.fc_own, f32[12,8,128]{2,1,0:T(8,128)S(1)} %collective-permute-done.10.xlo, f32[12,8,128]{2,1,0:T(8,128)S(1)} %collective-permute-done.11.xhi, ...), custom_call_target="tpu_custom_call" | custom-call | tf_op jit(solution)/shard_map/coarse_levels/pallas_call | solution.py:719
  (37 shorter events, 1.2 us)
Async XLA Ops:
  0.6 5.3 %copy-start.1 = (f32[32,32,256]{2,1,0:T(8,128)S(1)}, f32[32,32,256]{2,1,0:T(8,128)}, u32[]{:S(2)}) copy-start(f32[32,32,256]{2,1,0:T(8,128)} %c.3) | copy-start | bytes 3145732
  0.6 5.3 %copy-start = (f32[2,32,32,256]{3,2,1,0:T(8,128)S(1)}, f32[2,32,32,256]{3,2,1,0:T(8,128)}, u32[]{:S(2)}) copy-start(f32[2,32,32,256]{3,2,1,0:T(8,128)} %f.3) | copy-start | bytes 6291460
  2.6 9.6 %collective-permute-start = (f32[7,32,256]{2,1,0:T(8,128)}, f32[7,32,256]{2,1,0:T(8,128)S(1)}, u32[]{:S(2)}, u32[]{:S(2)}) collective-permute-start(f32[7,32,256]{2,1,0:T(8,128)} %get-tuple-element.56), channel_id=1, source_target_pairs={{0,32},{32,64},{64,96},{96,128},{128,160},{160,192},{192,224},{224... | collective-permute-start | bytes 688136 | tf_op jit(solution)/shard_map/ppermute | solution.py:565
  5.8 8.6 %collective-permute-start.1 = (f32[7,32,256]{2,1,0:T(8,128)}, f32[7,32,256]{2,1,0:T(8,128)}, u32[]{:S(2)}, u32[]{:S(2)}) collective-permute-start(f32[7,32,256]{2,1,0:T(8,128)} %get-tuple-element.57), channel_id=1, source_target_pairs={{32,0},{64,32},{96,64},{128,96},{160,128},{192,160},{224,192},{0,2... | collective-permute-start | bytes 688136 | tf_op jit(solution)/shard_map/ppermute | solution.py:566
  7.1 11.9 %collective-permute-start.2 = (f32[32,8,256]{2,1,0:T(8,128)S(1)}, f32[32,8,256]{2,1,0:T(8,128)S(1)}, u32[]{:S(2)}, u32[]{:S(2)}) collective-permute-start(f32[32,8,256]{2,1,0:T(8,128)S(1)} %get-tuple-element.74), channel_id=1, source_target_pairs={{0,1},{1,0},{2,3},{3,2},{4,5},{5,4},{6,7},{7,6},{8,9},{9,8},{10,11... | collective-permute-start | bytes 786440 | tf_op jit(solution)/shard_map/ppermute | solution.py:575
  7.2 11.8 %collective-permute-start.3 = (f32[32,8,256]{2,1,0:T(8,128)S(1)}, f32[32,8,256]{2,1,0:T(8,128)S(1)}, u32[]{:S(2)}, u32[]{:S(2)}) collective-permute-start(f32[32,8,256]{2,1,0:T(8,128)S(1)} %get-tuple-element.75), channel_id=1, source_target_pairs={{0,32},{1,2},{2,1},{3,4},{4,3},{5,6},{6,5},{7,8},{8,7},{9,10},{10,... | collective-permute-start | bytes 786440 | tf_op jit(solution)/shard_map/ppermute | solution.py:575
  15.8 6.1 %collective-permute-start.4 = (f32[10,4,256]{2,1,0:T(4,128)S(1)}, f32[10,4,256]{2,1,0:T(4,128)S(1)}, u32[]{:S(2)}, u32[]{:S(2)}) collective-permute-start(f32[10,4,256]{2,1,0:T(4,128)S(1)} %get-tuple-element.82), channel_id=1, source_target_pairs={{0,1},{1,0},{2,3},{3,2},{4,5},{5,4},{6,7},{7,6},{8,9},{9,8},{10,11... | collective-permute-start | bytes 122888 | tf_op jit(solution)/shard_map/ppermute | solution.py:575
  15.9 6.0 %collective-permute-start.5 = (f32[10,4,256]{2,1,0:T(4,128)S(1)}, f32[10,4,256]{2,1,0:T(4,128)S(1)}, u32[]{:S(2)}, u32[]{:S(2)}) collective-permute-start(f32[10,4,256]{2,1,0:T(4,128)S(1)} %get-tuple-element.83), channel_id=1, source_target_pairs={{0,32},{1,2},{2,1},{3,4},{4,3},{5,6},{6,5},{7,8},{8,7},{9,10},{10,... | collective-permute-start | bytes 122888 | tf_op jit(solution)/shard_map/ppermute | solution.py:575
  23.0 5.4 %collective-permute-start.6 = (f32[17,16,128]{2,1,0:T(8,128)S(1)}, f32[17,16,128]{2,1,0:T(8,128)S(1)}, u32[]{:S(2)}, u32[]{:S(2)}) collective-permute-start(f32[17,16,128]{2,1,0:T(8,128)S(1)} %pad_maximum_fusion), channel_id=1, source_target_pairs={{0,32},{32,64},{64,96},{96,128},{128,160},{160,192},{192,224},{224... | collective-permute-start | bytes 417800 | tf_op jit(solution)/shard_map/ppermute | solution.py:565
  23.8 6.3 %collective-permute-start.7 = (f32[17,16,128]{2,1,0:T(8,128)S(1)}, f32[17,16,128]{2,1,0:T(8,128)S(1)}, u32[]{:S(2)}, u32[]{:S(2)}) collective-permute-start(f32[17,16,128]{2,1,0:T(8,128)S(1)} %pad_maximum_fusion.1), channel_id=1, source_target_pairs={{32,0},{64,32},{96,64},{128,96},{160,128},{192,160},{224,192},{0,2... | collective-permute-start | bytes 417800 | tf_op jit(solution)/shard_map/ppermute | solution.py:566
  30.7 1.7 %collective-permute-start.8 = (f32[2,26,8,128]{3,2,1,0:T(8,128)S(1)}, f32[2,26,8,128]{3,2,1,0:T(8,128)S(1)}, u32[]{:S(2)}, u32[]{:S(2)}) collective-permute-start(f32[2,26,8,128]{3,2,1,0:T(8,128)S(1)} %get-tuple-element.98), channel_id=1, source_target_pairs={{0,1},{1,0},{2,3},{3,2},{4,5},{5,4},{6,7},{7,6},{8,9},{9,8},{10,11... | collective-permute-start | bytes 638984 | tf_op jit(solution)/shard_map/ppermute | solution.py:575
  30.8 7.6 %collective-permute-start.9 = (f32[2,26,8,128]{3,2,1,0:T(8,128)S(1)}, f32[2,26,8,128]{3,2,1,0:T(8,128)S(1)}, u32[]{:S(2)}, u32[]{:S(2)}) collective-permute-start(f32[2,26,8,128]{3,2,1,0:T(8,128)S(1)} %get-tuple-element.99), channel_id=1, source_target_pairs={{0,32},{1,2},{2,1},{3,4},{4,3},{5,6},{6,5},{7,8},{8,7},{9,10},{10,... | collective-permute-start | bytes 638984 | tf_op jit(solution)/shard_map/ppermute | solution.py:575
  40.4 4.2 %collective-permute-start.10 = (f32[12,8,128]{2,1,0:T(8,128)S(1)}, f32[12,8,128]{2,1,0:T(8,128)S(1)}, u32[]{:S(2)}, u32[]{:S(2)}) collective-permute-start(f32[12,8,128]{2,1,0:T(8,128)S(1)} %pad_maximum_fusion.2), channel_id=1, source_target_pairs={{0,32},{32,64},{64,96},{96,128},{128,160},{160,192},{192,224},{224... | collective-permute-start | bytes 147464 | tf_op jit(solution)/shard_map/ppermute | solution.py:565
  40.7 5.3 %collective-permute-start.11 = (f32[12,8,128]{2,1,0:T(8,128)S(1)}, f32[12,8,128]{2,1,0:T(8,128)S(1)}, u32[]{:S(2)}, u32[]{:S(2)}) collective-permute-start(f32[12,8,128]{2,1,0:T(8,128)S(1)} %pad_maximum_fusion.3), channel_id=1, source_target_pairs={{32,0},{64,32},{96,64},{128,96},{160,128},{192,160},{224,192},{0,2... | collective-permute-start | bytes 147464 | tf_op jit(solution)/shard_map/ppermute | solution.py:566
  46.1 6.9 %collective-permute-start.13 = (f32[39,8,128]{2,1,0:T(8,128)S(1)}, f32[39,8,128]{2,1,0:T(8,128)S(1)}, u32[]{:S(2)}, u32[]{:S(2)}) collective-permute-start(f32[39,8,128]{2,1,0:T(8,128)S(1)} %get-tuple-element.106), channel_id=1, source_target_pairs={{0,32},{1,2},{2,1},{3,4},{4,3},{5,6},{6,5},{7,8},{8,7},{9,10},{10,... | collective-permute-start | bytes 479240 | tf_op jit(solution)/shard_map/ppermute | solution.py:575
  46.4 6.6 %collective-permute-start.12 = (f32[39,8,128]{2,1,0:T(8,128)S(1)}, f32[39,8,128]{2,1,0:T(8,128)S(1)}, u32[]{:S(2)}, u32[]{:S(2)}) collective-permute-start(f32[39,8,128]{2,1,0:T(8,128)S(1)} %get-tuple-element.107), channel_id=1, source_target_pairs={{0,1},{1,0},{2,3},{3,2},{4,5},{5,4},{6,7},{7,6},{8,9},{9,8},{10,11... | collective-permute-start | bytes 479240 | tf_op jit(solution)/shard_map/ppermute | solution.py:575

commit v13 on v12

--- a/solution.py
+++ b/solution.py
@@ -378,35 +378,40 @@
         edge_out[0, k], edge_out[1, k] = val[4], val[5]
 
 
-def late_kernel(late, xsize, ysize, n, rows, place, u, e_in, r_in, ga, gb, e, r, out, t, part):
+def late_kernel(late, xsize, ysize, n, rows, place, u, e_in, r_in, ga, gb, e, r, out, fine, t, part, made, sems):
     halves = u.shape[2]
     ok = inside(place, n, rows, xsize, ysize)
     del e_in, r_in
     lo, hi = late
     low = PY - 4
+    own = pl.ds(PY, rows)
+    copies = []
+
+    def iterate(first, last):
+        for x in range(first, last):
+            for k in (0, 1):
+                for h in range(halves):
+                    made[k, x, :, pl.ds(LANES * h, LANES)] = e[k, x + PX, h, own, :] + 0.8 * u[k, x + PX, h, own, :]
+        at = pl.ds(first, last - first)
+        for k in (0, 1):
+            copies.append(pltpu.make_async_copy(made.at[k, at], fine.at[k, at], sems.at[len(copies)]))
+            copies[-1].start()
+
+    iterate(0, 2 * lo + 2)
+    iterate(2 * hi - 2, n)
     for x in range(PX + 2 * lo + 2, PX + 2 * hi - 2):
         second(u, ga, gb, e, x, low, rows + 8, 1.0, True)
     good = ok(PX, low, rows + 8)
     for x in range(PX + 2 * lo + 1, PX + 2 * hi - 1):
         finish(e, r, x, low, rows + 8, good)
+    iterate(2 * lo + 2, 2 * hi - 2)
     w = weights(LANES * halves, LANES * halves)
     for k in (0, 1):
         for i in range(lo, hi):
             restrict_xy(r, t, part, i - lo, 2 * i + PX - 1, PY - 1, rows // 2, k, (low, rows + 8))
         out[k] = split_dot(part[k], w)
-
-
-def iterate_kernel(u, e, out):
-    n, rows = out.shape[1:3]
-    at = pl.ds(PY, rows)
-
-    def step(x, carry):
-        for k in (0, 1):
-            for h in range(u.shape[2]):
-                out[k, x, :, pl.ds(LANES * h, LANES)] = e[k, x + PX, h, at, :] + 0.8 * u[k, x + PX, h, at, :]
-        return carry
-
-    lax.fori_loop(0, n, step, 0, unroll=8)
+    for copy in copies:
+        copy.wait()
 
 
 def whole_level(cells, u, e, r, ga, gb, planes, used, row, rows, scale, full, ok, u_put):
@@ -659,26 +664,17 @@
     h, over = halo_next, 1
     slab = lambda x, edge: jnp.concatenate([fc[:, x : x + h].reshape(3 * h, rows, lanes), edge], 0)
     xlo, xhi = planes_step(slab(0, edges[0]), slab(n - h, edges[1]))
-    e, _, fc_late = pl.pallas_call(
+    _, _, fc_late, fine = pl.pallas_call(
         functools.partial(late_kernel, late, 2 * xsize, 2 * ysize, 2 * n, 2 * rows),
         in_specs=[SMEM] + [VMEM] * 5,
-        out_specs=[VMEM] * 3,
-        out_shape=[two, two, S(2, late[1] - late[0], rows, lanes)],
+        out_specs=[VMEM] * 3 + [ANY],
+        out_shape=[two, two, S(2, late[1] - late[0], rows, lanes), fine_shape],
         input_output_aliases={2: 0, 3: 1},
-        scratch_shapes=[column, V(2, late[1] - late[0], rows, 2 * lanes)],
+        scratch_shapes=[column, V(2, late[1] - late[0], rows, 2 * lanes), V(*fine_shape.shape), pltpu.SemaphoreType.DMA((6,))],
         compiler_params=params(24),
         cost_estimate=pl.CostEstimate(flops=30_000_000, bytes_accessed=8_000_000, transcendentals=0),
         name="late_cells",
     )(place, u, e, r, ga, gb)
-    fine = pl.pallas_call(
-        iterate_kernel,
-        in_specs=[VMEM] * 2,
-        out_specs=VMEM,
-        out_shape=fine_shape,
-        compiler_params=params(24),
-        cost_estimate=pl.CostEstimate(flops=1_000_000, bytes_accessed=8_000_000, transcendentals=0),
-        name="fine_iterate",
-    )(u, e)
     xlo, xhi, fine, fc_late = lax.optimization_barrier((xlo, xhi, fine, fc_late))
     chip, other, window = pl.pallas_call(
         functools.partial(rows_kernel, xdev, h),

time: 56.3 us -> 56.3 us (level)
  Pallas kernels: 18.8 us -> 18.1 us
  waiting for transfers between devices: 20 us -> 20.7 us
    pallas_call x1 -> x0, Pallas kernels: 1.59 us -> none  [body(): pl.pallas_call(iterate_kernel, in_specs=[VMEM] * 2, out_specs=VMEM, out_s...]
    pallas_call x1, Pallas kernels: 1.65 us -> 2.51 us  [body(): pl.pallas_call(functools.partial(late_kernel, late, 2 * xsize, 2 * ysize,...]
  transfers between devices with their start and end apart: 14 -> 14, of which waited for: 6 -> 7; matrix products, arithmetic and copies ran while one was open for 0% -> 0% of each run, Pallas kernels for 19% -> 18%
where the time goes in v13:
time: 56.3 us; the launch traced here: 55.5 us
  waiting for transfers between devices  20.7 us (37%)
  Pallas kernels  18.1 us (32%)
  starting transfers between devices  15.6 us (28%)
  between operations  0.87 us (2%)
    ppermute x4, waiting for transfers between devices, rows_step(): lax.ppermute(other, ('gx', 'gy'), next_chip)  12.8 us
    ppermute x4, starting transfers between devices, rows_step(): lax.ppermute(other, ('gx', 'gy'), next_chip)  7.85 us
    ppermute x3, waiting for transfers between devices, planes_step(): lax.ppermute(first, 'gx', [((i + 1) % xdev, i) for i in range(xdev)])  5.44 us
    ppermute x3, starting transfers between devices, planes_step(): lax.ppermute(last, 'gx', [(i, (i + 1) % xdev) for i in range(xdev)])  4.01 us
    ppermute x3, starting transfers between devices, planes_step(): lax.ppermute(first, 'gx', [((i + 1) % xdev, i) for i in range(xdev)])  3.46 us
    pallas_call x1, Pallas kernels, body(): pl.pallas_call(functools.partial(faces_kernel, late, xsize, ysize), in_sp...  2.92 us
    pallas_call x1, Pallas kernels, body(): pl.pallas_call(functools.partial(coarse_kernel, n, 4, xsize, ysize, zsize...  2.61 us
    pallas_call x1, Pallas kernels, body(): pl.pallas_call(functools.partial(late_kernel, late, 2 * xsize, 2 * ysize,...  2.51 us
  transfers between devices with their start and end apart: 14, of which 7 were waited for; matrix products, arithmetic and copies ran while one was open for 0% of the time, Pallas kernels for 18%

profile of v13, /device:TPU:120, one launch (start us, length us, event | category | flops | bytes accessed | tf_op | source)
XLA Modules:
  0.0 55.5 jit_solution(713808849810902893)
XLA Ops:
  0.7 2.0 %pack_planes.1 = (f32[7,32,256]{2,1,0:T(8,128)}, f32[7,32,256]{2,1,0:T(8,128)}) custom-call(f32[2,32,32,256]{3,2,1,0:T(8,128)} %f.3, f32[32,32,256]{2,1,0:T(8,128)} %c.3), custom_call_target="tpu_custom_call" | custom-call | tf_op jit(solution)/shard_map/pack_planes/pallas_call | solution.py:595
  2.6 3.2 %collective-permute-start = (f32[7,32,256]{2,1,0:T(8,128)}, f32[7,32,256]{2,1,0:T(8,128)S(1)}, u32[]{:S(2)}, u32[]{:S(2)}) collective-permute-start(f32[7,32,256]{2,1,0:T(8,128)} %get-tuple-element.56), channel_id=1, source_target_pairs={{0,32},{32,64},{64,96},{96,128},{128,160},{160,192},{192,224},{224... | collective-permute-start | bytes 688136 | tf_op jit(solution)/shard_map/ppermute | solution.py:570
  5.9 1.2 %first_iterate.1 = (f32[2,36,2,48,128]{4,3,2,1,0:T(8,128)S(1)}, f32[36,2,48,128]{3,2,1,0:T(8,128)S(1)}, f32[36,2,48,128]{3,2,1,0:T(8,128)S(1)}, f32[32,8,256]{2,1,0:T(8,128)S(1)}, f32[32,8,256]{2,1,0:T(8,128)S(1)}) custom-call(s32[2]{0:T(128)S(1)} %pad_add_fusion.place, f32[2,32,32,256]{3,2,1,0:T(8,128)S(1)} %copy-done, f32[32,32,256]{2,1,0:T(8,128)S(1)} %copy-done.1), custom_call_target="tpu_custom_call" | custom-call | flops 30000000 | bytes 8000000 | tf_op jit(solution)/shard_map/first_iterate/pallas_call | solution.py:606
  7.2 3.0 %collective-permute-start.3 = (f32[32,8,256]{2,1,0:T(8,128)S(1)}, f32[32,8,256]{2,1,0:T(8,128)S(1)}, u32[]{:S(2)}, u32[]{:S(2)}) collective-permute-start(f32[32,8,256]{2,1,0:T(8,128)S(1)} %get-tuple-element.75), channel_id=1, source_target_pairs={{0,32},{1,2},{2,1},{3,4},{4,3},{5,6},{6,5},{7,8},{8,7},{9,10},{10,... | collective-permute-start | bytes 786440 | tf_op jit(solution)/shard_map/ppermute | solution.py:580
  10.2 1.9 %inner_cells.1 = (f32[2,36,2,48,128]{4,3,2,1,0:T(8,128)S(1)}, f32[2,36,2,48,128]{4,3,2,1,0:T(8,128)S(1)}, f32[3,16,16,128]{3,2,1,0:T(8,128)S(1)}) custom-call(f32[2,32,32,256]{3,2,1,0:T(8,128)S(1)} %copy-done, f32[32,32,256]{2,1,0:T(8,128)S(1)} %copy-done.1, f32[2,36,2,48,128]{4,3,2,1,0:T(8,128)S(1)} %get-tuple-element.66.u.u_in, ...), custom_call_target="tpu_custom_call" | custom-call | flops 70000000 | bytes 16000000 | tf_op jit(solution)/shard_map/inner_cells/pallas_call | solution.py:616
  12.2 2.2 %collective-permute-done.1.xhi = f32[7,32,256]{2,1,0:T(8,128)} collective-permute-done((f32[7,32,256]{2,1,0:T(8,128)}, f32[7,32,256]{2,1,0:T(8,128)}, u32[]{:S(2)}, u32[]{:S(2)}) %collective-permute-start.1) | collective-permute-done | bytes 229408 | tf_op jit(solution)/shard_map/ppermute | solution.py:571
  14.4 1.4 %pack_corners.1 = (f32[10,4,256]{2,1,0:T(4,128)S(1)}, f32[10,4,256]{2,1,0:T(4,128)S(1)}) custom-call(s32[2]{0:T(128)S(1)} %pad_add_fusion.place, f32[7,32,256]{2,1,0:T(8,128)S(1)} %collective-permute-done.xlo, f32[7,32,256]{2,1,0:T(8,128)} %collective-permute-done.1.xhi), custom_call_target="tpu_custom_call" | custom-call | tf_op jit(solution)/shard_map/pack_corners/pallas_call | solution.py:630
  15.9 3.0 %collective-permute-start.5 = (f32[10,4,256]{2,1,0:T(4,128)S(1)}, f32[10,4,256]{2,1,0:T(4,128)S(1)}, u32[]{:S(2)}, u32[]{:S(2)}) collective-permute-start(f32[10,4,256]{2,1,0:T(4,128)S(1)} %get-tuple-element.83), channel_id=1, source_target_pairs={{0,32},{1,2},{2,1},{3,4},{4,3},{5,6},{6,5},{7,8},{8,7},{9,10},{10,... | collective-permute-start | bytes 122888 | tf_op jit(solution)/shard_map/ppermute | solution.py:580
  19.0 2.9 %face_cells.1 = (f32[2,36,2,48,128]{4,3,2,1,0:T(8,128)S(1)}, f32[2,36,2,48,128]{4,3,2,1,0:T(8,128)S(1)}, f32[2,36,2,48,128]{4,3,2,1,0:T(8,128)S(1)}, f32[36,2,48...) custom-call(s32[2]{0:T(128)S(1)} %pad_add_fusion.place, ...), custom_call_target="tpu_custom_call", output_to_operand_aliasing={{0}: (1, {}), {1}: (2, {}), {2}: (3, {}), {3}: (4, {}), {4}... | custom-call | flops 50000000 | bytes 8000000 | tf_op jit(solution)/shard_map/face_cells/pallas_call | solution.py:641
  21.9 1.0 %corner_cells.1 = (f32[2,36,2,48,128]{4,3,2,1,0:T(8,128)S(1)}, f32[2,36,2,48,128]{4,3,2,1,0:T(8,128)S(1)}, f32[2,36,2,48,128]{4,3,2,1,0:T(8,128)S(1)}, f32[36,2,...) custom-call(s32[2]{0:T(128)S(1)} %pad_add_fusion.place, ...), custom_call_target="tpu_custom_call", output_to_operand_aliasing={{0}: (1, {}), {1}: (2, {}), {2}: (3, {}), {3}: (4, {}), {4}... | custom-call | tf_op jit(solution)/shard_map/corner_cells/pallas_call | solution.py:652
  23.0 0.7 %collective-permute-start.6 = (f32[17,16,128]{2,1,0:T(8,128)S(1)}, f32[17,16,128]{2,1,0:T(8,128)S(1)}, u32[]{:S(2)}, u32[]{:S(2)}) collective-permute-start(f32[17,16,128]{2,1,0:T(8,128)S(1)} %pad_maximum_fusion), channel_id=1, source_target_pairs={{0,32},{32,64},{64,96},{96,128},{128,160},{160,192},{192,224},{224... | collective-permute-start | bytes 417800 | tf_op jit(solution)/shard_map/ppermute | solution.py:570
  23.8 1.5 %collective-permute-start.7 = (f32[17,16,128]{2,1,0:T(8,128)S(1)}, f32[17,16,128]{2,1,0:T(8,128)S(1)}, u32[]{:S(2)}, u32[]{:S(2)}) collective-permute-start(f32[17,16,128]{2,1,0:T(8,128)S(1)} %pad_maximum_fusion.1), channel_id=1, source_target_pairs={{32,0},{64,32},{96,64},{128,96},{160,128},{192,160},{224,192},{0,2... | collective-permute-start | bytes 417800 | tf_op jit(solution)/shard_map/ppermute | solution.py:571
  25.2 2.5 %late_cells.1 = (f32[2,36,2,48,128]{4,3,2,1,0:T(8,128)S(1)}, f32[2,36,2,48,128]{4,3,2,1,0:T(8,128)S(1)}, f32[2,6,16,128]{3,2,1,0:T(8,128)S(1)}, f32[2,32,32,256]{3,2,1,0:T(8,128)}) custom-call(s32[2]{0:T(128)S(1)} %pad_add_fusion.place, f32[2,36,2,48,128]{4,3,2,1,0:T(8,128)S(1)} %get-tuple-element.86.u, ...), custom_call_target="tpu_custom_call", output_to_operand_aliasing={{0}: (2, {}), {1}: (3, {})} | custom-call | flops 30000000 | bytes 8000000 | tf_op jit(solution)/shard_map/late_cells/pallas_call | solution.py:667
  27.7 0.4 collective-permute-done.6.xlo
  28.2 1.9 %collective-permute-done.7.xhi = f32[17,16,128]{2,1,0:T(8,128)S(1)} collective-permute-done((f32[17,16,128]{2,1,0:T(8,128)S(1)}, f32[17,16,128]{2,1,0:T(8,128)S(1)}, u32[]{:S(2)}, u32[]{:S(2)}) %collective-permute-start.7) | collective-permute-done | bytes 139296 | tf_op jit(solution)/shard_map/ppermute | solution.py:571
  30.1 0.6 %second_rows.1 = (f32[2,26,8,128]{3,2,1,0:T(8,128)S(1)}, f32[2,26,8,128]{3,2,1,0:T(8,128)S(1)}, f32[3,26,16,128]{3,2,1,0:T(8,128)S(1)}) custom-call(s32[2]{0:T(128)S(1)} %pad_add_fusion.place, f32[17,16,128]{2,1,0:T(8,128)S(1)} %collective-permute-done.6.xlo, f32[3,16,16,128]{3,2,1,0:T(8,128)S(1)} %get-tuple-element.84.fc, ...), custom_call_target="tpu_custom_call" | custom-call | tf_op jit(solution)/shard_map/second_rows/pallas_call | solution.py:679
  30.8 1.5 %collective-permute-start.9 = (f32[2,26,8,128]{3,2,1,0:T(8,128)S(1)}, f32[2,26,8,128]{3,2,1,0:T(8,128)S(1)}, u32[]{:S(2)}, u32[]{:S(2)}) collective-permute-start(f32[2,26,8,128]{3,2,1,0:T(8,128)S(1)} %get-tuple-element.99), channel_id=1, source_target_pairs={{0,32},{1,2},{2,1},{3,4},{4,3},{5,6},{6,5},{7,8},{8,7},{9,10},{10,... | collective-permute-start | bytes 638984 | tf_op jit(solution)/shard_map/ppermute | solution.py:580
  32.4 6.1 %collective-permute-done.9.y_next = f32[2,26,8,128]{3,2,1,0:T(8,128)S(1)} collective-permute-done((f32[2,26,8,128]{3,2,1,0:T(8,128)S(1)}, f32[2,26,8,128]{3,2,1,0:T(8,128)S(1)}, u32[]{:S(2)}, u32[]{:S(2)}) %collective-permute-start.9) | collective-permute-done | bytes 213024 | tf_op jit(solution)/shard_map/ppermute | solution.py:580
  38.5 1.9 %second_level.1 = (f32[2,16,16,128]{3,2,1,0:T(8,128)}, f32[15,10,128]{2,1,0:T(8,128)S(1)}) custom-call(s32[2]{0:T(128)S(1)} %pad_add_fusion.place, f32[3,26,16,128]{3,2,1,0:T(8,128)S(1)} %get-tuple-element.97.window, f32[2,26,8,128]{3,2,1,0:T(8,128)S(1)} %collective-permute-done.8.y_chip, f32[2,26,8,128]{3,2,1,0:T(8,128)S(1)} %collective-permute-done.9.y_next), custom_call_target="tpu_custom_call" | custom-call | tf_op jit(solution)/shard_map/second_level/pallas_call | solution.py:691
  40.5 2.0 %collective-permute-start.11 = (f32[12,8,128]{2,1,0:T(8,128)S(1)}, f32[12,8,128]{2,1,0:T(8,128)S(1)}, u32[]{:S(2)}, u32[]{:S(2)}) collective-permute-start(f32[12,8,128]{2,1,0:T(8,128)S(1)} %pad_maximum_fusion.3), channel_id=1, source_target_pairs={{32,0},{64,32},{96,64},{128,96},{160,128},{192,160},{224,192},{0,2... | collective-permute-start | bytes 147464 | tf_op jit(solution)/shard_map/ppermute | solution.py:571
  42.5 2.1 %collective-permute-done.10.xlo = f32[12,8,128]{2,1,0:T(8,128)S(1)} collective-permute-done((f32[12,8,128]{2,1,0:T(8,128)S(1)}, f32[12,8,128]{2,1,0:T(8,128)S(1)}, u32[]{:S(2)}, u32[]{:S(2)}) %collective-permute-start.10) | collective-permute-done | bytes 49184 | tf_op jit(solution)/shard_map/ppermute | solution.py:570
  44.6 1.3 %collective-permute-done.11.xhi = f32[12,8,128]{2,1,0:T(8,128)S(1)} collective-permute-done((f32[12,8,128]{2,1,0:T(8,128)S(1)}, f32[12,8,128]{2,1,0:T(8,128)S(1)}, u32[]{:S(2)}, u32[]{:S(2)}) %collective-permute-start.11) | collective-permute-done | bytes 49184 | tf_op jit(solution)/shard_map/ppermute | solution.py:571
  46.2 6.7 %collective-permute-done.13.y_next = f32[39,8,128]{2,1,0:T(8,128)S(1)} collective-permute-done((f32[39,8,128]{2,1,0:T(8,128)S(1)}, f32[39,8,128]{2,1,0:T(8,128)S(1)}, u32[]{:S(2)}, u32[]{:S(2)}) %collective-permute-start.13) | collective-permute-done | bytes 159776 | tf_op jit(solution)/shard_map/ppermute | solution.py:580
  52.9 2.6 %coarse_levels.1 = (f32[2,8,8,64]{3,2,1,0:T(8,128)}, f32[2,4,4,32]{3,2,1,0:T(4,128)}) custom-call(s32[2]{0:T(128)S(1)} %pad_add_fusion.place, f32[15,10,128]{2,1,0:T(8,128)S(1)} %get-tuple-element.101.fc_own, f32[12,8,128]{2,1,0:T(8,128)S(1)} %collective-permute-done.10.xlo, f32[12,8,128]{2,1,0:T(8,128)S(1)} %collective-permute-done.11.xhi, ...), custom_call_target="tpu_custom_call" | custom-call | tf_op jit(solution)/shard_map/coarse_levels/pallas_call | solution.py:715
  (36 shorter events, 0.8 us)
Async XLA Ops:
  0.6 5.3 %copy-start.1 = (f32[32,32,256]{2,1,0:T(8,128)S(1)}, f32[32,32,256]{2,1,0:T(8,128)}, u32[]{:S(2)}) copy-start(f32[32,32,256]{2,1,0:T(8,128)} %c.3) | copy-start | bytes 3145732
  0.6 5.3 %copy-start = (f32[2,32,32,256]{3,2,1,0:T(8,128)S(1)}, f32[2,32,32,256]{3,2,1,0:T(8,128)}, u32[]{:S(2)}) copy-start(f32[2,32,32,256]{3,2,1,0:T(8,128)} %f.3) | copy-start | bytes 6291460
  2.6 9.6 %collective-permute-start = (f32[7,32,256]{2,1,0:T(8,128)}, f32[7,32,256]{2,1,0:T(8,128)S(1)}, u32[]{:S(2)}, u32[]{:S(2)}) collective-permute-start(f32[7,32,256]{2,1,0:T(8,128)} %get-tuple-element.56), channel_id=1, source_target_pairs={{0,32},{32,64},{64,96},{96,128},{128,160},{160,192},{192,224},{224... | collective-permute-start | bytes 688136 | tf_op jit(solution)/shard_map/ppermute | solution.py:570
  5.8 8.6 %collective-permute-start.1 = (f32[7,32,256]{2,1,0:T(8,128)}, f32[7,32,256]{2,1,0:T(8,128)}, u32[]{:S(2)}, u32[]{:S(2)}) collective-permute-start(f32[7,32,256]{2,1,0:T(8,128)} %get-tuple-element.57), channel_id=1, source_target_pairs={{32,0},{64,32},{96,64},{128,96},{160,128},{192,160},{224,192},{0,2... | collective-permute-start | bytes 688136 | tf_op jit(solution)/shard_map/ppermute | solution.py:571
  7.1 11.9 %collective-permute-start.2 = (f32[32,8,256]{2,1,0:T(8,128)S(1)}, f32[32,8,256]{2,1,0:T(8,128)S(1)}, u32[]{:S(2)}, u32[]{:S(2)}) collective-permute-start(f32[32,8,256]{2,1,0:T(8,128)S(1)} %get-tuple-element.74), channel_id=1, source_target_pairs={{0,1},{1,0},{2,3},{3,2},{4,5},{5,4},{6,7},{7,6},{8,9},{9,8},{10,11... | collective-permute-start | bytes 786440 | tf_op jit(solution)/shard_map/ppermute | solution.py:580
  7.2 11.8 %collective-permute-start.3 = (f32[32,8,256]{2,1,0:T(8,128)S(1)}, f32[32,8,256]{2,1,0:T(8,128)S(1)}, u32[]{:S(2)}, u32[]{:S(2)}) collective-permute-start(f32[32,8,256]{2,1,0:T(8,128)S(1)} %get-tuple-element.75), channel_id=1, source_target_pairs={{0,32},{1,2},{2,1},{3,4},{4,3},{5,6},{6,5},{7,8},{8,7},{9,10},{10,... | collective-permute-start | bytes 786440 | tf_op jit(solution)/shard_map/ppermute | solution.py:580
  15.8 6.1 %collective-permute-start.4 = (f32[10,4,256]{2,1,0:T(4,128)S(1)}, f32[10,4,256]{2,1,0:T(4,128)S(1)}, u32[]{:S(2)}, u32[]{:S(2)}) collective-permute-start(f32[10,4,256]{2,1,0:T(4,128)S(1)} %get-tuple-element.82), channel_id=1, source_target_pairs={{0,1},{1,0},{2,3},{3,2},{4,5},{5,4},{6,7},{7,6},{8,9},{9,8},{10,11... | collective-permute-start | bytes 122888 | tf_op jit(solution)/shard_map/ppermute | solution.py:580
  15.9 6.0 %collective-permute-start.5 = (f32[10,4,256]{2,1,0:T(4,128)S(1)}, f32[10,4,256]{2,1,0:T(4,128)S(1)}, u32[]{:S(2)}, u32[]{:S(2)}) collective-permute-start(f32[10,4,256]{2,1,0:T(4,128)S(1)} %get-tuple-element.83), channel_id=1, source_target_pairs={{0,32},{1,2},{2,1},{3,4},{4,3},{5,6},{6,5},{7,8},{8,7},{9,10},{10,... | collective-permute-start | bytes 122888 | tf_op jit(solution)/shard_map/ppermute | solution.py:580
  23.0 5.1 %collective-permute-start.6 = (f32[17,16,128]{2,1,0:T(8,128)S(1)}, f32[17,16,128]{2,1,0:T(8,128)S(1)}, u32[]{:S(2)}, u32[]{:S(2)}) collective-permute-start(f32[17,16,128]{2,1,0:T(8,128)S(1)} %pad_maximum_fusion), channel_id=1, source_target_pairs={{0,32},{32,64},{64,96},{96,128},{128,160},{160,192},{192,224},{224... | collective-permute-start | bytes 417800 | tf_op jit(solution)/shard_map/ppermute | solution.py:570
  23.8 6.3 %collective-permute-start.7 = (f32[17,16,128]{2,1,0:T(8,128)S(1)}, f32[17,16,128]{2,1,0:T(8,128)S(1)}, u32[]{:S(2)}, u32[]{:S(2)}) collective-permute-start(f32[17,16,128]{2,1,0:T(8,128)S(1)} %pad_maximum_fusion.1), channel_id=1, source_target_pairs={{32,0},{64,32},{96,64},{128,96},{160,128},{192,160},{224,192},{0,2... | collective-permute-start | bytes 417800 | tf_op jit(solution)/shard_map/ppermute | solution.py:571
  30.7 1.7 %collective-permute-start.8 = (f32[2,26,8,128]{3,2,1,0:T(8,128)S(1)}, f32[2,26,8,128]{3,2,1,0:T(8,128)S(1)}, u32[]{:S(2)}, u32[]{:S(2)}) collective-permute-start(f32[2,26,8,128]{3,2,1,0:T(8,128)S(1)} %get-tuple-element.98), channel_id=1, source_target_pairs={{0,1},{1,0},{2,3},{3,2},{4,5},{5,4},{6,7},{7,6},{8,9},{9,8},{10,11... | collective-permute-start | bytes 638984 | tf_op jit(solution)/shard_map/ppermute | solution.py:580
  30.8 7.6 %collective-permute-start.9 = (f32[2,26,8,128]{3,2,1,0:T(8,128)S(1)}, f32[2,26,8,128]{3,2,1,0:T(8,128)S(1)}, u32[]{:S(2)}, u32[]{:S(2)}) collective-permute-start(f32[2,26,8,128]{3,2,1,0:T(8,128)S(1)} %get-tuple-element.99), channel_id=1, source_target_pairs={{0,32},{1,2},{2,1},{3,4},{4,3},{5,6},{6,5},{7,8},{8,7},{9,10},{10,... | collective-permute-start | bytes 638984 | tf_op jit(solution)/shard_map/ppermute | solution.py:580
  40.4 4.2 %collective-permute-start.10 = (f32[12,8,128]{2,1,0:T(8,128)S(1)}, f32[12,8,128]{2,1,0:T(8,128)S(1)}, u32[]{:S(2)}, u32[]{:S(2)}) collective-permute-start(f32[12,8,128]{2,1,0:T(8,128)S(1)} %pad_maximum_fusion.2), channel_id=1, source_target_pairs={{0,32},{32,64},{64,96},{96,128},{128,160},{160,192},{192,224},{224... | collective-permute-start | bytes 147464 | tf_op jit(solution)/shard_map/ppermute | solution.py:570
  40.5 5.4 %collective-permute-start.11 = (f32[12,8,128]{2,1,0:T(8,128)S(1)}, f32[12,8,128]{2,1,0:T(8,128)S(1)}, u32[]{:S(2)}, u32[]{:S(2)}) collective-permute-start(f32[12,8,128]{2,1,0:T(8,128)S(1)} %pad_maximum_fusion.3), channel_id=1, source_target_pairs={{32,0},{64,32},{96,64},{128,96},{160,128},{192,160},{224,192},{0,2... | collective-permute-start | bytes 147464 | tf_op jit(solution)/shard_map/ppermute | solution.py:571
  46.0 6.9 %collective-permute-start.13 = (f32[39,8,128]{2,1,0:T(8,128)S(1)}, f32[39,8,128]{2,1,0:T(8,128)S(1)}, u32[]{:S(2)}, u32[]{:S(2)}) collective-permute-start(f32[39,8,128]{2,1,0:T(8,128)S(1)} %get-tuple-element.106), channel_id=1, source_target_pairs={{0,32},{1,2},{2,1},{3,4},{4,3},{5,6},{6,5},{7,8},{8,7},{9,10},{10,... | collective-permute-start | bytes 479240 | tf_op jit(solution)/shard_map/ppermute | solution.py:580
  46.2 6.7 %collective-permute-start.12 = (f32[39,8,128]{2,1,0:T(8,128)S(1)}, f32[39,8,128]{2,1,0:T(8,128)S(1)}, u32[]{:S(2)}, u32[]{:S(2)}) collective-permute-start(f32[39,8,128]{2,1,0:T(8,128)S(1)} %get-tuple-element.107), channel_id=1, source_target_pairs={{0,1},{1,0},{2,3},{3,2},{4,5},{5,4},{6,7},{7,6},{8,9},{9,8},{10,11... | collective-permute-start | bytes 479240 | tf_op jit(solution)/shard_map/ppermute | solution.py:580
